TPU v7x, 256 devices: a whole 4x4x8 slice. The times are simulated.
256 devices in a mesh: frame: 64 (over z, x, y_hi), strip: 4 (over y_lo, core).
Axes of the slice: x: 4, y: 4 (y_hi: 2, y_lo: 2; y = y_hi * 2 + y_lo), z: 8, core: 2. Of those that a mesh axis runs over, the one named last changes fastest.
Arguments:
- features: bfloat16 [64, 120, 32, 256], P('frame', None, 'strip'), may hold values from -6 to 6
- w_mutual: bfloat16 [2, 120, 360], replicated, may hold values from -4 to 4
- w_self: bfloat16 [2, 120, 360], replicated, may hold values from -4 to 4
- w_proj: bfloat16 [2, 240, 120], replicated, may hold values from -0.375 to 0.375
- w_gate: bfloat16 [2, 120, 240], replicated, may hold values from -0.5 to 0.5
- w_up: bfloat16 [2, 120, 240], replicated, may hold values from -0.5 to 0.5
- w_down: bfloat16 [2, 240, 120], replicated, may hold values from -0.375 to 0.375
Outputs:
- refined: bfloat16 [64, 120, 32, 256], P('frame', None, 'strip')
All inputs are finite; a program needn't handle non-finite values.
Results may differ from a plain program's by a relative error of at most 0.012.
The roundings to bfloat16 on the way count: a program that leaves them out, or rounds other values in their place, can miss the bound.
Values may be sent and summed in bfloat16 or wider, within the bound.
No kernel may reach another device: no remote copies, remote signals or barrier semaphores. Data moves between devices by JAX's collectives and lax.ppermute only.
A program may use at most 64 MiB of HBM per device.

v0:
```python
import jax
import jax.numpy as jnp
from jax import lax
from jax.sharding import PartitionSpec as P

C = 120
HEADS = 6
HEAD = 20
WIN = 8


epsilon = 1e-05
block_cols = 64


def swapped(block, axis, bit):
    count = lax.axis_size(axis)
    route = []
    for low in range(count):
        high = low | 1 << bit
        if high != low and high < count:
            route += [(low, high), (high, low)]
    return lax.ppermute(block, axis, route)


def from_behind(value, axis, steps):
    count = lax.axis_size(axis)
    pairs = [(source, (source + steps) % count) for source in range(count)]
    return lax.ppermute(value, axis, pairs)


def normed(values):
    centre_mean = jnp.mean(values, axis=0, keepdims=True)
    centred = values - centre_mean
    spread = jnp.mean(centred * centred, axis=0, keepdims=True)
    return (centred * lax.rsqrt(spread + epsilon)).astype(jnp.bfloat16)


def project(weight, values):
    return jnp.einsum("ck,crw->krw", weight, values, preferred_element_type=jnp.float32)


def to_windows(strip_data):
    win_count = strip_data.shape[2] // WIN
    shaped = strip_data.reshape(HEADS, HEAD, WIN, win_count, WIN)
    return shaped.transpose(3, 0, 2, 4, 1).reshape(win_count, HEADS, WIN * WIN, HEAD)


def from_windows(mixed_out):
    win_count = mixed_out.shape[0]
    shaped = mixed_out.reshape(win_count, HEADS, WIN, WIN, HEAD)
    return shaped.transpose(1, 4, 2, 0, 3).reshape(HEADS * HEAD, WIN, win_count * WIN)


def window_mix(queries, key_rows, values):
    scores = jnp.einsum(
        "nhqd,nhkd->nhqk", queries, key_rows, preferred_element_type=jnp.float32
    ) * HEAD ** (-0.5)
    row_max = jnp.max(scores, axis=-1, keepdims=True)
    weights = jnp.exp(scores - row_max)
    weights = (weights / jnp.sum(weights, axis=-1, keepdims=True)).astype(jnp.bfloat16)
    return jnp.einsum(
        "nhqk,nhkd->nhqd", weights, values, preferred_element_type=jnp.float32
    ).astype(jnp.bfloat16)


def attend(own_mut, own_self, other_kv):
    block_count = own_mut.shape[2] // block_cols

    def column_block(position):
        col_start = position * block_cols

        def take_cols(array):
            return lax.dynamic_slice_in_dim(array, col_start, block_cols, 2)

        mutual = window_mix(
            to_windows(take_cols(own_mut[:C])),
            to_windows(take_cols(other_kv[:C])),
            to_windows(take_cols(other_kv[C : 2 * C])),
        )
        key_rows = jnp.concatenate(
            [
                to_windows(take_cols(own_self[C : 2 * C])),
                to_windows(take_cols(other_kv[2 * C : 3 * C])),
            ],
            axis=2,
        )
        value_rows = jnp.concatenate(
            [to_windows(take_cols(own_self[2 * C :])), to_windows(take_cols(other_kv[3 * C :]))],
            axis=2,
        )
        selfish = window_mix(to_windows(take_cols(own_self[:C])), key_rows, value_rows)
        return jnp.concatenate([from_windows(mutual), from_windows(selfish)], axis=0)

    blocks = lax.map(column_block, jnp.arange(block_count, dtype=jnp.int32))
    return blocks.transpose(1, 2, 0, 3).reshape(2 * C, WIN, block_count * block_cols)


def project_all(current, w_mut, w_slf):
    normal_rows = normed(current.astype(jnp.float32))
    return (
        normal_rows,
        project(w_mut, normal_rows).astype(jnp.bfloat16),
        project(w_slf, normal_rows).astype(jnp.bfloat16),
    )


def partner_swap(own_mut, own_self):
    return swapped(jnp.concatenate([own_mut[C:], own_self[C:]], axis=0), "frame", 0)


def finish(current, own_mut, own_self, other_kv, w_prj, w_gte, w_upp, w_dwn):
    joined = attend(own_mut, own_self, other_kv)
    middle = current.astype(jnp.float32) + project(w_prj, joined)
    second_norm = normed(middle)
    hidden = (
        jax.nn.gelu(project(w_gte, second_norm), approximate=False) * project(w_upp, second_norm)
    ).astype(jnp.bfloat16)
    return (middle + project(w_dwn, hidden)).astype(jnp.bfloat16)


def on_device(features, w_mutual, w_self, w_proj, w_gate, w_up, w_down):
    half_win = WIN // 2
    current = features[0]
    norm_one, mut_one, self_one = project_all(current, w_mutual[0], w_self[0])
    partner_one = partner_swap(mut_one, self_one)
    layer_one = finish(
        current, mut_one, self_one, partner_one, w_proj[0], w_gate[0], w_up[0], w_down[0]
    )
    from_below = from_behind(layer_one[:, :half_win], "strip", -1)
    window = jnp.roll(
        jnp.concatenate([layer_one[:, half_win:], from_below], axis=1), -half_win, axis=2
    )
    moved = from_behind(window, "frame", -1)
    norm_two, mut_two, self_two = project_all(moved, w_mutual[1], w_self[1])
    partner_two = partner_swap(mut_two, self_two)
    result_two = finish(
        moved, mut_two, self_two, partner_two, w_proj[1], w_gate[1], w_up[1], w_down[1]
    )
    layer_two = from_behind(result_two, "frame", 1)
    layer_two = jnp.roll(layer_two, half_win, axis=2)
    from_above = from_behind(layer_two[:, half_win:], "strip", 1)
    return jnp.concatenate([from_above, layer_two[:, :half_win]], axis=1)[None]


def solution(mesh):
    in_specs = (P("frame", None, "strip", None), P(), P(), P(), P(), P(), P())
    out_specs = P("frame", None, "strip", None)
    return jax.shard_map(
        on_device, mesh=mesh, in_specs=in_specs, out_specs=out_specs, check_vma=False
    )
```

profile of v0, /device:TPU:1, one launch (start us, length us, event | category | flops | bytes accessed | tf_op | source)
XLA Modules:
  0.0 439.1 jit_solution(16847717767155564338)
XLA Ops:
  2.4 1.7 fusion.147
  4.8 1.4 pad_maximum_fusion
  6.2 3.7 collective-permute-start
  10.0 1.6 copy.79
  11.6 1.6 copy.77
  13.1 38.7 %collective-permute-done = bf16[480,8,256]{2,0,1:T(8,128)(2,1)} collective-permute-done((bf16[480,8,256]{2,0,1:T(8,128)(2,1)}, bf16[480,8,256]{2,0,1:T(8,128)(2,1)}, u32[]{:S(2)}, u32[]{:S(2)}) %collective-permute-start) | collective-permute-done | bytes 1966112 | tf_op jit(solution)/shard_map/ppermute | solution.py:23
  51.8 3.9 copy.78
  56.8 128.6 %while.20 = (s32[]{:T(128)}, bf16[4,240,8,64]{1,3,2,0:T(8,128)(2,1)}, bf16[360,8,256]{0,2,1:T(8,128)(2,1)}, s32[4]{0:T(128)S(1)}, bf16[480,8,256]{0,2,1:T(8,128)...) while((s32[]{:T(128)}, bf16[4,240,8,64]{1,3,2,0:T(8,128)(2,1)}, ...), condition=%wide.region_7.8_spmd, body=%wide.region_2.7_spmd.sunk | while | flops 77003136 | bytes 20193540 | solution.py:95
  59.8 3.9 fusion.409
  65.2 1.7 convolution_multiply_fusion.6
  67.4 2.5 convolution_convert_fusion.13
  78.3 2.1 fusion.410
  80.4 5.7 %convolution_convert_fusion.12 = bf16[8,6,64,20]{2,3,1,0:T(8,128)(2,1)S(1)} fusion(f32[8,6,64]{2,1,0:T(8,128)S(1)} %fusion.410, bf16[8,6,64,20]{2,3,1,0:T(8,128)(2,1)S(1)} %copy-done.1, bf16[8,6,64,20]{2,3,1,0:T(8,128)(2,1)S(1)} %copy.265, bf16[8,6,8,8,20]{4,1,3,0,2:T(8,128)(2,1)S(1)} %bitcast.558, bf16[8,6,64,20]{2,3,1,0:T(8,128)(2,1)S(1)} %copy-done.3, ...), kind=kOutput, calls=%fused_computation.11.clone.1 | convolution fusion | flops 34077824 | bytes 749568 | tf_op jit(solution)/shard_map/while/body/eval_jaxpr/nhqk,nhkd->nhqd/dot_general | solution.py:62
  91.9 3.9 fusion.409
  97.2 1.7 convolution_multiply_fusion.6
  99.4 2.5 convolution_convert_fusion.13
  110.4 2.1 fusion.410
  112.5 5.7 %convolution_convert_fusion.12 = bf16[8,6,64,20]{2,3,1,0:T(8,128)(2,1)S(1)} fusion(f32[8,6,64]{2,1,0:T(8,128)S(1)} %fusion.410, bf16[8,6,64,20]{2,3,1,0:T(8,128)(2,1)S(1)} %copy-done.1, bf16[8,6,64,20]{2,3,1,0:T(8,128)(2,1)S(1)} %copy.265, bf16[8,6,8,8,20]{4,1,3,0,2:T(8,128)(2,1)S(1)} %bitcast.558, bf16[8,6,64,20]{2,3,1,0:T(8,128)(2,1)S(1)} %copy-done.3, ...), kind=kOutput, calls=%fused_computation.11.clone.1 | convolution fusion | flops 34077824 | bytes 749568 | tf_op jit(solution)/shard_map/while/body/eval_jaxpr/nhqk,nhkd->nhqd/dot_general | solution.py:62
  123.9 3.9 fusion.409
  129.2 1.7 convolution_multiply_fusion.6
  131.4 2.5 convolution_convert_fusion.13
  142.4 2.1 fusion.410
  144.5 5.7 %convolution_convert_fusion.12 = bf16[8,6,64,20]{2,3,1,0:T(8,128)(2,1)S(1)} fusion(f32[8,6,64]{2,1,0:T(8,128)S(1)} %fusion.410, bf16[8,6,64,20]{2,3,1,0:T(8,128)(2,1)S(1)} %copy-done.1, bf16[8,6,64,20]{2,3,1,0:T(8,128)(2,1)S(1)} %copy.265, bf16[8,6,8,8,20]{4,1,3,0,2:T(8,128)(2,1)S(1)} %bitcast.558, bf16[8,6,64,20]{2,3,1,0:T(8,128)(2,1)S(1)} %copy-done.3, ...), kind=kOutput, calls=%fused_computation.11.clone.1 | convolution fusion | flops 34077824 | bytes 749568 | tf_op jit(solution)/shard_map/while/body/eval_jaxpr/nhqk,nhkd->nhqd/dot_general | solution.py:62
  155.9 3.9 fusion.409
  161.2 1.7 convolution_multiply_fusion.6
  163.4 2.5 convolution_convert_fusion.13
  174.4 2.1 fusion.410
  176.5 5.7 %convolution_convert_fusion.12 = bf16[8,6,64,20]{2,3,1,0:T(8,128)(2,1)S(1)} fusion(f32[8,6,64]{2,1,0:T(8,128)S(1)} %fusion.410, bf16[8,6,64,20]{2,3,1,0:T(8,128)(2,1)S(1)} %copy-done.1, bf16[8,6,64,20]{2,3,1,0:T(8,128)(2,1)S(1)} %copy.265, bf16[8,6,8,8,20]{4,1,3,0,2:T(8,128)(2,1)S(1)} %bitcast.558, bf16[8,6,64,20]{2,3,1,0:T(8,128)(2,1)S(1)} %copy-done.3, ...), kind=kOutput, calls=%fused_computation.11.clone.1 | convolution fusion | flops 34077824 | bytes 749568 | tf_op jit(solution)/shard_map/while/body/eval_jaxpr/nhqk,nhkd->nhqd/dot_general | solution.py:62
  185.4 1.3 copy.80
  188.1 5.9 %fusion.153 = bf16[120,8,256]{2,0,1:T(8,128)(2,1)S(1)} fusion(f32[120,8,256]{2,0,1:T(8,128)S(1)} %get-tuple-element.142, f32[8,256,240]{1,2,0:T(8,128)S(1)} %fusion.224, f32[8,256]{1,0:T(8,128)S(1)} %add_rsqrt_fusion.2, f32[8,256]{1,0:T(8,128)S(1)} %broadcast_multiply_fusion.2, bf16[2,240,120]{2,1,0:T(8,128)(2,1)} %param.17, bf16[2,120,240]{2,1,0:T(8,128)(2,1)} %param.15), kind=kOutput, calls=%fused_computation.171 | convolution fusion | flops 269598720 | bytes 4562944 | tf_op jit(solution)/shard_map/ck,crw->krw/dot_general | solution.py:40
  194.0 2.4 collective-permute-start.1
  196.4 5.1 %collective-permute-done.1 = bf16[120,4,256]{2,0,1:T(8,128)(2,1)S(1)} collective-permute-done((bf16[120,4,256]{2,0,1:T(8,128)(2,1)S(1)}, bf16[120,4,256]{2,0,1:T(8,128)(2,1)S(1)}, u32[]{:S(2)}, u32[]{:S(2)}) %collective-permute-start.1) | collective-permute-done | bytes 245792 | tf_op jit(solution)/shard_map/ppermute | solution.py:29
  201.9 10.2 %collective-permute-start.2 = (bf16[120,8,256]{2,0,1:T(8,128)(2,1)S(1)}, bf16[120,8,256]{2,0,1:T(8,128)(2,1)S(1)}, u32[]{:S(2)}, u32[]{:S(2)}) collective-permute-start(bf16[120,8,256]{2,0,1:T(8,128)(2,1)S(1)} %fusion.229), channel_id=1, source_target_pairs={{0,252},{4,0},{8,4},{12,8},{16,12},{20,16},{24,20},{28,24},{32,28}... | collective-permute-start | bytes 1474568 | tf_op jit(solution)/shard_map/ppermute | solution.py:29
  212.1 10.5 %collective-permute-done.2 = bf16[120,8,256]{2,0,1:T(8,128)(2,1)S(1)} collective-permute-done((bf16[120,8,256]{2,0,1:T(8,128)(2,1)S(1)}, bf16[120,8,256]{2,0,1:T(8,128)(2,1)S(1)}, u32[]{:S(2)}, u32[]{:S(2)}) %collective-permute-start.2) | collective-permute-done | bytes 491552 | tf_op jit(solution)/shard_map/ppermute | solution.py:29
  224.4 1.4 pad_maximum_fusion.1
  225.8 1.6 copy.89
  227.4 1.6 copy.87
  229.0 43.2 %collective-permute-done.3 = bf16[480,8,256]{2,0,1:T(8,128)(2,1)} collective-permute-done((bf16[480,8,256]{2,0,1:T(8,128)(2,1)}, bf16[480,8,256]{2,0,1:T(8,128)(2,1)}, u32[]{:S(2)}, u32[]{:S(2)}) %collective-permute-start.3) | collective-permute-done | bytes 1966112 | tf_op jit(solution)/shard_map/ppermute | solution.py:23
  272.2 3.9 copy.88
  277.1 128.4 %while.21 = (s32[]{:T(128)}, bf16[4,240,8,64]{1,3,2,0:T(8,128)(2,1)}, bf16[360,8,256]{0,2,1:T(8,128)(2,1)}, s32[4]{0:T(128)S(1)}, bf16[480,8,256]{0,2,1:T(8,128)...) while((s32[]{:T(128)}, ...), condition=%wide.region_17.18_spmd, body=%wide.region_12.17_spmd.sunk | while | flops 77003136 | bytes 20193540 | solution.py:95
  280.2 3.9 fusion.424
  285.5 1.7 convolution_multiply_fusion.7
  287.8 2.5 convolution_convert_fusion.15
  298.7 2.1 fusion.425
  300.8 5.7 %convolution_convert_fusion.14 = bf16[8,6,64,20]{2,3,1,0:T(8,128)(2,1)S(1)} fusion(f32[8,6,64]{2,1,0:T(8,128)S(1)} %fusion.425, bf16[8,6,64,20]{2,3,1,0:T(8,128)(2,1)S(1)} %copy-done.2, bf16[8,6,64,20]{2,3,1,0:T(8,128)(2,1)S(1)} %copy.284, bf16[8,6,8,8,20]{4,1,3,0,2:T(8,128)(2,1)S(1)} %bitcast.560, bf16[8,6,64,20]{2,3,1,0:T(8,128)(2,1)S(1)} %copy-done.4, ...), kind=kOutput, calls=%fused_computation.60.clone.1 | convolution fusion | flops 34077824 | bytes 749568 | tf_op jit(solution)/shard_map/while/body/eval_jaxpr/nhqk,nhkd->nhqd/dot_general | solution.py:62
  312.2 3.9 fusion.424
  317.6 1.7 convolution_multiply_fusion.7
  319.8 2.5 convolution_convert_fusion.15
  330.7 2.1 fusion.425
  332.8 5.7 %convolution_convert_fusion.14 = bf16[8,6,64,20]{2,3,1,0:T(8,128)(2,1)S(1)} fusion(f32[8,6,64]{2,1,0:T(8,128)S(1)} %fusion.425, bf16[8,6,64,20]{2,3,1,0:T(8,128)(2,1)S(1)} %copy-done.2, bf16[8,6,64,20]{2,3,1,0:T(8,128)(2,1)S(1)} %copy.284, bf16[8,6,8,8,20]{4,1,3,0,2:T(8,128)(2,1)S(1)} %bitcast.560, bf16[8,6,64,20]{2,3,1,0:T(8,128)(2,1)S(1)} %copy-done.4, ...), kind=kOutput, calls=%fused_computation.60.clone.1 | convolution fusion | flops 34077824 | bytes 749568 | tf_op jit(solution)/shard_map/while/body/eval_jaxpr/nhqk,nhkd->nhqd/dot_general | solution.py:62
  344.2 3.9 fusion.424
  349.6 1.7 convolution_multiply_fusion.7
  351.8 2.5 convolution_convert_fusion.15
  362.7 2.1 fusion.425
  364.8 5.7 %convolution_convert_fusion.14 = bf16[8,6,64,20]{2,3,1,0:T(8,128)(2,1)S(1)} fusion(f32[8,6,64]{2,1,0:T(8,128)S(1)} %fusion.425, bf16[8,6,64,20]{2,3,1,0:T(8,128)(2,1)S(1)} %copy-done.2, bf16[8,6,64,20]{2,3,1,0:T(8,128)(2,1)S(1)} %copy.284, bf16[8,6,8,8,20]{4,1,3,0,2:T(8,128)(2,1)S(1)} %bitcast.560, bf16[8,6,64,20]{2,3,1,0:T(8,128)(2,1)S(1)} %copy-done.4, ...), kind=kOutput, calls=%fused_computation.60.clone.1 | convolution fusion | flops 34077824 | bytes 749568 | tf_op jit(solution)/shard_map/while/body/eval_jaxpr/nhqk,nhkd->nhqd/dot_general | solution.py:62
  376.2 3.9 fusion.424
  381.6 1.7 convolution_multiply_fusion.7
  383.8 2.5 convolution_convert_fusion.15
  394.7 2.1 fusion.425
  396.9 5.7 %convolution_convert_fusion.14 = bf16[8,6,64,20]{2,3,1,0:T(8,128)(2,1)S(1)} fusion(f32[8,6,64]{2,1,0:T(8,128)S(1)} %fusion.425, bf16[8,6,64,20]{2,3,1,0:T(8,128)(2,1)S(1)} %copy-done.2, bf16[8,6,64,20]{2,3,1,0:T(8,128)(2,1)S(1)} %copy.284, bf16[8,6,8,8,20]{4,1,3,0,2:T(8,128)(2,1)S(1)} %bitcast.560, bf16[8,6,64,20]{2,3,1,0:T(8,128)(2,1)S(1)} %copy-done.4, ...), kind=kOutput, calls=%fused_computation.60.clone.1 | convolution fusion | flops 34077824 | bytes 749568 | tf_op jit(solution)/shard_map/while/body/eval_jaxpr/nhqk,nhkd->nhqd/dot_general | solution.py:62
  408.4 5.8 %fusion.154 = bf16[120,8,256]{2,0,1:T(8,128)(2,1)} fusion(f32[120,8,256]{2,0,1:T(8,128)S(1)} %get-tuple-element.144, f32[8,256,240]{1,2,0:T(8,128)S(1)} %fusion.225, f32[8,256]{1,0:T(8,128)S(1)} %add_rsqrt_fusion, f32[8,256]{1,0:T(8,128)S(1)} %broadcast_multiply_fusion, bf16[2,240,120]{2,1,0:T(8,128)(2,1)S(1)} %copy-done.12, ...), kind=kOutput, calls=%fused_computation.172 | convolution fusion | flops 269598720 | bytes 4562944 | tf_op jit(solution)/shard_map/ck,crw->krw/dot_general | solution.py:40
  414.5 17.9 %collective-permute-done.4 = bf16[120,8,256]{2,0,1:T(8,128)(2,1)S(1)} collective-permute-done((bf16[120,8,256]{2,0,1:T(8,128)(2,1)}, bf16[120,8,256]{2,0,1:T(8,128)(2,1)S(1)}, u32[]{:S(2)}, u32[]{:S(2)}) %collective-permute-start.4) | collective-permute-done | bytes 491552 | tf_op jit(solution)/shard_map/ppermute | solution.py:29
  432.7 2.0 collective-permute-start.5
  434.7 3.1 collective-permute-done.5
  (363 shorter events, 135.5 us)
Async XLA Ops:
  2.3 1.8 copy-start
  2.4 1.8 copy-start.6
  6.2 45.5 %collective-permute-start = (bf16[480,8,256]{2,0,1:T(8,128)(2,1)}, bf16[480,8,256]{2,0,1:T(8,128)(2,1)}, u32[]{:S(2)}, u32[]{:S(2)}) collective-permute-start(bf16[480,8,256]{2,0,1:T(8,128)(2,1)} %pad_maximum_fusion), channel_id=1, source_target_pairs={{0,4},{4,0},{8,12},{12,8},{16,20},{20,16},{24,28},{28,24},{32,36},... | collective-permute-start | bytes 5898248 | tf_op jit(solution)/shard_map/ppermute | solution.py:23
  77.8 2.6 copy-start.1
  77.8 2.6 copy-start.3
  109.8 2.6 copy-start.1
  109.8 2.7 copy-start.3
  141.8 2.6 copy-start.1
  141.8 2.6 copy-start.3
  173.8 2.6 copy-start.1
  173.8 2.7 copy-start.3
  185.4 1.4 copy-start.8
  186.7 0.9 copy-start.10
  194.0 28.8 %copy-start.5 = (bf16[2,120,360]{2,1,0:T(8,128)(2,1)S(1)}, bf16[2,120,360]{2,1,0:T(8,128)(2,1)}, u32[]{:S(2)}) copy-start(bf16[2,120,360]{2,1,0:T(8,128)(2,1)} %param.13) | copy-start | bytes 518404
  194.0 7.5 %collective-permute-start.1 = (bf16[120,4,256]{2,0,1:T(8,128)(2,1)S(1)}, bf16[120,4,256]{2,0,1:T(8,128)(2,1)S(1)}, u32[]{:S(2)}, u32[]{:S(2)}) collective-permute-start(bf16[120,4,256]{2,0,1:T(8,128)(2,1)S(1)} %get-tuple-element.140), channel_id=1, source_target_pairs={{0,3},{1,0},{2,1},{3,2},{4,7},{5,4},{6,5},{7,6},{8,11},{9,8},{10,9... | collective-permute-start | bytes 737288 | tf_op jit(solution)/shard_map/ppermute | solution.py:29
  201.9 20.6 %collective-permute-start.2 = (bf16[120,8,256]{2,0,1:T(8,128)(2,1)S(1)}, bf16[120,8,256]{2,0,1:T(8,128)(2,1)S(1)}, u32[]{:S(2)}, u32[]{:S(2)}) collective-permute-start(bf16[120,8,256]{2,0,1:T(8,128)(2,1)S(1)} %fusion.229), channel_id=1, source_target_pairs={{0,252},{4,0},{8,4},{12,8},{16,12},{20,16},{24,20},{28,24},{32,28}... | collective-permute-start | bytes 1474568 | tf_op jit(solution)/shard_map/ppermute | solution.py:29
  222.8 0.9 copy-start.7
  225.8 46.3 %collective-permute-start.3 = (bf16[480,8,256]{2,0,1:T(8,128)(2,1)}, bf16[480,8,256]{2,0,1:T(8,128)(2,1)}, u32[]{:S(2)}, u32[]{:S(2)}) collective-permute-start(bf16[480,8,256]{2,0,1:T(8,128)(2,1)} %pad_maximum_fusion.1), channel_id=1, source_target_pairs={{0,4},{4,0},{8,12},{12,8},{16,20},{20,16},{24,28},{28,24},{32,36},... | collective-permute-start | bytes 5898248 | tf_op jit(solution)/shard_map/ppermute | solution.py:23
  298.1 2.6 copy-start.2
  298.1 2.6 copy-start.4
  330.2 2.6 copy-start.2
  330.2 2.7 copy-start.4
  362.2 2.6 copy-start.2
  362.2 2.6 copy-start.4
  394.2 2.6 copy-start.2
  394.2 2.7 copy-start.4
  405.6 1.4 copy-start.9
  406.9 0.9 copy-start.11
  407.4 0.9 copy-start.12
  407.4 1.0 copy-start.13
  414.2 18.2 %collective-permute-start.4 = (bf16[120,8,256]{2,0,1:T(8,128)(2,1)}, bf16[120,8,256]{2,0,1:T(8,128)(2,1)S(1)}, u32[]{:S(2)}, u32[]{:S(2)}) collective-permute-start(bf16[120,8,256]{2,0,1:T(8,128)(2,1)} %fusion.154), channel_id=1, source_target_pairs={{0,4},{4,8},{8,12},{12,16},{16,20},{20,24},{24,28},{28,32},{32,36}... | collective-permute-start | bytes 1474568 | tf_op jit(solution)/shard_map/ppermute | solution.py:29
  432.7 5.1 %collective-permute-start.5 = (bf16[120,4,256]{2,0,1:T(8,128)(2,1)S(1)}, bf16[120,4,256]{2,0,1:T(8,128)(2,1)S(1)}, u32[]{:S(2)}, u32[]{:S(2)}) collective-permute-start(bf16[120,4,256]{2,0,1:T(8,128)(2,1)S(1)} %fusion.248), channel_id=1, source_target_pairs={{0,1},{1,2},{2,3},{3,0},{4,5},{5,6},{6,7},{7,4},{8,9},{9,10},{10,1... | collective-permute-start | bytes 737288 | tf_op jit(solution)/shard_map/ppermute | solution.py:29
where the time goes:
time: 443 us; the launch traced here: 439 us
  local copies, waits for them, and re-layouts  161 us (36%)
  matrix products  119 us (27%)
  waiting for transfers between devices  118 us (27%)
  starting transfers between devices  18.6 us (4%)
  other arithmetic  13.1 us (3%)
  loops' own time  8.09 us (2%)
    ppermute x2, waiting for transfers between devices, swapped(): return lax.ppermute(block, axis, route)  81.9 us
    dot_general x16, matrix products, window_mix(): jnp.einsum('nhqk,nhkd->nhqd', weights, values, preferred_element_type=jnp...  65.4 us
    ppermute x4, waiting for transfers between devices, from_behind(): return lax.ppermute(value, axis, pairs)  36.6 us
    reshape x64, local copies, waits for them, and re-layouts, to_windows(): shaped = strip_data.reshape(HEADS, HEAD, WIN, win_count, WIN)  34 us
    slice x8, local copies, waits for them, and re-layouts, column_block(): other_kv[:C]  30.9 us
    reshape x32, local copies, waits for them, and re-layouts, to_windows(): shaped.transpose(3, 0, 2, 4, 1).reshape(win_count, HEADS, WIN * WIN, HEAD)  23.9 us
    sub x16, matrix products, window_mix(): weights = jnp.exp(scores - row_max)  22.8 us
    dot_general x10, matrix products, project(): jnp.einsum('ck,crw->krw', weight, values, preferred_element_type=jnp.floa...  17 us
  transfers between devices with their start and end apart: 6, of which 6 were waited for; matrix products, arithmetic and copies ran while one was open for 1% of the time, Pallas kernels for 0%

commit v1 on v0

v1 whole, which is shorter than its diff:
```python
import jax
import jax.numpy as jnp
import numpy as np
from jax import lax
from jax.experimental import pallas as pl
from jax.experimental.pallas import tpu as pltpu
from jax.sharding import PartitionSpec as P

C = 120
HEADS = 6
HEAD = 20
FFN = 240
WIN = 8
LANES = 128
VHEAD = 24
HALF = 16
TOK = WIN * WIN
EPS = 1e-05
EXP2_SCALE = float(np.log2(np.e) * HEAD**-0.5)
VMEM_LIMIT = 56 * 1024 * 1024


def matmul(a, b):
    return lax.dot_general(a, b, (((1,), (0,)), ((), ())), preferred_element_type=jnp.float32)


def matmul_nt(a, b):
    return lax.dot_general(a, b, (((1,), (1,)), ((), ())), preferred_element_type=jnp.float32)


def matmul_tn(a, b):
    return lax.dot_general(a, b, (((0,), (0,)), ((), ())), preferred_element_type=jnp.float32)


def normed(x):
    lane = lax.broadcasted_iota(jnp.int32, x.shape, 1)
    mean = jnp.sum(x, axis=1, keepdims=True) * (1.0 / C)
    centred = jnp.where(lane < C, x - mean, 0.0)
    spread = jnp.sum(centred * centred, axis=1, keepdims=True) * (1.0 / C)
    return (centred * lax.rsqrt(spread + EPS)).astype(jnp.bfloat16)


def head_only(q_t, head):
    low = head * HEAD // 16 * 16
    high = -(-(head * HEAD + HEAD) // 16) * 16
    part = q_t[low:high].astype(jnp.float32)
    row = lax.broadcasted_iota(jnp.int32, part.shape, 0) + low
    keep = (row >= head * HEAD) & (row < head * HEAD + HEAD)
    part = jnp.where(keep, part, 0.0).astype(jnp.bfloat16)
    pieces = [part]
    if low:
        pieces.insert(0, jnp.zeros((low, q_t.shape[1]), jnp.bfloat16))
    if high < LANES:
        pieces.append(jnp.zeros((LANES - high, q_t.shape[1]), jnp.bfloat16))
    return jnp.concatenate(pieces, axis=0)


def softmax_rows(scores):
    top = jnp.max(scores, axis=0, keepdims=True)
    weights = jnp.exp2((scores - top) * EXP2_SCALE)
    total = jnp.sum(weights, axis=0, keepdims=True)
    return weights * (1.0 / total)


def attend(keys, q_t, v_t):
    outs = []
    lane = lax.broadcasted_iota(jnp.int32, (TOK, 2 * LANES), 1)
    of_first = (lane % LANES) < TOK
    for kind in range(2):
        kind_keys = keys[:, kind * LANES : (kind + 1) * LANES]
        kind_q = q_t[kind * LANES : (kind + 1) * LANES]
        for pair in range(HEADS // 2):
            queries = jnp.concatenate(
                [head_only(kind_q, 2 * pair), head_only(kind_q, 2 * pair + 1)], axis=1
            )
            scores = matmul(kind_keys, queries)
            if kind == 0:
                probs = softmax_rows(jnp.where(of_first, scores[TOK:], scores[:TOK]))
                probs = jnp.concatenate(
                    [jnp.where(of_first, 0.0, probs), jnp.where(of_first, probs, 0.0)], axis=0
                )
            else:
                probs = softmax_rows(scores)
            base = kind * HEADS * VHEAD + pair * 2 * VHEAD
            mixed = matmul(v_t[base : base + 2 * VHEAD], probs.astype(jnp.bfloat16))
            outs += [mixed[:VHEAD, :LANES], mixed[VHEAD:, LANES:]]
    return jnp.concatenate(outs, axis=0).astype(jnp.bfloat16)


def layer_tokens(x, w_k, w_qv, w_prj, w_gu, w_dwn):
    count = x.shape[0] // LANES
    normal = normed(x)
    keys = matmul(normal, w_k).astype(jnp.bfloat16)
    qv_t = matmul_nt(w_qv, normal).astype(jnp.bfloat16)
    middles = []
    for i in range(count):
        span = slice(i * LANES, (i + 1) * LANES)
        joined = attend(keys[span], qv_t[: 2 * LANES, span], qv_t[2 * LANES :, span])
        middles.append(x[span] + matmul_tn(joined, w_prj))
    middle = jnp.concatenate(middles, axis=0)
    both = matmul(normed(middle), w_gu)
    gate, up = both[:, : 2 * LANES], both[:, 2 * LANES :]
    gelu = 0.5 * gate * (1.0 + lax.erf(gate * float(np.sqrt(0.5))))
    hidden = (gelu * up).astype(jnp.bfloat16)
    return middle + matmul(hidden, w_dwn)


def to_tokens_kernel(h_ref, x_ref, send_ref, own_ref, wide, tiles):
    h = h_ref[0]
    wide[...] = x_ref[...].astype(jnp.float32)
    pad = jnp.zeros((LANES - C, LANES), jnp.float32)
    for k in range(2):
        half = 1 - h if k == 0 else h
        col = pl.multiple_of(half * LANES, LANES)
        for r in range(WIN):
            block = wide[:, r, pl.ds(col, LANES)]
            block = jnp.concatenate([block, pad], axis=0).T
            tiles[k, :HALF, r] = block.reshape(HALF, WIN, LANES)
    for k, ref in enumerate((send_ref, own_ref)):
        main = tiles[k, :HALF].reshape(HALF * TOK, LANES)
        ref[: HALF * TOK] = main.astype(jnp.bfloat16)
        ref[HALF * TOK :] = tiles[1 - k, 0].reshape(TOK, LANES).astype(jnp.bfloat16)


def layer_one_kernel(own_ref, oth_ref, w_k, w_qv, w_prj, w_gu, w_dwn, *rest):
    outs, (flat, tiles) = rest[:4], rest[4:]
    weights = (w_k, w_qv, w_prj, w_gu, w_dwn)

    def work(first, count):
        parts = []
        for i in range(count):
            start = pl.multiple_of((first + i) * TOK, TOK)
            parts += [own_ref[pl.ds(start, TOK)], oth_ref[pl.ds(start, TOK)]]
        x = jnp.concatenate(parts, axis=0).astype(jnp.float32)
        y = layer_tokens(x, *[w[...] for w in weights])
        y = y.reshape(count, 2, WIN, WIN, LANES)
        for i in range(count):
            col = pl.multiple_of((first + i) * WIN, WIN)
            for f in range(2):
                flat[f, :, pl.ds(col, WIN), :] = y[i, f]

    def body(step, carry):
        work(step * 2, 2)
        return carry

    lax.fori_loop(0, HALF // 2, body, 0)
    work(HALF, 1)
    for f in range(2):
        for r in range(WIN):
            block = flat[f, r, WIN // 2 : WIN // 2 + LANES, :]
            tiles[f, r // 4, :, r % 4] = block.reshape(HALF, WIN, LANES)
        for k in range(2):
            piece = tiles[f, k].reshape(HALF * TOK // 2, LANES)
            outs[2 * f + k][...] = piece.astype(jnp.bfloat16)


def layer_two_kernel(own_lo, own_up, oth_lo, oth_up, w_k, w_qv, w_prj, w_gu, w_dwn, *outs):
    weights = (w_k, w_qv, w_prj, w_gu, w_dwn)
    ins = (own_lo, own_up, oth_lo, oth_up)
    half_tok = TOK // 2

    def body(step, carry):
        parts = []
        starts = []
        for i in range(2):
            start = pl.multiple_of((step * 2 + i) * half_tok, half_tok)
            starts.append(start)
            parts += [ref[pl.ds(start, half_tok)] for ref in ins]
        x = jnp.concatenate(parts, axis=0).astype(jnp.float32)
        y = layer_tokens(x, *[w[...] for w in weights]).astype(jnp.bfloat16)
        for i in range(2):
            for j in range(4):
                low = i * LANES + j * half_tok
                outs[j][pl.ds(starts[i], half_tok)] = y[low : low + half_tok]
        return carry

    lax.fori_loop(0, HALF // 2, body, 0)


def from_tokens_kernel(h_ref, own_lo, own_up, oth_lo, oth_up, out_ref, tiles, wide):
    h = h_ref[0]
    for j, ref in enumerate((own_lo, own_up, oth_lo, oth_up)):
        half = h if j < 2 else 1 - h
        tiles[half, j % 2] = ref[...].astype(jnp.float32).reshape(HALF, 4, WIN, LANES)
    for r in range(WIN):
        lo = 0 if r >= 4 else 1
        row = [tiles[half, lo, :, r % 4].reshape(LANES, LANES).T for half in range(2)]
        row = pltpu.roll(jnp.concatenate(row, axis=1), WIN // 2, 1)
        wide[:, r, :] = row[:C]
    out_ref[...] = wide[...].astype(jnp.bfloat16)


VMEM = pl.BlockSpec(memory_space=pltpu.VMEM)
SMEM = pl.BlockSpec(memory_space=pltpu.SMEM)
PARAMS = pltpu.CompilerParams(vmem_limit_bytes=VMEM_LIMIT)


def tokens_shape(rows):
    return jax.ShapeDtypeStruct((rows, LANES), jnp.bfloat16)


def to_tokens(h, x):
    rows = (HALF + 1) * TOK
    return pl.pallas_call(
        to_tokens_kernel,
        out_shape=[tokens_shape(rows)] * 2,
        in_specs=[SMEM, VMEM],
        out_specs=[VMEM] * 2,
        scratch_shapes=[
            pltpu.VMEM((C, WIN, 2 * LANES), jnp.float32),
            pltpu.VMEM((2, HALF, WIN, WIN, LANES), jnp.float32),
        ],
        compiler_params=PARAMS,
        name="to_tokens",
    )(h, x)


def layer_one(own, oth, weights):
    return pl.pallas_call(
        layer_one_kernel,
        out_shape=[tokens_shape(HALF * TOK // 2)] * 4,
        in_specs=[VMEM] * 7,
        out_specs=[VMEM] * 4,
        scratch_shapes=[
            pltpu.VMEM((2, WIN, (HALF + 1) * WIN, LANES), jnp.float32),
            pltpu.VMEM((2, 2, HALF, 4, WIN, LANES), jnp.float32),
        ],
        compiler_params=PARAMS,
        name="layer_one",
    )(own, oth, *weights)


def layer_two(pieces, weights):
    return pl.pallas_call(
        layer_two_kernel,
        out_shape=[tokens_shape(HALF * TOK // 2)] * 4,
        in_specs=[VMEM] * 9,
        out_specs=[VMEM] * 4,
        compiler_params=PARAMS,
        name="layer_two",
    )(*pieces, *weights)


def from_tokens(h, pieces):
    return pl.pallas_call(
        from_tokens_kernel,
        out_shape=jax.ShapeDtypeStruct((C, WIN, 2 * LANES), jnp.bfloat16),
        in_specs=[SMEM] + [VMEM] * 4,
        out_specs=VMEM,
        scratch_shapes=[
            pltpu.VMEM((2, 2, HALF, 4, WIN, LANES), jnp.float32),
            pltpu.VMEM((C, WIN, 2 * LANES), jnp.float32),
        ],
        compiler_params=PARAMS,
        name="from_tokens",
    )(h, *pieces)


def pad_to(array, rows, cols):
    return jnp.pad(array, ((0, rows - array.shape[0]), (0, cols - array.shape[1])))


def by_head(array):
    spread = array.reshape(HEADS, HEAD, array.shape[1])
    spread = jnp.pad(spread, ((0, 0), (0, VHEAD - HEAD), (0, 0)))
    return spread.reshape(HEADS * VHEAD, array.shape[1])


def prepared(w_mut, w_slf, w_prj, w_gte, w_upp, w_dwn):
    w_k = [pad_to(w[:, C : 2 * C], LANES, LANES) for w in (w_mut, w_slf)]
    w_q = [pad_to(w[:, :C].T, LANES, LANES) for w in (w_mut, w_slf)]
    w_v = [pad_to(by_head(w[:, 2 * C :].T), HEADS * VHEAD, LANES) for w in (w_mut, w_slf)]
    w_p = [pad_to(by_head(w), HEADS * VHEAD, LANES) for w in (w_prj[:C], w_prj[C:])]
    return (
        jnp.concatenate(w_k, axis=1),
        jnp.concatenate(w_q + w_v, axis=0),
        jnp.concatenate(w_p, axis=0),
        jnp.concatenate([pad_to(w, LANES, 2 * LANES) for w in (w_gte, w_upp)], axis=1),
        pad_to(w_dwn, 2 * LANES, LANES),
    )


def on_device(features, *weights):
    frames, strips = lax.axis_size("frame"), lax.axis_size("strip")

    def route(frame_step, strip_step):
        pairs = []
        for f in range(frames):
            for s in range(strips):
                to = (f + frame_step * (1 - 2 * (f % 2))) % frames
                pairs.append((f * strips + s, to * strips + (s + strip_step) % strips))
        return pairs

    def send(value, frame_step, strip_step):
        return lax.ppermute(value, ("frame", "strip"), route(frame_step, strip_step))

    h = (lax.axis_index("frame") % 2).astype(jnp.int32).reshape(1)
    w_one = prepared(*[w[0] for w in weights])
    w_two = prepared(*[w[1] for w in weights])
    to_send, own = to_tokens(h, features[0])
    oth = send(to_send, 1, 0)
    own_up, own_lo, oth_up, oth_lo = layer_one(own, oth, w_one)
    oth_lo = send(oth_lo, 2, 0)
    oth_up = send(oth_up, 2, -1)
    own_up = send(own_up, 0, -1)
    own_lo, own_up, oth_lo, oth_up = layer_two((own_lo, own_up, oth_lo, oth_up), w_two)
    oth_lo = send(oth_lo, -1, 0)
    oth_up = send(oth_up, -1, 1)
    own_up = send(own_up, 0, 1)
    return from_tokens(h, (own_lo, own_up, oth_lo, oth_up))[None]


def solution(mesh):
    in_specs = (P("frame", None, "strip", None), P(), P(), P(), P(), P(), P())
    out_specs = P("frame", None, "strip", None)
    return jax.shard_map(
        on_device, mesh=mesh, in_specs=in_specs, out_specs=out_specs, check_vma=False
    )
```

time: 443 us -> 121 us (0.27)
  local copies, waits for them, and re-layouts: 161 us -> 8.91 us
  matrix products: 119 us -> 0 us
  waiting for transfers between devices: 118 us -> 19.4 us
  Pallas kernels: 0 us -> 72.8 us
  other arithmetic: 13.1 us -> 4.04 us
  loops' own time: 8.09 us -> 0 us
    ppermute x6 -> x7, waiting for transfers between devices: 118 us -> 19.4 us  [send(): lax.ppermute(value, ('frame', 'strip'), route(frame_step, strip_step))]
    dot_general x34 -> x0, matrix products: 96 us -> none  [the longest x16 65.4 us: window_mix(): jnp.einsum('nhqk,nhkd->nhqd', weights, values, preferred_element_type=jnp...]
    pallas_call x0 -> x4, Pallas kernels: none -> 72.8 us  [the longest x1 35.1 us: layer_one(): pl.pallas_call(layer_one_kernel, out_shape=[tokens_shape(HALF * TOK // 2)...]
    reshape x112 -> x8, local copies, waits for them, and re-layouts: 67 us -> 0.13 us  [by_head(): spread = array.reshape(HEADS, HEAD, array.shape[1])]
    slice x22 -> x3, local copies, waits for them, and re-layouts: 39.9 us -> 0.05 us  [the longest x2 0.04 us: on_device(): w_two = prepared(*[w[1] for w in weights])]
    transpose x50 -> x2, local copies, waits for them, and re-layouts: 24.1 us -> 0.04 us  [prepared(): w_q = [pad_to(w[:, :C].T, LANES, LANES) for w in (w_mut, w_slf)]]
    sub x16 -> x0, matrix products: 22.8 us -> none  [window_mix(): weights = jnp.exp(scores - row_max)]
    while x38 -> x0, local copies, waits for them, and re-layouts: 14.1 us -> none  [the longest x6 14 us: attend(): blocks = lax.map(column_block, jnp.arange(block_count, dtype=jnp.int32))]
  transfers between devices with their start and end apart: 6 -> 7, of which waited for: 6 -> 4; matrix products, arithmetic and copies ran while one was open for 1% -> 6% of each run, Pallas kernels for 0% -> 0%
where the time goes in v1:
time: 121 us
  Pallas kernels  72.8 us (60%)
  waiting for transfers between devices  19.4 us (16%)
  starting transfers between devices  15.6 us (13%)
  local copies, waits for them, and re-layouts  8.91 us (7%)
  other arithmetic  4.04 us (3%)
    pallas_call x1, Pallas kernels, layer_one(): pl.pallas_call(layer_one_kernel, out_shape=[tokens_shape(HALF * TOK // 2)...  35.1 us
    pallas_call x1, Pallas kernels, layer_two(): pl.pallas_call(layer_two_kernel, out_shape=[tokens_shape(HALF * TOK // 2)...  32.7 us
    ppermute x7, waiting for transfers between devices, send(): lax.ppermute(value, ('frame', 'strip'), route(frame_step, strip_step))  19.4 us
    ppermute x7, starting transfers between devices, send(): lax.ppermute(value, ('frame', 'strip'), route(frame_step, strip_step))  15.6 us
    unnamed x30, local copies, waits for them, and re-layouts  5.82 us
    pallas_call x1, Pallas kernels, from_tokens(): pl.pallas_call(from_tokens_kernel, out_shape=jax.ShapeDtypeStruct((C, WIN...  2.69 us
  transfers between devices with their start and end apart: 7, of which 4 were waited for; matrix products, arithmetic and copies ran while one was open for 6% of the time, Pallas kernels for 0%

profile of v1, /device:TPU:1, one launch (start us, length us, event | category | flops | bytes accessed | tf_op | source)
XLA Modules:
  0.0 121.0 jit_solution(7647571335674917238)
XLA Ops:
  0.0 0.0 copy-start.1
  0.0 2.3 %to_tokens.1 = (bf16[1088,128]{1,0:T(8,128)(2,1)}, bf16[1088,128]{1,0:T(8,128)(2,1)}) custom-call(s32[1]{0:T(128)} %bitcast.h_ref, bf16[120,8,256]{2,1,0:T(8,128)(2,1)} %bitcast.43), custom_call_target="tpu_custom_call" | custom-call | tf_op jit(solution)/shard_map/to_tokens/pallas_call | solution.py:204
  2.3 3.7 %collective-permute-start = (bf16[1088,128]{1,0:T(8,128)(2,1)}, bf16[1088,128]{1,0:T(8,128)(2,1)S(1)}, u32[]{:S(2)}, u32[]{:S(2)}) collective-permute-start(bf16[1088,128]{1,0:T(8,128)(2,1)} %get-tuple-element.16), channel_id=1, source_target_pairs={{0,4},{1,5},{2,6},{3,7},{4,0},{5,1},{6,2},{7,3},{8,12},{9,13},{10,... | collective-permute-start | bytes 835592 | tf_op jit(solution)/shard_map/ppermute | solution.py:295
  6.1 0.0 copy-done.1
  6.1 0.0 copy-start.2
  6.1 0.1 copy.14
  6.2 0.8 copy-done.2
  7.1 0.1 copy.15
  7.2 0.0 copy-start.9
  7.3 0.8 copy-done.9
  8.2 0.0 copy-start.10
  8.2 0.8 copy-done.10
  9.1 0.0 copy-start.12
  9.1 0.0 copy-start.11
  9.2 0.8 copy-done.12
  10.0 0.1 copy-done.11
  10.1 0.7 fusion.24.w_gu
  10.8 0.6 fusion.30.w_prj
  11.4 0.7 fusion.25.w_gu
  12.1 0.6 fusion.31.w_prj
  12.7 0.7 fusion.20.w_qv
  13.4 0.7 copy.10.w_k
  14.1 0.6 pad.109.w_dwn
  14.8 0.1 copy.16
  14.9 0.1 copy.17
  15.1 0.0 collective-permute-done.oth_ref
  15.1 0.0 copy-start
  15.1 0.7 copy-done
  15.8 35.1 %layer_one.1 = (bf16[512,128]{1,0:T(8,128)(2,1)}, bf16[512,128]{1,0:T(8,128)(2,1)}, bf16[512,128]{1,0:T(8,128)(2,1)}, bf16[512,128]{1,0:T(8,128)(2,1)}) custom-call(bf16[1088,128]{1,0:T(8,128)(2,1)} %get-tuple-element.15.own_ref, bf16[1088,128]{1,0:T(8,128)(2,1)} %copy-done, bf16[128,256]{1,0:T(8,128)(2,1)} %copy.10.w_k, bf16[544,128]{1,0:T(8,128)(2,1)} %fusion.20.w_qv, ...), custom_call_target="tpu_custom_call" | custom-call | tf_op jit(solution)/shard_map/layer_one/pallas_call | solution.py:219
  50.8 1.0 collective-permute-start.1
  51.8 1.2 %collective-permute-start.2 = (bf16[512,128]{1,0:T(8,128)(2,1)}, bf16[512,128]{1,0:T(8,128)(2,1)S(1)}, u32[]{:S(2)}, u32[]{:S(2)}) collective-permute-start(bf16[512,128]{1,0:T(8,128)(2,1)} %get-tuple-element.19), channel_id=1, source_target_pairs={{0,8},{1,9},{2,10},{3,11},{4,252},{5,253},{6,254},{7,255},{8,16},{... | collective-permute-start | bytes 393224 | tf_op jit(solution)/shard_map/ppermute | solution.py:295
  53.0 1.4 %collective-permute-start.3 = (bf16[512,128]{1,0:T(8,128)(2,1)}, bf16[512,128]{1,0:T(8,128)(2,1)S(1)}, u32[]{:S(2)}, u32[]{:S(2)}) collective-permute-start(bf16[512,128]{1,0:T(8,128)(2,1)} %get-tuple-element.20), channel_id=1, source_target_pairs={{0,11},{1,8},{2,9},{3,10},{4,255},{5,252},{6,253},{7,254},{8,19},{... | collective-permute-start | bytes 393224 | tf_op jit(solution)/shard_map/ppermute | solution.py:295
  54.5 0.7 copy.13.w_k
  55.3 0.6 pad.124.w_dwn
  55.9 0.7 fusion.23.w_qv
  56.6 0.0 collective-permute-done.1.own_up
  56.6 0.0 copy-start.3
  56.6 7.1 %collective-permute-done.2.oth_lo = bf16[512,128]{1,0:T(8,128)(2,1)S(1)} collective-permute-done((bf16[512,128]{1,0:T(8,128)(2,1)}, bf16[512,128]{1,0:T(8,128)(2,1)S(1)}, u32[]{:S(2)}, u32[]{:S(2)}) %collective-permute-start.2) | collective-permute-done | bytes 131104 | tf_op jit(solution)/shard_map/ppermute | solution.py:295
  63.6 0.0 copy-start.4
  63.6 2.8 %collective-permute-done.3.oth_up = bf16[512,128]{1,0:T(8,128)(2,1)S(1)} collective-permute-done((bf16[512,128]{1,0:T(8,128)(2,1)}, bf16[512,128]{1,0:T(8,128)(2,1)S(1)}, u32[]{:S(2)}, u32[]{:S(2)}) %collective-permute-start.3) | collective-permute-done | bytes 131104 | tf_op jit(solution)/shard_map/ppermute | solution.py:295
  66.5 0.0 copy-start.5
  66.5 0.0 copy-done.3
  66.5 0.0 copy-done.4
  66.5 0.6 copy-done.5
  67.1 32.7 %layer_two.1 = (bf16[512,128]{1,0:T(8,128)(2,1)}, bf16[512,128]{1,0:T(8,128)(2,1)}, bf16[512,128]{1,0:T(8,128)(2,1)}, bf16[512,128]{1,0:T(8,128)(2,1)}) custom-call(bf16[512,128]{1,0:T(8,128)(2,1)} %get-tuple-element.17.own_lo, bf16[512,128]{1,0:T(8,128)(2,1)} %copy-done.3, bf16[512,128]{1,0:T(8,128)(2,1)} %copy-done.4, bf16[512,128]{1,0:T(8,128)(2,1)} %copy-done.5, ...), custom_call_target="tpu_custom_call" | custom-call | tf_op jit(solution)/shard_map/layer_two/pallas_call | solution.py:234
  99.9 0.2 collective-permute-start.4
  100.1 6.3 %collective-permute-start.5 = (bf16[512,128]{1,0:T(8,128)(2,1)}, bf16[512,128]{1,0:T(8,128)(2,1)S(1)}, u32[]{:S(2)}, u32[]{:S(2)}) collective-permute-start(bf16[512,128]{1,0:T(8,128)(2,1)} %get-tuple-element.23), channel_id=1, source_target_pairs={{0,252},{1,253},{2,254},{3,255},{4,8},{5,9},{6,10},{7,11},{8,4},{9... | collective-permute-start | bytes 393224 | tf_op jit(solution)/shard_map/ppermute | solution.py:295
  106.4 1.8 %collective-permute-start.6 = (bf16[512,128]{1,0:T(8,128)(2,1)}, bf16[512,128]{1,0:T(8,128)(2,1)S(1)}, u32[]{:S(2)}, u32[]{:S(2)}) collective-permute-start(bf16[512,128]{1,0:T(8,128)(2,1)} %get-tuple-element.24), channel_id=1, source_target_pairs={{0,253},{1,254},{2,255},{3,252},{4,9},{5,10},{6,11},{7,8},{8,5},{9... | collective-permute-start | bytes 393224 | tf_op jit(solution)/shard_map/ppermute | solution.py:295
  108.2 0.0 collective-permute-done.4.own_up
  108.2 0.0 copy-start.6
  108.2 2.6 %collective-permute-done.5.oth_lo = bf16[512,128]{1,0:T(8,128)(2,1)S(1)} collective-permute-done((bf16[512,128]{1,0:T(8,128)(2,1)}, bf16[512,128]{1,0:T(8,128)(2,1)S(1)}, u32[]{:S(2)}, u32[]{:S(2)}) %collective-permute-start.5) | collective-permute-done | bytes 131104 | tf_op jit(solution)/shard_map/ppermute | solution.py:295
  110.8 0.0 copy-start.7
  110.8 6.8 %collective-permute-done.6.oth_up = bf16[512,128]{1,0:T(8,128)(2,1)S(1)} collective-permute-done((bf16[512,128]{1,0:T(8,128)(2,1)}, bf16[512,128]{1,0:T(8,128)(2,1)S(1)}, u32[]{:S(2)}, u32[]{:S(2)}) %collective-permute-start.6) | collective-permute-done | bytes 131104 | tf_op jit(solution)/shard_map/ppermute | solution.py:295
  117.7 0.0 copy-start.8
  117.7 0.0 copy-done.6
  117.7 0.0 copy-done.7
  117.7 0.6 copy-done.8
  118.3 2.7 %from_tokens.1 = bf16[120,8,256]{2,1,0:T(8,128)(2,1)} custom-call(s32[1]{0:T(128)} %bitcast.h_ref, bf16[512,128]{1,0:T(8,128)(2,1)} %get-tuple-element.21.own_lo, bf16[512,128]{1,0:T(8,128)(2,1)} %copy-done.6, bf16[512,128]{1,0:T(8,128)(2,1)} %copy-done.7, bf16[512,128]{1,0:T(8,128)(2,1)} %copy-done.8), custom_call_target="tpu_custom_call" | custom-call | tf_op jit(solution)/shard_map/from_tokens/pallas_call | solution.py:245
  (25 shorter events, 0.4 us)
Async XLA Ops:
  0.0 6.1 %copy-start.1 = (bf16[2,120,360]{2,1,0:T(8,128)(2,1)S(1)}, bf16[2,120,360]{2,1,0:T(8,128)(2,1)}, u32[]{:S(2)}) copy-start(bf16[2,120,360]{2,1,0:T(8,128)(2,1)} %param.8) | copy-start | bytes 518404
  2.3 12.7 %collective-permute-start = (bf16[1088,128]{1,0:T(8,128)(2,1)}, bf16[1088,128]{1,0:T(8,128)(2,1)S(1)}, u32[]{:S(2)}, u32[]{:S(2)}) collective-permute-start(bf16[1088,128]{1,0:T(8,128)(2,1)} %get-tuple-element.16), channel_id=1, source_target_pairs={{0,4},{1,5},{2,6},{3,7},{4,0},{5,1},{6,2},{7,3},{8,12},{9,13},{10,... | collective-permute-start | bytes 835592 | tf_op jit(solution)/shard_map/ppermute | solution.py:295
  6.1 0.9 copy-start.2
  7.2 0.9 copy-start.9
  8.2 0.9 copy-start.10
  9.1 0.9 copy-start.12
  9.1 0.9 copy-start.11
  15.1 0.7 copy-start
  50.8 5.7 %collective-permute-start.1 = (bf16[512,128]{1,0:T(8,128)(2,1)}, bf16[512,128]{1,0:T(8,128)(2,1)S(1)}, u32[]{:S(2)}, u32[]{:S(2)}) collective-permute-start(bf16[512,128]{1,0:T(8,128)(2,1)} %get-tuple-element.18), channel_id=1, source_target_pairs={{0,3},{1,0},{2,1},{3,2},{4,7},{5,4},{6,5},{7,6},{8,11},{9,8},{10,9... | collective-permute-start | bytes 393224 | tf_op jit(solution)/shard_map/ppermute | solution.py:295
  51.8 11.8 %collective-permute-start.2 = (bf16[512,128]{1,0:T(8,128)(2,1)}, bf16[512,128]{1,0:T(8,128)(2,1)S(1)}, u32[]{:S(2)}, u32[]{:S(2)}) collective-permute-start(bf16[512,128]{1,0:T(8,128)(2,1)} %get-tuple-element.19), channel_id=1, source_target_pairs={{0,8},{1,9},{2,10},{3,11},{4,252},{5,253},{6,254},{7,255},{8,16},{... | collective-permute-start | bytes 393224 | tf_op jit(solution)/shard_map/ppermute | solution.py:295
  53.0 13.5 %collective-permute-start.3 = (bf16[512,128]{1,0:T(8,128)(2,1)}, bf16[512,128]{1,0:T(8,128)(2,1)S(1)}, u32[]{:S(2)}, u32[]{:S(2)}) collective-permute-start(bf16[512,128]{1,0:T(8,128)(2,1)} %get-tuple-element.20), channel_id=1, source_target_pairs={{0,11},{1,8},{2,9},{3,10},{4,255},{5,252},{6,253},{7,254},{8,19},{... | collective-permute-start | bytes 393224 | tf_op jit(solution)/shard_map/ppermute | solution.py:295
  56.6 9.9 %copy-start.3 = (bf16[512,128]{1,0:T(8,128)(2,1)}, bf16[512,128]{1,0:T(8,128)(2,1)S(1)}, u32[]{:S(2)}) copy-start(bf16[512,128]{1,0:T(8,128)(2,1)S(1)} %collective-permute-done.1.own_up) | copy-start | bytes 393220
  63.6 2.9 %copy-start.4 = (bf16[512,128]{1,0:T(8,128)(2,1)}, bf16[512,128]{1,0:T(8,128)(2,1)S(1)}, u32[]{:S(2)}) copy-start(bf16[512,128]{1,0:T(8,128)(2,1)S(1)} %collective-permute-done.2.oth_lo) | copy-start | bytes 393220
  66.5 0.7 copy-start.5
  99.9 8.3 %collective-permute-start.4 = (bf16[512,128]{1,0:T(8,128)(2,1)}, bf16[512,128]{1,0:T(8,128)(2,1)S(1)}, u32[]{:S(2)}, u32[]{:S(2)}) collective-permute-start(bf16[512,128]{1,0:T(8,128)(2,1)} %get-tuple-element.22), channel_id=1, source_target_pairs={{0,1},{1,2},{2,3},{3,0},{4,5},{5,6},{6,7},{7,4},{8,9},{9,10},{10,1... | collective-permute-start | bytes 393224 | tf_op jit(solution)/shard_map/ppermute | solution.py:295
  100.1 10.7 %collective-permute-start.5 = (bf16[512,128]{1,0:T(8,128)(2,1)}, bf16[512,128]{1,0:T(8,128)(2,1)S(1)}, u32[]{:S(2)}, u32[]{:S(2)}) collective-permute-start(bf16[512,128]{1,0:T(8,128)(2,1)} %get-tuple-element.23), channel_id=1, source_target_pairs={{0,252},{1,253},{2,254},{3,255},{4,8},{5,9},{6,10},{7,11},{8,4},{9... | collective-permute-start | bytes 393224 | tf_op jit(solution)/shard_map/ppermute | solution.py:295
  106.4 11.3 %collective-permute-start.6 = (bf16[512,128]{1,0:T(8,128)(2,1)}, bf16[512,128]{1,0:T(8,128)(2,1)S(1)}, u32[]{:S(2)}, u32[]{:S(2)}) collective-permute-start(bf16[512,128]{1,0:T(8,128)(2,1)} %get-tuple-element.24), channel_id=1, source_target_pairs={{0,253},{1,254},{2,255},{3,252},{4,9},{5,10},{6,11},{7,8},{8,5},{9... | collective-permute-start | bytes 393224 | tf_op jit(solution)/shard_map/ppermute | solution.py:295
  108.2 9.5 %copy-start.6 = (bf16[512,128]{1,0:T(8,128)(2,1)}, bf16[512,128]{1,0:T(8,128)(2,1)S(1)}, u32[]{:S(2)}) copy-start(bf16[512,128]{1,0:T(8,128)(2,1)S(1)} %collective-permute-done.4.own_up) | copy-start | bytes 393220
  110.8 6.8 %copy-start.7 = (bf16[512,128]{1,0:T(8,128)(2,1)}, bf16[512,128]{1,0:T(8,128)(2,1)S(1)}, u32[]{:S(2)}) copy-start(bf16[512,128]{1,0:T(8,128)(2,1)S(1)} %collective-permute-done.5.oth_lo) | copy-start | bytes 393220
  117.7 0.6 copy-start.8

commit v2 on v1

--- a/solution.py
+++ b/solution.py
@@ -13,6 +13,7 @@
 WIN = 8
 LANES = 128
 VHEAD = 24
+GROUP = 8
 HALF = 16
 TOK = WIN * WIN
 EPS = 1e-05
@@ -62,47 +63,67 @@
     return weights * (1.0 / total)
 
 
-def attend(keys, q_t, v_t):
-    outs = []
-    lane = lax.broadcasted_iota(jnp.int32, (TOK, 2 * LANES), 1)
-    of_first = (lane % LANES) < TOK
-    for kind in range(2):
-        kind_keys = keys[:, kind * LANES : (kind + 1) * LANES]
-        kind_q = q_t[kind * LANES : (kind + 1) * LANES]
-        for pair in range(HEADS // 2):
-            queries = jnp.concatenate(
-                [head_only(kind_q, 2 * pair), head_only(kind_q, 2 * pair + 1)], axis=1
-            )
-            scores = matmul(kind_keys, queries)
-            if kind == 0:
-                probs = softmax_rows(jnp.where(of_first, scores[TOK:], scores[:TOK]))
-                probs = jnp.concatenate(
-                    [jnp.where(of_first, 0.0, probs), jnp.where(of_first, probs, 0.0)], axis=0
-                )
-            else:
-                probs = softmax_rows(scores)
-            base = kind * HEADS * VHEAD + pair * 2 * VHEAD
-            mixed = matmul(v_t[base : base + 2 * VHEAD], probs.astype(jnp.bfloat16))
-            outs += [mixed[:VHEAD, :LANES], mixed[VHEAD:, LANES:]]
-    return jnp.concatenate(outs, axis=0).astype(jnp.bfloat16)
-
-
-def layer_tokens(x, w_k, w_qv, w_prj, w_gu, w_dwn):
-    count = x.shape[0] // LANES
+def project_windows(x, w_k, w_qv, keys, qv_t, first):
     normal = normed(x)
-    keys = matmul(normal, w_k).astype(jnp.bfloat16)
-    qv_t = matmul_nt(w_qv, normal).astype(jnp.bfloat16)
-    middles = []
-    for i in range(count):
+    new_keys = matmul(normal, w_k[...]).astype(jnp.bfloat16)
+    new_qv = matmul_nt(w_qv[...], normal).astype(jnp.bfloat16)
+    for i in range(x.shape[0] // LANES):
         span = slice(i * LANES, (i + 1) * LANES)
-        joined = attend(keys[span], qv_t[: 2 * LANES, span], qv_t[2 * LANES :, span])
-        middles.append(x[span] + matmul_tn(joined, w_prj))
-    middle = jnp.concatenate(middles, axis=0)
-    both = matmul(normed(middle), w_gu)
+        keys[first + i] = new_keys[span]
+        qv_t[first + i] = new_qv[:, span]
+
+
+def score_block(kind, pair, keys, qv_t, window, of_first):
+    kind_q = qv_t[window, kind * LANES : (kind + 1) * LANES]
+    queries = jnp.concatenate(
+        [head_only(kind_q, 2 * pair), head_only(kind_q, 2 * pair + 1)], axis=1
+    )
+    scores = matmul(keys[window, :, kind * LANES : (kind + 1) * LANES], queries)
+    if kind == 0:
+        scores = jnp.where(of_first, scores[TOK:], scores[:TOK])
+    return scores
+
+
+def mix_block(kind, pair, scores, qv_t, window, of_first):
+    probs = [softmax_rows(scores[:, i * LANES : (i + 1) * LANES]) for i in range(2)]
+    probs = jnp.concatenate(probs, axis=1)
+    if kind == 0:
+        probs = jnp.concatenate(
+            [jnp.where(of_first, 0.0, probs), jnp.where(of_first, probs, 0.0)], axis=0
+        )
+    base = 2 * LANES + (kind * HEADS + 2 * pair) * VHEAD
+    mixed = matmul(qv_t[window, base : base + 2 * VHEAD], probs.astype(jnp.bfloat16))
+    return [mixed[:VHEAD, :LANES], mixed[VHEAD:, LANES:]]
+
+
+def attend(count, keys, qv_t, mutual_scores, self_scores, joined):
+    scores = (mutual_scores, self_scores)
+
+    def body(step, carry):
+        lane = lax.broadcasted_iota(jnp.int32, (TOK, 2 * LANES), 1)
+        of_first = (lane % LANES) < TOK
+        now = jnp.minimum(step, count - 1)
+        old = jnp.maximum(step - 1, 0)
+        outs = []
+        for kind in range(2):
+            for pair in range(HEADS // 2):
+                ref = scores[kind]
+                outs += mix_block(kind, pair, ref[pair], qv_t, old, of_first)
+                ref[pair] = score_block(kind, pair, keys, qv_t, now, of_first)
+        joined[old] = jnp.concatenate(outs, axis=0).astype(jnp.bfloat16)
+        return carry
+
+    lax.fori_loop(0, count + 1, body, 0)
+
+
+def finished(x, joined, w_prj, w_gu, w_dwn):
+    mixed = [matmul_tn(block, w_prj[...]) for block in joined]
+    middle = x + jnp.concatenate(mixed, axis=0)
+    both = matmul(normed(middle), w_gu[...])
     gate, up = both[:, : 2 * LANES], both[:, 2 * LANES :]
     gelu = 0.5 * gate * (1.0 + lax.erf(gate * float(np.sqrt(0.5))))
     hidden = (gelu * up).astype(jnp.bfloat16)
-    return middle + matmul(hidden, w_dwn)
+    return middle + matmul(hidden, w_dwn[...])
 
 
 def to_tokens_kernel(h_ref, x_ref, send_ref, own_ref, wide, tiles):
@@ -123,28 +144,39 @@
 
 
 def layer_one_kernel(own_ref, oth_ref, w_k, w_qv, w_prj, w_gu, w_dwn, *rest):
-    outs, (flat, tiles) = rest[:4], rest[4:]
-    weights = (w_k, w_qv, w_prj, w_gu, w_dwn)
-
-    def work(first, count):
+    outs, (flat, tiles), scratch = rest[:4], rest[4:6], rest[6:]
+    keys, qv_t, joined = scratch[0], scratch[1], scratch[-1]
+
+    def tokens(first, count):
         parts = []
         for i in range(count):
             start = pl.multiple_of((first + i) * TOK, TOK)
             parts += [own_ref[pl.ds(start, TOK)], oth_ref[pl.ds(start, TOK)]]
-        x = jnp.concatenate(parts, axis=0).astype(jnp.float32)
-        y = layer_tokens(x, *[w[...] for w in weights])
+        return jnp.concatenate(parts, axis=0).astype(jnp.float32)
+
+    def front(first, count):
+        project_windows(tokens(first, count), w_k, w_qv, keys, qv_t, first)
+
+    def back(first, count):
+        blocks = [joined[first + i] for i in range(count)]
+        y = finished(tokens(first, count), blocks, w_prj, w_gu, w_dwn)
         y = y.reshape(count, 2, WIN, WIN, LANES)
         for i in range(count):
             col = pl.multiple_of((first + i) * WIN, WIN)
             for f in range(2):
                 flat[f, :, pl.ds(col, WIN), :] = y[i, f]
 
-    def body(step, carry):
-        work(step * 2, 2)
-        return carry
-
-    lax.fori_loop(0, HALF // 2, body, 0)
-    work(HALF, 1)
+    def pairs(work):
+        def body(step, carry):
+            work(step * GROUP, GROUP)
+            return carry
+
+        lax.fori_loop(0, HALF // GROUP, body, 0)
+        work(HALF, 1)
+
+    pairs(front)
+    attend(HALF + 1, *scratch)
+    pairs(back)
     for f in range(2):
         for r in range(WIN):
             block = flat[f, r, WIN // 2 : WIN // 2 + LANES, :]
@@ -154,27 +186,35 @@
             outs[2 * f + k][...] = piece.astype(jnp.bfloat16)
 
 
-def layer_two_kernel(own_lo, own_up, oth_lo, oth_up, w_k, w_qv, w_prj, w_gu, w_dwn, *outs):
-    weights = (w_k, w_qv, w_prj, w_gu, w_dwn)
+def layer_two_kernel(own_lo, own_up, oth_lo, oth_up, w_k, w_qv, w_prj, w_gu, w_dwn, *rest):
+    outs, scratch = rest[:4], rest[4:]
+    keys, qv_t, joined = scratch[0], scratch[1], scratch[-1]
     ins = (own_lo, own_up, oth_lo, oth_up)
     half_tok = TOK // 2
 
-    def body(step, carry):
-        parts = []
-        starts = []
-        for i in range(2):
-            start = pl.multiple_of((step * 2 + i) * half_tok, half_tok)
-            starts.append(start)
-            parts += [ref[pl.ds(start, half_tok)] for ref in ins]
-        x = jnp.concatenate(parts, axis=0).astype(jnp.float32)
-        y = layer_tokens(x, *[w[...] for w in weights]).astype(jnp.bfloat16)
-        for i in range(2):
+    def starts(step):
+        return [pl.multiple_of((step * GROUP + i) * half_tok, half_tok) for i in range(GROUP)]
+
+    def tokens(step):
+        parts = [ref[pl.ds(start, half_tok)] for start in starts(step) for ref in ins]
+        return jnp.concatenate(parts, axis=0).astype(jnp.float32)
+
+    def front(step, carry):
+        project_windows(tokens(step), w_k, w_qv, keys, qv_t, step * GROUP)
+        return carry
+
+    def back(step, carry):
+        blocks = [joined[step * GROUP + i] for i in range(GROUP)]
+        y = finished(tokens(step), blocks, w_prj, w_gu, w_dwn).astype(jnp.bfloat16)
+        for i, start in enumerate(starts(step)):
             for j in range(4):
                 low = i * LANES + j * half_tok
-                outs[j][pl.ds(starts[i], half_tok)] = y[low : low + half_tok]
+                outs[j][pl.ds(start, half_tok)] = y[low : low + half_tok]
         return carry
 
-    lax.fori_loop(0, HALF // 2, body, 0)
+    lax.fori_loop(0, HALF // GROUP, front, 0)
+    attend(HALF, *scratch)
+    lax.fori_loop(0, HALF // GROUP, back, 0)
 
 
 def from_tokens_kernel(h_ref, own_lo, own_up, oth_lo, oth_up, out_ref, tiles, wide):
@@ -193,6 +233,16 @@
 VMEM = pl.BlockSpec(memory_space=pltpu.VMEM)
 SMEM = pl.BlockSpec(memory_space=pltpu.SMEM)
 PARAMS = pltpu.CompilerParams(vmem_limit_bytes=VMEM_LIMIT)
+
+
+def attention_scratch(count):
+    return [
+        pltpu.VMEM((count, LANES, 2 * LANES), jnp.bfloat16),
+        pltpu.VMEM((count, 2 * LANES + 2 * HEADS * VHEAD, LANES), jnp.bfloat16),
+        pltpu.VMEM((HEADS // 2, TOK, 2 * LANES), jnp.float32),
+        pltpu.VMEM((HEADS // 2, 2 * TOK, 2 * LANES), jnp.float32),
+        pltpu.VMEM((count, 2 * HEADS * VHEAD, LANES), jnp.bfloat16),
+    ]
 
 
 def tokens_shape(rows):
@@ -224,6 +274,7 @@
         scratch_shapes=[
             pltpu.VMEM((2, WIN, (HALF + 1) * WIN, LANES), jnp.float32),
             pltpu.VMEM((2, 2, HALF, 4, WIN, LANES), jnp.float32),
+            *attention_scratch(HALF + 1),
         ],
         compiler_params=PARAMS,
         name="layer_one",
@@ -236,6 +287,7 @@
         out_shape=[tokens_shape(HALF * TOK // 2)] * 4,
         in_specs=[VMEM] * 9,
         out_specs=[VMEM] * 4,
+        scratch_shapes=attention_scratch(HALF),
         compiler_params=PARAMS,
         name="layer_two",
     )(*pieces, *weights)

time: 121 us -> 80.6 us (0.67)
  Pallas kernels: 72.8 us -> 32.2 us
    pallas_call x1, Pallas kernels: 35.1 us -> 14.2 us  [layer_one(): pl.pallas_call(layer_one_kernel, out_shape=[tokens_shape(HALF * TOK // 2)...]
    pallas_call x1, Pallas kernels: 32.7 us -> 12.9 us  [layer_two(): pl.pallas_call(layer_two_kernel, out_shape=[tokens_shape(HALF * TOK // 2)...]
  transfers between devices with their start and end apart: 7 -> 7, of which waited for: 4 -> 4; matrix products, arithmetic and copies ran while one was open for 6% -> 9% of each run, Pallas kernels for 0% -> 0%
where the time goes in v2:
time: 80.6 us; the launch traced here: 80.4 us
  Pallas kernels  32.2 us (40%)
  waiting for transfers between devices  19.3 us (24%)
  starting transfers between devices  15.7 us (19%)
  local copies, waits for them, and re-layouts  8.91 us (11%)
  other arithmetic  4.04 us (5%)
    ppermute x7, waiting for transfers between devices, send(): lax.ppermute(value, ('frame', 'strip'), route(frame_step, strip_step))  19.3 us
    ppermute x7, starting transfers between devices, send(): lax.ppermute(value, ('frame', 'strip'), route(frame_step, strip_step))  15.7 us
    pallas_call x1, Pallas kernels, layer_one(): pl.pallas_call(layer_one_kernel, out_shape=[tokens_shape(HALF * TOK // 2)...  14.2 us
    pallas_call x1, Pallas kernels, layer_two(): pl.pallas_call(layer_two_kernel, out_shape=[tokens_shape(HALF * TOK // 2)...  12.9 us
    unnamed x30, local copies, waits for them, and re-layouts  5.82 us
    pallas_call x1, Pallas kernels, from_tokens(): pl.pallas_call(from_tokens_kernel, out_shape=jax.ShapeDtypeStruct((C, WIN...  2.69 us
    pallas_call x1, Pallas kernels, to_tokens(): pl.pallas_call(to_tokens_kernel, out_shape=[tokens_shape(rows)] * 2, in_s...  2.33 us
  transfers between devices with their start and end apart: 7, of which 4 were waited for; matrix products, arithmetic and copies ran while one was open for 9% of the time, Pallas kernels for 0%

profile of v2, /device:TPU:1, one launch (start us, length us, event | category | flops | bytes accessed | tf_op | source)
XLA Modules:
  0.0 80.4 jit_solution(6611875965628786405)
XLA Ops:
  0.0 0.0 copy-start.1
  0.0 2.3 %to_tokens.1 = (bf16[1088,128]{1,0:T(8,128)(2,1)}, bf16[1088,128]{1,0:T(8,128)(2,1)}) custom-call(s32[1]{0:T(128)} %bitcast.h_ref, bf16[120,8,256]{2,1,0:T(8,128)(2,1)} %bitcast.43), custom_call_target="tpu_custom_call" | custom-call | tf_op jit(solution)/shard_map/to_tokens/pallas_call | solution.py:254
  2.3 3.7 %collective-permute-start = (bf16[1088,128]{1,0:T(8,128)(2,1)}, bf16[1088,128]{1,0:T(8,128)(2,1)S(1)}, u32[]{:S(2)}, u32[]{:S(2)}) collective-permute-start(bf16[1088,128]{1,0:T(8,128)(2,1)} %get-tuple-element.16), channel_id=1, source_target_pairs={{0,4},{1,5},{2,6},{3,7},{4,0},{5,1},{6,2},{7,3},{8,12},{9,13},{10,... | collective-permute-start | bytes 835592 | tf_op jit(solution)/shard_map/ppermute | solution.py:347
  6.1 0.0 copy-done.1
  6.1 0.0 copy-start.2
  6.1 0.1 copy.14
  6.2 0.8 copy-done.2
  7.1 0.1 copy.15
  7.2 0.0 copy-start.9
  7.3 0.8 %copy-done.9 = bf16[2,240,120]{2,1,0:T(8,128)(2,1)S(1)} copy-done((bf16[2,240,120]{2,1,0:T(8,128)(2,1)S(1)}, bf16[2,240,120]{2,1,0:T(8,128)(2,1)}, u32[]{:S(2)}) %copy-start.9) | copy-done | bytes 115224
  8.2 0.0 copy-start.10
  8.2 0.8 %copy-done.10 = bf16[2,240,120]{2,1,0:T(8,128)(2,1)S(1)} copy-done((bf16[2,240,120]{2,1,0:T(8,128)(2,1)S(1)}, bf16[2,240,120]{2,1,0:T(8,128)(2,1)}, u32[]{:S(2)}) %copy-start.10) | copy-done | bytes 115224
  9.1 0.0 copy-start.12
  9.1 0.0 copy-start.11
  9.2 0.8 copy-done.12
  10.0 0.1 copy-done.11
  10.1 0.7 fusion.24.w_gu
  10.8 0.6 fusion.30.w_prj
  11.4 0.7 fusion.25.w_gu
  12.1 0.6 fusion.31.w_prj
  12.7 0.7 fusion.20.w_qv
  13.4 0.7 copy.10.w_k
  14.1 0.6 pad.109.w_dwn
  14.8 0.1 copy.16
  14.9 0.1 copy.17
  15.1 0.0 collective-permute-done.oth_ref
  15.1 0.0 copy-start
  15.1 0.7 copy-done
  15.8 14.2 %layer_one.1 = (bf16[512,128]{1,0:T(8,128)(2,1)}, bf16[512,128]{1,0:T(8,128)(2,1)}, bf16[512,128]{1,0:T(8,128)(2,1)}, bf16[512,128]{1,0:T(8,128)(2,1)}) custom-call(bf16[1088,128]{1,0:T(8,128)(2,1)} %get-tuple-element.15.own_ref, bf16[1088,128]{1,0:T(8,128)(2,1)} %copy-done, bf16[128,256]{1,0:T(8,128)(2,1)} %copy.10.w_k, bf16[544,128]{1,0:T(8,128)(2,1)} %fusion.20.w_qv, ...), custom_call_target="tpu_custom_call" | custom-call | tf_op jit(solution)/shard_map/layer_one/pallas_call | solution.py:269
  30.0 1.0 %collective-permute-start.1 = (bf16[512,128]{1,0:T(8,128)(2,1)}, bf16[512,128]{1,0:T(8,128)(2,1)S(1)}, u32[]{:S(2)}, u32[]{:S(2)}) collective-permute-start(bf16[512,128]{1,0:T(8,128)(2,1)} %get-tuple-element.18), channel_id=1, source_target_pairs={{0,3},{1,0},{2,1},{3,2},{4,7},{5,4},{6,5},{7,6},{8,11},{9,8},{10,9... | collective-permute-start | bytes 393224 | tf_op jit(solution)/shard_map/ppermute | solution.py:347
  30.9 1.2 %collective-permute-start.2 = (bf16[512,128]{1,0:T(8,128)(2,1)}, bf16[512,128]{1,0:T(8,128)(2,1)S(1)}, u32[]{:S(2)}, u32[]{:S(2)}) collective-permute-start(bf16[512,128]{1,0:T(8,128)(2,1)} %get-tuple-element.19), channel_id=1, source_target_pairs={{0,8},{1,9},{2,10},{3,11},{4,252},{5,253},{6,254},{7,255},{8,16},{... | collective-permute-start | bytes 393224 | tf_op jit(solution)/shard_map/ppermute | solution.py:347
  32.1 1.4 %collective-permute-start.3 = (bf16[512,128]{1,0:T(8,128)(2,1)}, bf16[512,128]{1,0:T(8,128)(2,1)S(1)}, u32[]{:S(2)}, u32[]{:S(2)}) collective-permute-start(bf16[512,128]{1,0:T(8,128)(2,1)} %get-tuple-element.20), channel_id=1, source_target_pairs={{0,11},{1,8},{2,9},{3,10},{4,255},{5,252},{6,253},{7,254},{8,19},{... | collective-permute-start | bytes 393224 | tf_op jit(solution)/shard_map/ppermute | solution.py:347
  33.6 0.7 copy.13.w_k
  34.4 0.6 pad.124.w_dwn
  35.0 0.7 fusion.23.w_qv
  35.7 0.0 collective-permute-done.1.own_up
  35.7 0.0 copy-start.3
  35.7 7.1 %collective-permute-done.2.oth_lo = bf16[512,128]{1,0:T(8,128)(2,1)S(1)} collective-permute-done((bf16[512,128]{1,0:T(8,128)(2,1)}, bf16[512,128]{1,0:T(8,128)(2,1)S(1)}, u32[]{:S(2)}, u32[]{:S(2)}) %collective-permute-start.2) | collective-permute-done | bytes 131104 | tf_op jit(solution)/shard_map/ppermute | solution.py:347
  42.8 0.0 copy-start.4
  42.8 2.8 %collective-permute-done.3.oth_up = bf16[512,128]{1,0:T(8,128)(2,1)S(1)} collective-permute-done((bf16[512,128]{1,0:T(8,128)(2,1)}, bf16[512,128]{1,0:T(8,128)(2,1)S(1)}, u32[]{:S(2)}, u32[]{:S(2)}) %collective-permute-start.3) | collective-permute-done | bytes 131104 | tf_op jit(solution)/shard_map/ppermute | solution.py:347
  45.6 0.0 copy-start.5
  45.6 0.0 copy-done.3
  45.6 0.0 copy-done.4
  45.6 0.6 copy-done.5
  46.3 12.9 %layer_two.1 = (bf16[512,128]{1,0:T(8,128)(2,1)}, bf16[512,128]{1,0:T(8,128)(2,1)}, bf16[512,128]{1,0:T(8,128)(2,1)}, bf16[512,128]{1,0:T(8,128)(2,1)}) custom-call(bf16[512,128]{1,0:T(8,128)(2,1)} %get-tuple-element.17.own_lo, bf16[512,128]{1,0:T(8,128)(2,1)} %copy-done.3, bf16[512,128]{1,0:T(8,128)(2,1)} %copy-done.4, bf16[512,128]{1,0:T(8,128)(2,1)} %copy-done.5, ...), custom_call_target="tpu_custom_call" | custom-call | tf_op jit(solution)/shard_map/layer_two/pallas_call | solution.py:285
  59.2 0.2 collective-permute-start.4
  59.4 6.3 %collective-permute-start.5 = (bf16[512,128]{1,0:T(8,128)(2,1)}, bf16[512,128]{1,0:T(8,128)(2,1)S(1)}, u32[]{:S(2)}, u32[]{:S(2)}) collective-permute-start(bf16[512,128]{1,0:T(8,128)(2,1)} %get-tuple-element.23), channel_id=1, source_target_pairs={{0,252},{1,253},{2,254},{3,255},{4,8},{5,9},{6,10},{7,11},{8,4},{9... | collective-permute-start | bytes 393224 | tf_op jit(solution)/shard_map/ppermute | solution.py:347
  65.7 1.8 %collective-permute-start.6 = (bf16[512,128]{1,0:T(8,128)(2,1)}, bf16[512,128]{1,0:T(8,128)(2,1)S(1)}, u32[]{:S(2)}, u32[]{:S(2)}) collective-permute-start(bf16[512,128]{1,0:T(8,128)(2,1)} %get-tuple-element.24), channel_id=1, source_target_pairs={{0,253},{1,254},{2,255},{3,252},{4,9},{5,10},{6,11},{7,8},{8,5},{9... | collective-permute-start | bytes 393224 | tf_op jit(solution)/shard_map/ppermute | solution.py:347
  67.6 0.0 collective-permute-done.4.own_up
  67.6 0.0 copy-start.6
  67.6 2.6 %collective-permute-done.5.oth_lo = bf16[512,128]{1,0:T(8,128)(2,1)S(1)} collective-permute-done((bf16[512,128]{1,0:T(8,128)(2,1)}, bf16[512,128]{1,0:T(8,128)(2,1)S(1)}, u32[]{:S(2)}, u32[]{:S(2)}) %collective-permute-start.5) | collective-permute-done | bytes 131104 | tf_op jit(solution)/shard_map/ppermute | solution.py:347
  70.1 0.0 copy-start.7
  70.1 6.9 %collective-permute-done.6.oth_up = bf16[512,128]{1,0:T(8,128)(2,1)S(1)} collective-permute-done((bf16[512,128]{1,0:T(8,128)(2,1)}, bf16[512,128]{1,0:T(8,128)(2,1)S(1)}, u32[]{:S(2)}, u32[]{:S(2)}) %collective-permute-start.6) | collective-permute-done | bytes 131104 | tf_op jit(solution)/shard_map/ppermute | solution.py:347
  77.0 0.0 copy-start.8
  77.0 0.0 copy-done.6
  77.0 0.0 copy-done.7
  77.0 0.6 copy-done.8
  77.7 2.7 %from_tokens.1 = bf16[120,8,256]{2,1,0:T(8,128)(2,1)} custom-call(s32[1]{0:T(128)} %bitcast.h_ref, bf16[512,128]{1,0:T(8,128)(2,1)} %get-tuple-element.21.own_lo, bf16[512,128]{1,0:T(8,128)(2,1)} %copy-done.6, bf16[512,128]{1,0:T(8,128)(2,1)} %copy-done.7, bf16[512,128]{1,0:T(8,128)(2,1)} %copy-done.8), custom_call_target="tpu_custom_call" | custom-call | tf_op jit(solution)/shard_map/from_tokens/pallas_call | solution.py:297
  (25 shorter events, 0.4 us)
Async XLA Ops:
  0.0 6.1 %copy-start.1 = (bf16[2,120,360]{2,1,0:T(8,128)(2,1)S(1)}, bf16[2,120,360]{2,1,0:T(8,128)(2,1)}, u32[]{:S(2)}) copy-start(bf16[2,120,360]{2,1,0:T(8,128)(2,1)} %param.8) | copy-start | bytes 518404
  2.3 12.7 %collective-permute-start = (bf16[1088,128]{1,0:T(8,128)(2,1)}, bf16[1088,128]{1,0:T(8,128)(2,1)S(1)}, u32[]{:S(2)}, u32[]{:S(2)}) collective-permute-start(bf16[1088,128]{1,0:T(8,128)(2,1)} %get-tuple-element.16), channel_id=1, source_target_pairs={{0,4},{1,5},{2,6},{3,7},{4,0},{5,1},{6,2},{7,3},{8,12},{9,13},{10,... | collective-permute-start | bytes 835592 | tf_op jit(solution)/shard_map/ppermute | solution.py:347
  6.1 0.9 %copy-start.2 = (bf16[2,120,360]{2,1,0:T(8,128)(2,1)S(1)}, bf16[2,120,360]{2,1,0:T(8,128)(2,1)}, u32[]{:S(2)}) copy-start(bf16[2,120,360]{2,1,0:T(8,128)(2,1)} %param.9) | copy-start | bytes 518404
  7.2 0.9 %copy-start.9 = (bf16[2,240,120]{2,1,0:T(8,128)(2,1)S(1)}, bf16[2,240,120]{2,1,0:T(8,128)(2,1)}, u32[]{:S(2)}) copy-start(bf16[2,240,120]{2,1,0:T(8,128)(2,1)} %param.10) | copy-start | bytes 345604
  8.2 0.9 %copy-start.10 = (bf16[2,240,120]{2,1,0:T(8,128)(2,1)S(1)}, bf16[2,240,120]{2,1,0:T(8,128)(2,1)}, u32[]{:S(2)}) copy-start(bf16[2,240,120]{2,1,0:T(8,128)(2,1)} %param.13) | copy-start | bytes 345604
  9.1 0.9 %copy-start.12 = (bf16[2,120,240]{2,1,0:T(8,128)(2,1)S(1)}, bf16[2,120,240]{2,1,0:T(8,128)(2,1)}, u32[]{:S(2)}) copy-start(bf16[2,120,240]{2,1,0:T(8,128)(2,1)} %param.11) | copy-start | bytes 345604
  9.1 0.9 %copy-start.11 = (bf16[2,120,240]{2,1,0:T(8,128)(2,1)S(1)}, bf16[2,120,240]{2,1,0:T(8,128)(2,1)}, u32[]{:S(2)}) copy-start(bf16[2,120,240]{2,1,0:T(8,128)(2,1)} %param.12) | copy-start | bytes 345604
  15.1 0.7 copy-start
  30.0 5.7 %collective-permute-start.1 = (bf16[512,128]{1,0:T(8,128)(2,1)}, bf16[512,128]{1,0:T(8,128)(2,1)S(1)}, u32[]{:S(2)}, u32[]{:S(2)}) collective-permute-start(bf16[512,128]{1,0:T(8,128)(2,1)} %get-tuple-element.18), channel_id=1, source_target_pairs={{0,3},{1,0},{2,1},{3,2},{4,7},{5,4},{6,5},{7,6},{8,11},{9,8},{10,9... | collective-permute-start | bytes 393224 | tf_op jit(solution)/shard_map/ppermute | solution.py:347
  30.9 11.8 %collective-permute-start.2 = (bf16[512,128]{1,0:T(8,128)(2,1)}, bf16[512,128]{1,0:T(8,128)(2,1)S(1)}, u32[]{:S(2)}, u32[]{:S(2)}) collective-permute-start(bf16[512,128]{1,0:T(8,128)(2,1)} %get-tuple-element.19), channel_id=1, source_target_pairs={{0,8},{1,9},{2,10},{3,11},{4,252},{5,253},{6,254},{7,255},{8,16},{... | collective-permute-start | bytes 393224 | tf_op jit(solution)/shard_map/ppermute | solution.py:347
  32.1 13.5 %collective-permute-start.3 = (bf16[512,128]{1,0:T(8,128)(2,1)}, bf16[512,128]{1,0:T(8,128)(2,1)S(1)}, u32[]{:S(2)}, u32[]{:S(2)}) collective-permute-start(bf16[512,128]{1,0:T(8,128)(2,1)} %get-tuple-element.20), channel_id=1, source_target_pairs={{0,11},{1,8},{2,9},{3,10},{4,255},{5,252},{6,253},{7,254},{8,19},{... | collective-permute-start | bytes 393224 | tf_op jit(solution)/shard_map/ppermute | solution.py:347
  35.7 9.9 %copy-start.3 = (bf16[512,128]{1,0:T(8,128)(2,1)}, bf16[512,128]{1,0:T(8,128)(2,1)S(1)}, u32[]{:S(2)}) copy-start(bf16[512,128]{1,0:T(8,128)(2,1)S(1)} %collective-permute-done.1.own_up) | copy-start | bytes 393220
  42.8 2.8 %copy-start.4 = (bf16[512,128]{1,0:T(8,128)(2,1)}, bf16[512,128]{1,0:T(8,128)(2,1)S(1)}, u32[]{:S(2)}) copy-start(bf16[512,128]{1,0:T(8,128)(2,1)S(1)} %collective-permute-done.2.oth_lo) | copy-start | bytes 393220
  45.6 0.7 copy-start.5
  59.2 8.4 %collective-permute-start.4 = (bf16[512,128]{1,0:T(8,128)(2,1)}, bf16[512,128]{1,0:T(8,128)(2,1)S(1)}, u32[]{:S(2)}, u32[]{:S(2)}) collective-permute-start(bf16[512,128]{1,0:T(8,128)(2,1)} %get-tuple-element.22), channel_id=1, source_target_pairs={{0,1},{1,2},{2,3},{3,0},{4,5},{5,6},{6,7},{7,4},{8,9},{9,10},{10,1... | collective-permute-start | bytes 393224 | tf_op jit(solution)/shard_map/ppermute | solution.py:347
  59.4 10.7 %collective-permute-start.5 = (bf16[512,128]{1,0:T(8,128)(2,1)}, bf16[512,128]{1,0:T(8,128)(2,1)S(1)}, u32[]{:S(2)}, u32[]{:S(2)}) collective-permute-start(bf16[512,128]{1,0:T(8,128)(2,1)} %get-tuple-element.23), channel_id=1, source_target_pairs={{0,252},{1,253},{2,254},{3,255},{4,8},{5,9},{6,10},{7,11},{8,4},{9... | collective-permute-start | bytes 393224 | tf_op jit(solution)/shard_map/ppermute | solution.py:347
  65.7 11.3 %collective-permute-start.6 = (bf16[512,128]{1,0:T(8,128)(2,1)}, bf16[512,128]{1,0:T(8,128)(2,1)S(1)}, u32[]{:S(2)}, u32[]{:S(2)}) collective-permute-start(bf16[512,128]{1,0:T(8,128)(2,1)} %get-tuple-element.24), channel_id=1, source_target_pairs={{0,253},{1,254},{2,255},{3,252},{4,9},{5,10},{6,11},{7,8},{8,5},{9... | collective-permute-start | bytes 393224 | tf_op jit(solution)/shard_map/ppermute | solution.py:347
  67.6 9.5 %copy-start.6 = (bf16[512,128]{1,0:T(8,128)(2,1)}, bf16[512,128]{1,0:T(8,128)(2,1)S(1)}, u32[]{:S(2)}) copy-start(bf16[512,128]{1,0:T(8,128)(2,1)S(1)} %collective-permute-done.4.own_up) | copy-start | bytes 393220
  70.1 6.9 %copy-start.7 = (bf16[512,128]{1,0:T(8,128)(2,1)}, bf16[512,128]{1,0:T(8,128)(2,1)S(1)}, u32[]{:S(2)}) copy-start(bf16[512,128]{1,0:T(8,128)(2,1)S(1)} %collective-permute-done.5.oth_lo) | copy-start | bytes 393220
  77.0 0.6 copy-start.8

commit v3 on v2

--- a/solution.py
+++ b/solution.py
@@ -1,3 +1,5 @@
+import functools
+
 import jax
 import jax.numpy as jnp
 import numpy as np
@@ -13,10 +15,11 @@
 WIN = 8
 LANES = 128
 VHEAD = 24
-GROUP = 8
 HALF = 16
 TOK = WIN * WIN
 EPS = 1e-05
+SHIFTED = ((0, 8), (8, 16))
+WINDOWS = ((0, 9), (9, 17))
 EXP2_SCALE = float(np.log2(np.e) * HEAD**-0.5)
 VMEM_LIMIT = 56 * 1024 * 1024
 
@@ -126,108 +129,105 @@
     return middle + matmul(hidden, w_dwn[...])
 
 
-def to_tokens_kernel(h_ref, x_ref, send_ref, own_ref, wide, tiles):
+def to_tokens_kernel(h_ref, x_ref, *rest):
+    outs, (wide, tiles) = rest[:-2], rest[-2:]
     h = h_ref[0]
-    wide[...] = x_ref[...].astype(jnp.float32)
+    for half in range(2):
+        part = x_ref[:, :, half * LANES : (half + 1) * LANES].astype(jnp.float32)
+        wide[half] = part.reshape(C * WIN, LANES)
     pad = jnp.zeros((LANES - C, LANES), jnp.float32)
     for k in range(2):
         half = 1 - h if k == 0 else h
-        col = pl.multiple_of(half * LANES, LANES)
         for r in range(WIN):
-            block = wide[:, r, pl.ds(col, LANES)]
+            block = wide.at[half][pl.ds(r, C, stride=WIN), :]
             block = jnp.concatenate([block, pad], axis=0).T
             tiles[k, :HALF, r] = block.reshape(HALF, WIN, LANES)
-    for k, ref in enumerate((send_ref, own_ref)):
-        main = tiles[k, :HALF].reshape(HALF * TOK, LANES)
-        ref[: HALF * TOK] = main.astype(jnp.bfloat16)
-        ref[HALF * TOK :] = tiles[1 - k, 0].reshape(TOK, LANES).astype(jnp.bfloat16)
-
-
-def layer_one_kernel(own_ref, oth_ref, w_k, w_qv, w_prj, w_gu, w_dwn, *rest):
-    outs, (flat, tiles), scratch = rest[:4], rest[4:6], rest[6:]
+    for k in range(2):
+        tiles[k, HALF] = tiles[1 - k, 0]
+    for k in range(2):
+        for j, (low, high) in enumerate(WINDOWS):
+            part = tiles[k, low:high].reshape((high - low) * TOK, LANES)
+            outs[k * len(WINDOWS) + j][...] = part.astype(jnp.bfloat16)
+
+
+def layer_one_kernel(count, first, last, own_ref, oth_ref, *rest):
+    if not first:
+        before, rest = rest[0], rest[1:]
+    w_k, w_qv, w_prj, w_gu, w_dwn = rest[:5]
+    outs, rest = rest[5:9], rest[9:]
+    if not last:
+        after, rest = rest[0], rest[1:]
+    flat, tiles, *scratch = rest
     keys, qv_t, joined = scratch[0], scratch[1], scratch[-1]
-
-    def tokens(first, count):
+    shift = 0 if first else WIN
+
+    def tokens():
         parts = []
         for i in range(count):
-            start = pl.multiple_of((first + i) * TOK, TOK)
-            parts += [own_ref[pl.ds(start, TOK)], oth_ref[pl.ds(start, TOK)]]
+            span = slice(i * TOK, (i + 1) * TOK)
+            parts += [own_ref[span], oth_ref[span]]
         return jnp.concatenate(parts, axis=0).astype(jnp.float32)
 
-    def front(first, count):
-        project_windows(tokens(first, count), w_k, w_qv, keys, qv_t, first)
-
-    def back(first, count):
-        blocks = [joined[first + i] for i in range(count)]
-        y = finished(tokens(first, count), blocks, w_prj, w_gu, w_dwn)
-        y = y.reshape(count, 2, WIN, WIN, LANES)
-        for i in range(count):
-            col = pl.multiple_of((first + i) * WIN, WIN)
-            for f in range(2):
-                flat[f, :, pl.ds(col, WIN), :] = y[i, f]
-
-    def pairs(work):
-        def body(step, carry):
-            work(step * GROUP, GROUP)
-            return carry
-
-        lax.fori_loop(0, HALF // GROUP, body, 0)
-        work(HALF, 1)
-
-    pairs(front)
-    attend(HALF + 1, *scratch)
-    pairs(back)
+    project_windows(tokens(), w_k, w_qv, keys, qv_t, 0)
+    attend(count, *scratch)
+    y = finished(tokens(), [joined[i] for i in range(count)], w_prj, w_gu, w_dwn)
+    y = y.reshape(count, 2, WIN, WIN, LANES)
+    if not first:
+        flat[:, :, :WIN, :] = before[...]
+    for i in range(count):
+        for f in range(2):
+            flat[f, :, shift + i * WIN : shift + (i + 1) * WIN, :] = y[i, f]
+    width = shift + (count - 1) * WIN
+    if not last:
+        after[...] = flat[:, :, width : width + WIN, :]
     for f in range(2):
         for r in range(WIN):
-            block = flat[f, r, WIN // 2 : WIN // 2 + LANES, :]
-            tiles[f, r // 4, :, r % 4] = block.reshape(HALF, WIN, LANES)
+            block = flat[f, r, WIN // 2 : WIN // 2 + width, :]
+            tiles[f, r // 4, :, r % 4] = block.reshape(width // WIN, WIN, LANES)
         for k in range(2):
-            piece = tiles[f, k].reshape(HALF * TOK // 2, LANES)
+            piece = tiles[f, k].reshape(width * 4, LANES)
             outs[2 * f + k][...] = piece.astype(jnp.bfloat16)
 
 
-def layer_two_kernel(own_lo, own_up, oth_lo, oth_up, w_k, w_qv, w_prj, w_gu, w_dwn, *rest):
-    outs, scratch = rest[:4], rest[4:]
+def layer_two_kernel(count, *rest):
+    ins, rest = rest[:4], rest[4:]
+    w_k, w_qv, w_prj, w_gu, w_dwn = rest[:5]
+    outs, scratch = rest[5:9], rest[9:]
     keys, qv_t, joined = scratch[0], scratch[1], scratch[-1]
-    ins = (own_lo, own_up, oth_lo, oth_up)
     half_tok = TOK // 2
-
-    def starts(step):
-        return [pl.multiple_of((step * GROUP + i) * half_tok, half_tok) for i in range(GROUP)]
-
-    def tokens(step):
-        parts = [ref[pl.ds(start, half_tok)] for start in starts(step) for ref in ins]
-        return jnp.concatenate(parts, axis=0).astype(jnp.float32)
-
-    def front(step, carry):
-        project_windows(tokens(step), w_k, w_qv, keys, qv_t, step * GROUP)
-        return carry
-
-    def back(step, carry):
-        blocks = [joined[step * GROUP + i] for i in range(GROUP)]
-        y = finished(tokens(step), blocks, w_prj, w_gu, w_dwn).astype(jnp.bfloat16)
-        for i, start in enumerate(starts(step)):
-            for j in range(4):
-                low = i * LANES + j * half_tok
-                outs[j][pl.ds(start, half_tok)] = y[low : low + half_tok]
-        return carry
-
-    lax.fori_loop(0, HALF // GROUP, front, 0)
-    attend(HALF, *scratch)
-    lax.fori_loop(0, HALF // GROUP, back, 0)
-
-
-def from_tokens_kernel(h_ref, own_lo, own_up, oth_lo, oth_up, out_ref, tiles, wide):
+    spans = [slice(i * half_tok, (i + 1) * half_tok) for i in range(count)]
+
+    def tokens():
+        return jnp.concatenate([ref[s] for s in spans for ref in ins], axis=0).astype(jnp.float32)
+
+    project_windows(tokens(), w_k, w_qv, keys, qv_t, 0)
+    attend(count, *scratch)
+    y = finished(tokens(), [joined[i] for i in range(count)], w_prj, w_gu, w_dwn)
+    y = y.astype(jnp.bfloat16)
+    for i in range(count):
+        for j in range(4):
+            low = i * LANES + j * half_tok
+            outs[j][spans[i]] = y[low : low + half_tok]
+
+
+def from_tokens_kernel(h_ref, *rest):
+    ins, (out_ref, tiles, wide) = rest[:-3], rest[-3:]
     h = h_ref[0]
-    for j, ref in enumerate((own_lo, own_up, oth_lo, oth_up)):
-        half = h if j < 2 else 1 - h
-        tiles[half, j % 2] = ref[...].astype(jnp.float32).reshape(HALF, 4, WIN, LANES)
+    for k, (low, high) in enumerate(SHIFTED):
+        for j in range(4):
+            half = h if j < 2 else 1 - h
+            part = ins[4 * k + j][...].astype(jnp.float32)
+            tiles[half, j % 2, low:high] = part.reshape(high - low, 4, WIN, LANES)
     for r in range(WIN):
         lo = 0 if r >= 4 else 1
         row = [tiles[half, lo, :, r % 4].reshape(LANES, LANES).T for half in range(2)]
         row = pltpu.roll(jnp.concatenate(row, axis=1), WIN // 2, 1)
-        wide[:, r, :] = row[:C]
-    out_ref[...] = wide[...].astype(jnp.bfloat16)
+        for half in range(2):
+            part = row[:C, half * LANES : (half + 1) * LANES]
+            wide.at[half][pl.ds(r, C, stride=WIN), :] = part
+    for half in range(2):
+        part = wide[half].reshape(C, WIN, LANES).astype(jnp.bfloat16)
+        out_ref[:, :, half * LANES : (half + 1) * LANES] = part
 
 
 VMEM = pl.BlockSpec(memory_space=pltpu.VMEM)
@@ -250,44 +250,51 @@
 
 
 def to_tokens(h, x):
-    rows = (HALF + 1) * TOK
+    shapes = [tokens_shape((high - low) * TOK) for low, high in WINDOWS]
     return pl.pallas_call(
         to_tokens_kernel,
-        out_shape=[tokens_shape(rows)] * 2,
+        out_shape=shapes * 2,
         in_specs=[SMEM, VMEM],
-        out_specs=[VMEM] * 2,
+        out_specs=[VMEM] * (2 * len(shapes)),
         scratch_shapes=[
-            pltpu.VMEM((C, WIN, 2 * LANES), jnp.float32),
-            pltpu.VMEM((2, HALF, WIN, WIN, LANES), jnp.float32),
+            pltpu.VMEM((2, C * WIN, LANES), jnp.float32),
+            pltpu.VMEM((2, HALF + 1, WIN, WIN, LANES), jnp.float32),
         ],
         compiler_params=PARAMS,
         name="to_tokens",
     )(h, x)
 
 
-def layer_one(own, oth, weights):
+def layer_one(chunk, own, oth, before, weights):
+    first, last = chunk == 0, chunk == len(WINDOWS) - 1
+    count = WINDOWS[chunk][1] - WINDOWS[chunk][0]
+    width = SHIFTED[chunk][1] - SHIFTED[chunk][0]
+    edge = [] if last else [jax.ShapeDtypeStruct((2, WIN, WIN, LANES), jnp.float32)]
+    shapes = [tokens_shape(width * TOK // 2)] * 4 + edge
+    args = (own, oth, *before, *weights)
     return pl.pallas_call(
-        layer_one_kernel,
-        out_shape=[tokens_shape(HALF * TOK // 2)] * 4,
-        in_specs=[VMEM] * 7,
-        out_specs=[VMEM] * 4,
+        functools.partial(layer_one_kernel, count, first, last),
+        out_shape=shapes,
+        in_specs=[VMEM] * len(args),
+        out_specs=[VMEM] * len(shapes),
         scratch_shapes=[
-            pltpu.VMEM((2, WIN, (HALF + 1) * WIN, LANES), jnp.float32),
-            pltpu.VMEM((2, 2, HALF, 4, WIN, LANES), jnp.float32),
-            *attention_scratch(HALF + 1),
+            pltpu.VMEM((2, WIN, (width + 1) * WIN, LANES), jnp.float32),
+            pltpu.VMEM((2, 2, width, 4, WIN, LANES), jnp.float32),
+            *attention_scratch(count),
         ],
         compiler_params=PARAMS,
         name="layer_one",
-    )(own, oth, *weights)
-
-
-def layer_two(pieces, weights):
+    )(*args)
+
+
+def layer_two(chunk, pieces, weights):
+    count = SHIFTED[chunk][1] - SHIFTED[chunk][0]
     return pl.pallas_call(
-        layer_two_kernel,
-        out_shape=[tokens_shape(HALF * TOK // 2)] * 4,
+        functools.partial(layer_two_kernel, count),
+        out_shape=[tokens_shape(count * TOK // 2)] * 4,
         in_specs=[VMEM] * 9,
         out_specs=[VMEM] * 4,
-        scratch_shapes=attention_scratch(HALF),
+        scratch_shapes=attention_scratch(count),
         compiler_params=PARAMS,
         name="layer_two",
     )(*pieces, *weights)
@@ -297,11 +304,11 @@
     return pl.pallas_call(
         from_tokens_kernel,
         out_shape=jax.ShapeDtypeStruct((C, WIN, 2 * LANES), jnp.bfloat16),
-        in_specs=[SMEM] + [VMEM] * 4,
+        in_specs=[SMEM] + [VMEM] * len(pieces),
         out_specs=VMEM,
         scratch_shapes=[
             pltpu.VMEM((2, 2, HALF, 4, WIN, LANES), jnp.float32),
-            pltpu.VMEM((C, WIN, 2 * LANES), jnp.float32),
+            pltpu.VMEM((2, C * WIN, LANES), jnp.float32),
         ],
         compiler_params=PARAMS,
         name="from_tokens",
@@ -349,17 +356,27 @@
     h = (lax.axis_index("frame") % 2).astype(jnp.int32).reshape(1)
     w_one = prepared(*[w[0] for w in weights])
     w_two = prepared(*[w[1] for w in weights])
-    to_send, own = to_tokens(h, features[0])
-    oth = send(to_send, 1, 0)
-    own_up, own_lo, oth_up, oth_lo = layer_one(own, oth, w_one)
-    oth_lo = send(oth_lo, 2, 0)
-    oth_up = send(oth_up, 2, -1)
-    own_up = send(own_up, 0, -1)
-    own_lo, own_up, oth_lo, oth_up = layer_two((own_lo, own_up, oth_lo, oth_up), w_two)
-    oth_lo = send(oth_lo, -1, 0)
-    oth_up = send(oth_up, -1, 1)
-    own_up = send(own_up, 0, 1)
-    return from_tokens(h, (own_lo, own_up, oth_lo, oth_up))[None]
+    parts = to_tokens(h, features[0])
+    chunks = range(len(WINDOWS))
+    others = [send(parts[k], 1, 0) for k in chunks]
+    edge = ()
+    pieces = []
+    for k in chunks:
+        own_up, own_lo, oth_up, oth_lo, *edge = layer_one(
+            k, parts[len(WINDOWS) + k], others[k], edge, w_one
+        )
+        oth_lo = send(oth_lo, 2, 0)
+        oth_up = send(oth_up, 2, -1)
+        own_up = send(own_up, 0, -1)
+        pieces.append((own_lo, own_up, oth_lo, oth_up))
+    home = []
+    for k in chunks:
+        own_lo, own_up, oth_lo, oth_up = layer_two(k, pieces[k], w_two)
+        oth_lo = send(oth_lo, -1, 0)
+        oth_up = send(oth_up, -1, 1)
+        own_up = send(own_up, 0, 1)
+        home += [own_lo, own_up, oth_lo, oth_up]
+    return from_tokens(h, home)[None]
 
 
 def solution(mesh):

time: 80.6 us -> 92.4 us (1.15)
  starting transfers between devices: 15.7 us -> 27.1 us
  waiting for transfers between devices: 19.3 us -> 15.3 us
  Pallas kernels: 32.2 us -> 35.2 us
  local copies, waits for them, and re-layouts: 8.91 us -> 10 us
    ppermute x7 -> x14, starting transfers between devices: 15.7 us -> 27.1 us  [send(): lax.ppermute(value, ('frame', 'strip'), route(frame_step, strip_step))]
    ppermute x7 -> x14, waiting for transfers between devices: 19.3 us -> 15.3 us  [send(): lax.ppermute(value, ('frame', 'strip'), route(frame_step, strip_step))]
    pallas_call x3 -> x5, Pallas kernels: 29.5 us -> 32.5 us  [the longest x2 15.6 us: layer_one(): pl.pallas_call(functools.partial(layer_one_kernel, count, first, last), o...]
    unnamed x30 -> x50, local copies, waits for them, and re-layouts: 5.82 us -> 6.95 us
  transfers between devices with their start and end apart: 7 -> 14, of which waited for: 4 -> 3; matrix products, arithmetic and copies ran while one was open for 9% -> 8% of each run, Pallas kernels for 0% -> 25%
where the time goes in v3:
time: 92.4 us; the launch traced here: 92 us
  Pallas kernels  35.2 us (38%)
  starting transfers between devices  27.1 us (29%)
  waiting for transfers between devices  15.3 us (17%)
  local copies, waits for them, and re-layouts  10 us (11%)
  other arithmetic  4.01 us (4%)
    ppermute x14, starting transfers between devices, send(): lax.ppermute(value, ('frame', 'strip'), route(frame_step, strip_step))  27.1 us
    pallas_call x2, Pallas kernels, layer_one(): pl.pallas_call(functools.partial(layer_one_kernel, count, first, last), o...  15.6 us
    ppermute x14, waiting for transfers between devices, send(): lax.ppermute(value, ('frame', 'strip'), route(frame_step, strip_step))  15.3 us
    pallas_call x2, Pallas kernels, layer_two(): pl.pallas_call(functools.partial(layer_two_kernel, count), out_shape=[tok...  14.9 us
    unnamed x50, local copies, waits for them, and re-layouts  6.95 us
    pallas_call x1, Pallas kernels, from_tokens(): pl.pallas_call(from_tokens_kernel, out_shape=jax.ShapeDtypeStruct((C, WIN...  2.69 us
    pallas_call x1, Pallas kernels, to_tokens(): pl.pallas_call(to_tokens_kernel, out_shape=shapes * 2, in_specs=[SMEM, VM...  2.07 us
  transfers between devices with their start and end apart: 14, of which 3 were waited for; matrix products, arithmetic and copies ran while one was open for 8% of the time, Pallas kernels for 25%

profile of v3, /device:TPU:1, one launch (start us, length us, event | category | flops | bytes accessed | tf_op | source)
XLA Modules:
  0.0 92.0 jit_solution(3102072329094530799)
XLA Ops:
  0.0 2.1 %to_tokens.1 = (bf16[576,128]{1,0:T(8,128)(2,1)}, bf16[512,128]{1,0:T(8,128)(2,1)}, bf16[576,128]{1,0:T(8,128)(2,1)}, bf16[512,128]{1,0:T(8,128)(2,1)}) custom-call(s32[1]{0:T(128)} %bitcast.h_ref, bf16[120,8,256]{2,1,0:T(8,128)(2,1)} %bitcast.43), custom_call_target="tpu_custom_call" | custom-call | tf_op jit(solution)/shard_map/to_tokens/pallas_call | solution.py:254
  2.1 3.7 %collective-permute-start = (bf16[576,128]{1,0:T(8,128)(2,1)}, bf16[576,128]{1,0:T(8,128)(2,1)S(1)}, u32[]{:S(2)}, u32[]{:S(2)}) collective-permute-start(bf16[576,128]{1,0:T(8,128)(2,1)} %get-tuple-element.27), channel_id=1, source_target_pairs={{0,4},{1,5},{2,6},{3,7},{4,0},{5,1},{6,2},{7,3},{8,12},{9,13},{10,... | collective-permute-start | bytes 442376 | tf_op jit(solution)/shard_map/ppermute | solution.py:354
  5.8 0.0 collective-permute-start.7
  5.9 0.0 copy-start.1
  5.9 0.1 copy.16
  6.0 0.8 copy-done.1
  6.8 0.1 copy.17
  7.0 0.0 copy-start.4
  7.1 0.8 copy-done.4
  7.9 0.0 copy-start.5
  8.0 0.8 copy-done.5
  8.9 0.1 copy.18
  9.0 0.0 copy-start.6
  9.0 0.0 copy-start.7
  9.0 0.1 copy.19
  9.2 0.7 copy-done.6
  9.9 0.1 copy-done.7
  10.0 0.7 fusion.24.rest_3_.rest_4_
  10.6 0.6 fusion.30.rest_2_.rest_3_
  11.3 0.7 fusion.25.rest_7_
  12.0 0.7 fusion.20.rest_1_.rest_2_
  12.7 0.7 copy.10.rest_0_.rest_1_
  13.4 0.6 pad.109.rest_4_.rest_5_
  14.1 0.7 copy.13.rest_4_
  14.9 0.7 fusion.23.rest_5_
  15.6 0.0 collective-permute-done.oth_ref
  15.6 0.7 copy-done.2
  16.3 8.0 %layer_one.2 = (bf16[256,128]{1,0:T(8,128)(2,1)}, bf16[256,128]{1,0:T(8,128)(2,1)}, bf16[256,128]{1,0:T(8,128)(2,1)}, bf16[256,128]{1,0:T(8,128)(2,1)}, f32[2,8,8,128]{3,2,1,0:T(8,128)}) custom-call(bf16[576,128]{1,0:T(8,128)(2,1)} %get-tuple-element.26.own_ref, bf16[576,128]{1,0:T(8,128)(2,1)} %copy-done.2, bf16[128,256]{1,0:T(8,128)(2,1)} %copy.10.rest_0_.rest_1_, ...), custom_call_target="tpu_custom_call" | custom-call | tf_op jit(solution)/shard_map/layer_one/pallas_call | solution.py:275
  24.3 0.0 collective-permute-done.7.oth_ref
  24.3 0.7 copy-done.3
  24.9 7.6 %layer_one.3 = (bf16[256,128]{1,0:T(8,128)(2,1)}, bf16[256,128]{1,0:T(8,128)(2,1)}, bf16[256,128]{1,0:T(8,128)(2,1)}, bf16[256,128]{1,0:T(8,128)(2,1)}) custom-call(bf16[512,128]{1,0:T(8,128)(2,1)} %get-tuple-element.36.own_ref, bf16[512,128]{1,0:T(8,128)(2,1)} %copy-done.3, f32[2,8,8,128]{3,2,1,0:T(8,128)} %get-tuple-element.38.rest_0_, ...), custom_call_target="tpu_custom_call" | custom-call | tf_op jit(solution)/shard_map/layer_one/pallas_call | solution.py:275
  32.5 2.3 %collective-permute-start.10 = (bf16[256,128]{1,0:T(8,128)(2,1)}, bf16[256,128]{1,0:T(8,128)(2,1)S(1)}, u32[]{:S(2)}, u32[]{:S(2)}) collective-permute-start(bf16[256,128]{1,0:T(8,128)(2,1)} %get-tuple-element.42), channel_id=1, source_target_pairs={{0,11},{1,8},{2,9},{3,10},{4,255},{5,252},{6,253},{7,254},{8,19},{... | collective-permute-start | bytes 196616 | tf_op jit(solution)/shard_map/ppermute | solution.py:354
  34.9 0.7 collective-permute-start.8
  35.6 0.8 collective-permute-start.9
  36.4 0.6 fusion.31.rest_6_
  37.0 1.7 %collective-permute-start.1 = (bf16[256,128]{1,0:T(8,128)(2,1)S(1)}, bf16[256,128]{1,0:T(8,128)(2,1)S(1)}, u32[]{:S(2)}, u32[]{:S(2)}) collective-permute-start(bf16[256,128]{1,0:T(8,128)(2,1)S(1)} %copy-done.22), channel_id=1, source_target_pairs={{0,3},{1,0},{2,1},{3,2},{4,7},{5,4},{6,5},{7,6},{8,11},{9,8},{10,9... | collective-permute-start | bytes 196616 | tf_op jit(solution)/shard_map/ppermute | solution.py:354
  38.7 0.9 %collective-permute-start.2 = (bf16[256,128]{1,0:T(8,128)(2,1)S(1)}, bf16[256,128]{1,0:T(8,128)(2,1)S(1)}, u32[]{:S(2)}, u32[]{:S(2)}) collective-permute-start(bf16[256,128]{1,0:T(8,128)(2,1)S(1)} %copy-done.21), channel_id=1, source_target_pairs={{0,8},{1,9},{2,10},{3,11},{4,252},{5,253},{6,254},{7,255},{8,16},{... | collective-permute-start | bytes 196616 | tf_op jit(solution)/shard_map/ppermute | solution.py:354
  39.6 5.7 %collective-permute-done.10.rest_3_ = bf16[256,128]{1,0:T(8,128)(2,1)S(1)} collective-permute-done((bf16[256,128]{1,0:T(8,128)(2,1)}, bf16[256,128]{1,0:T(8,128)(2,1)S(1)}, u32[]{:S(2)}, u32[]{:S(2)}) %collective-permute-start.10) | collective-permute-done | bytes 65568 | tf_op jit(solution)/shard_map/ppermute | solution.py:354
  45.3 0.0 collective-permute-start.3
  45.3 0.6 pad.124.rest_8_
  45.9 0.0 collective-permute-done.8.rest_1_
  46.0 0.0 collective-permute-done.9.rest_2_
  46.0 0.6 copy-done.15
  46.6 0.0 copy-done.17
  46.6 7.5 %layer_two.3 = (bf16[256,128]{1,0:T(8,128)(2,1)}, bf16[256,128]{1,0:T(8,128)(2,1)}, bf16[256,128]{1,0:T(8,128)(2,1)}, bf16[256,128]{1,0:T(8,128)(2,1)}) custom-call(bf16[256,128]{1,0:T(8,128)(2,1)} %get-tuple-element.39.rest_0_, bf16[256,128]{1,0:T(8,128)(2,1)} %copy-done.15, bf16[256,128]{1,0:T(8,128)(2,1)} %copy-done.17, bf16[256,128]{1,0:T(8,128)(2,1)} %copy-done.14, ...), custom_call_target="tpu_custom_call" | custom-call | tf_op jit(solution)/shard_map/layer_two/pallas_call | solution.py:292
  54.1 1.5 %collective-permute-start.11 = (bf16[256,128]{1,0:T(8,128)(2,1)}, bf16[256,128]{1,0:T(8,128)(2,1)S(1)}, u32[]{:S(2)}, u32[]{:S(2)}) collective-permute-start(bf16[256,128]{1,0:T(8,128)(2,1)} %get-tuple-element.44), channel_id=1, source_target_pairs={{0,1},{1,2},{2,3},{3,0},{4,5},{5,6},{6,7},{7,4},{8,9},{9,10},{10,1... | collective-permute-start | bytes 196616 | tf_op jit(solution)/shard_map/ppermute | solution.py:354
  55.5 7.0 %collective-permute-start.12 = (bf16[256,128]{1,0:T(8,128)(2,1)}, bf16[256,128]{1,0:T(8,128)(2,1)S(1)}, u32[]{:S(2)}, u32[]{:S(2)}) collective-permute-start(bf16[256,128]{1,0:T(8,128)(2,1)} %get-tuple-element.45), channel_id=1, source_target_pairs={{0,252},{1,253},{2,254},{3,255},{4,8},{5,9},{6,10},{7,11},{8,4},{9... | collective-permute-start | bytes 196616 | tf_op jit(solution)/shard_map/ppermute | solution.py:354
  62.5 0.0 collective-permute-done.1.rest_1_
  62.5 0.0 collective-permute-start.13
  62.5 0.0 collective-permute-done.2.rest_2_
  62.5 0.0 collective-permute-done.3.rest_3_
  62.5 0.6 copy-done.10
  63.1 0.0 copy-done.11
  63.1 0.0 copy-done.13
  63.1 7.4 %layer_two.2 = (bf16[256,128]{1,0:T(8,128)(2,1)}, bf16[256,128]{1,0:T(8,128)(2,1)}, bf16[256,128]{1,0:T(8,128)(2,1)}, bf16[256,128]{1,0:T(8,128)(2,1)}) custom-call(bf16[256,128]{1,0:T(8,128)(2,1)} %get-tuple-element.28.rest_0_, bf16[256,128]{1,0:T(8,128)(2,1)} %copy-done.10, bf16[256,128]{1,0:T(8,128)(2,1)} %copy-done.11, bf16[256,128]{1,0:T(8,128)(2,1)} %copy-done.13, ...), custom_call_target="tpu_custom_call" | custom-call | tf_op jit(solution)/shard_map/layer_two/pallas_call | solution.py:292
  70.6 0.7 collective-permute-start.4
  71.3 7.7 %collective-permute-start.5 = (bf16[256,128]{1,0:T(8,128)(2,1)}, bf16[256,128]{1,0:T(8,128)(2,1)S(1)}, u32[]{:S(2)}, u32[]{:S(2)}) collective-permute-start(bf16[256,128]{1,0:T(8,128)(2,1)} %get-tuple-element.34), channel_id=1, source_target_pairs={{0,252},{1,253},{2,254},{3,255},{4,8},{5,9},{6,10},{7,11},{8,4},{9... | collective-permute-start | bytes 196616 | tf_op jit(solution)/shard_map/ppermute | solution.py:354
  79.0 0.0 collective-permute-done.11.rest_5_
  79.0 0.0 collective-permute-done.12.rest_6_
  79.1 0.0 collective-permute-done.4.rest_1_
  79.1 2.5 %collective-permute-done.5.rest_2_ = bf16[256,128]{1,0:T(8,128)(2,1)S(1)} collective-permute-done((bf16[256,128]{1,0:T(8,128)(2,1)}, bf16[256,128]{1,0:T(8,128)(2,1)S(1)}, u32[]{:S(2)}, u32[]{:S(2)}) %collective-permute-start.5) | collective-permute-done | bytes 65568 | tf_op jit(solution)/shard_map/ppermute | solution.py:354
  81.7 7.0 %collective-permute-done.6.rest_3_ = bf16[256,128]{1,0:T(8,128)(2,1)S(1)} collective-permute-done((bf16[256,128]{1,0:T(8,128)(2,1)}, bf16[256,128]{1,0:T(8,128)(2,1)S(1)}, u32[]{:S(2)}, u32[]{:S(2)}) %collective-permute-start.6) | collective-permute-done | bytes 65568 | tf_op jit(solution)/shard_map/ppermute | solution.py:354
  88.7 0.6 copy-done.19
  89.3 2.7 %from_tokens.1 = bf16[120,8,256]{2,1,0:T(8,128)(2,1)} custom-call(s32[1]{0:T(128)} %bitcast.h_ref, bf16[256,128]{1,0:T(8,128)(2,1)} %get-tuple-element.32.rest_0_, bf16[256,128]{1,0:T(8,128)(2,1)} %copy-done.16, bf16[256,128]{1,0:T(8,128)(2,1)} %copy-done.18, bf16[256,128]{1,0:T(8,128)(2,1)} %copy-done.19, bf16[256,128]{1,0:T(8,128)(2,1)} %get-tuple-element.43.rest_4_, ...), custom_call_target="tpu_custom_call" | custom-call | tf_op jit(solution)/shard_map/from_tokens/pallas_call | solution.py:304
  (55 shorter events, 0.5 us)
Async XLA Ops:
  0.0 5.8 %copy-start = (bf16[2,120,360]{2,1,0:T(8,128)(2,1)S(1)}, bf16[2,120,360]{2,1,0:T(8,128)(2,1)}, u32[]{:S(2)}) copy-start(bf16[2,120,360]{2,1,0:T(8,128)(2,1)} %param.8) | copy-start | bytes 518404
  2.1 13.5 %collective-permute-start = (bf16[576,128]{1,0:T(8,128)(2,1)}, bf16[576,128]{1,0:T(8,128)(2,1)S(1)}, u32[]{:S(2)}, u32[]{:S(2)}) collective-permute-start(bf16[576,128]{1,0:T(8,128)(2,1)} %get-tuple-element.27), channel_id=1, source_target_pairs={{0,4},{1,5},{2,6},{3,7},{4,0},{5,1},{6,2},{7,3},{8,12},{9,13},{10,... | collective-permute-start | bytes 442376 | tf_op jit(solution)/shard_map/ppermute | solution.py:354
  5.8 18.5 %collective-permute-start.7 = (bf16[512,128]{1,0:T(8,128)(2,1)}, bf16[512,128]{1,0:T(8,128)(2,1)S(1)}, u32[]{:S(2)}, u32[]{:S(2)}) collective-permute-start(bf16[512,128]{1,0:T(8,128)(2,1)} %get-tuple-element.37), channel_id=1, source_target_pairs={{0,4},{1,5},{2,6},{3,7},{4,0},{5,1},{6,2},{7,3},{8,12},{9,13},{10,... | collective-permute-start | bytes 393224 | tf_op jit(solution)/shard_map/ppermute | solution.py:354
  5.9 0.9 %copy-start.1 = (bf16[2,120,360]{2,1,0:T(8,128)(2,1)S(1)}, bf16[2,120,360]{2,1,0:T(8,128)(2,1)}, u32[]{:S(2)}) copy-start(bf16[2,120,360]{2,1,0:T(8,128)(2,1)} %param.9) | copy-start | bytes 518404
  7.0 0.9 copy-start.4
  7.9 0.9 copy-start.5
  9.0 0.9 copy-start.6
  9.0 1.0 %copy-start.7 = (bf16[2,120,240]{2,1,0:T(8,128)(2,1)S(1)}, bf16[2,120,240]{2,1,0:T(8,128)(2,1)}, u32[]{:S(2)}) copy-start(bf16[2,120,240]{2,1,0:T(8,128)(2,1)} %param.11) | copy-start | bytes 345604
  15.6 0.7 copy-start.2
  24.3 0.7 copy-start.3
  24.9 12.1 %copy-start.22 = (bf16[256,128]{1,0:T(8,128)(2,1)S(1)}, bf16[256,128]{1,0:T(8,128)(2,1)}, u32[]{:S(2)}) copy-start(bf16[256,128]{1,0:T(8,128)(2,1)} %get-tuple-element.29) | copy-start | bytes 196612
  32.5 12.8 %collective-permute-start.10 = (bf16[256,128]{1,0:T(8,128)(2,1)}, bf16[256,128]{1,0:T(8,128)(2,1)S(1)}, u32[]{:S(2)}, u32[]{:S(2)}) collective-permute-start(bf16[256,128]{1,0:T(8,128)(2,1)} %get-tuple-element.42), channel_id=1, source_target_pairs={{0,11},{1,8},{2,9},{3,10},{4,255},{5,252},{6,253},{7,254},{8,19},{... | collective-permute-start | bytes 196616 | tf_op jit(solution)/shard_map/ppermute | solution.py:354
  34.9 11.1 %collective-permute-start.8 = (bf16[256,128]{1,0:T(8,128)(2,1)}, bf16[256,128]{1,0:T(8,128)(2,1)S(1)}, u32[]{:S(2)}, u32[]{:S(2)}) collective-permute-start(bf16[256,128]{1,0:T(8,128)(2,1)} %get-tuple-element.40), channel_id=1, source_target_pairs={{0,3},{1,0},{2,1},{3,2},{4,7},{5,4},{6,5},{7,6},{8,11},{9,8},{10,9... | collective-permute-start | bytes 196616 | tf_op jit(solution)/shard_map/ppermute | solution.py:354
  35.6 10.4 %collective-permute-start.9 = (bf16[256,128]{1,0:T(8,128)(2,1)}, bf16[256,128]{1,0:T(8,128)(2,1)S(1)}, u32[]{:S(2)}, u32[]{:S(2)}) collective-permute-start(bf16[256,128]{1,0:T(8,128)(2,1)} %get-tuple-element.41), channel_id=1, source_target_pairs={{0,8},{1,9},{2,10},{3,11},{4,252},{5,253},{6,254},{7,255},{8,16},{... | collective-permute-start | bytes 196616 | tf_op jit(solution)/shard_map/ppermute | solution.py:354
  36.4 2.3 %copy-start.21 = (bf16[256,128]{1,0:T(8,128)(2,1)S(1)}, bf16[256,128]{1,0:T(8,128)(2,1)}, u32[]{:S(2)}) copy-start(bf16[256,128]{1,0:T(8,128)(2,1)} %get-tuple-element.30) | copy-start | bytes 196612
  36.4 8.9 %copy-start.20 = (bf16[256,128]{1,0:T(8,128)(2,1)S(1)}, bf16[256,128]{1,0:T(8,128)(2,1)}, u32[]{:S(2)}) copy-start(bf16[256,128]{1,0:T(8,128)(2,1)} %get-tuple-element.31) | copy-start | bytes 196612
  37.0 25.4 %collective-permute-start.1 = (bf16[256,128]{1,0:T(8,128)(2,1)S(1)}, bf16[256,128]{1,0:T(8,128)(2,1)S(1)}, u32[]{:S(2)}, u32[]{:S(2)}) collective-permute-start(bf16[256,128]{1,0:T(8,128)(2,1)S(1)} %copy-done.22), channel_id=1, source_target_pairs={{0,3},{1,0},{2,1},{3,2},{4,7},{5,4},{6,5},{7,6},{8,11},{9,8},{10,9... | collective-permute-start | bytes 196616 | tf_op jit(solution)/shard_map/ppermute | solution.py:354
  38.7 23.8 %collective-permute-start.2 = (bf16[256,128]{1,0:T(8,128)(2,1)S(1)}, bf16[256,128]{1,0:T(8,128)(2,1)S(1)}, u32[]{:S(2)}, u32[]{:S(2)}) collective-permute-start(bf16[256,128]{1,0:T(8,128)(2,1)S(1)} %copy-done.21), channel_id=1, source_target_pairs={{0,8},{1,9},{2,10},{3,11},{4,252},{5,253},{6,254},{7,255},{8,16},{... | collective-permute-start | bytes 196616 | tf_op jit(solution)/shard_map/ppermute | solution.py:354
  45.3 0.7 copy-start.14
  45.3 17.2 %collective-permute-start.3 = (bf16[256,128]{1,0:T(8,128)(2,1)S(1)}, bf16[256,128]{1,0:T(8,128)(2,1)S(1)}, u32[]{:S(2)}, u32[]{:S(2)}) collective-permute-start(bf16[256,128]{1,0:T(8,128)(2,1)S(1)} %copy-done.20), channel_id=1, source_target_pairs={{0,11},{1,8},{2,9},{3,10},{4,255},{5,252},{6,253},{7,254},{8,19},{... | collective-permute-start | bytes 196616 | tf_op jit(solution)/shard_map/ppermute | solution.py:354
  46.0 0.6 copy-start.15
  46.0 0.6 copy-start.17
  54.1 25.0 %collective-permute-start.11 = (bf16[256,128]{1,0:T(8,128)(2,1)}, bf16[256,128]{1,0:T(8,128)(2,1)S(1)}, u32[]{:S(2)}, u32[]{:S(2)}) collective-permute-start(bf16[256,128]{1,0:T(8,128)(2,1)} %get-tuple-element.44), channel_id=1, source_target_pairs={{0,1},{1,2},{2,3},{3,0},{4,5},{5,6},{6,7},{7,4},{8,9},{9,10},{10,1... | collective-permute-start | bytes 196616 | tf_op jit(solution)/shard_map/ppermute | solution.py:354
  55.5 23.5 %collective-permute-start.12 = (bf16[256,128]{1,0:T(8,128)(2,1)}, bf16[256,128]{1,0:T(8,128)(2,1)S(1)}, u32[]{:S(2)}, u32[]{:S(2)}) collective-permute-start(bf16[256,128]{1,0:T(8,128)(2,1)} %get-tuple-element.45), channel_id=1, source_target_pairs={{0,252},{1,253},{2,254},{3,255},{4,8},{5,9},{6,10},{7,11},{8,4},{9... | collective-permute-start | bytes 196616 | tf_op jit(solution)/shard_map/ppermute | solution.py:354
  62.5 0.6 copy-start.10
  62.5 16.6 %collective-permute-start.13 = (bf16[256,128]{1,0:T(8,128)(2,1)}, bf16[256,128]{1,0:T(8,128)(2,1)S(1)}, u32[]{:S(2)}, u32[]{:S(2)}) collective-permute-start(bf16[256,128]{1,0:T(8,128)(2,1)} %get-tuple-element.46), channel_id=1, source_target_pairs={{0,253},{1,254},{2,255},{3,252},{4,9},{5,10},{6,11},{7,8},{8,5},{9... | collective-permute-start | bytes 196616 | tf_op jit(solution)/shard_map/ppermute | solution.py:354
  62.5 0.6 copy-start.11
  62.5 0.6 copy-start.13
  70.6 8.5 %collective-permute-start.4 = (bf16[256,128]{1,0:T(8,128)(2,1)}, bf16[256,128]{1,0:T(8,128)(2,1)S(1)}, u32[]{:S(2)}, u32[]{:S(2)}) collective-permute-start(bf16[256,128]{1,0:T(8,128)(2,1)} %get-tuple-element.33), channel_id=1, source_target_pairs={{0,1},{1,2},{2,3},{3,0},{4,5},{5,6},{6,7},{7,4},{8,9},{9,10},{10,1... | collective-permute-start | bytes 196616 | tf_op jit(solution)/shard_map/ppermute | solution.py:354
  71.3 10.3 %collective-permute-start.5 = (bf16[256,128]{1,0:T(8,128)(2,1)}, bf16[256,128]{1,0:T(8,128)(2,1)S(1)}, u32[]{:S(2)}, u32[]{:S(2)}) collective-permute-start(bf16[256,128]{1,0:T(8,128)(2,1)} %get-tuple-element.34), channel_id=1, source_target_pairs={{0,252},{1,253},{2,254},{3,255},{4,8},{5,9},{6,10},{7,11},{8,4},{9... | collective-permute-start | bytes 196616 | tf_op jit(solution)/shard_map/ppermute | solution.py:354
  79.0 9.6 %copy-start.8 = (bf16[256,128]{1,0:T(8,128)(2,1)}, bf16[256,128]{1,0:T(8,128)(2,1)S(1)}, u32[]{:S(2)}) copy-start(bf16[256,128]{1,0:T(8,128)(2,1)S(1)} %collective-permute-done.11.rest_5_) | copy-start | bytes 196612
  79.0 9.6 %collective-permute-start.6 = (bf16[256,128]{1,0:T(8,128)(2,1)}, bf16[256,128]{1,0:T(8,128)(2,1)S(1)}, u32[]{:S(2)}, u32[]{:S(2)}) collective-permute-start(bf16[256,128]{1,0:T(8,128)(2,1)} %get-tuple-element.35), channel_id=1, source_target_pairs={{0,253},{1,254},{2,255},{3,252},{4,9},{5,10},{6,11},{7,8},{8,5},{9... | collective-permute-start | bytes 196616 | tf_op jit(solution)/shard_map/ppermute | solution.py:354
  79.1 9.6 %copy-start.9 = (bf16[256,128]{1,0:T(8,128)(2,1)}, bf16[256,128]{1,0:T(8,128)(2,1)S(1)}, u32[]{:S(2)}) copy-start(bf16[256,128]{1,0:T(8,128)(2,1)S(1)} %collective-permute-done.12.rest_6_) | copy-start | bytes 196612
  79.1 9.6 %copy-start.12 = (bf16[256,128]{1,0:T(8,128)(2,1)}, bf16[256,128]{1,0:T(8,128)(2,1)S(1)}, u32[]{:S(2)}) copy-start(bf16[256,128]{1,0:T(8,128)(2,1)S(1)} %collective-permute-done.13.rest_7_) | copy-start | bytes 196612
  79.1 9.6 %copy-start.16 = (bf16[256,128]{1,0:T(8,128)(2,1)}, bf16[256,128]{1,0:T(8,128)(2,1)S(1)}, u32[]{:S(2)}) copy-start(bf16[256,128]{1,0:T(8,128)(2,1)S(1)} %collective-permute-done.4.rest_1_) | copy-start | bytes 196612
  81.6 7.0 %copy-start.18 = (bf16[256,128]{1,0:T(8,128)(2,1)}, bf16[256,128]{1,0:T(8,128)(2,1)S(1)}, u32[]{:S(2)}) copy-start(bf16[256,128]{1,0:T(8,128)(2,1)S(1)} %collective-permute-done.5.rest_2_) | copy-start | bytes 196612
  88.7 0.6 copy-start.19

commit v4 on v3

--- a/solution.py
+++ b/solution.py
@@ -101,22 +101,19 @@
 
 def attend(count, keys, qv_t, mutual_scores, self_scores, joined):
     scores = (mutual_scores, self_scores)
-
-    def body(step, carry):
-        lane = lax.broadcasted_iota(jnp.int32, (TOK, 2 * LANES), 1)
-        of_first = (lane % LANES) < TOK
-        now = jnp.minimum(step, count - 1)
-        old = jnp.maximum(step - 1, 0)
+    lane = lax.broadcasted_iota(jnp.int32, (TOK, 2 * LANES), 1)
+    of_first = (lane % LANES) < TOK
+    blocks = [(kind, pair) for kind in range(2) for pair in range(HEADS // 2)]
+    for kind, pair in blocks:
+        scores[kind][0, pair] = score_block(kind, pair, keys, qv_t, 0, of_first)
+    for i in range(count):
         outs = []
-        for kind in range(2):
-            for pair in range(HEADS // 2):
-                ref = scores[kind]
-                outs += mix_block(kind, pair, ref[pair], qv_t, old, of_first)
-                ref[pair] = score_block(kind, pair, keys, qv_t, now, of_first)
-        joined[old] = jnp.concatenate(outs, axis=0).astype(jnp.bfloat16)
-        return carry
-
-    lax.fori_loop(0, count + 1, body, 0)
+        for kind, pair in blocks:
+            ref = scores[kind]
+            if i + 1 < count:
+                ref[(i + 1) % 2, pair] = score_block(kind, pair, keys, qv_t, i + 1, of_first)
+            outs += mix_block(kind, pair, ref[i % 2, pair], qv_t, i, of_first)
+        joined[i] = jnp.concatenate(outs, axis=0).astype(jnp.bfloat16)
 
 
 def finished(x, joined, w_prj, w_gu, w_dwn):
@@ -232,6 +229,7 @@
 
 VMEM = pl.BlockSpec(memory_space=pltpu.VMEM)
 SMEM = pl.BlockSpec(memory_space=pltpu.SMEM)
+COST = pl.CostEstimate(flops=8 * 10**9, bytes_accessed=2**20, transcendentals=2**20)
 PARAMS = pltpu.CompilerParams(vmem_limit_bytes=VMEM_LIMIT)
 
 
@@ -239,8 +237,8 @@
     return [
         pltpu.VMEM((count, LANES, 2 * LANES), jnp.bfloat16),
         pltpu.VMEM((count, 2 * LANES + 2 * HEADS * VHEAD, LANES), jnp.bfloat16),
-        pltpu.VMEM((HEADS // 2, TOK, 2 * LANES), jnp.float32),
-        pltpu.VMEM((HEADS // 2, 2 * TOK, 2 * LANES), jnp.float32),
+        pltpu.VMEM((2, HEADS // 2, TOK, 2 * LANES), jnp.float32),
+        pltpu.VMEM((2, HEADS // 2, 2 * TOK, 2 * LANES), jnp.float32),
         pltpu.VMEM((count, 2 * HEADS * VHEAD, LANES), jnp.bfloat16),
     ]
 
@@ -283,6 +281,7 @@
             *attention_scratch(count),
         ],
         compiler_params=PARAMS,
+        cost_estimate=COST,
         name="layer_one",
     )(*args)
 
@@ -296,6 +295,7 @@
         out_specs=[VMEM] * 4,
         scratch_shapes=attention_scratch(count),
         compiler_params=PARAMS,
+        cost_estimate=COST,
         name="layer_two",
     )(*pieces, *weights)
 
@@ -315,28 +315,57 @@
     )(h, *pieces)
 
 
-def pad_to(array, rows, cols):
-    return jnp.pad(array, ((0, rows - array.shape[0]), (0, cols - array.shape[1])))
-
-
-def by_head(array):
-    spread = array.reshape(HEADS, HEAD, array.shape[1])
-    spread = jnp.pad(spread, ((0, 0), (0, VHEAD - HEAD), (0, 0)))
-    return spread.reshape(HEADS * VHEAD, array.shape[1])
-
-
-def prepared(w_mut, w_slf, w_prj, w_gte, w_upp, w_dwn):
-    w_k = [pad_to(w[:, C : 2 * C], LANES, LANES) for w in (w_mut, w_slf)]
-    w_q = [pad_to(w[:, :C].T, LANES, LANES) for w in (w_mut, w_slf)]
-    w_v = [pad_to(by_head(w[:, 2 * C :].T), HEADS * VHEAD, LANES) for w in (w_mut, w_slf)]
-    w_p = [pad_to(by_head(w), HEADS * VHEAD, LANES) for w in (w_prj[:C], w_prj[C:])]
-    return (
-        jnp.concatenate(w_k, axis=1),
-        jnp.concatenate(w_q + w_v, axis=0),
-        jnp.concatenate(w_p, axis=0),
-        jnp.concatenate([pad_to(w, LANES, 2 * LANES) for w in (w_gte, w_upp)], axis=1),
-        pad_to(w_dwn, 2 * LANES, LANES),
-    )
+def prepare_kernel(w_mut, w_slf, w_prj, w_gte, w_upp, w_dwn, *outs):
+    def selector(rows, cols, picks):
+        row = lax.broadcasted_iota(jnp.int32, (rows, cols), 0)
+        col = lax.broadcasted_iota(jnp.int32, (rows, cols), 1)
+        hit = None
+        for first_row, first_col, size in picks:
+            inside = (row >= first_row) & (row < first_row + size)
+            run = inside & (col - first_col == row - first_row)
+            hit = run if hit is None else hit | run
+        return jnp.where(hit, 1.0, 0.0).astype(jnp.bfloat16)
+
+    by_head = [(h * VHEAD, h * HEAD, HEAD) for h in range(HEADS)]
+    pick_q = selector(LANES, 3 * C, [(0, 0, C)])
+    pick_v = selector(HEADS * VHEAD, 3 * C, [(r, 2 * C + c, n) for r, c, n in by_head])
+    pick_k = selector(LANES, 3 * C, [(0, C, C)])
+    spread = selector(HEADS * VHEAD, C, by_head)
+    for layer in range(2):
+        w_k, w_qv, w_p, w_gu, w_d = outs[5 * layer : 5 * layer + 5]
+        for ref in (w_k, w_qv, w_p, w_gu, w_d):
+            ref[...] = jnp.zeros(ref.shape, jnp.bfloat16)
+        v_rows = HEADS * VHEAD
+        for i, w in enumerate((w_mut, w_slf)):
+            w = w[layer]
+            w_k[:C, i * LANES : (i + 1) * LANES] = matmul_nt(w, pick_k).astype(jnp.bfloat16)
+            w_qv[i * LANES : (i + 1) * LANES, :C] = matmul_nt(pick_q, w).astype(jnp.bfloat16)
+            low = 2 * LANES + i * v_rows
+            w_qv[low : low + v_rows, :C] = matmul_nt(pick_v, w).astype(jnp.bfloat16)
+            part = matmul(spread, w_prj[layer, i * C : (i + 1) * C])
+            w_p[i * v_rows : (i + 1) * v_rows, :C] = part.astype(jnp.bfloat16)
+        w_gu[:C, :FFN] = w_gte[layer]
+        w_gu[:C, 2 * LANES : 2 * LANES + FFN] = w_upp[layer]
+        w_d[:FFN, :C] = w_dwn[layer]
+
+
+def prepared(*weights):
+    v_rows = HEADS * VHEAD
+    shapes = [
+        (LANES, 2 * LANES),
+        (2 * LANES + 2 * v_rows, LANES),
+        (2 * v_rows, LANES),
+        (LANES, 4 * LANES),
+        (2 * LANES, LANES),
+    ] * 2
+    return pl.pallas_call(
+        prepare_kernel,
+        out_shape=[jax.ShapeDtypeStruct(shape, jnp.bfloat16) for shape in shapes],
+        in_specs=[VMEM] * len(weights),
+        out_specs=[VMEM] * len(shapes),
+        compiler_params=PARAMS,
+        name="prepare",
+    )(*weights)
 
 
 def on_device(features, *weights):
@@ -354,8 +383,8 @@
         return lax.ppermute(value, ("frame", "strip"), route(frame_step, strip_step))
 
     h = (lax.axis_index("frame") % 2).astype(jnp.int32).reshape(1)
-    w_one = prepared(*[w[0] for w in weights])
-    w_two = prepared(*[w[1] for w in weights])
+    ready = prepared(*weights)
+    w_one, w_two = ready[:5], ready[5:]
     parts = to_tokens(h, features[0])
     chunks = range(len(WINDOWS))
     others = [send(parts[k], 1, 0) for k in chunks]

time: 92.4 us -> 77 us (0.83)
  local copies, waits for them, and re-layouts: 10 us -> 3.18 us
  waiting for transfers between devices: 15.3 us -> 9.61 us
  starting transfers between devices: 27.1 us -> 32 us
  other arithmetic: 4.01 us -> 0 us
  Pallas kernels: 35.2 us -> 31.7 us
    ppermute x14, waiting for transfers between devices: 15.3 us -> 9.61 us  [send(): lax.ppermute(value, ('frame', 'strip'), route(frame_step, strip_step))]
    ppermute x14, starting transfers between devices: 27.1 us -> 32 us  [send(): lax.ppermute(value, ('frame', 'strip'), route(frame_step, strip_step))]
    concatenate x8 -> x0, other arithmetic: 4.01 us -> none  [the longest x2 1.36 us: prepared(): jnp.concatenate(w_q + w_v, axis=0)]
    unnamed x50 -> x28, local copies, waits for them, and re-layouts: 6.95 us -> 3.18 us
    pallas_call x2, Pallas kernels: 14.9 us -> 11.7 us  [layer_two(): pl.pallas_call(functools.partial(layer_two_kernel, count), out_shape=[tok...]
    pallas_call x2, Pallas kernels: 15.6 us -> 12.5 us  [layer_one(): pl.pallas_call(functools.partial(layer_one_kernel, count, first, last), o...]
    pallas_call x0 -> x1, Pallas kernels: none -> 2.77 us  [prepared(): pl.pallas_call(prepare_kernel, out_shape=[jax.ShapeDtypeStruct(shape, jnp...]
    concatenate x2 -> x0, local copies, waits for them, and re-layouts: 1.47 us -> none  [prepared(): jnp.concatenate(w_k, axis=1)]
  transfers between devices with their start and end apart: 14 -> 14, of which waited for: 3 -> 2; matrix products, arithmetic and copies ran while one was open for 8% -> 0% of each run, Pallas kernels for 25% -> 35%
where the time goes in v4:
time: 77 us; the launch traced here: 76.7 us
  starting transfers between devices  32 us (42%)
  Pallas kernels  31.7 us (41%)
  waiting for transfers between devices  9.61 us (12%)
  local copies, waits for them, and re-layouts  3.18 us (4%)
    ppermute x14, starting transfers between devices, send(): lax.ppermute(value, ('frame', 'strip'), route(frame_step, strip_step))  32 us
    pallas_call x2, Pallas kernels, layer_one(): pl.pallas_call(functools.partial(layer_one_kernel, count, first, last), o...  12.5 us
    pallas_call x2, Pallas kernels, layer_two(): pl.pallas_call(functools.partial(layer_two_kernel, count), out_shape=[tok...  11.7 us
    ppermute x14, waiting for transfers between devices, send(): lax.ppermute(value, ('frame', 'strip'), route(frame_step, strip_step))  9.61 us
    unnamed x28, local copies, waits for them, and re-layouts  3.18 us
    pallas_call x1, Pallas kernels, prepared(): pl.pallas_call(prepare_kernel, out_shape=[jax.ShapeDtypeStruct(shape, jnp...  2.77 us
    pallas_call x1, Pallas kernels, from_tokens(): pl.pallas_call(from_tokens_kernel, out_shape=jax.ShapeDtypeStruct((C, WIN...  2.69 us
    pallas_call x1, Pallas kernels, to_tokens(): pl.pallas_call(to_tokens_kernel, out_shape=shapes * 2, in_specs=[SMEM, VM...  2.03 us
  transfers between devices with their start and end apart: 14, of which 2 were waited for; matrix products, arithmetic and copies ran while one was open for 0% of the time, Pallas kernels for 35%

profile of v4, /device:TPU:1, one launch (start us, length us, event | category | flops | bytes accessed | tf_op | source)
XLA Modules:
  0.0 76.7 jit_solution(5853886265575676470)
XLA Ops:
  0.0 2.0 %to_tokens.1 = (bf16[576,128]{1,0:T(8,128)(2,1)}, bf16[512,128]{1,0:T(8,128)(2,1)}, bf16[576,128]{1,0:T(8,128)(2,1)}, bf16[512,128]{1,0:T(8,128)(2,1)}) custom-call(s32[1]{0:T(128)} %bitcast.h_ref, bf16[120,8,256]{2,1,0:T(8,128)(2,1)} %bitcast.3), custom_call_target="tpu_custom_call" | custom-call | tf_op jit(solution)/shard_map/to_tokens/pallas_call | solution.py:252
  2.0 3.7 %collective-permute-start = (bf16[576,128]{1,0:T(8,128)(2,1)}, bf16[576,128]{1,0:T(8,128)(2,1)S(1)}, u32[]{:S(2)}, u32[]{:S(2)}) collective-permute-start(bf16[576,128]{1,0:T(8,128)(2,1)} %get-tuple-element.37), channel_id=1, source_target_pairs={{0,4},{1,5},{2,6},{3,7},{4,0},{5,1},{6,2},{7,3},{8,12},{9,13},{10,... | collective-permute-start | bytes 442376 | tf_op jit(solution)/shard_map/ppermute | solution.py:383
  5.8 0.0 collective-permute-start.7
  5.8 2.8 %prepare.1 = (bf16[128,256]{1,0:T(8,128)(2,1)}, bf16[544,128]{1,0:T(8,128)(2,1)}, bf16[288,128]{1,0:T(8,128)(2,1)}, bf16[128,512]{1,0:T(8,128)(2,1)}, bf16[256,1...) custom-call(bf16[2,120,360]{2,1,0:T(8,128)(2,1)} %w_mut.1, ...), custom_call_target="tpu_custom_call" | custom-call | tf_op jit(solution)/shard_map/prepare/pallas_call | solution.py:361
  8.6 0.0 collective-permute-done.oth_ref
  8.6 0.0 copy-start.6
  8.6 0.7 copy-done.6
  9.3 6.5 %layer_one.2 = (bf16[256,128]{1,0:T(8,128)(2,1)}, bf16[256,128]{1,0:T(8,128)(2,1)}, bf16[256,128]{1,0:T(8,128)(2,1)}, bf16[256,128]{1,0:T(8,128)(2,1)}, f32[2,8,8,128]{3,2,1,0:T(8,128)}) custom-call(bf16[576,128]{1,0:T(8,128)(2,1)} %get-tuple-element.36.own_ref, bf16[576,128]{1,0:T(8,128)(2,1)} %copy-done.6, ...), custom_call_target="tpu_custom_call" | custom-call | flops 8000000000 | bytes 1048576 | tf_op jit(solution)/shard_map/layer_one/pallas_call | solution.py:273
  15.8 4.9 %collective-permute-start.1 = (bf16[256,128]{1,0:T(8,128)(2,1)}, bf16[256,128]{1,0:T(8,128)(2,1)S(1)}, u32[]{:S(2)}, u32[]{:S(2)}) collective-permute-start(bf16[256,128]{1,0:T(8,128)(2,1)} %get-tuple-element.44), channel_id=1, source_target_pairs={{0,3},{1,0},{2,1},{3,2},{4,7},{5,4},{6,5},{7,6},{8,11},{9,8},{10,9... | collective-permute-start | bytes 196616 | tf_op jit(solution)/shard_map/ppermute | solution.py:383
  20.7 0.0 collective-permute-start.2
  20.7 0.4 collective-permute-start.3
  21.1 0.0 collective-permute-done.7.oth_ref
  21.1 0.0 copy-start.7
  21.1 0.7 copy-done.7
  21.7 6.0 %layer_one.3 = (bf16[256,128]{1,0:T(8,128)(2,1)}, bf16[256,128]{1,0:T(8,128)(2,1)}, bf16[256,128]{1,0:T(8,128)(2,1)}, bf16[256,128]{1,0:T(8,128)(2,1)}) custom-call(bf16[512,128]{1,0:T(8,128)(2,1)} %get-tuple-element.56.own_ref, bf16[512,128]{1,0:T(8,128)(2,1)} %copy-done.7, f32[2,8,8,128]{3,2,1,0:T(8,128)} %get-tuple-element.58.rest_0_, ...), custom_call_target="tpu_custom_call" | custom-call | flops 8000000000 | bytes 1048576 | tf_op jit(solution)/shard_map/layer_one/pallas_call | solution.py:273
  27.7 1.9 %collective-permute-start.8 = (bf16[256,128]{1,0:T(8,128)(2,1)}, bf16[256,128]{1,0:T(8,128)(2,1)S(1)}, u32[]{:S(2)}, u32[]{:S(2)}) collective-permute-start(bf16[256,128]{1,0:T(8,128)(2,1)} %get-tuple-element.60), channel_id=1, source_target_pairs={{0,3},{1,0},{2,1},{3,2},{4,7},{5,4},{6,5},{7,6},{8,11},{9,8},{10,9... | collective-permute-start | bytes 196616 | tf_op jit(solution)/shard_map/ppermute | solution.py:383
  29.6 0.9 %collective-permute-start.9 = (bf16[256,128]{1,0:T(8,128)(2,1)}, bf16[256,128]{1,0:T(8,128)(2,1)S(1)}, u32[]{:S(2)}, u32[]{:S(2)}) collective-permute-start(bf16[256,128]{1,0:T(8,128)(2,1)} %get-tuple-element.61), channel_id=1, source_target_pairs={{0,8},{1,9},{2,10},{3,11},{4,252},{5,253},{6,254},{7,255},{8,16},{... | collective-permute-start | bytes 196616 | tf_op jit(solution)/shard_map/ppermute | solution.py:383
  30.5 0.0 collective-permute-done.1.rest_1_
  30.5 0.0 copy-start.10
  30.5 2.2 %collective-permute-start.10 = (bf16[256,128]{1,0:T(8,128)(2,1)}, bf16[256,128]{1,0:T(8,128)(2,1)S(1)}, u32[]{:S(2)}, u32[]{:S(2)}) collective-permute-start(bf16[256,128]{1,0:T(8,128)(2,1)} %get-tuple-element.62), channel_id=1, source_target_pairs={{0,11},{1,8},{2,9},{3,10},{4,255},{5,252},{6,253},{7,254},{8,19},{... | collective-permute-start | bytes 196616 | tf_op jit(solution)/shard_map/ppermute | solution.py:383
  32.7 0.0 collective-permute-done.2.rest_2_
  32.7 0.0 copy-start.12
  32.7 0.0 collective-permute-done.3.rest_3_
  32.7 0.0 copy-start.13
  32.8 0.0 copy-done.10
  32.8 0.6 copy-done.12
  33.4 0.0 copy-done.13
  33.4 5.9 %layer_two.2 = (bf16[256,128]{1,0:T(8,128)(2,1)}, bf16[256,128]{1,0:T(8,128)(2,1)}, bf16[256,128]{1,0:T(8,128)(2,1)}, bf16[256,128]{1,0:T(8,128)(2,1)}) custom-call(bf16[256,128]{1,0:T(8,128)(2,1)} %get-tuple-element.43.rest_0_, bf16[256,128]{1,0:T(8,128)(2,1)} %copy-done.10, bf16[256,128]{1,0:T(8,128)(2,1)} %copy-done.12, bf16[256,128]{1,0:T(8,128)(2,1)} %copy-done.13, ...), custom_call_target="tpu_custom_call" | custom-call | flops 8000000000 | bytes 1048576 | tf_op jit(solution)/shard_map/layer_two/pallas_call | solution.py:291
  39.3 0.8 %collective-permute-start.4 = (bf16[256,128]{1,0:T(8,128)(2,1)}, bf16[256,128]{1,0:T(8,128)(2,1)S(1)}, u32[]{:S(2)}, u32[]{:S(2)}) collective-permute-start(bf16[256,128]{1,0:T(8,128)(2,1)} %get-tuple-element.53), channel_id=1, source_target_pairs={{0,1},{1,2},{2,3},{3,0},{4,5},{5,6},{6,7},{7,4},{8,9},{9,10},{10,1... | collective-permute-start | bytes 196616 | tf_op jit(solution)/shard_map/ppermute | solution.py:383
  40.1 9.2 %collective-permute-start.5 = (bf16[256,128]{1,0:T(8,128)(2,1)}, bf16[256,128]{1,0:T(8,128)(2,1)S(1)}, u32[]{:S(2)}, u32[]{:S(2)}) collective-permute-start(bf16[256,128]{1,0:T(8,128)(2,1)} %get-tuple-element.54), channel_id=1, source_target_pairs={{0,252},{1,253},{2,254},{3,255},{4,8},{5,9},{6,10},{7,11},{8,4},{9... | collective-permute-start | bytes 196616 | tf_op jit(solution)/shard_map/ppermute | solution.py:383
  49.3 0.0 collective-permute-done.8.rest_1_
  49.3 0.0 copy-start.8
  49.3 0.0 collective-permute-start.6
  49.3 0.0 collective-permute-done.9.rest_2_
  49.3 0.0 copy-start.9
  49.3 0.0 collective-permute-done.10.rest_3_
  49.3 0.0 copy-start.11
  49.3 0.6 copy-done.8
  49.9 0.0 copy-done.9
  49.9 0.0 copy-done.11
  49.9 5.9 %layer_two.3 = (bf16[256,128]{1,0:T(8,128)(2,1)}, bf16[256,128]{1,0:T(8,128)(2,1)}, bf16[256,128]{1,0:T(8,128)(2,1)}, bf16[256,128]{1,0:T(8,128)(2,1)}) custom-call(bf16[256,128]{1,0:T(8,128)(2,1)} %get-tuple-element.59.rest_0_, bf16[256,128]{1,0:T(8,128)(2,1)} %copy-done.8, bf16[256,128]{1,0:T(8,128)(2,1)} %copy-done.9, bf16[256,128]{1,0:T(8,128)(2,1)} %copy-done.11, ...), custom_call_target="tpu_custom_call" | custom-call | flops 8000000000 | bytes 1048576 | tf_op jit(solution)/shard_map/layer_two/pallas_call | solution.py:291
  55.8 0.4 collective-permute-start.11
  56.2 7.5 %collective-permute-start.12 = (bf16[256,128]{1,0:T(8,128)(2,1)}, bf16[256,128]{1,0:T(8,128)(2,1)S(1)}, u32[]{:S(2)}, u32[]{:S(2)}) collective-permute-start(bf16[256,128]{1,0:T(8,128)(2,1)} %get-tuple-element.65), channel_id=1, source_target_pairs={{0,252},{1,253},{2,254},{3,255},{4,8},{5,9},{6,10},{7,11},{8,4},{9... | collective-permute-start | bytes 196616 | tf_op jit(solution)/shard_map/ppermute | solution.py:383
  63.7 0.0 collective-permute-done.4.rest_1_
  63.7 0.0 copy-start
  63.7 0.0 collective-permute-start.13
  63.7 0.0 collective-permute-done.5.rest_2_
  63.8 0.0 copy-start.1
  63.8 0.0 collective-permute-done.6.rest_3_
  63.8 0.0 copy-start.2
  63.8 0.0 collective-permute-done.11.rest_5_
  63.8 0.0 copy-start.3
  63.8 2.4 %collective-permute-done.12.rest_6_ = bf16[256,128]{1,0:T(8,128)(2,1)S(1)} collective-permute-done((bf16[256,128]{1,0:T(8,128)(2,1)}, bf16[256,128]{1,0:T(8,128)(2,1)S(1)}, u32[]{:S(2)}, u32[]{:S(2)}) %collective-permute-start.12) | collective-permute-done | bytes 65568 | tf_op jit(solution)/shard_map/ppermute | solution.py:383
  66.2 0.0 copy-start.4
  66.2 7.2 %collective-permute-done.13.rest_7_ = bf16[256,128]{1,0:T(8,128)(2,1)S(1)} collective-permute-done((bf16[256,128]{1,0:T(8,128)(2,1)}, bf16[256,128]{1,0:T(8,128)(2,1)S(1)}, u32[]{:S(2)}, u32[]{:S(2)}) %collective-permute-start.13) | collective-permute-done | bytes 65568 | tf_op jit(solution)/shard_map/ppermute | solution.py:383
  73.4 0.0 copy-start.5
  73.4 0.0 copy-done
  73.4 0.0 copy-done.1
  73.4 0.0 copy-done.2
  73.4 0.0 copy-done.3
  73.4 0.0 copy-done.4
  73.4 0.6 copy-done.5
  74.0 2.7 %from_tokens.1 = bf16[120,8,256]{2,1,0:T(8,128)(2,1)} custom-call(s32[1]{0:T(128)} %bitcast.h_ref, bf16[256,128]{1,0:T(8,128)(2,1)} %get-tuple-element.52.rest_0_, bf16[256,128]{1,0:T(8,128)(2,1)} %copy-done, bf16[256,128]{1,0:T(8,128)(2,1)} %copy-done.1, bf16[256,128]{1,0:T(8,128)(2,1)} %copy-done.2, bf16[256,128]{1,0:T(8,128)(2,1)} %get-tuple-element.63.rest_4_, ...), custom_call_target="tpu_custom_call" | custom-call | tf_op jit(solution)/shard_map/from_tokens/pallas_call | solution.py:304
Async XLA Ops:
  2.0 6.6 %collective-permute-start = (bf16[576,128]{1,0:T(8,128)(2,1)}, bf16[576,128]{1,0:T(8,128)(2,1)S(1)}, u32[]{:S(2)}, u32[]{:S(2)}) collective-permute-start(bf16[576,128]{1,0:T(8,128)(2,1)} %get-tuple-element.37), channel_id=1, source_target_pairs={{0,4},{1,5},{2,6},{3,7},{4,0},{5,1},{6,2},{7,3},{8,12},{9,13},{10,... | collective-permute-start | bytes 442376 | tf_op jit(solution)/shard_map/ppermute | solution.py:383
  5.8 15.3 %collective-permute-start.7 = (bf16[512,128]{1,0:T(8,128)(2,1)}, bf16[512,128]{1,0:T(8,128)(2,1)S(1)}, u32[]{:S(2)}, u32[]{:S(2)}) collective-permute-start(bf16[512,128]{1,0:T(8,128)(2,1)} %get-tuple-element.57), channel_id=1, source_target_pairs={{0,4},{1,5},{2,6},{3,7},{4,0},{5,1},{6,2},{7,3},{8,12},{9,13},{10,... | collective-permute-start | bytes 393224 | tf_op jit(solution)/shard_map/ppermute | solution.py:383
  8.6 0.7 copy-start.6
  15.8 14.8 %collective-permute-start.1 = (bf16[256,128]{1,0:T(8,128)(2,1)}, bf16[256,128]{1,0:T(8,128)(2,1)S(1)}, u32[]{:S(2)}, u32[]{:S(2)}) collective-permute-start(bf16[256,128]{1,0:T(8,128)(2,1)} %get-tuple-element.44), channel_id=1, source_target_pairs={{0,3},{1,0},{2,1},{3,2},{4,7},{5,4},{6,5},{7,6},{8,11},{9,8},{10,9... | collective-permute-start | bytes 196616 | tf_op jit(solution)/shard_map/ppermute | solution.py:383
  20.7 12.0 %collective-permute-start.2 = (bf16[256,128]{1,0:T(8,128)(2,1)}, bf16[256,128]{1,0:T(8,128)(2,1)S(1)}, u32[]{:S(2)}, u32[]{:S(2)}) collective-permute-start(bf16[256,128]{1,0:T(8,128)(2,1)} %get-tuple-element.45), channel_id=1, source_target_pairs={{0,8},{1,9},{2,10},{3,11},{4,252},{5,253},{6,254},{7,255},{8,16},{... | collective-permute-start | bytes 196616 | tf_op jit(solution)/shard_map/ppermute | solution.py:383
  20.7 12.0 %collective-permute-start.3 = (bf16[256,128]{1,0:T(8,128)(2,1)}, bf16[256,128]{1,0:T(8,128)(2,1)S(1)}, u32[]{:S(2)}, u32[]{:S(2)}) collective-permute-start(bf16[256,128]{1,0:T(8,128)(2,1)} %get-tuple-element.46), channel_id=1, source_target_pairs={{0,11},{1,8},{2,9},{3,10},{4,255},{5,252},{6,253},{7,254},{8,19},{... | collective-permute-start | bytes 196616 | tf_op jit(solution)/shard_map/ppermute | solution.py:383
  21.1 0.7 copy-start.7
  27.7 21.6 %collective-permute-start.8 = (bf16[256,128]{1,0:T(8,128)(2,1)}, bf16[256,128]{1,0:T(8,128)(2,1)S(1)}, u32[]{:S(2)}, u32[]{:S(2)}) collective-permute-start(bf16[256,128]{1,0:T(8,128)(2,1)} %get-tuple-element.60), channel_id=1, source_target_pairs={{0,3},{1,0},{2,1},{3,2},{4,7},{5,4},{6,5},{7,6},{8,11},{9,8},{10,9... | collective-permute-start | bytes 196616 | tf_op jit(solution)/shard_map/ppermute | solution.py:383
  29.6 19.7 %collective-permute-start.9 = (bf16[256,128]{1,0:T(8,128)(2,1)}, bf16[256,128]{1,0:T(8,128)(2,1)S(1)}, u32[]{:S(2)}, u32[]{:S(2)}) collective-permute-start(bf16[256,128]{1,0:T(8,128)(2,1)} %get-tuple-element.61), channel_id=1, source_target_pairs={{0,8},{1,9},{2,10},{3,11},{4,252},{5,253},{6,254},{7,255},{8,16},{... | collective-permute-start | bytes 196616 | tf_op jit(solution)/shard_map/ppermute | solution.py:383
  30.5 2.2 %copy-start.10 = (bf16[256,128]{1,0:T(8,128)(2,1)}, bf16[256,128]{1,0:T(8,128)(2,1)S(1)}, u32[]{:S(2)}) copy-start(bf16[256,128]{1,0:T(8,128)(2,1)S(1)} %collective-permute-done.1.rest_1_) | copy-start | bytes 196612
  30.5 18.8 %collective-permute-start.10 = (bf16[256,128]{1,0:T(8,128)(2,1)}, bf16[256,128]{1,0:T(8,128)(2,1)S(1)}, u32[]{:S(2)}, u32[]{:S(2)}) collective-permute-start(bf16[256,128]{1,0:T(8,128)(2,1)} %get-tuple-element.62), channel_id=1, source_target_pairs={{0,11},{1,8},{2,9},{3,10},{4,255},{5,252},{6,253},{7,254},{8,19},{... | collective-permute-start | bytes 196616 | tf_op jit(solution)/shard_map/ppermute | solution.py:383
  32.7 0.6 copy-start.12
  32.7 0.6 copy-start.13
  39.3 24.5 %collective-permute-start.4 = (bf16[256,128]{1,0:T(8,128)(2,1)}, bf16[256,128]{1,0:T(8,128)(2,1)S(1)}, u32[]{:S(2)}, u32[]{:S(2)}) collective-permute-start(bf16[256,128]{1,0:T(8,128)(2,1)} %get-tuple-element.53), channel_id=1, source_target_pairs={{0,1},{1,2},{2,3},{3,0},{4,5},{5,6},{6,7},{7,4},{8,9},{9,10},{10,1... | collective-permute-start | bytes 196616 | tf_op jit(solution)/shard_map/ppermute | solution.py:383
  40.1 23.7 %collective-permute-start.5 = (bf16[256,128]{1,0:T(8,128)(2,1)}, bf16[256,128]{1,0:T(8,128)(2,1)S(1)}, u32[]{:S(2)}, u32[]{:S(2)}) collective-permute-start(bf16[256,128]{1,0:T(8,128)(2,1)} %get-tuple-element.54), channel_id=1, source_target_pairs={{0,252},{1,253},{2,254},{3,255},{4,8},{5,9},{6,10},{7,11},{8,4},{9... | collective-permute-start | bytes 196616 | tf_op jit(solution)/shard_map/ppermute | solution.py:383
  49.3 0.6 copy-start.8
  49.3 14.5 %collective-permute-start.6 = (bf16[256,128]{1,0:T(8,128)(2,1)}, bf16[256,128]{1,0:T(8,128)(2,1)S(1)}, u32[]{:S(2)}, u32[]{:S(2)}) collective-permute-start(bf16[256,128]{1,0:T(8,128)(2,1)} %get-tuple-element.55), channel_id=1, source_target_pairs={{0,253},{1,254},{2,255},{3,252},{4,9},{5,10},{6,11},{7,8},{8,5},{9... | collective-permute-start | bytes 196616 | tf_op jit(solution)/shard_map/ppermute | solution.py:383
  49.3 0.6 copy-start.9
  49.3 0.6 copy-start.11
  55.8 8.0 %collective-permute-start.11 = (bf16[256,128]{1,0:T(8,128)(2,1)}, bf16[256,128]{1,0:T(8,128)(2,1)S(1)}, u32[]{:S(2)}, u32[]{:S(2)}) collective-permute-start(bf16[256,128]{1,0:T(8,128)(2,1)} %get-tuple-element.64), channel_id=1, source_target_pairs={{0,1},{1,2},{2,3},{3,0},{4,5},{5,6},{6,7},{7,4},{8,9},{9,10},{10,1... | collective-permute-start | bytes 196616 | tf_op jit(solution)/shard_map/ppermute | solution.py:383
  56.2 9.9 %collective-permute-start.12 = (bf16[256,128]{1,0:T(8,128)(2,1)}, bf16[256,128]{1,0:T(8,128)(2,1)S(1)}, u32[]{:S(2)}, u32[]{:S(2)}) collective-permute-start(bf16[256,128]{1,0:T(8,128)(2,1)} %get-tuple-element.65), channel_id=1, source_target_pairs={{0,252},{1,253},{2,254},{3,255},{4,8},{5,9},{6,10},{7,11},{8,4},{9... | collective-permute-start | bytes 196616 | tf_op jit(solution)/shard_map/ppermute | solution.py:383
  63.7 9.6 %copy-start = (bf16[256,128]{1,0:T(8,128)(2,1)}, bf16[256,128]{1,0:T(8,128)(2,1)S(1)}, u32[]{:S(2)}) copy-start(bf16[256,128]{1,0:T(8,128)(2,1)S(1)} %collective-permute-done.4.rest_1_) | copy-start | bytes 196612
  63.7 9.6 %collective-permute-start.13 = (bf16[256,128]{1,0:T(8,128)(2,1)}, bf16[256,128]{1,0:T(8,128)(2,1)S(1)}, u32[]{:S(2)}, u32[]{:S(2)}) collective-permute-start(bf16[256,128]{1,0:T(8,128)(2,1)} %get-tuple-element.66), channel_id=1, source_target_pairs={{0,253},{1,254},{2,255},{3,252},{4,9},{5,10},{6,11},{7,8},{8,5},{9... | collective-permute-start | bytes 196616 | tf_op jit(solution)/shard_map/ppermute | solution.py:383
  63.8 9.6 %copy-start.1 = (bf16[256,128]{1,0:T(8,128)(2,1)}, bf16[256,128]{1,0:T(8,128)(2,1)S(1)}, u32[]{:S(2)}) copy-start(bf16[256,128]{1,0:T(8,128)(2,1)S(1)} %collective-permute-done.5.rest_2_) | copy-start | bytes 196612
  63.8 9.6 %copy-start.2 = (bf16[256,128]{1,0:T(8,128)(2,1)}, bf16[256,128]{1,0:T(8,128)(2,1)S(1)}, u32[]{:S(2)}) copy-start(bf16[256,128]{1,0:T(8,128)(2,1)S(1)} %collective-permute-done.6.rest_3_) | copy-start | bytes 196612
  63.8 9.6 %copy-start.3 = (bf16[256,128]{1,0:T(8,128)(2,1)}, bf16[256,128]{1,0:T(8,128)(2,1)S(1)}, u32[]{:S(2)}) copy-start(bf16[256,128]{1,0:T(8,128)(2,1)S(1)} %collective-permute-done.11.rest_5_) | copy-start | bytes 196612
  66.2 7.2 %copy-start.4 = (bf16[256,128]{1,0:T(8,128)(2,1)}, bf16[256,128]{1,0:T(8,128)(2,1)S(1)}, u32[]{:S(2)}) copy-start(bf16[256,128]{1,0:T(8,128)(2,1)S(1)} %collective-permute-done.12.rest_6_) | copy-start | bytes 196612
  73.4 0.6 copy-start.5

commit v5 on v4

--- a/solution.py
+++ b/solution.py
@@ -16,10 +16,11 @@
 LANES = 128
 VHEAD = 24
 HALF = 16
+GROUP = 8
 TOK = WIN * WIN
 EPS = 1e-05
-SHIFTED = ((0, 8), (8, 16))
-WINDOWS = ((0, 9), (9, 17))
+SHIFTED = ((0, 16),)
+WINDOWS = ((0, 17),)
 EXP2_SCALE = float(np.log2(np.e) * HEAD**-0.5)
 VMEM_LIMIT = 56 * 1024 * 1024
 
@@ -147,6 +148,12 @@
             outs[k * len(WINDOWS) + j][...] = part.astype(jnp.bfloat16)
 
 
+def grouped(count):
+    parts = max(1, count // GROUP)
+    cuts = [count * i // parts for i in range(parts + 1)]
+    return [range(low, high) for low, high in zip(cuts[:-1], cuts[1:])]
+
+
 def layer_one_kernel(count, first, last, own_ref, oth_ref, *rest):
     if not first:
         before, rest = rest[0], rest[1:]
@@ -158,22 +165,24 @@
     keys, qv_t, joined = scratch[0], scratch[1], scratch[-1]
     shift = 0 if first else WIN
 
-    def tokens():
+    def tokens(group):
         parts = []
-        for i in range(count):
+        for i in group:
             span = slice(i * TOK, (i + 1) * TOK)
             parts += [own_ref[span], oth_ref[span]]
         return jnp.concatenate(parts, axis=0).astype(jnp.float32)
 
-    project_windows(tokens(), w_k, w_qv, keys, qv_t, 0)
+    for group in grouped(count):
+        project_windows(tokens(group), w_k, w_qv, keys, qv_t, group[0])
     attend(count, *scratch)
-    y = finished(tokens(), [joined[i] for i in range(count)], w_prj, w_gu, w_dwn)
-    y = y.reshape(count, 2, WIN, WIN, LANES)
     if not first:
         flat[:, :, :WIN, :] = before[...]
-    for i in range(count):
-        for f in range(2):
-            flat[f, :, shift + i * WIN : shift + (i + 1) * WIN, :] = y[i, f]
+    for group in grouped(count):
+        y = finished(tokens(group), [joined[i] for i in group], w_prj, w_gu, w_dwn)
+        y = y.reshape(len(group), 2, WIN, WIN, LANES)
+        for j, i in enumerate(group):
+            for f in range(2):
+                flat[f, :, shift + i * WIN : shift + (i + 1) * WIN, :] = y[j, f]
     width = shift + (count - 1) * WIN
     if not last:
         after[...] = flat[:, :, width : width + WIN, :]
@@ -194,17 +203,20 @@
     half_tok = TOK // 2
     spans = [slice(i * half_tok, (i + 1) * half_tok) for i in range(count)]
 
-    def tokens():
-        return jnp.concatenate([ref[s] for s in spans for ref in ins], axis=0).astype(jnp.float32)
-
-    project_windows(tokens(), w_k, w_qv, keys, qv_t, 0)
+    def tokens(group):
+        parts = [ref[spans[i]] for i in group for ref in ins]
+        return jnp.concatenate(parts, axis=0).astype(jnp.float32)
+
+    for group in grouped(count):
+        project_windows(tokens(group), w_k, w_qv, keys, qv_t, group[0])
     attend(count, *scratch)
-    y = finished(tokens(), [joined[i] for i in range(count)], w_prj, w_gu, w_dwn)
-    y = y.astype(jnp.bfloat16)
-    for i in range(count):
-        for j in range(4):
-            low = i * LANES + j * half_tok
-            outs[j][spans[i]] = y[low : low + half_tok]
+    for group in grouped(count):
+        y = finished(tokens(group), [joined[i] for i in group], w_prj, w_gu, w_dwn)
+        y = y.astype(jnp.bfloat16)
+        for k, i in enumerate(group):
+            for j in range(4):
+                low = k * LANES + j * half_tok
+                outs[j][spans[i]] = y[low : low + half_tok]
 
 
 def from_tokens_kernel(h_ref, *rest):

time: 77 us -> 72.2 us (0.938)
  waiting for transfers between devices: 9.61 us -> 26.7 us
  starting transfers between devices: 32 us -> 16.3 us
  Pallas kernels: 31.7 us -> 26.8 us
  local copies, waits for them, and re-layouts: 3.18 us -> 2.01 us
    ppermute x14 -> x7, waiting for transfers between devices: 9.61 us -> 26.7 us  [send(): lax.ppermute(value, ('frame', 'strip'), route(frame_step, strip_step))]
    ppermute x14 -> x7, starting transfers between devices: 32 us -> 16.3 us  [send(): lax.ppermute(value, ('frame', 'strip'), route(frame_step, strip_step))]
    pallas_call x2 -> x1, Pallas kernels: 12.5 us -> 9.89 us  [layer_one(): pl.pallas_call(functools.partial(layer_one_kernel, count, first, last), o...]
    pallas_call x2 -> x1, Pallas kernels: 11.7 us -> 9.41 us  [layer_two(): pl.pallas_call(functools.partial(layer_two_kernel, count), out_shape=[tok...]
    unnamed x28 -> x14, local copies, waits for them, and re-layouts: 3.18 us -> 2.01 us
  transfers between devices with their start and end apart: 14 -> 7, of which waited for: 2 -> 6; matrix products, arithmetic and copies ran while one was open for 0% -> 0% of each run, Pallas kernels for 35% -> 4%
where the time goes in v5:
time: 72.2 us; the launch traced here: 72 us
  Pallas kernels  26.8 us (37%)
  waiting for transfers between devices  26.7 us (37%)
  starting transfers between devices  16.3 us (23%)
  local copies, waits for them, and re-layouts  2.01 us (3%)
    ppermute x7, waiting for transfers between devices, send(): lax.ppermute(value, ('frame', 'strip'), route(frame_step, strip_step))  26.7 us
    ppermute x7, starting transfers between devices, send(): lax.ppermute(value, ('frame', 'strip'), route(frame_step, strip_step))  16.3 us
    pallas_call x1, Pallas kernels, layer_one(): pl.pallas_call(functools.partial(layer_one_kernel, count, first, last), o...  9.89 us
    pallas_call x1, Pallas kernels, layer_two(): pl.pallas_call(functools.partial(layer_two_kernel, count), out_shape=[tok...  9.41 us
    pallas_call x1, Pallas kernels, prepared(): pl.pallas_call(prepare_kernel, out_shape=[jax.ShapeDtypeStruct(shape, jnp...  2.74 us
    pallas_call x1, Pallas kernels, from_tokens(): pl.pallas_call(from_tokens_kernel, out_shape=jax.ShapeDtypeStruct((C, WIN...  2.73 us
    pallas_call x1, Pallas kernels, to_tokens(): pl.pallas_call(to_tokens_kernel, out_shape=shapes * 2, in_specs=[SMEM, VM...  2.08 us
    unnamed x14, local copies, waits for them, and re-layouts  2.01 us
  transfers between devices with their start and end apart: 7, of which 6 were waited for; matrix products, arithmetic and copies ran while one was open for 0% of the time, Pallas kernels for 4%

profile of v5, /device:TPU:1, one launch (start us, length us, event | category | flops | bytes accessed | tf_op | source)
XLA Modules:
  0.0 72.0 jit_solution(7718523759650461580)
XLA Ops:
  0.0 2.1 %to_tokens.1 = (bf16[1088,128]{1,0:T(8,128)(2,1)}, bf16[1088,128]{1,0:T(8,128)(2,1)}) custom-call(s32[1]{0:T(128)} %bitcast.h_ref, bf16[120,8,256]{2,1,0:T(8,128)(2,1)} %bitcast.3), custom_call_target="tpu_custom_call" | custom-call | tf_op jit(solution)/shard_map/to_tokens/pallas_call | solution.py:264
  2.1 3.7 %collective-permute-start = (bf16[1088,128]{1,0:T(8,128)(2,1)}, bf16[1088,128]{1,0:T(8,128)(2,1)S(1)}, u32[]{:S(2)}, u32[]{:S(2)}) collective-permute-start(bf16[1088,128]{1,0:T(8,128)(2,1)} %get-tuple-element.26), channel_id=1, source_target_pairs={{0,4},{1,5},{2,6},{3,7},{4,0},{5,1},{6,2},{7,3},{8,12},{9,13},{10,... | collective-permute-start | bytes 835592 | tf_op jit(solution)/shard_map/ppermute | solution.py:395
  5.8 2.7 %prepare.1 = (bf16[128,256]{1,0:T(8,128)(2,1)}, bf16[544,128]{1,0:T(8,128)(2,1)}, bf16[288,128]{1,0:T(8,128)(2,1)}, bf16[128,512]{1,0:T(8,128)(2,1)}, bf16[256,1...) custom-call(bf16[2,120,360]{2,1,0:T(8,128)(2,1)} %w_mut.1, ...), custom_call_target="tpu_custom_call" | custom-call | tf_op jit(solution)/shard_map/prepare/pallas_call | solution.py:373
  8.6 2.9 %collective-permute-done.oth_ref = bf16[1088,128]{1,0:T(8,128)(2,1)S(1)} collective-permute-done((bf16[1088,128]{1,0:T(8,128)(2,1)}, bf16[1088,128]{1,0:T(8,128)(2,1)S(1)}, u32[]{:S(2)}, u32[]{:S(2)}) %collective-permute-start) | collective-permute-done | bytes 278560 | tf_op jit(solution)/shard_map/ppermute | solution.py:395
  11.5 0.0 copy-start.3
  11.5 0.7 copy-done.3
  12.2 9.9 %layer_one.1 = (bf16[512,128]{1,0:T(8,128)(2,1)}, bf16[512,128]{1,0:T(8,128)(2,1)}, bf16[512,128]{1,0:T(8,128)(2,1)}, bf16[512,128]{1,0:T(8,128)(2,1)}) custom-call(bf16[1088,128]{1,0:T(8,128)(2,1)} %get-tuple-element.25.own_ref, bf16[1088,128]{1,0:T(8,128)(2,1)} %copy-done.3, bf16[128,256]{1,0:T(8,128)(2,1)} %get-tuple-element.27.rest_0_, ...), custom_call_target="tpu_custom_call" | custom-call | flops 8000000000 | bytes 1048576 | tf_op jit(solution)/shard_map/layer_one/pallas_call | solution.py:285
  22.1 2.2 %collective-permute-start.1 = (bf16[512,128]{1,0:T(8,128)(2,1)}, bf16[512,128]{1,0:T(8,128)(2,1)S(1)}, u32[]{:S(2)}, u32[]{:S(2)}) collective-permute-start(bf16[512,128]{1,0:T(8,128)(2,1)} %get-tuple-element.33), channel_id=1, source_target_pairs={{0,3},{1,0},{2,1},{3,2},{4,7},{5,4},{6,5},{7,6},{8,11},{9,8},{10,9... | collective-permute-start | bytes 393224 | tf_op jit(solution)/shard_map/ppermute | solution.py:395
  24.2 1.3 %collective-permute-start.2 = (bf16[512,128]{1,0:T(8,128)(2,1)}, bf16[512,128]{1,0:T(8,128)(2,1)S(1)}, u32[]{:S(2)}, u32[]{:S(2)}) collective-permute-start(bf16[512,128]{1,0:T(8,128)(2,1)} %get-tuple-element.34), channel_id=1, source_target_pairs={{0,8},{1,9},{2,10},{3,11},{4,252},{5,253},{6,254},{7,255},{8,16},{... | collective-permute-start | bytes 393224 | tf_op jit(solution)/shard_map/ppermute | solution.py:395
  25.5 1.5 %collective-permute-start.3 = (bf16[512,128]{1,0:T(8,128)(2,1)}, bf16[512,128]{1,0:T(8,128)(2,1)S(1)}, u32[]{:S(2)}, u32[]{:S(2)}) collective-permute-start(bf16[512,128]{1,0:T(8,128)(2,1)} %get-tuple-element.35), channel_id=1, source_target_pairs={{0,11},{1,8},{2,9},{3,10},{4,255},{5,252},{6,253},{7,254},{8,19},{... | collective-permute-start | bytes 393224 | tf_op jit(solution)/shard_map/ppermute | solution.py:395
  27.0 1.3 %collective-permute-done.1.rest_1_ = bf16[512,128]{1,0:T(8,128)(2,1)S(1)} collective-permute-done((bf16[512,128]{1,0:T(8,128)(2,1)}, bf16[512,128]{1,0:T(8,128)(2,1)S(1)}, u32[]{:S(2)}, u32[]{:S(2)}) %collective-permute-start.1) | collective-permute-done | bytes 131104 | tf_op jit(solution)/shard_map/ppermute | solution.py:395
  28.3 0.0 copy-start.4
  28.3 7.7 %collective-permute-done.2.rest_2_ = bf16[512,128]{1,0:T(8,128)(2,1)S(1)} collective-permute-done((bf16[512,128]{1,0:T(8,128)(2,1)}, bf16[512,128]{1,0:T(8,128)(2,1)S(1)}, u32[]{:S(2)}, u32[]{:S(2)}) %collective-permute-start.2) | collective-permute-done | bytes 131104 | tf_op jit(solution)/shard_map/ppermute | solution.py:395
  36.0 0.0 copy-start.5
  36.0 3.8 %collective-permute-done.3.rest_3_ = bf16[512,128]{1,0:T(8,128)(2,1)S(1)} collective-permute-done((bf16[512,128]{1,0:T(8,128)(2,1)}, bf16[512,128]{1,0:T(8,128)(2,1)S(1)}, u32[]{:S(2)}, u32[]{:S(2)}) %collective-permute-start.3) | collective-permute-done | bytes 131104 | tf_op jit(solution)/shard_map/ppermute | solution.py:395
  39.9 0.0 copy-start.6
  39.9 0.0 copy-done.4
  39.9 0.0 copy-done.5
  39.9 0.6 copy-done.6
  40.5 9.4 %layer_two.1 = (bf16[512,128]{1,0:T(8,128)(2,1)}, bf16[512,128]{1,0:T(8,128)(2,1)}, bf16[512,128]{1,0:T(8,128)(2,1)}, bf16[512,128]{1,0:T(8,128)(2,1)}) custom-call(bf16[512,128]{1,0:T(8,128)(2,1)} %get-tuple-element.32.rest_0_, bf16[512,128]{1,0:T(8,128)(2,1)} %copy-done.4, bf16[512,128]{1,0:T(8,128)(2,1)} %copy-done.5, bf16[512,128]{1,0:T(8,128)(2,1)} %copy-done.6, ...), custom_call_target="tpu_custom_call" | custom-call | flops 8000000000 | bytes 1048576 | tf_op jit(solution)/shard_map/layer_two/pallas_call | solution.py:303
  49.9 0.7 collective-permute-start.4
  50.6 6.9 %collective-permute-start.5 = (bf16[512,128]{1,0:T(8,128)(2,1)}, bf16[512,128]{1,0:T(8,128)(2,1)S(1)}, u32[]{:S(2)}, u32[]{:S(2)}) collective-permute-start(bf16[512,128]{1,0:T(8,128)(2,1)} %get-tuple-element.43), channel_id=1, source_target_pairs={{0,252},{1,253},{2,254},{3,255},{4,8},{5,9},{6,10},{7,11},{8,4},{9... | collective-permute-start | bytes 393224 | tf_op jit(solution)/shard_map/ppermute | solution.py:395
  57.5 0.0 collective-permute-start.6
  57.5 0.0 collective-permute-done.4.rest_1_
  57.6 0.0 copy-start
  57.6 4.2 %collective-permute-done.5.rest_2_ = bf16[512,128]{1,0:T(8,128)(2,1)S(1)} collective-permute-done((bf16[512,128]{1,0:T(8,128)(2,1)}, bf16[512,128]{1,0:T(8,128)(2,1)S(1)}, u32[]{:S(2)}, u32[]{:S(2)}) %collective-permute-start.5) | collective-permute-done | bytes 131104 | tf_op jit(solution)/shard_map/ppermute | solution.py:395
  61.7 0.0 copy-start.1
  61.7 6.8 %collective-permute-done.6.rest_3_ = bf16[512,128]{1,0:T(8,128)(2,1)S(1)} collective-permute-done((bf16[512,128]{1,0:T(8,128)(2,1)}, bf16[512,128]{1,0:T(8,128)(2,1)S(1)}, u32[]{:S(2)}, u32[]{:S(2)}) %collective-permute-start.6) | collective-permute-done | bytes 131104 | tf_op jit(solution)/shard_map/ppermute | solution.py:395
  68.6 0.0 copy-start.2
  68.6 0.0 copy-done
  68.6 0.0 copy-done.1
  68.6 0.6 copy-done.2
  69.2 2.7 %from_tokens.1 = bf16[120,8,256]{2,1,0:T(8,128)(2,1)} custom-call(s32[1]{0:T(128)} %bitcast.h_ref, bf16[512,128]{1,0:T(8,128)(2,1)} %get-tuple-element.41.rest_0_, bf16[512,128]{1,0:T(8,128)(2,1)} %copy-done, bf16[512,128]{1,0:T(8,128)(2,1)} %copy-done.1, bf16[512,128]{1,0:T(8,128)(2,1)} %copy-done.2), custom_call_target="tpu_custom_call" | custom-call | tf_op jit(solution)/shard_map/from_tokens/pallas_call | solution.py:316
Async XLA Ops:
  2.1 9.4 %collective-permute-start = (bf16[1088,128]{1,0:T(8,128)(2,1)}, bf16[1088,128]{1,0:T(8,128)(2,1)S(1)}, u32[]{:S(2)}, u32[]{:S(2)}) collective-permute-start(bf16[1088,128]{1,0:T(8,128)(2,1)} %get-tuple-element.26), channel_id=1, source_target_pairs={{0,4},{1,5},{2,6},{3,7},{4,0},{5,1},{6,2},{7,3},{8,12},{9,13},{10,... | collective-permute-start | bytes 835592 | tf_op jit(solution)/shard_map/ppermute | solution.py:395
  11.5 0.7 copy-start.3
  22.1 6.3 %collective-permute-start.1 = (bf16[512,128]{1,0:T(8,128)(2,1)}, bf16[512,128]{1,0:T(8,128)(2,1)S(1)}, u32[]{:S(2)}, u32[]{:S(2)}) collective-permute-start(bf16[512,128]{1,0:T(8,128)(2,1)} %get-tuple-element.33), channel_id=1, source_target_pairs={{0,3},{1,0},{2,1},{3,2},{4,7},{5,4},{6,5},{7,6},{8,11},{9,8},{10,9... | collective-permute-start | bytes 393224 | tf_op jit(solution)/shard_map/ppermute | solution.py:395
  24.2 11.8 %collective-permute-start.2 = (bf16[512,128]{1,0:T(8,128)(2,1)}, bf16[512,128]{1,0:T(8,128)(2,1)S(1)}, u32[]{:S(2)}, u32[]{:S(2)}) collective-permute-start(bf16[512,128]{1,0:T(8,128)(2,1)} %get-tuple-element.34), channel_id=1, source_target_pairs={{0,8},{1,9},{2,10},{3,11},{4,252},{5,253},{6,254},{7,255},{8,16},{... | collective-permute-start | bytes 393224 | tf_op jit(solution)/shard_map/ppermute | solution.py:395
  25.5 14.4 %collective-permute-start.3 = (bf16[512,128]{1,0:T(8,128)(2,1)}, bf16[512,128]{1,0:T(8,128)(2,1)S(1)}, u32[]{:S(2)}, u32[]{:S(2)}) collective-permute-start(bf16[512,128]{1,0:T(8,128)(2,1)} %get-tuple-element.35), channel_id=1, source_target_pairs={{0,11},{1,8},{2,9},{3,10},{4,255},{5,252},{6,253},{7,254},{8,19},{... | collective-permute-start | bytes 393224 | tf_op jit(solution)/shard_map/ppermute | solution.py:395
  28.3 11.5 %copy-start.4 = (bf16[512,128]{1,0:T(8,128)(2,1)}, bf16[512,128]{1,0:T(8,128)(2,1)S(1)}, u32[]{:S(2)}) copy-start(bf16[512,128]{1,0:T(8,128)(2,1)S(1)} %collective-permute-done.1.rest_1_) | copy-start | bytes 393220
  36.0 3.9 %copy-start.5 = (bf16[512,128]{1,0:T(8,128)(2,1)}, bf16[512,128]{1,0:T(8,128)(2,1)S(1)}, u32[]{:S(2)}) copy-start(bf16[512,128]{1,0:T(8,128)(2,1)S(1)} %collective-permute-done.2.rest_2_) | copy-start | bytes 393220
  39.9 0.6 copy-start.6
  49.9 7.6 %collective-permute-start.4 = (bf16[512,128]{1,0:T(8,128)(2,1)}, bf16[512,128]{1,0:T(8,128)(2,1)S(1)}, u32[]{:S(2)}, u32[]{:S(2)}) collective-permute-start(bf16[512,128]{1,0:T(8,128)(2,1)} %get-tuple-element.42), channel_id=1, source_target_pairs={{0,1},{1,2},{2,3},{3,0},{4,5},{5,6},{6,7},{7,4},{8,9},{9,10},{10,1... | collective-permute-start | bytes 393224 | tf_op jit(solution)/shard_map/ppermute | solution.py:395
  50.6 11.1 %collective-permute-start.5 = (bf16[512,128]{1,0:T(8,128)(2,1)}, bf16[512,128]{1,0:T(8,128)(2,1)S(1)}, u32[]{:S(2)}, u32[]{:S(2)}) collective-permute-start(bf16[512,128]{1,0:T(8,128)(2,1)} %get-tuple-element.43), channel_id=1, source_target_pairs={{0,252},{1,253},{2,254},{3,255},{4,8},{5,9},{6,10},{7,11},{8,4},{9... | collective-permute-start | bytes 393224 | tf_op jit(solution)/shard_map/ppermute | solution.py:395
  57.5 11.1 %collective-permute-start.6 = (bf16[512,128]{1,0:T(8,128)(2,1)}, bf16[512,128]{1,0:T(8,128)(2,1)S(1)}, u32[]{:S(2)}, u32[]{:S(2)}) collective-permute-start(bf16[512,128]{1,0:T(8,128)(2,1)} %get-tuple-element.44), channel_id=1, source_target_pairs={{0,253},{1,254},{2,255},{3,252},{4,9},{5,10},{6,11},{7,8},{8,5},{9... | collective-permute-start | bytes 393224 | tf_op jit(solution)/shard_map/ppermute | solution.py:395
  57.6 11.0 %copy-start = (bf16[512,128]{1,0:T(8,128)(2,1)}, bf16[512,128]{1,0:T(8,128)(2,1)S(1)}, u32[]{:S(2)}) copy-start(bf16[512,128]{1,0:T(8,128)(2,1)S(1)} %collective-permute-done.4.rest_1_) | copy-start | bytes 393220
  61.7 6.8 %copy-start.1 = (bf16[512,128]{1,0:T(8,128)(2,1)}, bf16[512,128]{1,0:T(8,128)(2,1)S(1)}, u32[]{:S(2)}) copy-start(bf16[512,128]{1,0:T(8,128)(2,1)S(1)} %collective-permute-done.5.rest_2_) | copy-start | bytes 393220
  68.6 0.7 copy-start.2

commit v6 on v5

--- a/solution.py
+++ b/solution.py
@@ -224,9 +224,9 @@
     h = h_ref[0]
     for k, (low, high) in enumerate(SHIFTED):
         for j in range(4):
-            half = h if j < 2 else 1 - h
+            half = 1 - h if j < 2 else h
             part = ins[4 * k + j][...].astype(jnp.float32)
-            tiles[half, j % 2, low:high] = part.reshape(high - low, 4, WIN, LANES)
+            tiles[half, 1 - j % 2, low:high] = part.reshape(high - low, 4, WIN, LANES)
     for r in range(WIN):
         lo = 0 if r >= 4 else 1
         row = [tiles[half, lo, :, r % 4].reshape(LANES, LANES).T for half in range(2)]
@@ -406,17 +406,17 @@
         own_up, own_lo, oth_up, oth_lo, *edge = layer_one(
             k, parts[len(WINDOWS) + k], others[k], edge, w_one
         )
+        oth_up = send(oth_up, 2, -1)
         oth_lo = send(oth_lo, 2, 0)
-        oth_up = send(oth_up, 2, -1)
         own_up = send(own_up, 0, -1)
-        pieces.append((own_lo, own_up, oth_lo, oth_up))
+        pieces.append((oth_up, oth_lo, own_up, own_lo))
     home = []
     for k in chunks:
-        own_lo, own_up, oth_lo, oth_up = layer_two(k, pieces[k], w_two)
+        oth_up, oth_lo, own_up, own_lo = layer_two(k, pieces[k], w_two)
+        oth_up = send(oth_up, -1, 1)
         oth_lo = send(oth_lo, -1, 0)
-        oth_up = send(oth_up, -1, 1)
         own_up = send(own_up, 0, 1)
-        home += [own_lo, own_up, oth_lo, oth_up]
+        home += [oth_up, oth_lo, own_up, own_lo]
     return from_tokens(h, home)[None]
 
 

time: 72.2 us -> 68.9 us (0.954)
  waiting for transfers between devices: 26.7 us -> 21.7 us
  starting transfers between devices: 16.3 us -> 17.8 us
    ppermute x7, waiting for transfers between devices: 26.7 us -> 21.7 us  [send(): lax.ppermute(value, ('frame', 'strip'), route(frame_step, strip_step))]
    ppermute x7, starting transfers between devices: 16.3 us -> 17.8 us  [send(): lax.ppermute(value, ('frame', 'strip'), route(frame_step, strip_step))]
  transfers between devices with their start and end apart: 7 -> 7, of which waited for: 6 -> 4; matrix products, arithmetic and copies ran while one was open for 0% -> 0% of each run, Pallas kernels for 4% -> 4%
where the time goes in v6:
time: 68.9 us; the launch traced here: 68.5 us
  Pallas kernels  26.9 us (39%)
  waiting for transfers between devices  21.7 us (31%)
  starting transfers between devices  17.8 us (26%)
  local copies, waits for them, and re-layouts  2.11 us (3%)
    ppermute x7, waiting for transfers between devices, send(): lax.ppermute(value, ('frame', 'strip'), route(frame_step, strip_step))  21.7 us
    ppermute x7, starting transfers between devices, send(): lax.ppermute(value, ('frame', 'strip'), route(frame_step, strip_step))  17.8 us
    pallas_call x1, Pallas kernels, layer_one(): pl.pallas_call(functools.partial(layer_one_kernel, count, first, last), o...  9.9 us
    pallas_call x1, Pallas kernels, layer_two(): pl.pallas_call(functools.partial(layer_two_kernel, count), out_shape=[tok...  9.41 us
    pallas_call x1, Pallas kernels, prepared(): pl.pallas_call(prepare_kernel, out_shape=[jax.ShapeDtypeStruct(shape, jnp...  2.74 us
    pallas_call x1, Pallas kernels, from_tokens(): pl.pallas_call(from_tokens_kernel, out_shape=jax.ShapeDtypeStruct((C, WIN...  2.73 us
    unnamed x14, local copies, waits for them, and re-layouts  2.11 us
    pallas_call x1, Pallas kernels, to_tokens(): pl.pallas_call(to_tokens_kernel, out_shape=shapes * 2, in_specs=[SMEM, VM...  2.08 us
  transfers between devices with their start and end apart: 7, of which 4 were waited for; matrix products, arithmetic and copies ran while one was open for 0% of the time, Pallas kernels for 4%

profile of v6, /device:TPU:1, one launch (start us, length us, event | category | flops | bytes accessed | tf_op | source)
XLA Modules:
  0.0 68.5 jit_solution(11732745237379360747)
XLA Ops:
  0.0 2.1 %to_tokens.1 = (bf16[1088,128]{1,0:T(8,128)(2,1)}, bf16[1088,128]{1,0:T(8,128)(2,1)}) custom-call(s32[1]{0:T(128)} %bitcast.h_ref, bf16[120,8,256]{2,1,0:T(8,128)(2,1)} %bitcast.3), custom_call_target="tpu_custom_call" | custom-call | tf_op jit(solution)/shard_map/to_tokens/pallas_call | solution.py:264
  2.1 3.7 %collective-permute-start = (bf16[1088,128]{1,0:T(8,128)(2,1)}, bf16[1088,128]{1,0:T(8,128)(2,1)S(1)}, u32[]{:S(2)}, u32[]{:S(2)}) collective-permute-start(bf16[1088,128]{1,0:T(8,128)(2,1)} %get-tuple-element.26), channel_id=1, source_target_pairs={{0,4},{1,5},{2,6},{3,7},{4,0},{5,1},{6,2},{7,3},{8,12},{9,13},{10,... | collective-permute-start | bytes 835592 | tf_op jit(solution)/shard_map/ppermute | solution.py:395
  5.8 2.7 %prepare.1 = (bf16[128,256]{1,0:T(8,128)(2,1)}, bf16[544,128]{1,0:T(8,128)(2,1)}, bf16[288,128]{1,0:T(8,128)(2,1)}, bf16[128,512]{1,0:T(8,128)(2,1)}, bf16[256,1...) custom-call(bf16[2,120,360]{2,1,0:T(8,128)(2,1)} %w_mut.1, ...), custom_call_target="tpu_custom_call" | custom-call | tf_op jit(solution)/shard_map/prepare/pallas_call | solution.py:373
  8.6 2.9 %collective-permute-done.oth_ref = bf16[1088,128]{1,0:T(8,128)(2,1)S(1)} collective-permute-done((bf16[1088,128]{1,0:T(8,128)(2,1)}, bf16[1088,128]{1,0:T(8,128)(2,1)S(1)}, u32[]{:S(2)}, u32[]{:S(2)}) %collective-permute-start) | collective-permute-done | bytes 278560 | tf_op jit(solution)/shard_map/ppermute | solution.py:395
  11.5 0.0 copy-start.3
  11.5 0.7 %copy-done.3 = bf16[1088,128]{1,0:T(8,128)(2,1)} copy-done((bf16[1088,128]{1,0:T(8,128)(2,1)}, bf16[1088,128]{1,0:T(8,128)(2,1)S(1)}, u32[]{:S(2)}) %copy-start.3) | copy-done | bytes 278552
  12.2 9.9 %layer_one.1 = (bf16[512,128]{1,0:T(8,128)(2,1)}, bf16[512,128]{1,0:T(8,128)(2,1)}, bf16[512,128]{1,0:T(8,128)(2,1)}, bf16[512,128]{1,0:T(8,128)(2,1)}) custom-call(bf16[1088,128]{1,0:T(8,128)(2,1)} %get-tuple-element.25.own_ref, bf16[1088,128]{1,0:T(8,128)(2,1)} %copy-done.3, bf16[128,256]{1,0:T(8,128)(2,1)} %get-tuple-element.27.rest_0_, ...), custom_call_target="tpu_custom_call" | custom-call | flops 8000000000 | bytes 1048576 | tf_op jit(solution)/shard_map/layer_one/pallas_call | solution.py:285
  22.1 3.3 %collective-permute-start.1 = (bf16[512,128]{1,0:T(8,128)(2,1)}, bf16[512,128]{1,0:T(8,128)(2,1)S(1)}, u32[]{:S(2)}, u32[]{:S(2)}) collective-permute-start(bf16[512,128]{1,0:T(8,128)(2,1)} %get-tuple-element.32), channel_id=1, source_target_pairs={{0,11},{1,8},{2,9},{3,10},{4,255},{5,252},{6,253},{7,254},{8,19},{... | collective-permute-start | bytes 393224 | tf_op jit(solution)/shard_map/ppermute | solution.py:395
  25.4 1.2 %collective-permute-start.2 = (bf16[512,128]{1,0:T(8,128)(2,1)}, bf16[512,128]{1,0:T(8,128)(2,1)S(1)}, u32[]{:S(2)}, u32[]{:S(2)}) collective-permute-start(bf16[512,128]{1,0:T(8,128)(2,1)} %get-tuple-element.33), channel_id=1, source_target_pairs={{0,8},{1,9},{2,10},{3,11},{4,252},{5,253},{6,254},{7,255},{8,16},{... | collective-permute-start | bytes 393224 | tf_op jit(solution)/shard_map/ppermute | solution.py:395
  26.6 0.2 collective-permute-start.3
  26.9 10.1 %collective-permute-done.1.rest_0_ = bf16[512,128]{1,0:T(8,128)(2,1)S(1)} collective-permute-done((bf16[512,128]{1,0:T(8,128)(2,1)}, bf16[512,128]{1,0:T(8,128)(2,1)S(1)}, u32[]{:S(2)}, u32[]{:S(2)}) %collective-permute-start.1) | collective-permute-done | bytes 131104 | tf_op jit(solution)/shard_map/ppermute | solution.py:395
  36.9 0.0 copy-start.4
  36.9 0.0 collective-permute-done.2.rest_1_
  36.9 0.0 copy-start.5
  36.9 0.0 collective-permute-done.3.rest_2_
  36.9 0.0 copy-start.6
  36.9 0.6 copy-done.4
  37.6 0.0 copy-done.5
  37.6 0.0 copy-done.6
  37.6 9.4 %layer_two.1 = (bf16[512,128]{1,0:T(8,128)(2,1)}, bf16[512,128]{1,0:T(8,128)(2,1)}, bf16[512,128]{1,0:T(8,128)(2,1)}, bf16[512,128]{1,0:T(8,128)(2,1)}) custom-call(bf16[512,128]{1,0:T(8,128)(2,1)} %copy-done.4, bf16[512,128]{1,0:T(8,128)(2,1)} %copy-done.5, bf16[512,128]{1,0:T(8,128)(2,1)} %copy-done.6, bf16[512,128]{1,0:T(8,128)(2,1)} %get-tuple-element.35.rest_3_, ...), custom_call_target="tpu_custom_call" | custom-call | flops 8000000000 | bytes 1048576 | tf_op jit(solution)/shard_map/layer_two/pallas_call | solution.py:303
  47.1 8.3 %collective-permute-start.4 = (bf16[512,128]{1,0:T(8,128)(2,1)}, bf16[512,128]{1,0:T(8,128)(2,1)S(1)}, u32[]{:S(2)}, u32[]{:S(2)}) collective-permute-start(bf16[512,128]{1,0:T(8,128)(2,1)} %get-tuple-element.41), channel_id=1, source_target_pairs={{0,253},{1,254},{2,255},{3,252},{4,9},{5,10},{6,11},{7,8},{8,5},{9... | collective-permute-start | bytes 393224 | tf_op jit(solution)/shard_map/ppermute | solution.py:395
  55.4 1.0 %collective-permute-start.5 = (bf16[512,128]{1,0:T(8,128)(2,1)}, bf16[512,128]{1,0:T(8,128)(2,1)S(1)}, u32[]{:S(2)}, u32[]{:S(2)}) collective-permute-start(bf16[512,128]{1,0:T(8,128)(2,1)} %get-tuple-element.42), channel_id=1, source_target_pairs={{0,252},{1,253},{2,254},{3,255},{4,8},{5,9},{6,10},{7,11},{8,4},{9... | collective-permute-start | bytes 393224 | tf_op jit(solution)/shard_map/ppermute | solution.py:395
  56.3 0.0 collective-permute-start.6
  56.3 3.9 %collective-permute-done.4.rest_0_ = bf16[512,128]{1,0:T(8,128)(2,1)S(1)} collective-permute-done((bf16[512,128]{1,0:T(8,128)(2,1)}, bf16[512,128]{1,0:T(8,128)(2,1)S(1)}, u32[]{:S(2)}, u32[]{:S(2)}) %collective-permute-start.4) | collective-permute-done | bytes 131104 | tf_op jit(solution)/shard_map/ppermute | solution.py:395
  60.3 0.0 copy-start
  60.3 4.9 %collective-permute-done.5.rest_1_ = bf16[512,128]{1,0:T(8,128)(2,1)S(1)} collective-permute-done((bf16[512,128]{1,0:T(8,128)(2,1)}, bf16[512,128]{1,0:T(8,128)(2,1)S(1)}, u32[]{:S(2)}, u32[]{:S(2)}) %collective-permute-start.5) | collective-permute-done | bytes 131104 | tf_op jit(solution)/shard_map/ppermute | solution.py:395
  65.1 0.0 copy-start.1
  65.1 0.0 collective-permute-done.6.rest_2_
  65.1 0.0 copy-start.2
  65.1 0.0 copy-done
  65.1 0.6 copy-done.1
  65.8 0.1 copy-done.2
  65.8 2.7 %from_tokens.1 = bf16[120,8,256]{2,1,0:T(8,128)(2,1)} custom-call(s32[1]{0:T(128)} %bitcast.h_ref, bf16[512,128]{1,0:T(8,128)(2,1)} %copy-done, bf16[512,128]{1,0:T(8,128)(2,1)} %copy-done.1, bf16[512,128]{1,0:T(8,128)(2,1)} %copy-done.2, bf16[512,128]{1,0:T(8,128)(2,1)} %get-tuple-element.44.rest_3_), custom_call_target="tpu_custom_call" | custom-call | tf_op jit(solution)/shard_map/from_tokens/pallas_call | solution.py:316
Async XLA Ops:
  2.1 9.4 %collective-permute-start = (bf16[1088,128]{1,0:T(8,128)(2,1)}, bf16[1088,128]{1,0:T(8,128)(2,1)S(1)}, u32[]{:S(2)}, u32[]{:S(2)}) collective-permute-start(bf16[1088,128]{1,0:T(8,128)(2,1)} %get-tuple-element.26), channel_id=1, source_target_pairs={{0,4},{1,5},{2,6},{3,7},{4,0},{5,1},{6,2},{7,3},{8,12},{9,13},{10,... | collective-permute-start | bytes 835592 | tf_op jit(solution)/shard_map/ppermute | solution.py:395
  11.5 0.7 %copy-start.3 = (bf16[1088,128]{1,0:T(8,128)(2,1)}, bf16[1088,128]{1,0:T(8,128)(2,1)S(1)}, u32[]{:S(2)}) copy-start(bf16[1088,128]{1,0:T(8,128)(2,1)S(1)} %collective-permute-done.oth_ref) | copy-start | bytes 835588
  22.1 14.8 %collective-permute-start.1 = (bf16[512,128]{1,0:T(8,128)(2,1)}, bf16[512,128]{1,0:T(8,128)(2,1)S(1)}, u32[]{:S(2)}, u32[]{:S(2)}) collective-permute-start(bf16[512,128]{1,0:T(8,128)(2,1)} %get-tuple-element.32), channel_id=1, source_target_pairs={{0,11},{1,8},{2,9},{3,10},{4,255},{5,252},{6,253},{7,254},{8,19},{... | collective-permute-start | bytes 393224 | tf_op jit(solution)/shard_map/ppermute | solution.py:395
  25.4 11.5 %collective-permute-start.2 = (bf16[512,128]{1,0:T(8,128)(2,1)}, bf16[512,128]{1,0:T(8,128)(2,1)S(1)}, u32[]{:S(2)}, u32[]{:S(2)}) collective-permute-start(bf16[512,128]{1,0:T(8,128)(2,1)} %get-tuple-element.33), channel_id=1, source_target_pairs={{0,8},{1,9},{2,10},{3,11},{4,252},{5,253},{6,254},{7,255},{8,16},{... | collective-permute-start | bytes 393224 | tf_op jit(solution)/shard_map/ppermute | solution.py:395
  26.6 10.3 %collective-permute-start.3 = (bf16[512,128]{1,0:T(8,128)(2,1)}, bf16[512,128]{1,0:T(8,128)(2,1)S(1)}, u32[]{:S(2)}, u32[]{:S(2)}) collective-permute-start(bf16[512,128]{1,0:T(8,128)(2,1)} %get-tuple-element.34), channel_id=1, source_target_pairs={{0,3},{1,0},{2,1},{3,2},{4,7},{5,4},{6,5},{7,6},{8,11},{9,8},{10,9... | collective-permute-start | bytes 393224 | tf_op jit(solution)/shard_map/ppermute | solution.py:395
  36.9 0.7 copy-start.4
  36.9 0.7 copy-start.5
  36.9 0.7 %copy-start.6 = (bf16[512,128]{1,0:T(8,128)(2,1)}, bf16[512,128]{1,0:T(8,128)(2,1)S(1)}, u32[]{:S(2)}) copy-start(bf16[512,128]{1,0:T(8,128)(2,1)S(1)} %collective-permute-done.3.rest_2_) | copy-start | bytes 393220
  47.1 13.2 %collective-permute-start.4 = (bf16[512,128]{1,0:T(8,128)(2,1)}, bf16[512,128]{1,0:T(8,128)(2,1)S(1)}, u32[]{:S(2)}, u32[]{:S(2)}) collective-permute-start(bf16[512,128]{1,0:T(8,128)(2,1)} %get-tuple-element.41), channel_id=1, source_target_pairs={{0,253},{1,254},{2,255},{3,252},{4,9},{5,10},{6,11},{7,8},{8,5},{9... | collective-permute-start | bytes 393224 | tf_op jit(solution)/shard_map/ppermute | solution.py:395
  55.4 9.8 %collective-permute-start.5 = (bf16[512,128]{1,0:T(8,128)(2,1)}, bf16[512,128]{1,0:T(8,128)(2,1)S(1)}, u32[]{:S(2)}, u32[]{:S(2)}) collective-permute-start(bf16[512,128]{1,0:T(8,128)(2,1)} %get-tuple-element.42), channel_id=1, source_target_pairs={{0,252},{1,253},{2,254},{3,255},{4,8},{5,9},{6,10},{7,11},{8,4},{9... | collective-permute-start | bytes 393224 | tf_op jit(solution)/shard_map/ppermute | solution.py:395
  56.3 8.8 %collective-permute-start.6 = (bf16[512,128]{1,0:T(8,128)(2,1)}, bf16[512,128]{1,0:T(8,128)(2,1)S(1)}, u32[]{:S(2)}, u32[]{:S(2)}) collective-permute-start(bf16[512,128]{1,0:T(8,128)(2,1)} %get-tuple-element.43), channel_id=1, source_target_pairs={{0,1},{1,2},{2,3},{3,0},{4,5},{5,6},{6,7},{7,4},{8,9},{9,10},{10,1... | collective-permute-start | bytes 393224 | tf_op jit(solution)/shard_map/ppermute | solution.py:395
  60.3 4.9 %copy-start = (bf16[512,128]{1,0:T(8,128)(2,1)}, bf16[512,128]{1,0:T(8,128)(2,1)S(1)}, u32[]{:S(2)}) copy-start(bf16[512,128]{1,0:T(8,128)(2,1)S(1)} %collective-permute-done.4.rest_0_) | copy-start | bytes 393220
  65.1 0.6 copy-start.1
  65.1 0.7 %copy-start.2 = (bf16[512,128]{1,0:T(8,128)(2,1)}, bf16[512,128]{1,0:T(8,128)(2,1)S(1)}, u32[]{:S(2)}) copy-start(bf16[512,128]{1,0:T(8,128)(2,1)S(1)} %collective-permute-done.6.rest_2_) | copy-start | bytes 393220

commit v7 on v6

--- a/solution.py
+++ b/solution.py
@@ -198,7 +198,7 @@
 def layer_two_kernel(count, *rest):
     ins, rest = rest[:4], rest[4:]
     w_k, w_qv, w_prj, w_gu, w_dwn = rest[:5]
-    outs, scratch = rest[5:9], rest[9:]
+    outs, scratch = rest[5:11], rest[11:]
     keys, qv_t, joined = scratch[0], scratch[1], scratch[-1]
     half_tok = TOK // 2
     spans = [slice(i * half_tok, (i + 1) * half_tok) for i in range(count)]
@@ -214,19 +214,29 @@
         y = finished(tokens(group), [joined[i] for i in group], w_prj, w_gu, w_dwn)
         y = y.astype(jnp.bfloat16)
         for k, i in enumerate(group):
-            for j in range(4):
-                low = k * LANES + j * half_tok
-                outs[j][spans[i]] = y[low : low + half_tok]
+            for j, ref in enumerate(outs):
+                low = k * LANES + (j % 2 if j < 4 else j - 2) * half_tok
+                ref[spans[i]] = y[low : low + half_tok]
 
 
 def from_tokens_kernel(h_ref, *rest):
     ins, (out_ref, tiles, wide) = rest[:-3], rest[-3:]
     h = h_ref[0]
     for k, (low, high) in enumerate(SHIFTED):
-        for j in range(4):
-            half = 1 - h if j < 2 else h
-            part = ins[4 * k + j][...].astype(jnp.float32)
+
+        def place(j, half):
+            part = ins[6 * k + j][...].astype(jnp.float32)
             tiles[half, 1 - j % 2, low:high] = part.reshape(high - low, 4, WIN, LANES)
+
+        for side in range(2):
+
+            @pl.when(h == side)
+            def _():
+                place(2 * side, 1 - side)
+                place(2 * side + 1, 1 - side)
+
+        place(4, h)
+        place(5, h)
     for r in range(WIN):
         lo = 0 if r >= 4 else 1
         row = [tiles[half, lo, :, r % 4].reshape(LANES, LANES).T for half in range(2)]
@@ -302,9 +312,9 @@
     count = SHIFTED[chunk][1] - SHIFTED[chunk][0]
     return pl.pallas_call(
         functools.partial(layer_two_kernel, count),
-        out_shape=[tokens_shape(count * TOK // 2)] * 4,
+        out_shape=[tokens_shape(count * TOK // 2)] * 6,
         in_specs=[VMEM] * 9,
-        out_specs=[VMEM] * 4,
+        out_specs=[VMEM] * 6,
         scratch_shapes=attention_scratch(count),
         compiler_params=PARAMS,
         cost_estimate=COST,
@@ -383,16 +393,18 @@
 def on_device(features, *weights):
     frames, strips = lax.axis_size("frame"), lax.axis_size("strip")
 
-    def route(frame_step, strip_step):
+    def route(frame_step, strip_step, parity):
         pairs = []
         for f in range(frames):
+            if parity not in (None, f % 2):
+                continue
             for s in range(strips):
                 to = (f + frame_step * (1 - 2 * (f % 2))) % frames
                 pairs.append((f * strips + s, to * strips + (s + strip_step) % strips))
         return pairs
 
-    def send(value, frame_step, strip_step):
-        return lax.ppermute(value, ("frame", "strip"), route(frame_step, strip_step))
+    def send(value, frame_step, strip_step, parity=None):
+        return lax.ppermute(value, ("frame", "strip"), route(frame_step, strip_step, parity))
 
     h = (lax.axis_index("frame") % 2).astype(jnp.int32).reshape(1)
     ready = prepared(*weights)
@@ -412,11 +424,9 @@
         pieces.append((oth_up, oth_lo, own_up, own_lo))
     home = []
     for k in chunks:
-        oth_up, oth_lo, own_up, own_lo = layer_two(k, pieces[k], w_two)
-        oth_up = send(oth_up, -1, 1)
-        oth_lo = send(oth_lo, -1, 0)
-        own_up = send(own_up, 0, 1)
-        home += [oth_up, oth_lo, own_up, own_lo]
+        *far, own_up, own_lo = layer_two(k, pieces[k], w_two)
+        home += [send(far[j], -1, 1 - j % 2, 1 - j // 2) for j in range(4)]
+        home += [send(own_up, 0, 1), own_lo]
     return from_tokens(h, home)[None]
 
 

time: 68.9 us -> 71.6 us (1.039)
  starting transfers between devices: 17.8 us -> 25 us
  waiting for transfers between devices: 21.7 us -> 17.1 us
    ppermute x7 -> x9, starting transfers between devices: 17.8 us -> 25 us  [send(): lax.ppermute(value, ('frame', 'strip'), route(frame_step, strip_step, par...]
    ppermute x7 -> x9, waiting for transfers between devices: 21.7 us -> 17.1 us  [send(): lax.ppermute(value, ('frame', 'strip'), route(frame_step, strip_step, par...]
    unnamed x14 -> x18, local copies, waits for them, and re-layouts: 2.11 us -> 2.1 us
  transfers between devices with their start and end apart: 7 -> 9, of which waited for: 4 -> 5; matrix products, arithmetic and copies ran while one was open for 0% -> 0% of each run, Pallas kernels for 4% -> 4%
where the time goes in v7:
time: 71.6 us; the launch traced here: 71.3 us
  Pallas kernels  27 us (38%)
  starting transfers between devices  25 us (35%)
  waiting for transfers between devices  17.1 us (24%)
  local copies, waits for them, and re-layouts  2.1 us (3%)
    ppermute x9, starting transfers between devices, send(): lax.ppermute(value, ('frame', 'strip'), route(frame_step, strip_step, par...  25 us
    ppermute x9, waiting for transfers between devices, send(): lax.ppermute(value, ('frame', 'strip'), route(frame_step, strip_step, par...  17.1 us
    pallas_call x1, Pallas kernels, layer_one(): pl.pallas_call(functools.partial(layer_one_kernel, count, first, last), o...  9.85 us
    pallas_call x1, Pallas kernels, layer_two(): pl.pallas_call(functools.partial(layer_two_kernel, count), out_shape=[tok...  9.51 us
    pallas_call x1, Pallas kernels, from_tokens(): pl.pallas_call(from_tokens_kernel, out_shape=jax.ShapeDtypeStruct((C, WIN...  2.84 us
    pallas_call x1, Pallas kernels, prepared(): pl.pallas_call(prepare_kernel, out_shape=[jax.ShapeDtypeStruct(shape, jnp...  2.73 us
    unnamed x18, local copies, waits for them, and re-layouts  2.1 us
    pallas_call x1, Pallas kernels, to_tokens(): pl.pallas_call(to_tokens_kernel, out_shape=shapes * 2, in_specs=[SMEM, VM...  2.08 us
  transfers between devices with their start and end apart: 9, of which 5 were waited for; matrix products, arithmetic and copies ran while one was open for 0% of the time, Pallas kernels for 4%

profile of v7, /device:TPU:1, one launch (start us, length us, event | category | flops | bytes accessed | tf_op | source)
XLA Modules:
  0.0 71.3 jit_solution(6755115908491112536)
XLA Ops:
  0.0 2.1 %to_tokens.1 = (bf16[1088,128]{1,0:T(8,128)(2,1)}, bf16[1088,128]{1,0:T(8,128)(2,1)}) custom-call(s32[1]{0:T(128)} %bitcast.h_ref, bf16[120,8,256]{2,1,0:T(8,128)(2,1)} %bitcast.3), custom_call_target="tpu_custom_call" | custom-call | tf_op jit(solution)/shard_map/to_tokens/pallas_call | solution.py:274
  2.1 3.7 %collective-permute-start = (bf16[1088,128]{1,0:T(8,128)(2,1)}, bf16[1088,128]{1,0:T(8,128)(2,1)S(1)}, u32[]{:S(2)}, u32[]{:S(2)}) collective-permute-start(bf16[1088,128]{1,0:T(8,128)(2,1)} %get-tuple-element.28), channel_id=1, source_target_pairs={{0,4},{1,5},{2,6},{3,7},{4,0},{5,1},{6,2},{7,3},{8,12},{9,13},{10,... | collective-permute-start | bytes 835592 | tf_op jit(solution)/shard_map/ppermute | solution.py:407
  5.8 2.7 %prepare.1 = (bf16[128,256]{1,0:T(8,128)(2,1)}, bf16[544,128]{1,0:T(8,128)(2,1)}, bf16[288,128]{1,0:T(8,128)(2,1)}, bf16[128,512]{1,0:T(8,128)(2,1)}, bf16[256,1...) custom-call(bf16[2,120,360]{2,1,0:T(8,128)(2,1)} %w_mut.1, ...), custom_call_target="tpu_custom_call" | custom-call | tf_op jit(solution)/shard_map/prepare/pallas_call | solution.py:383
  8.6 2.9 %collective-permute-done.oth_ref = bf16[1088,128]{1,0:T(8,128)(2,1)S(1)} collective-permute-done((bf16[1088,128]{1,0:T(8,128)(2,1)}, bf16[1088,128]{1,0:T(8,128)(2,1)S(1)}, u32[]{:S(2)}, u32[]{:S(2)}) %collective-permute-start) | collective-permute-done | bytes 278560 | tf_op jit(solution)/shard_map/ppermute | solution.py:407
  11.5 0.0 copy-start.5
  11.5 0.7 copy-done.5
  12.2 9.9 %layer_one.1 = (bf16[512,128]{1,0:T(8,128)(2,1)}, bf16[512,128]{1,0:T(8,128)(2,1)}, bf16[512,128]{1,0:T(8,128)(2,1)}, bf16[512,128]{1,0:T(8,128)(2,1)}) custom-call(bf16[1088,128]{1,0:T(8,128)(2,1)} %get-tuple-element.27.own_ref, bf16[1088,128]{1,0:T(8,128)(2,1)} %copy-done.5, bf16[128,256]{1,0:T(8,128)(2,1)} %get-tuple-element.29.rest_0_, ...), custom_call_target="tpu_custom_call" | custom-call | flops 8000000000 | bytes 1048576 | tf_op jit(solution)/shard_map/layer_one/pallas_call | solution.py:295
  22.0 3.3 %collective-permute-start.1 = (bf16[512,128]{1,0:T(8,128)(2,1)}, bf16[512,128]{1,0:T(8,128)(2,1)S(1)}, u32[]{:S(2)}, u32[]{:S(2)}) collective-permute-start(bf16[512,128]{1,0:T(8,128)(2,1)} %get-tuple-element.34), channel_id=1, source_target_pairs={{0,11},{1,8},{2,9},{3,10},{4,255},{5,252},{6,253},{7,254},{8,19},{... | collective-permute-start | bytes 393224 | tf_op jit(solution)/shard_map/ppermute | solution.py:407
  25.4 1.2 %collective-permute-start.2 = (bf16[512,128]{1,0:T(8,128)(2,1)}, bf16[512,128]{1,0:T(8,128)(2,1)S(1)}, u32[]{:S(2)}, u32[]{:S(2)}) collective-permute-start(bf16[512,128]{1,0:T(8,128)(2,1)} %get-tuple-element.35), channel_id=1, source_target_pairs={{0,8},{1,9},{2,10},{3,11},{4,252},{5,253},{6,254},{7,255},{8,16},{... | collective-permute-start | bytes 393224 | tf_op jit(solution)/shard_map/ppermute | solution.py:407
  26.6 0.3 collective-permute-start.3
  26.8 10.0 %collective-permute-done.1.rest_0_ = bf16[512,128]{1,0:T(8,128)(2,1)S(1)} collective-permute-done((bf16[512,128]{1,0:T(8,128)(2,1)}, bf16[512,128]{1,0:T(8,128)(2,1)S(1)}, u32[]{:S(2)}, u32[]{:S(2)}) %collective-permute-start.1) | collective-permute-done | bytes 131104 | tf_op jit(solution)/shard_map/ppermute | solution.py:407
  36.9 0.0 copy-start.6
  36.9 0.0 collective-permute-done.2.rest_1_
  36.9 0.0 copy-start.7
  36.9 0.0 collective-permute-done.3.rest_2_
  36.9 0.0 copy-start.8
  36.9 0.6 copy-done.6
  37.5 0.0 copy-done.7
  37.6 0.0 copy-done.8
  37.6 9.5 %layer_two.1 = (bf16[512,128]{1,0:T(8,128)(2,1)}, bf16[512,128]{1,0:T(8,128)(2,1)}, bf16[512,128]{1,0:T(8,128)(2,1)}, bf16[512,128]{1,0:T(8,128)(2,1)}, bf16[512...) custom-call(bf16[512,128]{1,0:T(8,128)(2,1)} %copy-done.6, bf16[512,128]{1,0:T(8,128)(2,1)} %copy-done.7, ...), custom_call_target="tpu_custom_call" | custom-call | flops 8000000000 | bytes 1048576 | tf_op jit(solution)/shard_map/layer_two/pallas_call | solution.py:313
  47.1 1.3 %collective-permute-start.4 = (bf16[512,128]{1,0:T(8,128)(2,1)}, bf16[512,128]{1,0:T(8,128)(2,1)S(1)}, u32[]{:S(2)}, u32[]{:S(2)}) collective-permute-start(bf16[512,128]{1,0:T(8,128)(2,1)} %get-tuple-element.43), channel_id=1, source_target_pairs={{4,9},{5,10},{6,11},{7,8},{12,17},{13,18},{14,19},{15,16},{20,25},... | collective-permute-start | bytes 393224 | tf_op jit(solution)/shard_map/ppermute | solution.py:407
  48.4 1.3 %collective-permute-start.5 = (bf16[512,128]{1,0:T(8,128)(2,1)}, bf16[512,128]{1,0:T(8,128)(2,1)S(1)}, u32[]{:S(2)}, u32[]{:S(2)}) collective-permute-start(bf16[512,128]{1,0:T(8,128)(2,1)} %get-tuple-element.44), channel_id=1, source_target_pairs={{4,8},{5,9},{6,10},{7,11},{12,16},{13,17},{14,18},{15,19},{20,24},... | collective-permute-start | bytes 393224 | tf_op jit(solution)/shard_map/ppermute | solution.py:407
  49.7 11.7 %collective-permute-start.6 = (bf16[512,128]{1,0:T(8,128)(2,1)}, bf16[512,128]{1,0:T(8,128)(2,1)S(1)}, u32[]{:S(2)}, u32[]{:S(2)}) collective-permute-start(bf16[512,128]{1,0:T(8,128)(2,1)} %get-tuple-element.45), channel_id=1, source_target_pairs={{0,253},{1,254},{2,255},{3,252},{8,5},{9,6},{10,7},{11,4},{16,13},... | collective-permute-start | bytes 393224 | tf_op jit(solution)/shard_map/ppermute | solution.py:407
  61.4 1.3 %collective-permute-start.7 = (bf16[512,128]{1,0:T(8,128)(2,1)}, bf16[512,128]{1,0:T(8,128)(2,1)S(1)}, u32[]{:S(2)}, u32[]{:S(2)}) collective-permute-start(bf16[512,128]{1,0:T(8,128)(2,1)} %get-tuple-element.46), channel_id=1, source_target_pairs={{0,252},{1,253},{2,254},{3,255},{8,4},{9,5},{10,6},{11,7},{16,12},... | collective-permute-start | bytes 393224 | tf_op jit(solution)/shard_map/ppermute | solution.py:407
  62.7 0.9 %collective-permute-start.8 = (bf16[512,128]{1,0:T(8,128)(2,1)}, bf16[512,128]{1,0:T(8,128)(2,1)S(1)}, u32[]{:S(2)}, u32[]{:S(2)}) collective-permute-start(bf16[512,128]{1,0:T(8,128)(2,1)} %get-tuple-element.47), channel_id=1, source_target_pairs={{0,1},{1,2},{2,3},{3,0},{4,5},{5,6},{6,7},{7,4},{8,9},{9,10},{10,1... | collective-permute-start | bytes 393224 | tf_op jit(solution)/shard_map/ppermute | solution.py:407
  63.6 0.0 collective-permute-done.4.rest_0_
  63.6 0.0 copy-start
  63.6 0.6 collective-permute-done.5.rest_1_
  64.2 0.0 copy-start.1
  64.2 0.7 %collective-permute-done.6.rest_2_ = bf16[512,128]{1,0:T(8,128)(2,1)S(1)} collective-permute-done((bf16[512,128]{1,0:T(8,128)(2,1)}, bf16[512,128]{1,0:T(8,128)(2,1)S(1)}, u32[]{:S(2)}, u32[]{:S(2)}) %collective-permute-start.6) | collective-permute-done | bytes 131104 | tf_op jit(solution)/shard_map/ppermute | solution.py:407
  64.9 0.0 copy-start.2
  64.9 2.8 %collective-permute-done.7.rest_3_ = bf16[512,128]{1,0:T(8,128)(2,1)S(1)} collective-permute-done((bf16[512,128]{1,0:T(8,128)(2,1)}, bf16[512,128]{1,0:T(8,128)(2,1)S(1)}, u32[]{:S(2)}, u32[]{:S(2)}) %collective-permute-start.7) | collective-permute-done | bytes 131104 | tf_op jit(solution)/shard_map/ppermute | solution.py:407
  67.7 0.0 copy-start.3
  67.7 0.0 collective-permute-done.8.rest_4_
  67.7 0.0 copy-start.4
  67.7 0.0 copy-done
  67.7 0.0 copy-done.1
  67.7 0.0 copy-done.2
  67.8 0.6 copy-done.3
  68.4 0.1 copy-done.4
  68.4 2.8 %from_tokens.1 = bf16[120,8,256]{2,1,0:T(8,128)(2,1)} custom-call(s32[1]{0:T(128)} %bitcast.h_ref, bf16[512,128]{1,0:T(8,128)(2,1)} %copy-done, bf16[512,128]{1,0:T(8,128)(2,1)} %copy-done.1, bf16[512,128]{1,0:T(8,128)(2,1)} %copy-done.2, bf16[512,128]{1,0:T(8,128)(2,1)} %copy-done.3, bf16[512,128]{1,0:T(8,128)(2,1)} %copy-done.4, ...), custom_call_target="tpu_custom_call" | custom-call | tf_op jit(solution)/shard_map/from_tokens/pallas_call | solution.py:326
Async XLA Ops:
  2.1 9.4 %collective-permute-start = (bf16[1088,128]{1,0:T(8,128)(2,1)}, bf16[1088,128]{1,0:T(8,128)(2,1)S(1)}, u32[]{:S(2)}, u32[]{:S(2)}) collective-permute-start(bf16[1088,128]{1,0:T(8,128)(2,1)} %get-tuple-element.28), channel_id=1, source_target_pairs={{0,4},{1,5},{2,6},{3,7},{4,0},{5,1},{6,2},{7,3},{8,12},{9,13},{10,... | collective-permute-start | bytes 835592 | tf_op jit(solution)/shard_map/ppermute | solution.py:407
  11.5 0.7 copy-start.5
  22.0 14.9 %collective-permute-start.1 = (bf16[512,128]{1,0:T(8,128)(2,1)}, bf16[512,128]{1,0:T(8,128)(2,1)S(1)}, u32[]{:S(2)}, u32[]{:S(2)}) collective-permute-start(bf16[512,128]{1,0:T(8,128)(2,1)} %get-tuple-element.34), channel_id=1, source_target_pairs={{0,11},{1,8},{2,9},{3,10},{4,255},{5,252},{6,253},{7,254},{8,19},{... | collective-permute-start | bytes 393224 | tf_op jit(solution)/shard_map/ppermute | solution.py:407
  25.4 11.5 %collective-permute-start.2 = (bf16[512,128]{1,0:T(8,128)(2,1)}, bf16[512,128]{1,0:T(8,128)(2,1)S(1)}, u32[]{:S(2)}, u32[]{:S(2)}) collective-permute-start(bf16[512,128]{1,0:T(8,128)(2,1)} %get-tuple-element.35), channel_id=1, source_target_pairs={{0,8},{1,9},{2,10},{3,11},{4,252},{5,253},{6,254},{7,255},{8,16},{... | collective-permute-start | bytes 393224 | tf_op jit(solution)/shard_map/ppermute | solution.py:407
  26.6 10.3 %collective-permute-start.3 = (bf16[512,128]{1,0:T(8,128)(2,1)}, bf16[512,128]{1,0:T(8,128)(2,1)S(1)}, u32[]{:S(2)}, u32[]{:S(2)}) collective-permute-start(bf16[512,128]{1,0:T(8,128)(2,1)} %get-tuple-element.36), channel_id=1, source_target_pairs={{0,3},{1,0},{2,1},{3,2},{4,7},{5,4},{6,5},{7,6},{8,11},{9,8},{10,9... | collective-permute-start | bytes 393224 | tf_op jit(solution)/shard_map/ppermute | solution.py:407
  36.9 0.7 copy-start.6
  36.9 0.7 copy-start.7
  36.9 0.7 %copy-start.8 = (bf16[512,128]{1,0:T(8,128)(2,1)}, bf16[512,128]{1,0:T(8,128)(2,1)S(1)}, u32[]{:S(2)}) copy-start(bf16[512,128]{1,0:T(8,128)(2,1)S(1)} %collective-permute-done.3.rest_2_) | copy-start | bytes 393220
  47.1 16.5 %collective-permute-start.4 = (bf16[512,128]{1,0:T(8,128)(2,1)}, bf16[512,128]{1,0:T(8,128)(2,1)S(1)}, u32[]{:S(2)}, u32[]{:S(2)}) collective-permute-start(bf16[512,128]{1,0:T(8,128)(2,1)} %get-tuple-element.43), channel_id=1, source_target_pairs={{4,9},{5,10},{6,11},{7,8},{12,17},{13,18},{14,19},{15,16},{20,25},... | collective-permute-start | bytes 393224 | tf_op jit(solution)/shard_map/ppermute | solution.py:407
  48.4 15.8 %collective-permute-start.5 = (bf16[512,128]{1,0:T(8,128)(2,1)}, bf16[512,128]{1,0:T(8,128)(2,1)S(1)}, u32[]{:S(2)}, u32[]{:S(2)}) collective-permute-start(bf16[512,128]{1,0:T(8,128)(2,1)} %get-tuple-element.44), channel_id=1, source_target_pairs={{4,8},{5,9},{6,10},{7,11},{12,16},{13,17},{14,18},{15,19},{20,24},... | collective-permute-start | bytes 393224 | tf_op jit(solution)/shard_map/ppermute | solution.py:407
  49.7 15.2 %collective-permute-start.6 = (bf16[512,128]{1,0:T(8,128)(2,1)}, bf16[512,128]{1,0:T(8,128)(2,1)S(1)}, u32[]{:S(2)}, u32[]{:S(2)}) collective-permute-start(bf16[512,128]{1,0:T(8,128)(2,1)} %get-tuple-element.45), channel_id=1, source_target_pairs={{0,253},{1,254},{2,255},{3,252},{8,5},{9,6},{10,7},{11,4},{16,13},... | collective-permute-start | bytes 393224 | tf_op jit(solution)/shard_map/ppermute | solution.py:407
  61.4 6.3 %collective-permute-start.7 = (bf16[512,128]{1,0:T(8,128)(2,1)}, bf16[512,128]{1,0:T(8,128)(2,1)S(1)}, u32[]{:S(2)}, u32[]{:S(2)}) collective-permute-start(bf16[512,128]{1,0:T(8,128)(2,1)} %get-tuple-element.46), channel_id=1, source_target_pairs={{0,252},{1,253},{2,254},{3,255},{8,4},{9,5},{10,6},{11,7},{16,12},... | collective-permute-start | bytes 393224 | tf_op jit(solution)/shard_map/ppermute | solution.py:407
  62.7 5.0 %collective-permute-start.8 = (bf16[512,128]{1,0:T(8,128)(2,1)}, bf16[512,128]{1,0:T(8,128)(2,1)S(1)}, u32[]{:S(2)}, u32[]{:S(2)}) collective-permute-start(bf16[512,128]{1,0:T(8,128)(2,1)} %get-tuple-element.47), channel_id=1, source_target_pairs={{0,1},{1,2},{2,3},{3,0},{4,5},{5,6},{6,7},{7,4},{8,9},{9,10},{10,1... | collective-permute-start | bytes 393224 | tf_op jit(solution)/shard_map/ppermute | solution.py:407
  63.6 4.1 %copy-start = (bf16[512,128]{1,0:T(8,128)(2,1)}, bf16[512,128]{1,0:T(8,128)(2,1)S(1)}, u32[]{:S(2)}) copy-start(bf16[512,128]{1,0:T(8,128)(2,1)S(1)} %collective-permute-done.4.rest_0_) | copy-start | bytes 393220
  64.2 3.6 %copy-start.1 = (bf16[512,128]{1,0:T(8,128)(2,1)}, bf16[512,128]{1,0:T(8,128)(2,1)S(1)}, u32[]{:S(2)}) copy-start(bf16[512,128]{1,0:T(8,128)(2,1)S(1)} %collective-permute-done.5.rest_1_) | copy-start | bytes 393220
  64.9 2.8 %copy-start.2 = (bf16[512,128]{1,0:T(8,128)(2,1)}, bf16[512,128]{1,0:T(8,128)(2,1)S(1)}, u32[]{:S(2)}) copy-start(bf16[512,128]{1,0:T(8,128)(2,1)S(1)} %collective-permute-done.6.rest_2_) | copy-start | bytes 393220
  67.7 0.6 copy-start.3
  67.7 0.7 copy-start.4

commit v8 on v6

--- a/solution.py
+++ b/solution.py
@@ -14,7 +14,6 @@
 FFN = 240
 WIN = 8
 LANES = 128
-VHEAD = 24
 HALF = 16
 GROUP = 8
 TOK = WIN * WIN
@@ -48,11 +47,9 @@
 def head_only(q_t, head):
     low = head * HEAD // 16 * 16
     high = -(-(head * HEAD + HEAD) // 16) * 16
-    part = q_t[low:high].astype(jnp.float32)
-    row = lax.broadcasted_iota(jnp.int32, part.shape, 0) + low
+    row = lax.broadcasted_iota(jnp.int32, (high - low, q_t.shape[1]), 0) + low
     keep = (row >= head * HEAD) & (row < head * HEAD + HEAD)
-    part = jnp.where(keep, part, 0.0).astype(jnp.bfloat16)
-    pieces = [part]
+    pieces = [q_t[low:high] * jnp.where(keep, 1.0, 0.0).astype(jnp.bfloat16)]
     if low:
         pieces.insert(0, jnp.zeros((low, q_t.shape[1]), jnp.bfloat16))
     if high < LANES:
@@ -90,14 +87,19 @@
 
 def mix_block(kind, pair, scores, qv_t, window, of_first):
     probs = [softmax_rows(scores[:, i * LANES : (i + 1) * LANES]) for i in range(2)]
-    probs = jnp.concatenate(probs, axis=1)
+    probs = jnp.concatenate(probs, axis=1).astype(jnp.bfloat16)
     if kind == 0:
-        probs = jnp.concatenate(
-            [jnp.where(of_first, 0.0, probs), jnp.where(of_first, probs, 0.0)], axis=0
-        )
-    base = 2 * LANES + (kind * HEADS + 2 * pair) * VHEAD
-    mixed = matmul(qv_t[window, base : base + 2 * VHEAD], probs.astype(jnp.bfloat16))
-    return [mixed[:VHEAD, :LANES], mixed[VHEAD:, LANES:]]
+        first = jnp.where(of_first, 1.0, 0.0).astype(jnp.bfloat16)
+        second = jnp.where(of_first, 0.0, 1.0).astype(jnp.bfloat16)
+        probs = jnp.concatenate([probs * second, probs * first], axis=0)
+    want = pair * 2 * HEAD
+    low = want // 16 * 16
+    base = (2 + kind) * LANES + low
+    mixed = matmul(qv_t[window, base : base + 48], probs)[want - low : want - low + 2 * HEAD]
+    one, two = mixed[:, :LANES], mixed[:, LANES:]
+    row = lax.broadcasted_iota(jnp.int32, (8, LANES), 0)
+    shared = jnp.where(row < HEAD - 16, one[16:24], two[16:24])
+    return jnp.concatenate([one[:16], shared, two[24:]], axis=0)
 
 
 def attend(count, keys, qv_t, mutual_scores, self_scores, joined):
@@ -113,7 +115,7 @@
             ref = scores[kind]
             if i + 1 < count:
                 ref[(i + 1) % 2, pair] = score_block(kind, pair, keys, qv_t, i + 1, of_first)
-            outs += mix_block(kind, pair, ref[i % 2, pair], qv_t, i, of_first)
+            outs.append(mix_block(kind, pair, ref[i % 2, pair], qv_t, i, of_first))
         joined[i] = jnp.concatenate(outs, axis=0).astype(jnp.bfloat16)
 
 
@@ -154,7 +156,8 @@
     return [range(low, high) for low, high in zip(cuts[:-1], cuts[1:])]
 
 
-def layer_one_kernel(count, first, last, own_ref, oth_ref, *rest):
+def layer_one_kernel(count, first, last, h_ref, own_ref, oth_ref, *rest):
+    h = h_ref[0]
     if not first:
         before, rest = rest[0], rest[1:]
     w_k, w_qv, w_prj, w_gu, w_dwn = rest[:5]
@@ -182,7 +185,7 @@
         y = y.reshape(len(group), 2, WIN, WIN, LANES)
         for j, i in enumerate(group):
             for f in range(2):
-                flat[f, :, shift + i * WIN : shift + (i + 1) * WIN, :] = y[j, f]
+                flat[1 - h if f else h, :, shift + i * WIN : shift + (i + 1) * WIN, :] = y[j, f]
     width = shift + (count - 1) * WIN
     if not last:
         after[...] = flat[:, :, width : width + WIN, :]
@@ -195,7 +198,8 @@
             outs[2 * f + k][...] = piece.astype(jnp.bfloat16)
 
 
-def layer_two_kernel(count, *rest):
+def layer_two_kernel(count, h_ref, *rest):
+    even = h_ref[0] == 0
     ins, rest = rest[:4], rest[4:]
     w_k, w_qv, w_prj, w_gu, w_dwn = rest[:5]
     outs, scratch = rest[5:9], rest[9:]
@@ -212,11 +216,13 @@
     attend(count, *scratch)
     for group in grouped(count):
         y = finished(tokens(group), [joined[i] for i in group], w_prj, w_gu, w_dwn)
-        y = y.astype(jnp.bfloat16)
         for k, i in enumerate(group):
-            for j in range(4):
-                low = k * LANES + j * half_tok
-                outs[j][spans[i]] = y[low : low + half_tok]
+            moved, kept = (y[k * LANES + f * TOK : k * LANES + (f + 1) * TOK] for f in range(2))
+            pair = (jnp.where(even, moved, kept), jnp.where(even, kept, moved))
+            for f in range(2):
+                part = pair[f].astype(jnp.bfloat16)
+                for j in range(2):
+                    outs[2 * f + j][spans[i]] = part[j * half_tok : (j + 1) * half_tok]
 
 
 def from_tokens_kernel(h_ref, *rest):
@@ -248,10 +254,10 @@
 def attention_scratch(count):
     return [
         pltpu.VMEM((count, LANES, 2 * LANES), jnp.bfloat16),
-        pltpu.VMEM((count, 2 * LANES + 2 * HEADS * VHEAD, LANES), jnp.bfloat16),
+        pltpu.VMEM((count, 4 * LANES, LANES), jnp.bfloat16),
         pltpu.VMEM((2, HEADS // 2, TOK, 2 * LANES), jnp.float32),
         pltpu.VMEM((2, HEADS // 2, 2 * TOK, 2 * LANES), jnp.float32),
-        pltpu.VMEM((count, 2 * HEADS * VHEAD, LANES), jnp.bfloat16),
+        pltpu.VMEM((count, 2 * C, LANES), jnp.bfloat16),
     ]
 
 
@@ -275,17 +281,17 @@
     )(h, x)
 
 
-def layer_one(chunk, own, oth, before, weights):
+def layer_one(chunk, h, own, oth, before, weights):
     first, last = chunk == 0, chunk == len(WINDOWS) - 1
     count = WINDOWS[chunk][1] - WINDOWS[chunk][0]
     width = SHIFTED[chunk][1] - SHIFTED[chunk][0]
     edge = [] if last else [jax.ShapeDtypeStruct((2, WIN, WIN, LANES), jnp.float32)]
     shapes = [tokens_shape(width * TOK // 2)] * 4 + edge
-    args = (own, oth, *before, *weights)
+    args = (h, own, oth, *before, *weights)
     return pl.pallas_call(
         functools.partial(layer_one_kernel, count, first, last),
         out_shape=shapes,
-        in_specs=[VMEM] * len(args),
+        in_specs=[SMEM] + [VMEM] * (len(args) - 1),
         out_specs=[VMEM] * len(shapes),
         scratch_shapes=[
             pltpu.VMEM((2, WIN, (width + 1) * WIN, LANES), jnp.float32),
@@ -298,18 +304,18 @@
     )(*args)
 
 
-def layer_two(chunk, pieces, weights):
+def layer_two(chunk, h, pieces, weights):
     count = SHIFTED[chunk][1] - SHIFTED[chunk][0]
     return pl.pallas_call(
         functools.partial(layer_two_kernel, count),
         out_shape=[tokens_shape(count * TOK // 2)] * 4,
-        in_specs=[VMEM] * 9,
+        in_specs=[SMEM] + [VMEM] * 9,
         out_specs=[VMEM] * 4,
         scratch_shapes=attention_scratch(count),
         compiler_params=PARAMS,
         cost_estimate=COST,
         name="layer_two",
-    )(*pieces, *weights)
+    )(h, *pieces, *weights)
 
 
 def from_tokens(h, pieces):
@@ -328,45 +334,34 @@
 
 
 def prepare_kernel(w_mut, w_slf, w_prj, w_gte, w_upp, w_dwn, *outs):
-    def selector(rows, cols, picks):
-        row = lax.broadcasted_iota(jnp.int32, (rows, cols), 0)
-        col = lax.broadcasted_iota(jnp.int32, (rows, cols), 1)
-        hit = None
-        for first_row, first_col, size in picks:
-            inside = (row >= first_row) & (row < first_row + size)
-            run = inside & (col - first_col == row - first_row)
-            hit = run if hit is None else hit | run
-        return jnp.where(hit, 1.0, 0.0).astype(jnp.bfloat16)
-
-    by_head = [(h * VHEAD, h * HEAD, HEAD) for h in range(HEADS)]
-    pick_q = selector(LANES, 3 * C, [(0, 0, C)])
-    pick_v = selector(HEADS * VHEAD, 3 * C, [(r, 2 * C + c, n) for r, c, n in by_head])
-    pick_k = selector(LANES, 3 * C, [(0, C, C)])
-    spread = selector(HEADS * VHEAD, C, by_head)
+    row = lax.broadcasted_iota(jnp.int32, (LANES, 3 * C), 0)
+    col = lax.broadcasted_iota(jnp.int32, (LANES, 3 * C), 1)
+    picks = []
+    for part in range(3):
+        hit = (col == row + part * C) & (row < C)
+        picks.append(jnp.where(hit, 1.0, 0.0).astype(jnp.bfloat16))
     for layer in range(2):
         w_k, w_qv, w_p, w_gu, w_d = outs[5 * layer : 5 * layer + 5]
         for ref in (w_k, w_qv, w_p, w_gu, w_d):
             ref[...] = jnp.zeros(ref.shape, jnp.bfloat16)
-        v_rows = HEADS * VHEAD
         for i, w in enumerate((w_mut, w_slf)):
             w = w[layer]
-            w_k[:C, i * LANES : (i + 1) * LANES] = matmul_nt(w, pick_k).astype(jnp.bfloat16)
-            w_qv[i * LANES : (i + 1) * LANES, :C] = matmul_nt(pick_q, w).astype(jnp.bfloat16)
-            low = 2 * LANES + i * v_rows
-            w_qv[low : low + v_rows, :C] = matmul_nt(pick_v, w).astype(jnp.bfloat16)
-            part = matmul(spread, w_prj[layer, i * C : (i + 1) * C])
-            w_p[i * v_rows : (i + 1) * v_rows, :C] = part.astype(jnp.bfloat16)
+            span = slice(i * LANES, (i + 1) * LANES)
+            w_k[:C, span] = matmul_nt(w, picks[1]).astype(jnp.bfloat16)
+            w_qv[span, :C] = matmul_nt(picks[0], w).astype(jnp.bfloat16)
+            span = slice((2 + i) * LANES, (3 + i) * LANES)
+            w_qv[span, :C] = matmul_nt(picks[2], w).astype(jnp.bfloat16)
+        w_p[:, :C] = w_prj[layer]
         w_gu[:C, :FFN] = w_gte[layer]
         w_gu[:C, 2 * LANES : 2 * LANES + FFN] = w_upp[layer]
         w_d[:FFN, :C] = w_dwn[layer]
 
 
 def prepared(*weights):
-    v_rows = HEADS * VHEAD
     shapes = [
         (LANES, 2 * LANES),
-        (2 * LANES + 2 * v_rows, LANES),
-        (2 * v_rows, LANES),
+        (4 * LANES, LANES),
+        (2 * C, LANES),
         (LANES, 4 * LANES),
         (2 * LANES, LANES),
     ] * 2
@@ -383,40 +378,38 @@
 def on_device(features, *weights):
     frames, strips = lax.axis_size("frame"), lax.axis_size("strip")
 
-    def route(frame_step, strip_step):
+    def send(value, even_step, odd_step, strip_step):
         pairs = []
         for f in range(frames):
             for s in range(strips):
-                to = (f + frame_step * (1 - 2 * (f % 2))) % frames
+                to = (f + (odd_step if f % 2 else even_step)) % frames
                 pairs.append((f * strips + s, to * strips + (s + strip_step) % strips))
-        return pairs
-
-    def send(value, frame_step, strip_step):
-        return lax.ppermute(value, ("frame", "strip"), route(frame_step, strip_step))
+        return lax.ppermute(value, ("frame", "strip"), pairs)
 
     h = (lax.axis_index("frame") % 2).astype(jnp.int32).reshape(1)
     ready = prepared(*weights)
     w_one, w_two = ready[:5], ready[5:]
     parts = to_tokens(h, features[0])
     chunks = range(len(WINDOWS))
-    others = [send(parts[k], 1, 0) for k in chunks]
+    others = [send(parts[k], 1, -1, 0) for k in chunks]
     edge = ()
     pieces = []
     for k in chunks:
-        own_up, own_lo, oth_up, oth_lo, *edge = layer_one(
-            k, parts[len(WINDOWS) + k], others[k], edge, w_one
+        kept_up, kept_lo, moved_up, moved_lo, *edge = layer_one(
+            k, h, parts[len(WINDOWS) + k], others[k], edge, w_one
         )
-        oth_up = send(oth_up, 2, -1)
-        oth_lo = send(oth_lo, 2, 0)
-        own_up = send(own_up, 0, -1)
-        pieces.append((oth_up, oth_lo, own_up, own_lo))
+        moved_up = send(moved_up, 2, 2, -1)
+        moved_lo = send(moved_lo, 2, 2, 0)
+        kept_up = send(kept_up, 0, 0, -1)
+        pieces.append((moved_up, moved_lo, kept_up, kept_lo))
     home = []
     for k in chunks:
-        oth_up, oth_lo, own_up, own_lo = layer_two(k, pieces[k], w_two)
-        oth_up = send(oth_up, -1, 1)
-        oth_lo = send(oth_lo, -1, 0)
-        own_up = send(own_up, 0, 1)
-        home += [oth_up, oth_lo, own_up, own_lo]
+        far_up, far_lo, near_up, near_lo = layer_two(k, h, pieces[k], w_two)
+        far_up = send(far_up, -1, -1, 1)
+        far_lo = send(far_lo, -1, -1, 0)
+        near_up = send(near_up, 0, -2, 1)
+        near_lo = send(near_lo, 0, -2, 0)
+        home += [far_up, far_lo, near_up, near_lo]
     return from_tokens(h, home)[None]
 
 

time: 68.9 us -> 64.1 us (0.930)
  the two profiles are of different devices: /device:TPU:1 before, /device:TPU:17 now
where the time goes in v8:
time: 64.1 us; the launch traced here: 63.9 us
  Pallas kernels  26.4 us (41%)
  waiting for transfers between devices  22 us (34%)
  starting transfers between devices  13.4 us (21%)
  local copies, waits for them, and re-layouts  2.08 us (3%)
    ppermute x8, waiting for transfers between devices, send(): return lax.ppermute(value, ('frame', 'strip'), pairs)  22 us
    ppermute x8, starting transfers between devices, send(): return lax.ppermute(value, ('frame', 'strip'), pairs)  13.4 us
    pallas_call x1, Pallas kernels, layer_one(): pl.pallas_call(functools.partial(layer_one_kernel, count, first, last), o...  9.69 us
    pallas_call x1, Pallas kernels, layer_two(): pl.pallas_call(functools.partial(layer_two_kernel, count), out_shape=[tok...  9.19 us
    pallas_call x1, Pallas kernels, from_tokens(): pl.pallas_call(from_tokens_kernel, out_shape=jax.ShapeDtypeStruct((C, WIN...  2.73 us
    pallas_call x1, Pallas kernels, prepared(): pl.pallas_call(prepare_kernel, out_shape=[jax.ShapeDtypeStruct(shape, jnp...  2.67 us
    unnamed x16, local copies, waits for them, and re-layouts  2.08 us
    pallas_call x1, Pallas kernels, to_tokens(): pl.pallas_call(to_tokens_kernel, out_shape=shapes * 2, in_specs=[SMEM, VM...  2.07 us
  transfers between devices with their start and end apart: 8, of which 4 were waited for; matrix products, arithmetic and copies ran while one was open for 0% of the time, Pallas kernels for 4%

profile of v8, /device:TPU:17, one launch (start us, length us, event | category | flops | bytes accessed | tf_op | source)
XLA Modules:
  0.0 63.9 jit_solution(2029054721243062487)
XLA Ops:
  0.0 2.1 %to_tokens.1 = (bf16[1088,128]{1,0:T(8,128)(2,1)}, bf16[1088,128]{1,0:T(8,128)(2,1)}) custom-call(s32[1]{0:T(128)} %bitcast.h_ref, bf16[120,8,256]{2,1,0:T(8,128)(2,1)} %bitcast.3), custom_call_target="tpu_custom_call" | custom-call | tf_op jit(solution)/shard_map/to_tokens/pallas_call | solution.py:270
  2.1 0.0 collective-permute-start
  2.1 2.7 %prepare.1 = (bf16[128,256]{1,0:T(8,128)(2,1)}, bf16[512,128]{1,0:T(8,128)(2,1)}, bf16[240,128]{1,0:T(8,128)(2,1)}, bf16[128,512]{1,0:T(8,128)(2,1)}, bf16[256,1...) custom-call(bf16[2,120,360]{2,1,0:T(8,128)(2,1)} %w_mut.1, ...), custom_call_target="tpu_custom_call" | custom-call | tf_op jit(solution)/shard_map/prepare/pallas_call | solution.py:368
  4.7 6.6 %collective-permute-done.oth_ref = bf16[1088,128]{1,0:T(8,128)(2,1)S(1)} collective-permute-done((bf16[1088,128]{1,0:T(8,128)(2,1)}, bf16[1088,128]{1,0:T(8,128)(2,1)S(1)}, u32[]{:S(2)}, u32[]{:S(2)}) %collective-permute-start) | collective-permute-done | bytes 278560 | tf_op jit(solution)/shard_map/ppermute | solution.py:387
  11.3 0.0 copy-start.4
  11.3 0.7 %copy-done.4 = bf16[1088,128]{1,0:T(8,128)(2,1)} copy-done((bf16[1088,128]{1,0:T(8,128)(2,1)}, bf16[1088,128]{1,0:T(8,128)(2,1)S(1)}, u32[]{:S(2)}) %copy-start.4) | copy-done | bytes 278552
  12.0 9.7 %layer_one.1 = (bf16[512,128]{1,0:T(8,128)(2,1)}, bf16[512,128]{1,0:T(8,128)(2,1)}, bf16[512,128]{1,0:T(8,128)(2,1)}, bf16[512,128]{1,0:T(8,128)(2,1)}) custom-call(s32[1]{0:T(128)} %bitcast.h_ref, bf16[1088,128]{1,0:T(8,128)(2,1)} %get-tuple-element.25.own_ref, bf16[1088,128]{1,0:T(8,128)(2,1)} %copy-done.4, bf16[128,256]{1,0:T(8,128)(2,1)} %get-tuple-element.27.rest_0_, ...), custom_call_target="tpu_custom_call" | custom-call | flops 8000000000 | bytes 1048576 | tf_op jit(solution)/shard_map/layer_one/pallas_call | solution.py:291
  21.7 2.6 %collective-permute-start.1 = (bf16[512,128]{1,0:T(8,128)(2,1)}, bf16[512,128]{1,0:T(8,128)(2,1)S(1)}, u32[]{:S(2)}, u32[]{:S(2)}) collective-permute-start(bf16[512,128]{1,0:T(8,128)(2,1)} %get-tuple-element.32), channel_id=1, source_target_pairs={{0,11},{1,8},{2,9},{3,10},{4,15},{5,12},{6,13},{7,14},{8,19},{9,16... | collective-permute-start | bytes 393224 | tf_op jit(solution)/shard_map/ppermute | solution.py:387
  24.4 1.2 %collective-permute-start.2 = (bf16[512,128]{1,0:T(8,128)(2,1)}, bf16[512,128]{1,0:T(8,128)(2,1)S(1)}, u32[]{:S(2)}, u32[]{:S(2)}) collective-permute-start(bf16[512,128]{1,0:T(8,128)(2,1)} %get-tuple-element.33), channel_id=1, source_target_pairs={{0,8},{1,9},{2,10},{3,11},{4,12},{5,13},{6,14},{7,15},{8,16},{9,17... | collective-permute-start | bytes 393224 | tf_op jit(solution)/shard_map/ppermute | solution.py:387
  25.6 0.0 collective-permute-start.3
  25.6 10.0 %collective-permute-done.1.rest_0_ = bf16[512,128]{1,0:T(8,128)(2,1)S(1)} collective-permute-done((bf16[512,128]{1,0:T(8,128)(2,1)}, bf16[512,128]{1,0:T(8,128)(2,1)S(1)}, u32[]{:S(2)}, u32[]{:S(2)}) %collective-permute-start.1) | collective-permute-done | bytes 131104 | tf_op jit(solution)/shard_map/ppermute | solution.py:387
  35.6 0.0 copy-start.5
  35.6 0.0 collective-permute-done.2.rest_1_
  35.6 0.0 copy-start.6
  35.6 0.0 collective-permute-done.3.rest_2_
  35.6 0.0 copy-start.7
  35.6 0.6 copy-done.5
  36.2 0.0 copy-done.6
  36.3 0.0 copy-done.7
  36.3 9.2 %layer_two.1 = (bf16[512,128]{1,0:T(8,128)(2,1)}, bf16[512,128]{1,0:T(8,128)(2,1)}, bf16[512,128]{1,0:T(8,128)(2,1)}, bf16[512,128]{1,0:T(8,128)(2,1)}) custom-call(s32[1]{0:T(128)} %bitcast.h_ref, bf16[512,128]{1,0:T(8,128)(2,1)} %copy-done.5, bf16[512,128]{1,0:T(8,128)(2,1)} %copy-done.6, bf16[512,128]{1,0:T(8,128)(2,1)} %copy-done.7, ...), custom_call_target="tpu_custom_call" | custom-call | flops 8000000000 | bytes 1048576 | tf_op jit(solution)/shard_map/layer_two/pallas_call | solution.py:309
  45.5 1.4 %collective-permute-start.4 = (bf16[512,128]{1,0:T(8,128)(2,1)}, bf16[512,128]{1,0:T(8,128)(2,1)S(1)}, u32[]{:S(2)}, u32[]{:S(2)}) collective-permute-start(bf16[512,128]{1,0:T(8,128)(2,1)} %get-tuple-element.41), channel_id=1, source_target_pairs={{0,253},{1,254},{2,255},{3,252},{4,1},{5,2},{6,3},{7,0},{8,5},{9,6... | collective-permute-start | bytes 393224 | tf_op jit(solution)/shard_map/ppermute | solution.py:387
  46.9 4.0 %collective-permute-start.5 = (bf16[512,128]{1,0:T(8,128)(2,1)}, bf16[512,128]{1,0:T(8,128)(2,1)S(1)}, u32[]{:S(2)}, u32[]{:S(2)}) collective-permute-start(bf16[512,128]{1,0:T(8,128)(2,1)} %get-tuple-element.42), channel_id=1, source_target_pairs={{0,252},{1,253},{2,254},{3,255},{4,0},{5,1},{6,2},{7,3},{8,4},{9,5... | collective-permute-start | bytes 393224 | tf_op jit(solution)/shard_map/ppermute | solution.py:387
  50.9 2.0 %collective-permute-start.6 = (bf16[512,128]{1,0:T(8,128)(2,1)}, bf16[512,128]{1,0:T(8,128)(2,1)S(1)}, u32[]{:S(2)}, u32[]{:S(2)}) collective-permute-start(bf16[512,128]{1,0:T(8,128)(2,1)} %get-tuple-element.43), channel_id=1, source_target_pairs={{0,1},{1,2},{2,3},{3,0},{4,253},{5,254},{6,255},{7,252},{8,9},{9,1... | collective-permute-start | bytes 393224 | tf_op jit(solution)/shard_map/ppermute | solution.py:387
  52.9 2.2 %collective-permute-start.7 = (bf16[512,128]{1,0:T(8,128)(2,1)}, bf16[512,128]{1,0:T(8,128)(2,1)S(1)}, u32[]{:S(2)}, u32[]{:S(2)}) collective-permute-start(bf16[512,128]{1,0:T(8,128)(2,1)} %get-tuple-element.44), channel_id=1, source_target_pairs={{0,0},{1,1},{2,2},{3,3},{4,252},{5,253},{6,254},{7,255},{8,8},{9,9... | collective-permute-start | bytes 393224 | tf_op jit(solution)/shard_map/ppermute | solution.py:387
  55.1 0.0 collective-permute-done.4.rest_0_
  55.1 0.0 copy-start
  55.1 1.8 %collective-permute-done.5.rest_1_ = bf16[512,128]{1,0:T(8,128)(2,1)S(1)} collective-permute-done((bf16[512,128]{1,0:T(8,128)(2,1)}, bf16[512,128]{1,0:T(8,128)(2,1)S(1)}, u32[]{:S(2)}, u32[]{:S(2)}) %collective-permute-start.5) | collective-permute-done | bytes 131104 | tf_op jit(solution)/shard_map/ppermute | solution.py:387
  56.8 0.0 copy-start.1
  56.8 0.0 collective-permute-done.6.rest_2_
  56.8 0.0 copy-start.2
  56.8 3.6 %collective-permute-done.7.rest_3_ = bf16[512,128]{1,0:T(8,128)(2,1)S(1)} collective-permute-done((bf16[512,128]{1,0:T(8,128)(2,1)}, bf16[512,128]{1,0:T(8,128)(2,1)S(1)}, u32[]{:S(2)}, u32[]{:S(2)}) %collective-permute-start.7) | collective-permute-done | bytes 131104 | tf_op jit(solution)/shard_map/ppermute | solution.py:387
  60.5 0.0 copy-done
  60.5 0.0 copy-done.1
  60.5 0.0 copy-done.2
  60.5 0.0 copy-start.3
  60.5 0.6 %copy-done.3 = bf16[512,128]{1,0:T(8,128)(2,1)} copy-done((bf16[512,128]{1,0:T(8,128)(2,1)}, bf16[512,128]{1,0:T(8,128)(2,1)S(1)}, u32[]{:S(2)}) %copy-start.3) | copy-done | bytes 131096
  61.1 2.7 %from_tokens.1 = bf16[120,8,256]{2,1,0:T(8,128)(2,1)} custom-call(s32[1]{0:T(128)} %bitcast.h_ref, bf16[512,128]{1,0:T(8,128)(2,1)} %copy-done, bf16[512,128]{1,0:T(8,128)(2,1)} %copy-done.1, bf16[512,128]{1,0:T(8,128)(2,1)} %copy-done.2, bf16[512,128]{1,0:T(8,128)(2,1)} %copy-done.3), custom_call_target="tpu_custom_call" | custom-call | tf_op jit(solution)/shard_map/from_tokens/pallas_call | solution.py:322
Async XLA Ops:
  2.1 9.2 %collective-permute-start = (bf16[1088,128]{1,0:T(8,128)(2,1)}, bf16[1088,128]{1,0:T(8,128)(2,1)S(1)}, u32[]{:S(2)}, u32[]{:S(2)}) collective-permute-start(bf16[1088,128]{1,0:T(8,128)(2,1)} %get-tuple-element.26), channel_id=1, source_target_pairs={{0,4},{1,5},{2,6},{3,7},{4,0},{5,1},{6,2},{7,3},{8,12},{9,13},{10,... | collective-permute-start | bytes 835592 | tf_op jit(solution)/shard_map/ppermute | solution.py:387
  11.3 0.7 %copy-start.4 = (bf16[1088,128]{1,0:T(8,128)(2,1)}, bf16[1088,128]{1,0:T(8,128)(2,1)S(1)}, u32[]{:S(2)}) copy-start(bf16[1088,128]{1,0:T(8,128)(2,1)S(1)} %collective-permute-done.oth_ref) | copy-start | bytes 835588
  21.7 13.9 %collective-permute-start.1 = (bf16[512,128]{1,0:T(8,128)(2,1)}, bf16[512,128]{1,0:T(8,128)(2,1)S(1)}, u32[]{:S(2)}, u32[]{:S(2)}) collective-permute-start(bf16[512,128]{1,0:T(8,128)(2,1)} %get-tuple-element.32), channel_id=1, source_target_pairs={{0,11},{1,8},{2,9},{3,10},{4,15},{5,12},{6,13},{7,14},{8,19},{9,16... | collective-permute-start | bytes 393224 | tf_op jit(solution)/shard_map/ppermute | solution.py:387
  24.4 11.2 %collective-permute-start.2 = (bf16[512,128]{1,0:T(8,128)(2,1)}, bf16[512,128]{1,0:T(8,128)(2,1)S(1)}, u32[]{:S(2)}, u32[]{:S(2)}) collective-permute-start(bf16[512,128]{1,0:T(8,128)(2,1)} %get-tuple-element.33), channel_id=1, source_target_pairs={{0,8},{1,9},{2,10},{3,11},{4,12},{5,13},{6,14},{7,15},{8,16},{9,17... | collective-permute-start | bytes 393224 | tf_op jit(solution)/shard_map/ppermute | solution.py:387
  25.6 10.0 %collective-permute-start.3 = (bf16[512,128]{1,0:T(8,128)(2,1)}, bf16[512,128]{1,0:T(8,128)(2,1)S(1)}, u32[]{:S(2)}, u32[]{:S(2)}) collective-permute-start(bf16[512,128]{1,0:T(8,128)(2,1)} %get-tuple-element.34), channel_id=1, source_target_pairs={{0,3},{1,0},{2,1},{3,2},{4,7},{5,4},{6,5},{7,6},{8,11},{9,8},{10,9... | collective-permute-start | bytes 393224 | tf_op jit(solution)/shard_map/ppermute | solution.py:387
  35.6 0.7 %copy-start.5 = (bf16[512,128]{1,0:T(8,128)(2,1)}, bf16[512,128]{1,0:T(8,128)(2,1)S(1)}, u32[]{:S(2)}) copy-start(bf16[512,128]{1,0:T(8,128)(2,1)S(1)} %collective-permute-done.1.rest_0_) | copy-start | bytes 393220
  35.6 0.7 %copy-start.6 = (bf16[512,128]{1,0:T(8,128)(2,1)}, bf16[512,128]{1,0:T(8,128)(2,1)S(1)}, u32[]{:S(2)}) copy-start(bf16[512,128]{1,0:T(8,128)(2,1)S(1)} %collective-permute-done.2.rest_1_) | copy-start | bytes 393220
  35.6 0.7 %copy-start.7 = (bf16[512,128]{1,0:T(8,128)(2,1)}, bf16[512,128]{1,0:T(8,128)(2,1)S(1)}, u32[]{:S(2)}) copy-start(bf16[512,128]{1,0:T(8,128)(2,1)S(1)} %collective-permute-done.3.rest_2_) | copy-start | bytes 393220
  45.5 9.5 %collective-permute-start.4 = (bf16[512,128]{1,0:T(8,128)(2,1)}, bf16[512,128]{1,0:T(8,128)(2,1)S(1)}, u32[]{:S(2)}, u32[]{:S(2)}) collective-permute-start(bf16[512,128]{1,0:T(8,128)(2,1)} %get-tuple-element.41), channel_id=1, source_target_pairs={{0,253},{1,254},{2,255},{3,252},{4,1},{5,2},{6,3},{7,0},{8,5},{9,6... | collective-permute-start | bytes 393224 | tf_op jit(solution)/shard_map/ppermute | solution.py:387
  46.9 9.9 %collective-permute-start.5 = (bf16[512,128]{1,0:T(8,128)(2,1)}, bf16[512,128]{1,0:T(8,128)(2,1)S(1)}, u32[]{:S(2)}, u32[]{:S(2)}) collective-permute-start(bf16[512,128]{1,0:T(8,128)(2,1)} %get-tuple-element.42), channel_id=1, source_target_pairs={{0,252},{1,253},{2,254},{3,255},{4,0},{5,1},{6,2},{7,3},{8,4},{9,5... | collective-permute-start | bytes 393224 | tf_op jit(solution)/shard_map/ppermute | solution.py:387
  50.9 5.9 %collective-permute-start.6 = (bf16[512,128]{1,0:T(8,128)(2,1)}, bf16[512,128]{1,0:T(8,128)(2,1)S(1)}, u32[]{:S(2)}, u32[]{:S(2)}) collective-permute-start(bf16[512,128]{1,0:T(8,128)(2,1)} %get-tuple-element.43), channel_id=1, source_target_pairs={{0,1},{1,2},{2,3},{3,0},{4,253},{5,254},{6,255},{7,252},{8,9},{9,1... | collective-permute-start | bytes 393224 | tf_op jit(solution)/shard_map/ppermute | solution.py:387
  52.9 7.6 %collective-permute-start.7 = (bf16[512,128]{1,0:T(8,128)(2,1)}, bf16[512,128]{1,0:T(8,128)(2,1)S(1)}, u32[]{:S(2)}, u32[]{:S(2)}) collective-permute-start(bf16[512,128]{1,0:T(8,128)(2,1)} %get-tuple-element.44), channel_id=1, source_target_pairs={{0,0},{1,1},{2,2},{3,3},{4,252},{5,253},{6,254},{7,255},{8,8},{9,9... | collective-permute-start | bytes 393224 | tf_op jit(solution)/shard_map/ppermute | solution.py:387
  55.1 5.4 %copy-start = (bf16[512,128]{1,0:T(8,128)(2,1)}, bf16[512,128]{1,0:T(8,128)(2,1)S(1)}, u32[]{:S(2)}) copy-start(bf16[512,128]{1,0:T(8,128)(2,1)S(1)} %collective-permute-done.4.rest_0_) | copy-start | bytes 393220
  56.8 3.7 %copy-start.1 = (bf16[512,128]{1,0:T(8,128)(2,1)}, bf16[512,128]{1,0:T(8,128)(2,1)S(1)}, u32[]{:S(2)}) copy-start(bf16[512,128]{1,0:T(8,128)(2,1)S(1)} %collective-permute-done.5.rest_1_) | copy-start | bytes 393220
  56.8 3.7 %copy-start.2 = (bf16[512,128]{1,0:T(8,128)(2,1)}, bf16[512,128]{1,0:T(8,128)(2,1)S(1)}, u32[]{:S(2)}) copy-start(bf16[512,128]{1,0:T(8,128)(2,1)S(1)} %collective-permute-done.6.rest_2_) | copy-start | bytes 393220
  60.5 0.7 %copy-start.3 = (bf16[512,128]{1,0:T(8,128)(2,1)}, bf16[512,128]{1,0:T(8,128)(2,1)S(1)}, u32[]{:S(2)}) copy-start(bf16[512,128]{1,0:T(8,128)(2,1)S(1)} %collective-permute-done.7.rest_3_) | copy-start | bytes 393220

commit v9 on v8

--- a/solution.py
+++ b/solution.py
@@ -129,25 +129,26 @@
     return middle + matmul(hidden, w_dwn[...])
 
 
-def to_tokens_kernel(h_ref, x_ref, *rest):
-    outs, (wide, tiles) = rest[:-2], rest[-2:]
+def to_tokens_kernel(h_ref, x_ref, send_ref, own_ref, raw, wide, tiles, sems):
     h = h_ref[0]
-    for half in range(2):
-        part = x_ref[:, :, half * LANES : (half + 1) * LANES].astype(jnp.float32)
-        wide[half] = part.reshape(C * WIN, LANES)
+    copies = []
+    for k in range(2):
+        half = 1 - h if k == 0 else h
+        source = x_ref.at[:, :, pl.ds(pl.multiple_of(half * LANES, LANES), LANES)]
+        copies.append(pltpu.make_async_copy(source, raw.at[k], sems.at[k]))
+        copies[-1].start()
     pad = jnp.zeros((LANES - C, LANES), jnp.float32)
     for k in range(2):
-        half = 1 - h if k == 0 else h
+        copies[k].wait()
+        wide[k] = raw[k].astype(jnp.float32).reshape(C * WIN, LANES)
         for r in range(WIN):
-            block = wide.at[half][pl.ds(r, C, stride=WIN), :]
+            block = wide.at[k][pl.ds(r, C, stride=WIN), :]
             block = jnp.concatenate([block, pad], axis=0).T
             tiles[k, :HALF, r] = block.reshape(HALF, WIN, LANES)
-    for k in range(2):
-        tiles[k, HALF] = tiles[1 - k, 0]
-    for k in range(2):
-        for j, (low, high) in enumerate(WINDOWS):
-            part = tiles[k, low:high].reshape((high - low) * TOK, LANES)
-            outs[k * len(WINDOWS) + j][...] = part.astype(jnp.bfloat16)
+    for k, ref in enumerate((send_ref, own_ref)):
+        main = tiles[k, :HALF].reshape(HALF * TOK, LANES)
+        ref[: HALF * TOK] = main.astype(jnp.bfloat16)
+        ref[HALF * TOK :] = tiles[1 - k, 0].reshape(TOK, LANES).astype(jnp.bfloat16)
 
 
 def grouped(count):
@@ -221,28 +222,41 @@
             pair = (jnp.where(even, moved, kept), jnp.where(even, kept, moved))
             for f in range(2):
                 part = pair[f].astype(jnp.bfloat16)
-                for j in range(2):
-                    outs[2 * f + j][spans[i]] = part[j * half_tok : (j + 1) * half_tok]
-
-
-def from_tokens_kernel(h_ref, *rest):
-    ins, (out_ref, tiles, wide) = rest[:-3], rest[-3:]
-    h = h_ref[0]
-    for k, (low, high) in enumerate(SHIFTED):
-        for j in range(4):
-            half = 1 - h if j < 2 else h
-            part = ins[4 * k + j][...].astype(jnp.float32)
-            tiles[half, 1 - j % 2, low:high] = part.reshape(high - low, 4, WIN, LANES)
-    for r in range(WIN):
-        lo = 0 if r >= 4 else 1
-        row = [tiles[half, lo, :, r % 4].reshape(LANES, LANES).T for half in range(2)]
-        row = pltpu.roll(jnp.concatenate(row, axis=1), WIN // 2, 1)
-        for half in range(2):
-            part = row[:C, half * LANES : (half + 1) * LANES]
-            wide.at[half][pl.ds(r, C, stride=WIN), :] = part
+                for j, out in enumerate((outs[f], outs[2 + f])):
+                    out[spans[i]] = part[j * half_tok : (j + 1) * half_tok]
+
+
+def from_tokens_kernel(h_ref, far_up, near_up, far_lo, near_lo, out_ref, rows, wide, ready, sems):
+    edge = WIN // 2
+
+    def place(h):
+        for lo, pair in enumerate(((far_up, near_up), (far_lo, near_lo))):
+            for half in range(2):
+                part = pair[int(half == h)][...].astype(jnp.float32)
+                part = part.reshape(HALF, 4, WIN, LANES)
+                for r in range(4):
+                    low = edge + half * LANES
+                    rows[4 * lo + r, low : low + LANES] = part[:, r].reshape(LANES, LANES)
+
+    for h in range(2):
+
+        @pl.when(h_ref[0] == h)
+        def _():
+            place(h)
+
+    copies = []
     for half in range(2):
-        part = wide[half].reshape(C, WIN, LANES).astype(jnp.bfloat16)
-        out_ref[:, :, half * LANES : (half + 1) * LANES] = part
+        for r in range(WIN):
+            if half == 0:
+                rows[r, :edge] = rows[r, 2 * LANES : 2 * LANES + edge]
+            block = rows[r, half * LANES : (half + 1) * LANES].T
+            wide.at[half][pl.ds(r, C, stride=WIN), :] = block[:C]
+        ready[half] = wide[half].reshape(C, WIN, LANES).astype(jnp.bfloat16)
+        target = out_ref.at[:, :, half * LANES : (half + 1) * LANES]
+        copies.append(pltpu.make_async_copy(ready.at[half], target, sems.at[half]))
+        copies[-1].start()
+    for copy in copies:
+        copy.wait()
 
 
 VMEM = pl.BlockSpec(memory_space=pltpu.VMEM)
@@ -266,15 +280,16 @@
 
 
 def to_tokens(h, x):
-    shapes = [tokens_shape((high - low) * TOK) for low, high in WINDOWS]
     return pl.pallas_call(
         to_tokens_kernel,
-        out_shape=shapes * 2,
-        in_specs=[SMEM, VMEM],
-        out_specs=[VMEM] * (2 * len(shapes)),
+        out_shape=[tokens_shape((HALF + 1) * TOK)] * 2,
+        in_specs=[SMEM, pl.BlockSpec(memory_space=pl.ANY)],
+        out_specs=[VMEM] * 2,
         scratch_shapes=[
+            pltpu.VMEM((2, C, WIN, LANES), jnp.bfloat16),
             pltpu.VMEM((2, C * WIN, LANES), jnp.float32),
-            pltpu.VMEM((2, HALF + 1, WIN, WIN, LANES), jnp.float32),
+            pltpu.VMEM((2, HALF, WIN, WIN, LANES), jnp.float32),
+            pltpu.SemaphoreType.DMA((2,)),
         ],
         compiler_params=PARAMS,
         name="to_tokens",
@@ -323,10 +338,12 @@
         from_tokens_kernel,
         out_shape=jax.ShapeDtypeStruct((C, WIN, 2 * LANES), jnp.bfloat16),
         in_specs=[SMEM] + [VMEM] * len(pieces),
-        out_specs=VMEM,
+        out_specs=pl.BlockSpec(memory_space=pl.ANY),
         scratch_shapes=[
-            pltpu.VMEM((2, 2, HALF, 4, WIN, LANES), jnp.float32),
+            pltpu.VMEM((WIN, 2 * LANES + WIN, LANES), jnp.float32),
             pltpu.VMEM((2, C * WIN, LANES), jnp.float32),
+            pltpu.VMEM((2, C, WIN, LANES), jnp.bfloat16),
+            pltpu.SemaphoreType.DMA((2,)),
         ],
         compiler_params=PARAMS,
         name="from_tokens",
@@ -404,12 +421,12 @@
         pieces.append((moved_up, moved_lo, kept_up, kept_lo))
     home = []
     for k in chunks:
-        far_up, far_lo, near_up, near_lo = layer_two(k, h, pieces[k], w_two)
+        far_up, near_up, far_lo, near_lo = layer_two(k, h, pieces[k], w_two)
         far_up = send(far_up, -1, -1, 1)
+        near_up = send(near_up, 0, -2, 1)
         far_lo = send(far_lo, -1, -1, 0)
-        near_up = send(near_up, 0, -2, 1)
         near_lo = send(near_lo, 0, -2, 0)
-        home += [far_up, far_lo, near_up, near_lo]
+        home += [far_up, near_up, far_lo, near_lo]
     return from_tokens(h, home)[None]
 
 

time: 64.1 us -> 63.3 us (0.988)
  the two profiles are of different devices: /device:TPU:17 before, /device:TPU:1 now
where the time goes in v9:
time: 63.3 us; the launch traced here: 62.8 us
  Pallas kernels  25.9 us (41%)
  starting transfers between devices  17.6 us (28%)
  waiting for transfers between devices  16.4 us (26%)
  local copies, waits for them, and re-layouts  2.71 us (4%)
    ppermute x8, starting transfers between devices, send(): return lax.ppermute(value, ('frame', 'strip'), pairs)  17.6 us
    ppermute x8, waiting for transfers between devices, send(): return lax.ppermute(value, ('frame', 'strip'), pairs)  16.4 us
    pallas_call x1, Pallas kernels, layer_one(): pl.pallas_call(functools.partial(layer_one_kernel, count, first, last), o...  9.69 us
    pallas_call x1, Pallas kernels, layer_two(): pl.pallas_call(functools.partial(layer_two_kernel, count), out_shape=[tok...  9.2 us
    unnamed x16, local copies, waits for them, and re-layouts  2.71 us
    pallas_call x1, Pallas kernels, prepared(): pl.pallas_call(prepare_kernel, out_shape=[jax.ShapeDtypeStruct(shape, jnp...  2.66 us
    pallas_call x1, Pallas kernels, from_tokens(): pl.pallas_call(from_tokens_kernel, out_shape=jax.ShapeDtypeStruct((C, WIN...  2.26 us
    pallas_call x1, Pallas kernels, to_tokens(): pl.pallas_call(to_tokens_kernel, out_shape=[tokens_shape((HALF + 1) * TOK...  2.07 us
  transfers between devices with their start and end apart: 8, of which 3 were waited for; matrix products, arithmetic and copies ran while one was open for 0% of the time, Pallas kernels for 4%

profile of v9, /device:TPU:1, one launch (start us, length us, event | category | flops | bytes accessed | tf_op | source)
XLA Modules:
  0.0 62.8 jit_solution(11631868751874231199)
XLA Ops:
  0.0 2.1 %to_tokens.1 = (bf16[1088,128]{1,0:T(8,128)(2,1)}, bf16[1088,128]{1,0:T(8,128)(2,1)}) custom-call(s32[1]{0:T(128)} %bitcast.h_ref, bf16[120,8,256]{2,1,0:T(8,128)(2,1)} %bitcast.3), custom_call_target="tpu_custom_call" | custom-call | tf_op jit(solution)/shard_map/to_tokens/pallas_call | solution.py:283
  2.1 3.8 %collective-permute-start = (bf16[1088,128]{1,0:T(8,128)(2,1)}, bf16[1088,128]{1,0:T(8,128)(2,1)S(1)}, u32[]{:S(2)}, u32[]{:S(2)}) collective-permute-start(bf16[1088,128]{1,0:T(8,128)(2,1)} %get-tuple-element.26), channel_id=1, source_target_pairs={{0,4},{1,5},{2,6},{3,7},{4,0},{5,1},{6,2},{7,3},{8,12},{9,13},{10,... | collective-permute-start | bytes 835592 | tf_op jit(solution)/shard_map/ppermute | solution.py:404
  5.9 2.7 %prepare.1 = (bf16[128,256]{1,0:T(8,128)(2,1)}, bf16[512,128]{1,0:T(8,128)(2,1)}, bf16[240,128]{1,0:T(8,128)(2,1)}, bf16[128,512]{1,0:T(8,128)(2,1)}, bf16[256,1...) custom-call(bf16[2,120,360]{2,1,0:T(8,128)(2,1)} %w_mut.1, ...), custom_call_target="tpu_custom_call" | custom-call | tf_op jit(solution)/shard_map/prepare/pallas_call | solution.py:385
  8.6 3.0 %collective-permute-done.oth_ref = bf16[1088,128]{1,0:T(8,128)(2,1)S(1)} collective-permute-done((bf16[1088,128]{1,0:T(8,128)(2,1)}, bf16[1088,128]{1,0:T(8,128)(2,1)S(1)}, u32[]{:S(2)}, u32[]{:S(2)}) %collective-permute-start) | collective-permute-done | bytes 278560 | tf_op jit(solution)/shard_map/ppermute | solution.py:404
  11.5 0.0 copy-start.4
  11.5 0.7 %copy-done.4 = bf16[1088,128]{1,0:T(8,128)(2,1)} copy-done((bf16[1088,128]{1,0:T(8,128)(2,1)}, bf16[1088,128]{1,0:T(8,128)(2,1)S(1)}, u32[]{:S(2)}) %copy-start.4) | copy-done | bytes 278552
  12.3 9.7 %layer_one.1 = (bf16[512,128]{1,0:T(8,128)(2,1)}, bf16[512,128]{1,0:T(8,128)(2,1)}, bf16[512,128]{1,0:T(8,128)(2,1)}, bf16[512,128]{1,0:T(8,128)(2,1)}) custom-call(s32[1]{0:T(128)} %bitcast.h_ref, bf16[1088,128]{1,0:T(8,128)(2,1)} %get-tuple-element.25.own_ref, bf16[1088,128]{1,0:T(8,128)(2,1)} %copy-done.4, bf16[128,256]{1,0:T(8,128)(2,1)} %get-tuple-element.27.rest_0_, ...), custom_call_target="tpu_custom_call" | custom-call | flops 8000000000 | bytes 1048576 | tf_op jit(solution)/shard_map/layer_one/pallas_call | solution.py:306
  21.9 3.3 %collective-permute-start.1 = (bf16[512,128]{1,0:T(8,128)(2,1)}, bf16[512,128]{1,0:T(8,128)(2,1)S(1)}, u32[]{:S(2)}, u32[]{:S(2)}) collective-permute-start(bf16[512,128]{1,0:T(8,128)(2,1)} %get-tuple-element.32), channel_id=1, source_target_pairs={{0,11},{1,8},{2,9},{3,10},{4,15},{5,12},{6,13},{7,14},{8,19},{9,16... | collective-permute-start | bytes 393224 | tf_op jit(solution)/shard_map/ppermute | solution.py:404
  25.3 1.2 %collective-permute-start.2 = (bf16[512,128]{1,0:T(8,128)(2,1)}, bf16[512,128]{1,0:T(8,128)(2,1)S(1)}, u32[]{:S(2)}, u32[]{:S(2)}) collective-permute-start(bf16[512,128]{1,0:T(8,128)(2,1)} %get-tuple-element.33), channel_id=1, source_target_pairs={{0,8},{1,9},{2,10},{3,11},{4,12},{5,13},{6,14},{7,15},{8,16},{9,17... | collective-permute-start | bytes 393224 | tf_op jit(solution)/shard_map/ppermute | solution.py:404
  26.5 0.3 collective-permute-start.3
  26.7 10.0 %collective-permute-done.1.rest_0_ = bf16[512,128]{1,0:T(8,128)(2,1)S(1)} collective-permute-done((bf16[512,128]{1,0:T(8,128)(2,1)}, bf16[512,128]{1,0:T(8,128)(2,1)S(1)}, u32[]{:S(2)}, u32[]{:S(2)}) %collective-permute-start.1) | collective-permute-done | bytes 131104 | tf_op jit(solution)/shard_map/ppermute | solution.py:404
  36.8 0.0 copy-start.5
  36.8 0.0 collective-permute-done.2.rest_1_
  36.8 0.0 copy-start.6
  36.8 0.0 collective-permute-done.3.rest_2_
  36.8 0.0 copy-start.7
  36.8 0.6 %copy-done.5 = bf16[512,128]{1,0:T(8,128)(2,1)} copy-done((bf16[512,128]{1,0:T(8,128)(2,1)}, bf16[512,128]{1,0:T(8,128)(2,1)S(1)}, u32[]{:S(2)}) %copy-start.5) | copy-done | bytes 131096
  37.4 0.0 copy-done.6
  37.5 0.0 copy-done.7
  37.5 9.2 %layer_two.1 = (bf16[512,128]{1,0:T(8,128)(2,1)}, bf16[512,128]{1,0:T(8,128)(2,1)}, bf16[512,128]{1,0:T(8,128)(2,1)}, bf16[512,128]{1,0:T(8,128)(2,1)}) custom-call(s32[1]{0:T(128)} %bitcast.h_ref, bf16[512,128]{1,0:T(8,128)(2,1)} %copy-done.5, bf16[512,128]{1,0:T(8,128)(2,1)} %copy-done.6, bf16[512,128]{1,0:T(8,128)(2,1)} %copy-done.7, ...), custom_call_target="tpu_custom_call" | custom-call | flops 8000000000 | bytes 1048576 | tf_op jit(solution)/shard_map/layer_two/pallas_call | solution.py:324
  46.7 5.1 %collective-permute-start.4 = (bf16[512,128]{1,0:T(8,128)(2,1)}, bf16[512,128]{1,0:T(8,128)(2,1)S(1)}, u32[]{:S(2)}, u32[]{:S(2)}) collective-permute-start(bf16[512,128]{1,0:T(8,128)(2,1)} %get-tuple-element.41), channel_id=1, source_target_pairs={{0,253},{1,254},{2,255},{3,252},{4,1},{5,2},{6,3},{7,0},{8,5},{9,6... | collective-permute-start | bytes 393224 | tf_op jit(solution)/shard_map/ppermute | solution.py:404
  51.8 0.9 %collective-permute-start.5 = (bf16[512,128]{1,0:T(8,128)(2,1)}, bf16[512,128]{1,0:T(8,128)(2,1)S(1)}, u32[]{:S(2)}, u32[]{:S(2)}) collective-permute-start(bf16[512,128]{1,0:T(8,128)(2,1)} %get-tuple-element.42), channel_id=1, source_target_pairs={{0,1},{1,2},{2,3},{3,0},{4,253},{5,254},{6,255},{7,252},{8,9},{9,1... | collective-permute-start | bytes 393224 | tf_op jit(solution)/shard_map/ppermute | solution.py:404
  52.7 1.5 %collective-permute-start.6 = (bf16[512,128]{1,0:T(8,128)(2,1)}, bf16[512,128]{1,0:T(8,128)(2,1)S(1)}, u32[]{:S(2)}, u32[]{:S(2)}) collective-permute-start(bf16[512,128]{1,0:T(8,128)(2,1)} %get-tuple-element.43), channel_id=1, source_target_pairs={{0,252},{1,253},{2,254},{3,255},{4,0},{5,1},{6,2},{7,3},{8,4},{9,5... | collective-permute-start | bytes 393224 | tf_op jit(solution)/shard_map/ppermute | solution.py:404
  54.2 1.6 %collective-permute-start.7 = (bf16[512,128]{1,0:T(8,128)(2,1)}, bf16[512,128]{1,0:T(8,128)(2,1)S(1)}, u32[]{:S(2)}, u32[]{:S(2)}) collective-permute-start(bf16[512,128]{1,0:T(8,128)(2,1)} %get-tuple-element.44), channel_id=1, source_target_pairs={{0,0},{1,1},{2,2},{3,3},{4,252},{5,253},{6,254},{7,255},{8,8},{9,9... | collective-permute-start | bytes 393224 | tf_op jit(solution)/shard_map/ppermute | solution.py:404
  55.7 0.0 collective-permute-done.4.far_up
  55.7 0.0 copy-start
  55.7 0.0 collective-permute-done.5.near_up
  55.7 0.0 copy-start.1
  55.8 3.3 %collective-permute-done.6.far_lo = bf16[512,128]{1,0:T(8,128)(2,1)S(1)} collective-permute-done((bf16[512,128]{1,0:T(8,128)(2,1)}, bf16[512,128]{1,0:T(8,128)(2,1)S(1)}, u32[]{:S(2)}, u32[]{:S(2)}) %collective-permute-start.6) | collective-permute-done | bytes 131104 | tf_op jit(solution)/shard_map/ppermute | solution.py:404
  59.1 0.0 copy-start.2
  59.1 0.0 collective-permute-done.7.near_lo
  59.1 0.0 copy-done
  59.1 0.0 copy-done.1
  59.1 0.6 copy-done.2
  59.7 0.0 copy-start.3
  59.8 0.7 %copy-done.3 = bf16[512,128]{1,0:T(8,128)(2,1)} copy-done((bf16[512,128]{1,0:T(8,128)(2,1)}, bf16[512,128]{1,0:T(8,128)(2,1)S(1)}, u32[]{:S(2)}) %copy-start.3) | copy-done | bytes 131096
  60.4 2.3 %from_tokens.1 = bf16[120,8,256]{2,1,0:T(8,128)(2,1)} custom-call(s32[1]{0:T(128)} %bitcast.h_ref, bf16[512,128]{1,0:T(8,128)(2,1)} %copy-done, bf16[512,128]{1,0:T(8,128)(2,1)} %copy-done.1, bf16[512,128]{1,0:T(8,128)(2,1)} %copy-done.2, bf16[512,128]{1,0:T(8,128)(2,1)} %copy-done.3), custom_call_target="tpu_custom_call" | custom-call | tf_op jit(solution)/shard_map/from_tokens/pallas_call | solution.py:337
Async XLA Ops:
  2.1 9.5 %collective-permute-start = (bf16[1088,128]{1,0:T(8,128)(2,1)}, bf16[1088,128]{1,0:T(8,128)(2,1)S(1)}, u32[]{:S(2)}, u32[]{:S(2)}) collective-permute-start(bf16[1088,128]{1,0:T(8,128)(2,1)} %get-tuple-element.26), channel_id=1, source_target_pairs={{0,4},{1,5},{2,6},{3,7},{4,0},{5,1},{6,2},{7,3},{8,12},{9,13},{10,... | collective-permute-start | bytes 835592 | tf_op jit(solution)/shard_map/ppermute | solution.py:404
  11.5 0.7 %copy-start.4 = (bf16[1088,128]{1,0:T(8,128)(2,1)}, bf16[1088,128]{1,0:T(8,128)(2,1)S(1)}, u32[]{:S(2)}) copy-start(bf16[1088,128]{1,0:T(8,128)(2,1)S(1)} %collective-permute-done.oth_ref) | copy-start | bytes 835588
  21.9 14.8 %collective-permute-start.1 = (bf16[512,128]{1,0:T(8,128)(2,1)}, bf16[512,128]{1,0:T(8,128)(2,1)S(1)}, u32[]{:S(2)}, u32[]{:S(2)}) collective-permute-start(bf16[512,128]{1,0:T(8,128)(2,1)} %get-tuple-element.32), channel_id=1, source_target_pairs={{0,11},{1,8},{2,9},{3,10},{4,15},{5,12},{6,13},{7,14},{8,19},{9,16... | collective-permute-start | bytes 393224 | tf_op jit(solution)/shard_map/ppermute | solution.py:404
  25.3 11.5 %collective-permute-start.2 = (bf16[512,128]{1,0:T(8,128)(2,1)}, bf16[512,128]{1,0:T(8,128)(2,1)S(1)}, u32[]{:S(2)}, u32[]{:S(2)}) collective-permute-start(bf16[512,128]{1,0:T(8,128)(2,1)} %get-tuple-element.33), channel_id=1, source_target_pairs={{0,8},{1,9},{2,10},{3,11},{4,12},{5,13},{6,14},{7,15},{8,16},{9,17... | collective-permute-start | bytes 393224 | tf_op jit(solution)/shard_map/ppermute | solution.py:404
  26.5 10.3 %collective-permute-start.3 = (bf16[512,128]{1,0:T(8,128)(2,1)}, bf16[512,128]{1,0:T(8,128)(2,1)S(1)}, u32[]{:S(2)}, u32[]{:S(2)}) collective-permute-start(bf16[512,128]{1,0:T(8,128)(2,1)} %get-tuple-element.34), channel_id=1, source_target_pairs={{0,3},{1,0},{2,1},{3,2},{4,7},{5,4},{6,5},{7,6},{8,11},{9,8},{10,9... | collective-permute-start | bytes 393224 | tf_op jit(solution)/shard_map/ppermute | solution.py:404
  36.8 0.7 %copy-start.5 = (bf16[512,128]{1,0:T(8,128)(2,1)}, bf16[512,128]{1,0:T(8,128)(2,1)S(1)}, u32[]{:S(2)}) copy-start(bf16[512,128]{1,0:T(8,128)(2,1)S(1)} %collective-permute-done.1.rest_0_) | copy-start | bytes 393220
  36.8 0.7 %copy-start.6 = (bf16[512,128]{1,0:T(8,128)(2,1)}, bf16[512,128]{1,0:T(8,128)(2,1)S(1)}, u32[]{:S(2)}) copy-start(bf16[512,128]{1,0:T(8,128)(2,1)S(1)} %collective-permute-done.2.rest_1_) | copy-start | bytes 393220
  36.8 0.7 %copy-start.7 = (bf16[512,128]{1,0:T(8,128)(2,1)}, bf16[512,128]{1,0:T(8,128)(2,1)S(1)}, u32[]{:S(2)}) copy-start(bf16[512,128]{1,0:T(8,128)(2,1)S(1)} %collective-permute-done.3.rest_2_) | copy-start | bytes 393220
  46.7 9.0 %collective-permute-start.4 = (bf16[512,128]{1,0:T(8,128)(2,1)}, bf16[512,128]{1,0:T(8,128)(2,1)S(1)}, u32[]{:S(2)}, u32[]{:S(2)}) collective-permute-start(bf16[512,128]{1,0:T(8,128)(2,1)} %get-tuple-element.41), channel_id=1, source_target_pairs={{0,253},{1,254},{2,255},{3,252},{4,1},{5,2},{6,3},{7,0},{8,5},{9,6... | collective-permute-start | bytes 393224 | tf_op jit(solution)/shard_map/ppermute | solution.py:404
  51.8 3.9 %collective-permute-start.5 = (bf16[512,128]{1,0:T(8,128)(2,1)}, bf16[512,128]{1,0:T(8,128)(2,1)S(1)}, u32[]{:S(2)}, u32[]{:S(2)}) collective-permute-start(bf16[512,128]{1,0:T(8,128)(2,1)} %get-tuple-element.42), channel_id=1, source_target_pairs={{0,1},{1,2},{2,3},{3,0},{4,253},{5,254},{6,255},{7,252},{8,9},{9,1... | collective-permute-start | bytes 393224 | tf_op jit(solution)/shard_map/ppermute | solution.py:404
  52.7 6.4 %collective-permute-start.6 = (bf16[512,128]{1,0:T(8,128)(2,1)}, bf16[512,128]{1,0:T(8,128)(2,1)S(1)}, u32[]{:S(2)}, u32[]{:S(2)}) collective-permute-start(bf16[512,128]{1,0:T(8,128)(2,1)} %get-tuple-element.43), channel_id=1, source_target_pairs={{0,252},{1,253},{2,254},{3,255},{4,0},{5,1},{6,2},{7,3},{8,4},{9,5... | collective-permute-start | bytes 393224 | tf_op jit(solution)/shard_map/ppermute | solution.py:404
  54.2 4.9 %collective-permute-start.7 = (bf16[512,128]{1,0:T(8,128)(2,1)}, bf16[512,128]{1,0:T(8,128)(2,1)S(1)}, u32[]{:S(2)}, u32[]{:S(2)}) collective-permute-start(bf16[512,128]{1,0:T(8,128)(2,1)} %get-tuple-element.44), channel_id=1, source_target_pairs={{0,0},{1,1},{2,2},{3,3},{4,252},{5,253},{6,254},{7,255},{8,8},{9,9... | collective-permute-start | bytes 393224 | tf_op jit(solution)/shard_map/ppermute | solution.py:404
  55.7 3.4 %copy-start = (bf16[512,128]{1,0:T(8,128)(2,1)}, bf16[512,128]{1,0:T(8,128)(2,1)S(1)}, u32[]{:S(2)}) copy-start(bf16[512,128]{1,0:T(8,128)(2,1)S(1)} %collective-permute-done.4.far_up) | copy-start | bytes 393220
  55.7 3.4 %copy-start.1 = (bf16[512,128]{1,0:T(8,128)(2,1)}, bf16[512,128]{1,0:T(8,128)(2,1)S(1)}, u32[]{:S(2)}) copy-start(bf16[512,128]{1,0:T(8,128)(2,1)S(1)} %collective-permute-done.5.near_up) | copy-start | bytes 393220
  59.1 0.6 %copy-start.2 = (bf16[512,128]{1,0:T(8,128)(2,1)}, bf16[512,128]{1,0:T(8,128)(2,1)S(1)}, u32[]{:S(2)}) copy-start(bf16[512,128]{1,0:T(8,128)(2,1)S(1)} %collective-permute-done.6.far_lo) | copy-start | bytes 393220
  59.7 0.7 %copy-start.3 = (bf16[512,128]{1,0:T(8,128)(2,1)}, bf16[512,128]{1,0:T(8,128)(2,1)S(1)}, u32[]{:S(2)}) copy-start(bf16[512,128]{1,0:T(8,128)(2,1)S(1)} %collective-permute-done.7.near_lo) | copy-start | bytes 393220

commit v10 on v9

--- a/solution.py
+++ b/solution.py
@@ -44,11 +44,18 @@
     return (centred * lax.rsqrt(spread + EPS)).astype(jnp.bfloat16)
 
 
-def head_only(q_t, head):
+def rows_of_head(head):
     low = head * HEAD // 16 * 16
-    high = -(-(head * HEAD + HEAD) // 16) * 16
+    return low, low + 32
+
+
+def head_only(q_t, head, lanes=None):
+    low, high = rows_of_head(head)
     row = lax.broadcasted_iota(jnp.int32, (high - low, q_t.shape[1]), 0) + low
     keep = (row >= head * HEAD) & (row < head * HEAD + HEAD)
+    if lanes is not None:
+        lane = lax.broadcasted_iota(jnp.int32, keep.shape, 1)
+        keep = keep & ((lane < TOK) if lanes == 0 else (lane >= TOK))
     pieces = [q_t[low:high] * jnp.where(keep, 1.0, 0.0).astype(jnp.bfloat16)]
     if low:
         pieces.insert(0, jnp.zeros((low, q_t.shape[1]), jnp.bfloat16))
@@ -64,59 +71,85 @@
     return weights * (1.0 / total)
 
 
-def project_windows(x, w_k, w_qv, keys, qv_t, first):
+def project_windows(x, w_k, w_qv, mutual_keys, self_keys, qv_t, first):
     normal = normed(x)
     new_keys = matmul(normal, w_k[...]).astype(jnp.bfloat16)
     new_qv = matmul_nt(w_qv[...], normal).astype(jnp.bfloat16)
     for i in range(x.shape[0] // LANES):
-        span = slice(i * LANES, (i + 1) * LANES)
-        keys[first + i] = new_keys[span]
-        qv_t[first + i] = new_qv[:, span]
-
-
-def score_block(kind, pair, keys, qv_t, window, of_first):
-    kind_q = qv_t[window, kind * LANES : (kind + 1) * LANES]
-    queries = jnp.concatenate(
-        [head_only(kind_q, 2 * pair), head_only(kind_q, 2 * pair + 1)], axis=1
+        low = i * LANES
+        for f in range(2):
+            span = slice(f * LANES, (f + 1) * LANES)
+            mutual_keys[first + i, :, span] = new_keys[low + f * TOK : low + (f + 1) * TOK, :LANES]
+        self_keys[first + i] = new_keys[low : low + LANES, LANES:]
+        qv_t[first + i] = new_qv[:, low : low + LANES]
+
+
+def score_mutual(pair, mutual_keys, qv_t, window):
+    heads = (2 * pair, 2 * pair + 1)
+    q_t = qv_t[window, :LANES]
+    queries = [
+        jnp.concatenate([head_only(q_t, head, lanes) for head in heads], axis=1) for lanes in (1, 0)
+    ]
+    return matmul(mutual_keys[window], jnp.concatenate(queries, axis=0))
+
+
+def score_self(pair, self_keys, qv_t, window):
+    heads = (2 * pair, 2 * pair + 1)
+    q_t = qv_t[window, LANES : 2 * LANES]
+    queries = jnp.concatenate([head_only(q_t, head) for head in heads], axis=1)
+    return matmul(self_keys[window], queries)
+
+
+def mix_head(head, mutual, own, qv_t, window):
+    lane = lax.broadcasted_iota(jnp.int32, (TOK, LANES), 1)
+    first = jnp.where(lane < TOK, 1.0, 0.0).astype(jnp.bfloat16)
+    second = jnp.where(lane < TOK, 0.0, 1.0).astype(jnp.bfloat16)
+    probs = softmax_rows(mutual).astype(jnp.bfloat16)
+    probs = jnp.concatenate([probs * second, probs * first], axis=0)
+    own = softmax_rows(own).astype(jnp.bfloat16)
+    nothing = jnp.zeros((LANES, LANES), jnp.bfloat16)
+    probs = jnp.concatenate(
+        [jnp.concatenate([probs, nothing], axis=1), jnp.concatenate([nothing, own], axis=1)], axis=0
     )
-    scores = matmul(keys[window, :, kind * LANES : (kind + 1) * LANES], queries)
-    if kind == 0:
-        scores = jnp.where(of_first, scores[TOK:], scores[:TOK])
-    return scores
-
-
-def mix_block(kind, pair, scores, qv_t, window, of_first):
-    probs = [softmax_rows(scores[:, i * LANES : (i + 1) * LANES]) for i in range(2)]
-    probs = jnp.concatenate(probs, axis=1).astype(jnp.bfloat16)
-    if kind == 0:
-        first = jnp.where(of_first, 1.0, 0.0).astype(jnp.bfloat16)
-        second = jnp.where(of_first, 0.0, 1.0).astype(jnp.bfloat16)
-        probs = jnp.concatenate([probs * second, probs * first], axis=0)
-    want = pair * 2 * HEAD
-    low = want // 16 * 16
-    base = (2 + kind) * LANES + low
-    mixed = matmul(qv_t[window, base : base + 48], probs)[want - low : want - low + 2 * HEAD]
-    one, two = mixed[:, :LANES], mixed[:, LANES:]
+    low, high = rows_of_head(head)
+    values = [qv_t[window, (2 + kind) * LANES + low : (2 + kind) * LANES + high] for kind in range(2)]
+    return matmul(jnp.concatenate(values, axis=1), probs)
+
+
+def by_channel(mixed):
     row = lax.broadcasted_iota(jnp.int32, (8, LANES), 0)
-    shared = jnp.where(row < HEAD - 16, one[16:24], two[16:24])
-    return jnp.concatenate([one[:16], shared, two[24:]], axis=0)
-
-
-def attend(count, keys, qv_t, mutual_scores, self_scores, joined):
-    scores = (mutual_scores, self_scores)
-    lane = lax.broadcasted_iota(jnp.int32, (TOK, 2 * LANES), 1)
-    of_first = (lane % LANES) < TOK
-    blocks = [(kind, pair) for kind in range(2) for pair in range(HEADS // 2)]
-    for kind, pair in blocks:
-        scores[kind][0, pair] = score_block(kind, pair, keys, qv_t, 0, of_first)
+    parts = []
+    for head in range(0, HEADS, 2):
+        base = head * HEAD
+        one, two = mixed[head], mixed[head + 1]
+        one_low, two_low = base - rows_of_head(head)[0], base - rows_of_head(head + 1)[0]
+        shared = jnp.where(
+            row < HEAD - 16, one[one_low + 16 : one_low + 24], two[two_low + 16 : two_low + 24]
+        )
+        parts += [one[one_low : one_low + 16], shared, two[two_low + 24 : two_low + 40]]
+    return jnp.concatenate(parts, axis=0)
+
+
+def attend(count, mutual_keys, self_keys, qv_t, mutual_scores, self_scores, joined):
+    def score(i, pair):
+        mutual_scores[i % 2, pair] = score_mutual(pair, mutual_keys, qv_t, i)
+        self_scores[i % 2, pair] = score_self(pair, self_keys, qv_t, i)
+
+    for pair in range(HEADS // 2):
+        score(0, pair)
     for i in range(count):
-        outs = []
-        for kind, pair in blocks:
-            ref = scores[kind]
+        mixed = []
+        for pair in range(HEADS // 2):
             if i + 1 < count:
-                ref[(i + 1) % 2, pair] = score_block(kind, pair, keys, qv_t, i + 1, of_first)
-            outs.append(mix_block(kind, pair, ref[i % 2, pair], qv_t, i, of_first))
-        joined[i] = jnp.concatenate(outs, axis=0).astype(jnp.bfloat16)
+                score(i + 1, pair)
+            for j in range(2):
+                span = slice(j * LANES, (j + 1) * LANES)
+                mutual, own = mutual_scores[i % 2, pair, :, span], self_scores[i % 2, pair, :, span]
+                mixed.append(mix_head(2 * pair + j, mutual, own, qv_t, i))
+        for kind in range(2):
+            span = slice(kind * LANES, (kind + 1) * LANES)
+            part = by_channel([block[:, span] for block in mixed])
+            joined[i, kind * C : (kind + 1) * C] = part.astype(jnp.bfloat16)
 
 
 def finished(x, joined, w_prj, w_gu, w_dwn):
@@ -166,7 +199,7 @@
     if not last:
         after, rest = rest[0], rest[1:]
     flat, tiles, *scratch = rest
-    keys, qv_t, joined = scratch[0], scratch[1], scratch[-1]
+    mutual_keys, self_keys, qv_t, joined = *scratch[:3], scratch[-1]
     shift = 0 if first else WIN
 
     def tokens(group):
@@ -177,7 +210,7 @@
         return jnp.concatenate(parts, axis=0).astype(jnp.float32)
 
     for group in grouped(count):
-        project_windows(tokens(group), w_k, w_qv, keys, qv_t, group[0])
+        project_windows(tokens(group), w_k, w_qv, mutual_keys, self_keys, qv_t, group[0])
     attend(count, *scratch)
     if not first:
         flat[:, :, :WIN, :] = before[...]
@@ -204,7 +237,7 @@
     ins, rest = rest[:4], rest[4:]
     w_k, w_qv, w_prj, w_gu, w_dwn = rest[:5]
     outs, scratch = rest[5:9], rest[9:]
-    keys, qv_t, joined = scratch[0], scratch[1], scratch[-1]
+    mutual_keys, self_keys, qv_t, joined = *scratch[:3], scratch[-1]
     half_tok = TOK // 2
     spans = [slice(i * half_tok, (i + 1) * half_tok) for i in range(count)]
 
@@ -213,7 +246,7 @@
         return jnp.concatenate(parts, axis=0).astype(jnp.float32)
 
     for group in grouped(count):
-        project_windows(tokens(group), w_k, w_qv, keys, qv_t, group[0])
+        project_windows(tokens(group), w_k, w_qv, mutual_keys, self_keys, qv_t, group[0])
     attend(count, *scratch)
     for group in grouped(count):
         y = finished(tokens(group), [joined[i] for i in group], w_prj, w_gu, w_dwn)
@@ -267,7 +300,8 @@
 
 def attention_scratch(count):
     return [
-        pltpu.VMEM((count, LANES, 2 * LANES), jnp.bfloat16),
+        pltpu.VMEM((count, TOK, 2 * LANES), jnp.bfloat16),
+        pltpu.VMEM((count, LANES, LANES), jnp.bfloat16),
         pltpu.VMEM((count, 4 * LANES, LANES), jnp.bfloat16),
         pltpu.VMEM((2, HEADS // 2, TOK, 2 * LANES), jnp.float32),
         pltpu.VMEM((2, HEADS // 2, 2 * TOK, 2 * LANES), jnp.float32),

time: 63.3 us -> 63 us (level)
  no operation moved by 1% of the time
where the time goes in v10:
time: 63 us; the launch traced here: 62.6 us
  Pallas kernels  25.6 us (41%)
  starting transfers between devices  17.7 us (28%)
  waiting for transfers between devices  16.4 us (26%)
  local copies, waits for them, and re-layouts  2.71 us (4%)
    ppermute x8, starting transfers between devices, send(): return lax.ppermute(value, ('frame', 'strip'), pairs)  17.7 us
    ppermute x8, waiting for transfers between devices, send(): return lax.ppermute(value, ('frame', 'strip'), pairs)  16.4 us
    pallas_call x1, Pallas kernels, layer_one(): pl.pallas_call(functools.partial(layer_one_kernel, count, first, last), o...  9.5 us
    pallas_call x1, Pallas kernels, layer_two(): pl.pallas_call(functools.partial(layer_two_kernel, count), out_shape=[tok...  9.14 us
    unnamed x16, local copies, waits for them, and re-layouts  2.71 us
    pallas_call x1, Pallas kernels, prepared(): pl.pallas_call(prepare_kernel, out_shape=[jax.ShapeDtypeStruct(shape, jnp...  2.66 us
    pallas_call x1, Pallas kernels, from_tokens(): pl.pallas_call(from_tokens_kernel, out_shape=jax.ShapeDtypeStruct((C, WIN...  2.26 us
    pallas_call x1, Pallas kernels, to_tokens(): pl.pallas_call(to_tokens_kernel, out_shape=[tokens_shape((HALF + 1) * TOK...  2.07 us
  transfers between devices with their start and end apart: 8, of which 3 were waited for; matrix products, arithmetic and copies ran while one was open for 0% of the time, Pallas kernels for 4%

profile of v10, /device:TPU:1, one launch (start us, length us, event | category | flops | bytes accessed | tf_op | source)
XLA Modules:
  0.0 62.6 jit_solution(3526141769747931333)
XLA Ops:
  0.0 2.1 %to_tokens.1 = (bf16[1088,128]{1,0:T(8,128)(2,1)}, bf16[1088,128]{1,0:T(8,128)(2,1)}) custom-call(s32[1]{0:T(128)} %bitcast.h_ref, bf16[120,8,256]{2,1,0:T(8,128)(2,1)} %bitcast.3), custom_call_target="tpu_custom_call" | custom-call | tf_op jit(solution)/shard_map/to_tokens/pallas_call | solution.py:317
  2.1 3.8 %collective-permute-start = (bf16[1088,128]{1,0:T(8,128)(2,1)}, bf16[1088,128]{1,0:T(8,128)(2,1)S(1)}, u32[]{:S(2)}, u32[]{:S(2)}) collective-permute-start(bf16[1088,128]{1,0:T(8,128)(2,1)} %get-tuple-element.26), channel_id=1, source_target_pairs={{0,4},{1,5},{2,6},{3,7},{4,0},{5,1},{6,2},{7,3},{8,12},{9,13},{10,... | collective-permute-start | bytes 835592 | tf_op jit(solution)/shard_map/ppermute | solution.py:438
  5.9 2.7 %prepare.1 = (bf16[128,256]{1,0:T(8,128)(2,1)}, bf16[512,128]{1,0:T(8,128)(2,1)}, bf16[240,128]{1,0:T(8,128)(2,1)}, bf16[128,512]{1,0:T(8,128)(2,1)}, bf16[256,1...) custom-call(bf16[2,120,360]{2,1,0:T(8,128)(2,1)} %w_mut.1, ...), custom_call_target="tpu_custom_call" | custom-call | tf_op jit(solution)/shard_map/prepare/pallas_call | solution.py:419
  8.6 3.0 %collective-permute-done.oth_ref = bf16[1088,128]{1,0:T(8,128)(2,1)S(1)} collective-permute-done((bf16[1088,128]{1,0:T(8,128)(2,1)}, bf16[1088,128]{1,0:T(8,128)(2,1)S(1)}, u32[]{:S(2)}, u32[]{:S(2)}) %collective-permute-start) | collective-permute-done | bytes 278560 | tf_op jit(solution)/shard_map/ppermute | solution.py:438
  11.5 0.0 copy-start.4
  11.5 0.7 %copy-done.4 = bf16[1088,128]{1,0:T(8,128)(2,1)} copy-done((bf16[1088,128]{1,0:T(8,128)(2,1)}, bf16[1088,128]{1,0:T(8,128)(2,1)S(1)}, u32[]{:S(2)}) %copy-start.4) | copy-done | bytes 278552
  12.3 9.5 %layer_one.1 = (bf16[512,128]{1,0:T(8,128)(2,1)}, bf16[512,128]{1,0:T(8,128)(2,1)}, bf16[512,128]{1,0:T(8,128)(2,1)}, bf16[512,128]{1,0:T(8,128)(2,1)}) custom-call(s32[1]{0:T(128)} %bitcast.h_ref, bf16[1088,128]{1,0:T(8,128)(2,1)} %get-tuple-element.25.own_ref, bf16[1088,128]{1,0:T(8,128)(2,1)} %copy-done.4, bf16[128,256]{1,0:T(8,128)(2,1)} %get-tuple-element.27.rest_0_, ...), custom_call_target="tpu_custom_call" | custom-call | flops 8000000000 | bytes 1048576 | tf_op jit(solution)/shard_map/layer_one/pallas_call | solution.py:340
  21.8 3.3 %collective-permute-start.1 = (bf16[512,128]{1,0:T(8,128)(2,1)}, bf16[512,128]{1,0:T(8,128)(2,1)S(1)}, u32[]{:S(2)}, u32[]{:S(2)}) collective-permute-start(bf16[512,128]{1,0:T(8,128)(2,1)} %get-tuple-element.32), channel_id=1, source_target_pairs={{0,11},{1,8},{2,9},{3,10},{4,15},{5,12},{6,13},{7,14},{8,19},{9,16... | collective-permute-start | bytes 393224 | tf_op jit(solution)/shard_map/ppermute | solution.py:438
  25.1 1.2 %collective-permute-start.2 = (bf16[512,128]{1,0:T(8,128)(2,1)}, bf16[512,128]{1,0:T(8,128)(2,1)S(1)}, u32[]{:S(2)}, u32[]{:S(2)}) collective-permute-start(bf16[512,128]{1,0:T(8,128)(2,1)} %get-tuple-element.33), channel_id=1, source_target_pairs={{0,8},{1,9},{2,10},{3,11},{4,12},{5,13},{6,14},{7,15},{8,16},{9,17... | collective-permute-start | bytes 393224 | tf_op jit(solution)/shard_map/ppermute | solution.py:438
  26.3 0.3 collective-permute-start.3
  26.5 10.1 %collective-permute-done.1.rest_0_ = bf16[512,128]{1,0:T(8,128)(2,1)S(1)} collective-permute-done((bf16[512,128]{1,0:T(8,128)(2,1)}, bf16[512,128]{1,0:T(8,128)(2,1)S(1)}, u32[]{:S(2)}, u32[]{:S(2)}) %collective-permute-start.1) | collective-permute-done | bytes 131104 | tf_op jit(solution)/shard_map/ppermute | solution.py:438
  36.6 0.0 copy-start.5
  36.6 0.0 collective-permute-done.2.rest_1_
  36.6 0.0 copy-start.6
  36.6 0.0 collective-permute-done.3.rest_2_
  36.6 0.0 copy-start.7
  36.6 0.6 %copy-done.5 = bf16[512,128]{1,0:T(8,128)(2,1)} copy-done((bf16[512,128]{1,0:T(8,128)(2,1)}, bf16[512,128]{1,0:T(8,128)(2,1)S(1)}, u32[]{:S(2)}) %copy-start.5) | copy-done | bytes 131096
  37.2 0.0 copy-done.6
  37.3 0.0 copy-done.7
  37.3 9.1 %layer_two.1 = (bf16[512,128]{1,0:T(8,128)(2,1)}, bf16[512,128]{1,0:T(8,128)(2,1)}, bf16[512,128]{1,0:T(8,128)(2,1)}, bf16[512,128]{1,0:T(8,128)(2,1)}) custom-call(s32[1]{0:T(128)} %bitcast.h_ref, bf16[512,128]{1,0:T(8,128)(2,1)} %copy-done.5, bf16[512,128]{1,0:T(8,128)(2,1)} %copy-done.6, bf16[512,128]{1,0:T(8,128)(2,1)} %copy-done.7, ...), custom_call_target="tpu_custom_call" | custom-call | flops 8000000000 | bytes 1048576 | tf_op jit(solution)/shard_map/layer_two/pallas_call | solution.py:358
  46.5 5.1 %collective-permute-start.4 = (bf16[512,128]{1,0:T(8,128)(2,1)}, bf16[512,128]{1,0:T(8,128)(2,1)S(1)}, u32[]{:S(2)}, u32[]{:S(2)}) collective-permute-start(bf16[512,128]{1,0:T(8,128)(2,1)} %get-tuple-element.41), channel_id=1, source_target_pairs={{0,253},{1,254},{2,255},{3,252},{4,1},{5,2},{6,3},{7,0},{8,5},{9,6... | collective-permute-start | bytes 393224 | tf_op jit(solution)/shard_map/ppermute | solution.py:438
  51.6 0.9 %collective-permute-start.5 = (bf16[512,128]{1,0:T(8,128)(2,1)}, bf16[512,128]{1,0:T(8,128)(2,1)S(1)}, u32[]{:S(2)}, u32[]{:S(2)}) collective-permute-start(bf16[512,128]{1,0:T(8,128)(2,1)} %get-tuple-element.42), channel_id=1, source_target_pairs={{0,1},{1,2},{2,3},{3,0},{4,253},{5,254},{6,255},{7,252},{8,9},{9,1... | collective-permute-start | bytes 393224 | tf_op jit(solution)/shard_map/ppermute | solution.py:438
  52.4 1.5 %collective-permute-start.6 = (bf16[512,128]{1,0:T(8,128)(2,1)}, bf16[512,128]{1,0:T(8,128)(2,1)S(1)}, u32[]{:S(2)}, u32[]{:S(2)}) collective-permute-start(bf16[512,128]{1,0:T(8,128)(2,1)} %get-tuple-element.43), channel_id=1, source_target_pairs={{0,252},{1,253},{2,254},{3,255},{4,0},{5,1},{6,2},{7,3},{8,4},{9,5... | collective-permute-start | bytes 393224 | tf_op jit(solution)/shard_map/ppermute | solution.py:438
  53.9 1.6 %collective-permute-start.7 = (bf16[512,128]{1,0:T(8,128)(2,1)}, bf16[512,128]{1,0:T(8,128)(2,1)S(1)}, u32[]{:S(2)}, u32[]{:S(2)}) collective-permute-start(bf16[512,128]{1,0:T(8,128)(2,1)} %get-tuple-element.44), channel_id=1, source_target_pairs={{0,0},{1,1},{2,2},{3,3},{4,252},{5,253},{6,254},{7,255},{8,8},{9,9... | collective-permute-start | bytes 393224 | tf_op jit(solution)/shard_map/ppermute | solution.py:438
  55.5 0.0 collective-permute-done.4.far_up
  55.5 0.0 copy-start
  55.5 0.0 collective-permute-done.5.near_up
  55.5 0.0 copy-start.1
  55.5 3.3 %collective-permute-done.6.far_lo = bf16[512,128]{1,0:T(8,128)(2,1)S(1)} collective-permute-done((bf16[512,128]{1,0:T(8,128)(2,1)}, bf16[512,128]{1,0:T(8,128)(2,1)S(1)}, u32[]{:S(2)}, u32[]{:S(2)}) %collective-permute-start.6) | collective-permute-done | bytes 131104 | tf_op jit(solution)/shard_map/ppermute | solution.py:438
  58.9 0.0 copy-start.2
  58.9 0.0 collective-permute-done.7.near_lo
  58.9 0.0 copy-done
  58.9 0.0 copy-done.1
  58.9 0.6 %copy-done.2 = bf16[512,128]{1,0:T(8,128)(2,1)} copy-done((bf16[512,128]{1,0:T(8,128)(2,1)}, bf16[512,128]{1,0:T(8,128)(2,1)S(1)}, u32[]{:S(2)}) %copy-start.2) | copy-done | bytes 131096
  59.5 0.0 copy-start.3
  59.5 0.7 %copy-done.3 = bf16[512,128]{1,0:T(8,128)(2,1)} copy-done((bf16[512,128]{1,0:T(8,128)(2,1)}, bf16[512,128]{1,0:T(8,128)(2,1)S(1)}, u32[]{:S(2)}) %copy-start.3) | copy-done | bytes 131096
  60.2 2.3 %from_tokens.1 = bf16[120,8,256]{2,1,0:T(8,128)(2,1)} custom-call(s32[1]{0:T(128)} %bitcast.h_ref, bf16[512,128]{1,0:T(8,128)(2,1)} %copy-done, bf16[512,128]{1,0:T(8,128)(2,1)} %copy-done.1, bf16[512,128]{1,0:T(8,128)(2,1)} %copy-done.2, bf16[512,128]{1,0:T(8,128)(2,1)} %copy-done.3), custom_call_target="tpu_custom_call" | custom-call | tf_op jit(solution)/shard_map/from_tokens/pallas_call | solution.py:371
Async XLA Ops:
  2.1 9.5 %collective-permute-start = (bf16[1088,128]{1,0:T(8,128)(2,1)}, bf16[1088,128]{1,0:T(8,128)(2,1)S(1)}, u32[]{:S(2)}, u32[]{:S(2)}) collective-permute-start(bf16[1088,128]{1,0:T(8,128)(2,1)} %get-tuple-element.26), channel_id=1, source_target_pairs={{0,4},{1,5},{2,6},{3,7},{4,0},{5,1},{6,2},{7,3},{8,12},{9,13},{10,... | collective-permute-start | bytes 835592 | tf_op jit(solution)/shard_map/ppermute | solution.py:438
  11.5 0.7 %copy-start.4 = (bf16[1088,128]{1,0:T(8,128)(2,1)}, bf16[1088,128]{1,0:T(8,128)(2,1)S(1)}, u32[]{:S(2)}) copy-start(bf16[1088,128]{1,0:T(8,128)(2,1)S(1)} %collective-permute-done.oth_ref) | copy-start | bytes 835588
  21.8 14.8 %collective-permute-start.1 = (bf16[512,128]{1,0:T(8,128)(2,1)}, bf16[512,128]{1,0:T(8,128)(2,1)S(1)}, u32[]{:S(2)}, u32[]{:S(2)}) collective-permute-start(bf16[512,128]{1,0:T(8,128)(2,1)} %get-tuple-element.32), channel_id=1, source_target_pairs={{0,11},{1,8},{2,9},{3,10},{4,15},{5,12},{6,13},{7,14},{8,19},{9,16... | collective-permute-start | bytes 393224 | tf_op jit(solution)/shard_map/ppermute | solution.py:438
  25.1 11.5 %collective-permute-start.2 = (bf16[512,128]{1,0:T(8,128)(2,1)}, bf16[512,128]{1,0:T(8,128)(2,1)S(1)}, u32[]{:S(2)}, u32[]{:S(2)}) collective-permute-start(bf16[512,128]{1,0:T(8,128)(2,1)} %get-tuple-element.33), channel_id=1, source_target_pairs={{0,8},{1,9},{2,10},{3,11},{4,12},{5,13},{6,14},{7,15},{8,16},{9,17... | collective-permute-start | bytes 393224 | tf_op jit(solution)/shard_map/ppermute | solution.py:438
  26.3 10.3 %collective-permute-start.3 = (bf16[512,128]{1,0:T(8,128)(2,1)}, bf16[512,128]{1,0:T(8,128)(2,1)S(1)}, u32[]{:S(2)}, u32[]{:S(2)}) collective-permute-start(bf16[512,128]{1,0:T(8,128)(2,1)} %get-tuple-element.34), channel_id=1, source_target_pairs={{0,3},{1,0},{2,1},{3,2},{4,7},{5,4},{6,5},{7,6},{8,11},{9,8},{10,9... | collective-permute-start | bytes 393224 | tf_op jit(solution)/shard_map/ppermute | solution.py:438
  36.6 0.7 %copy-start.5 = (bf16[512,128]{1,0:T(8,128)(2,1)}, bf16[512,128]{1,0:T(8,128)(2,1)S(1)}, u32[]{:S(2)}) copy-start(bf16[512,128]{1,0:T(8,128)(2,1)S(1)} %collective-permute-done.1.rest_0_) | copy-start | bytes 393220
  36.6 0.7 %copy-start.6 = (bf16[512,128]{1,0:T(8,128)(2,1)}, bf16[512,128]{1,0:T(8,128)(2,1)S(1)}, u32[]{:S(2)}) copy-start(bf16[512,128]{1,0:T(8,128)(2,1)S(1)} %collective-permute-done.2.rest_1_) | copy-start | bytes 393220
  36.6 0.7 %copy-start.7 = (bf16[512,128]{1,0:T(8,128)(2,1)}, bf16[512,128]{1,0:T(8,128)(2,1)S(1)}, u32[]{:S(2)}) copy-start(bf16[512,128]{1,0:T(8,128)(2,1)S(1)} %collective-permute-done.3.rest_2_) | copy-start | bytes 393220
  46.5 9.0 %collective-permute-start.4 = (bf16[512,128]{1,0:T(8,128)(2,1)}, bf16[512,128]{1,0:T(8,128)(2,1)S(1)}, u32[]{:S(2)}, u32[]{:S(2)}) collective-permute-start(bf16[512,128]{1,0:T(8,128)(2,1)} %get-tuple-element.41), channel_id=1, source_target_pairs={{0,253},{1,254},{2,255},{3,252},{4,1},{5,2},{6,3},{7,0},{8,5},{9,6... | collective-permute-start | bytes 393224 | tf_op jit(solution)/shard_map/ppermute | solution.py:438
  51.6 3.9 %collective-permute-start.5 = (bf16[512,128]{1,0:T(8,128)(2,1)}, bf16[512,128]{1,0:T(8,128)(2,1)S(1)}, u32[]{:S(2)}, u32[]{:S(2)}) collective-permute-start(bf16[512,128]{1,0:T(8,128)(2,1)} %get-tuple-element.42), channel_id=1, source_target_pairs={{0,1},{1,2},{2,3},{3,0},{4,253},{5,254},{6,255},{7,252},{8,9},{9,1... | collective-permute-start | bytes 393224 | tf_op jit(solution)/shard_map/ppermute | solution.py:438
  52.4 6.4 %collective-permute-start.6 = (bf16[512,128]{1,0:T(8,128)(2,1)}, bf16[512,128]{1,0:T(8,128)(2,1)S(1)}, u32[]{:S(2)}, u32[]{:S(2)}) collective-permute-start(bf16[512,128]{1,0:T(8,128)(2,1)} %get-tuple-element.43), channel_id=1, source_target_pairs={{0,252},{1,253},{2,254},{3,255},{4,0},{5,1},{6,2},{7,3},{8,4},{9,5... | collective-permute-start | bytes 393224 | tf_op jit(solution)/shard_map/ppermute | solution.py:438
  53.9 4.9 %collective-permute-start.7 = (bf16[512,128]{1,0:T(8,128)(2,1)}, bf16[512,128]{1,0:T(8,128)(2,1)S(1)}, u32[]{:S(2)}, u32[]{:S(2)}) collective-permute-start(bf16[512,128]{1,0:T(8,128)(2,1)} %get-tuple-element.44), channel_id=1, source_target_pairs={{0,0},{1,1},{2,2},{3,3},{4,252},{5,253},{6,254},{7,255},{8,8},{9,9... | collective-permute-start | bytes 393224 | tf_op jit(solution)/shard_map/ppermute | solution.py:438
  55.5 3.4 %copy-start = (bf16[512,128]{1,0:T(8,128)(2,1)}, bf16[512,128]{1,0:T(8,128)(2,1)S(1)}, u32[]{:S(2)}) copy-start(bf16[512,128]{1,0:T(8,128)(2,1)S(1)} %collective-permute-done.4.far_up) | copy-start | bytes 393220
  55.5 3.4 %copy-start.1 = (bf16[512,128]{1,0:T(8,128)(2,1)}, bf16[512,128]{1,0:T(8,128)(2,1)S(1)}, u32[]{:S(2)}) copy-start(bf16[512,128]{1,0:T(8,128)(2,1)S(1)} %collective-permute-done.5.near_up) | copy-start | bytes 393220
  58.9 0.6 %copy-start.2 = (bf16[512,128]{1,0:T(8,128)(2,1)}, bf16[512,128]{1,0:T(8,128)(2,1)S(1)}, u32[]{:S(2)}) copy-start(bf16[512,128]{1,0:T(8,128)(2,1)S(1)} %collective-permute-done.6.far_lo) | copy-start | bytes 393220
  59.5 0.7 %copy-start.3 = (bf16[512,128]{1,0:T(8,128)(2,1)}, bf16[512,128]{1,0:T(8,128)(2,1)S(1)}, u32[]{:S(2)}) copy-start(bf16[512,128]{1,0:T(8,128)(2,1)S(1)} %collective-permute-done.7.near_lo) | copy-start | bytes 393220

commit v11 on v10

--- a/solution.py
+++ b/solution.py
@@ -310,7 +310,11 @@
 
 
 def tokens_shape(rows):
-    return jax.ShapeDtypeStruct((rows, LANES), jnp.bfloat16)
+    return pltpu.VMEM((rows, LANES), jnp.bfloat16)
+
+
+def in_vmem(*arrays):
+    return [pltpu.with_memory_space_constraint(array, pltpu.VMEM) for array in arrays]
 
 
 def to_tokens(h, x):
@@ -336,7 +340,7 @@
     width = SHIFTED[chunk][1] - SHIFTED[chunk][0]
     edge = [] if last else [jax.ShapeDtypeStruct((2, WIN, WIN, LANES), jnp.float32)]
     shapes = [tokens_shape(width * TOK // 2)] * 4 + edge
-    args = (h, own, oth, *before, *weights)
+    args = (h, *in_vmem(own, oth, *before, *weights))
     return pl.pallas_call(
         functools.partial(layer_one_kernel, count, first, last),
         out_shape=shapes,
@@ -364,7 +368,7 @@
         compiler_params=PARAMS,
         cost_estimate=COST,
         name="layer_two",
-    )(h, *pieces, *weights)
+    )(h, *in_vmem(*pieces, *weights))
 
 
 def from_tokens(h, pieces):
@@ -381,7 +385,7 @@
         ],
         compiler_params=PARAMS,
         name="from_tokens",
-    )(h, *pieces)
+    )(h, *in_vmem(*pieces))
 
 
 def prepare_kernel(w_mut, w_slf, w_prj, w_gte, w_upp, w_dwn, *outs):
@@ -418,7 +422,7 @@
     ] * 2
     return pl.pallas_call(
         prepare_kernel,
-        out_shape=[jax.ShapeDtypeStruct(shape, jnp.bfloat16) for shape in shapes],
+        out_shape=[pltpu.VMEM(shape, jnp.bfloat16) for shape in shapes],
         in_specs=[VMEM] * len(weights),
         out_specs=[VMEM] * len(shapes),
         compiler_params=PARAMS,

time: 63 us -> 54.7 us (0.87)
  Pallas kernels: 25.6 us -> 19.2 us
  local copies, waits for them, and re-layouts: 2.71 us -> 0 us
  waiting for transfers between devices: 16.4 us -> 17.3 us
  starting transfers between devices: 17.7 us -> 17 us
    unnamed x16 -> x0, local copies, waits for them, and re-layouts: 2.71 us -> none
    pallas_call x1, Pallas kernels: 9.14 us -> 7.18 us  [layer_two(): pl.pallas_call(functools.partial(layer_two_kernel, count), out_shape=[tok...]
    pallas_call x1, Pallas kernels: 9.5 us -> 7.57 us  [layer_one(): pl.pallas_call(functools.partial(layer_one_kernel, count, first, last), o...]
    pallas_call x1, Pallas kernels: 2.26 us -> 1.17 us  [from_tokens(): pl.pallas_call(from_tokens_kernel, out_shape=jax.ShapeDtypeStruct((C, WIN...]
    ppermute x8, waiting for transfers between devices: 16.4 us -> 17.3 us  [send(): return lax.ppermute(value, ('frame', 'strip'), pairs)]
    pallas_call x1, Pallas kernels: 2.07 us -> 1.32 us  [to_tokens(): pl.pallas_call(to_tokens_kernel, out_shape=[tokens_shape((HALF + 1) * TOK...]
    pallas_call x1, Pallas kernels: 2.66 us -> 1.93 us  [prepared(): pl.pallas_call(prepare_kernel, out_shape=[pltpu.VMEM(shape, jnp.bfloat16)...]
where the time goes in v11:
time: 54.7 us; the launch traced here: 53.7 us
  Pallas kernels  19.2 us (35%)
  waiting for transfers between devices  17.3 us (32%)
  starting transfers between devices  17 us (31%)
    ppermute x8, waiting for transfers between devices, send(): return lax.ppermute(value, ('frame', 'strip'), pairs)  17.3 us
    ppermute x8, starting transfers between devices, send(): return lax.ppermute(value, ('frame', 'strip'), pairs)  17 us
    pallas_call x1, Pallas kernels, layer_one(): pl.pallas_call(functools.partial(layer_one_kernel, count, first, last), o...  7.57 us
    pallas_call x1, Pallas kernels, layer_two(): pl.pallas_call(functools.partial(layer_two_kernel, count), out_shape=[tok...  7.18 us
    pallas_call x1, Pallas kernels, prepared(): pl.pallas_call(prepare_kernel, out_shape=[pltpu.VMEM(shape, jnp.bfloat16)...  1.93 us
    pallas_call x1, Pallas kernels, to_tokens(): pl.pallas_call(to_tokens_kernel, out_shape=[tokens_shape((HALF + 1) * TOK...  1.32 us
    pallas_call x1, Pallas kernels, from_tokens(): pl.pallas_call(from_tokens_kernel, out_shape=jax.ShapeDtypeStruct((C, WIN...  1.17 us
  transfers between devices with their start and end apart: 8, of which 3 were waited for; matrix products, arithmetic and copies ran while one was open for 0% of the time, Pallas kernels for 4%

profile of v11, /device:TPU:1, one launch (start us, length us, event | category | flops | bytes accessed | tf_op | source)
XLA Modules:
  0.0 53.7 jit_solution(11043635858920327883)
XLA Ops:
  0.0 1.3 %to_tokens.1 = (bf16[1088,128]{1,0:T(8,128)(2,1)S(1)}, bf16[1088,128]{1,0:T(8,128)(2,1)S(1)}) custom-call(s32[1]{0:T(128)} %bitcast.h_ref, bf16[120,8,256]{2,1,0:T(8,128)(2,1)} %bitcast.3), custom_call_target="tpu_custom_call" | custom-call | tf_op jit(solution)/shard_map/to_tokens/pallas_call | solution.py:321
  1.3 3.8 %collective-permute-start = (bf16[1088,128]{1,0:T(8,128)(2,1)S(1)}, bf16[1088,128]{1,0:T(8,128)(2,1)S(1)}, u32[]{:S(2)}, u32[]{:S(2)}) collective-permute-start(bf16[1088,128]{1,0:T(8,128)(2,1)S(1)} %get-tuple-element.26), channel_id=1, source_target_pairs={{0,4},{1,5},{2,6},{3,7},{4,0},{5,1},{6,2},{7,3},{8,12},{9,13},{10,... | collective-permute-start | bytes 835592 | tf_op jit(solution)/shard_map/ppermute | solution.py:442
  5.2 1.9 %prepare.1 = (bf16[128,256]{1,0:T(8,128)(2,1)S(1)}, bf16[512,128]{1,0:T(8,128)(2,1)S(1)}, bf16[240,128]{1,0:T(8,128)(2,1)S(1)}, bf16[128,512]{1,0:T(8,128)(2,1)S...) custom-call(bf16[2,120,360]{2,1,0:T(8,128)(2,1)} %w_mut.1, ...), custom_call_target="tpu_custom_call" | custom-call | tf_op jit(solution)/shard_map/prepare/pallas_call | solution.py:423
  7.1 3.4 %collective-permute-done.oth_ref = bf16[1088,128]{1,0:T(8,128)(2,1)S(1)} collective-permute-done((bf16[1088,128]{1,0:T(8,128)(2,1)S(1)}, bf16[1088,128]{1,0:T(8,128)(2,1)S(1)}, u32[]{:S(2)}, u32[]{:S(2)}) %collective-permute-start) | collective-permute-done | bytes 278560 | tf_op jit(solution)/shard_map/ppermute | solution.py:442
  10.5 7.6 %layer_one.1 = (bf16[512,128]{1,0:T(8,128)(2,1)S(1)}, bf16[512,128]{1,0:T(8,128)(2,1)S(1)}, bf16[512,128]{1,0:T(8,128)(2,1)S(1)}, bf16[512,128]{1,0:T(8,128)(2,1)S(1)}) custom-call(s32[1]{0:T(128)} %bitcast.h_ref, bf16[1088,128]{1,0:T(8,128)(2,1)S(1)} %get-tuple-element.25.own_ref, bf16[1088,128]{1,0:T(8,128)(2,1)S(1)} %collective-permute-done.oth_ref, ...), custom_call_target="tpu_custom_call" | custom-call | flops 8000000000 | bytes 1048576 | tf_op jit(solution)/shard_map/layer_one/pallas_call | solution.py:344
  18.1 3.5 %collective-permute-start.1 = (bf16[512,128]{1,0:T(8,128)(2,1)S(1)}, bf16[512,128]{1,0:T(8,128)(2,1)S(1)}, u32[]{:S(2)}, u32[]{:S(2)}) collective-permute-start(bf16[512,128]{1,0:T(8,128)(2,1)S(1)} %get-tuple-element.32), channel_id=1, source_target_pairs={{0,11},{1,8},{2,9},{3,10},{4,15},{5,12},{6,13},{7,14},{8,19},{9,16... | collective-permute-start | bytes 393224 | tf_op jit(solution)/shard_map/ppermute | solution.py:442
  21.6 1.2 %collective-permute-start.2 = (bf16[512,128]{1,0:T(8,128)(2,1)S(1)}, bf16[512,128]{1,0:T(8,128)(2,1)S(1)}, u32[]{:S(2)}, u32[]{:S(2)}) collective-permute-start(bf16[512,128]{1,0:T(8,128)(2,1)S(1)} %get-tuple-element.33), channel_id=1, source_target_pairs={{0,8},{1,9},{2,10},{3,11},{4,12},{5,13},{6,14},{7,15},{8,16},{9,17... | collective-permute-start | bytes 393224 | tf_op jit(solution)/shard_map/ppermute | solution.py:442
  22.8 0.3 collective-permute-start.3
  23.0 9.8 %collective-permute-done.1.rest_0_ = bf16[512,128]{1,0:T(8,128)(2,1)S(1)} collective-permute-done((bf16[512,128]{1,0:T(8,128)(2,1)S(1)}, bf16[512,128]{1,0:T(8,128)(2,1)S(1)}, u32[]{:S(2)}, u32[]{:S(2)}) %collective-permute-start.1) | collective-permute-done | bytes 131104 | tf_op jit(solution)/shard_map/ppermute | solution.py:442
  32.9 0.0 collective-permute-done.2.rest_1_
  32.9 0.0 collective-permute-done.3.rest_2_
  32.9 7.2 %layer_two.1 = (bf16[512,128]{1,0:T(8,128)(2,1)S(1)}, bf16[512,128]{1,0:T(8,128)(2,1)S(1)}, bf16[512,128]{1,0:T(8,128)(2,1)S(1)}, bf16[512,128]{1,0:T(8,128)(2,1)S(1)}) custom-call(s32[1]{0:T(128)} %bitcast.h_ref, bf16[512,128]{1,0:T(8,128)(2,1)S(1)} %collective-permute-done.1.rest_0_, bf16[512,128]{1,0:T(8,128)(2,1)S(1)} %collective-permute-done.2.rest_1_, ...), custom_call_target="tpu_custom_call" | custom-call | flops 8000000000 | bytes 1048576 | tf_op jit(solution)/shard_map/layer_two/pallas_call | solution.py:362
  40.1 5.2 %collective-permute-start.4 = (bf16[512,128]{1,0:T(8,128)(2,1)S(1)}, bf16[512,128]{1,0:T(8,128)(2,1)S(1)}, u32[]{:S(2)}, u32[]{:S(2)}) collective-permute-start(bf16[512,128]{1,0:T(8,128)(2,1)S(1)} %get-tuple-element.41), channel_id=1, source_target_pairs={{0,253},{1,254},{2,255},{3,252},{4,1},{5,2},{6,3},{7,0},{8,5},{9,6... | collective-permute-start | bytes 393224 | tf_op jit(solution)/shard_map/ppermute | solution.py:442
  45.3 0.8 %collective-permute-start.5 = (bf16[512,128]{1,0:T(8,128)(2,1)S(1)}, bf16[512,128]{1,0:T(8,128)(2,1)S(1)}, u32[]{:S(2)}, u32[]{:S(2)}) collective-permute-start(bf16[512,128]{1,0:T(8,128)(2,1)S(1)} %get-tuple-element.42), channel_id=1, source_target_pairs={{0,1},{1,2},{2,3},{3,0},{4,253},{5,254},{6,255},{7,252},{8,9},{9,1... | collective-permute-start | bytes 393224 | tf_op jit(solution)/shard_map/ppermute | solution.py:442
  46.1 1.5 %collective-permute-start.6 = (bf16[512,128]{1,0:T(8,128)(2,1)S(1)}, bf16[512,128]{1,0:T(8,128)(2,1)S(1)}, u32[]{:S(2)}, u32[]{:S(2)}) collective-permute-start(bf16[512,128]{1,0:T(8,128)(2,1)S(1)} %get-tuple-element.43), channel_id=1, source_target_pairs={{0,252},{1,253},{2,254},{3,255},{4,0},{5,1},{6,2},{7,3},{8,4},{9,5... | collective-permute-start | bytes 393224 | tf_op jit(solution)/shard_map/ppermute | solution.py:442
  47.7 0.7 %collective-permute-start.7 = (bf16[512,128]{1,0:T(8,128)(2,1)S(1)}, bf16[512,128]{1,0:T(8,128)(2,1)S(1)}, u32[]{:S(2)}, u32[]{:S(2)}) collective-permute-start(bf16[512,128]{1,0:T(8,128)(2,1)S(1)} %get-tuple-element.44), channel_id=1, source_target_pairs={{0,0},{1,1},{2,2},{3,3},{4,252},{5,253},{6,254},{7,255},{8,8},{9,9... | collective-permute-start | bytes 393224 | tf_op jit(solution)/shard_map/ppermute | solution.py:442
  48.3 0.0 collective-permute-done.4.far_up
  48.3 0.0 collective-permute-done.5.near_up
  48.3 4.0 %collective-permute-done.6.far_lo = bf16[512,128]{1,0:T(8,128)(2,1)S(1)} collective-permute-done((bf16[512,128]{1,0:T(8,128)(2,1)S(1)}, bf16[512,128]{1,0:T(8,128)(2,1)S(1)}, u32[]{:S(2)}, u32[]{:S(2)}) %collective-permute-start.6) | collective-permute-done | bytes 131104 | tf_op jit(solution)/shard_map/ppermute | solution.py:442
  52.4 0.0 collective-permute-done.7.near_lo
  52.4 1.2 %from_tokens.1 = bf16[120,8,256]{2,1,0:T(8,128)(2,1)} custom-call(s32[1]{0:T(128)} %bitcast.h_ref, bf16[512,128]{1,0:T(8,128)(2,1)S(1)} %collective-permute-done.4.far_up, bf16[512,128]{1,0:T(8,128)(2,1)S(1)} %collective-permute-done.5.near_up, bf16[512,128]{1,0:T(8,128)(2,1)S(1)} %collective-permute-done.6.far_lo, ...), custom_call_target="tpu_custom_call" | custom-call | tf_op jit(solution)/shard_map/from_tokens/pallas_call | solution.py:375
Async XLA Ops:
  1.3 9.2 %collective-permute-start = (bf16[1088,128]{1,0:T(8,128)(2,1)S(1)}, bf16[1088,128]{1,0:T(8,128)(2,1)S(1)}, u32[]{:S(2)}, u32[]{:S(2)}) collective-permute-start(bf16[1088,128]{1,0:T(8,128)(2,1)S(1)} %get-tuple-element.26), channel_id=1, source_target_pairs={{0,4},{1,5},{2,6},{3,7},{4,0},{5,1},{6,2},{7,3},{8,12},{9,13},{10,... | collective-permute-start | bytes 835592 | tf_op jit(solution)/shard_map/ppermute | solution.py:442
  18.1 14.8 %collective-permute-start.1 = (bf16[512,128]{1,0:T(8,128)(2,1)S(1)}, bf16[512,128]{1,0:T(8,128)(2,1)S(1)}, u32[]{:S(2)}, u32[]{:S(2)}) collective-permute-start(bf16[512,128]{1,0:T(8,128)(2,1)S(1)} %get-tuple-element.32), channel_id=1, source_target_pairs={{0,11},{1,8},{2,9},{3,10},{4,15},{5,12},{6,13},{7,14},{8,19},{9,16... | collective-permute-start | bytes 393224 | tf_op jit(solution)/shard_map/ppermute | solution.py:442
  21.6 11.3 %collective-permute-start.2 = (bf16[512,128]{1,0:T(8,128)(2,1)S(1)}, bf16[512,128]{1,0:T(8,128)(2,1)S(1)}, u32[]{:S(2)}, u32[]{:S(2)}) collective-permute-start(bf16[512,128]{1,0:T(8,128)(2,1)S(1)} %get-tuple-element.33), channel_id=1, source_target_pairs={{0,8},{1,9},{2,10},{3,11},{4,12},{5,13},{6,14},{7,15},{8,16},{9,17... | collective-permute-start | bytes 393224 | tf_op jit(solution)/shard_map/ppermute | solution.py:442
  22.8 10.1 %collective-permute-start.3 = (bf16[512,128]{1,0:T(8,128)(2,1)S(1)}, bf16[512,128]{1,0:T(8,128)(2,1)S(1)}, u32[]{:S(2)}, u32[]{:S(2)}) collective-permute-start(bf16[512,128]{1,0:T(8,128)(2,1)S(1)} %get-tuple-element.34), channel_id=1, source_target_pairs={{0,3},{1,0},{2,1},{3,2},{4,7},{5,4},{6,5},{7,6},{8,11},{9,8},{10,9... | collective-permute-start | bytes 393224 | tf_op jit(solution)/shard_map/ppermute | solution.py:442
  40.1 8.3 %collective-permute-start.4 = (bf16[512,128]{1,0:T(8,128)(2,1)S(1)}, bf16[512,128]{1,0:T(8,128)(2,1)S(1)}, u32[]{:S(2)}, u32[]{:S(2)}) collective-permute-start(bf16[512,128]{1,0:T(8,128)(2,1)S(1)} %get-tuple-element.41), channel_id=1, source_target_pairs={{0,253},{1,254},{2,255},{3,252},{4,1},{5,2},{6,3},{7,0},{8,5},{9,6... | collective-permute-start | bytes 393224 | tf_op jit(solution)/shard_map/ppermute | solution.py:442
  45.3 3.1 %collective-permute-start.5 = (bf16[512,128]{1,0:T(8,128)(2,1)S(1)}, bf16[512,128]{1,0:T(8,128)(2,1)S(1)}, u32[]{:S(2)}, u32[]{:S(2)}) collective-permute-start(bf16[512,128]{1,0:T(8,128)(2,1)S(1)} %get-tuple-element.42), channel_id=1, source_target_pairs={{0,1},{1,2},{2,3},{3,0},{4,253},{5,254},{6,255},{7,252},{8,9},{9,1... | collective-permute-start | bytes 393224 | tf_op jit(solution)/shard_map/ppermute | solution.py:442
  46.1 6.2 %collective-permute-start.6 = (bf16[512,128]{1,0:T(8,128)(2,1)S(1)}, bf16[512,128]{1,0:T(8,128)(2,1)S(1)}, u32[]{:S(2)}, u32[]{:S(2)}) collective-permute-start(bf16[512,128]{1,0:T(8,128)(2,1)S(1)} %get-tuple-element.43), channel_id=1, source_target_pairs={{0,252},{1,253},{2,254},{3,255},{4,0},{5,1},{6,2},{7,3},{8,4},{9,5... | collective-permute-start | bytes 393224 | tf_op jit(solution)/shard_map/ppermute | solution.py:442
  47.7 4.7 %collective-permute-start.7 = (bf16[512,128]{1,0:T(8,128)(2,1)S(1)}, bf16[512,128]{1,0:T(8,128)(2,1)S(1)}, u32[]{:S(2)}, u32[]{:S(2)}) collective-permute-start(bf16[512,128]{1,0:T(8,128)(2,1)S(1)} %get-tuple-element.44), channel_id=1, source_target_pairs={{0,0},{1,1},{2,2},{3,3},{4,252},{5,253},{6,254},{7,255},{8,8},{9,9... | collective-permute-start | bytes 393224 | tf_op jit(solution)/shard_map/ppermute | solution.py:442

commit v12 on v11

--- a/solution.py
+++ b/solution.py
@@ -255,11 +255,11 @@
             pair = (jnp.where(even, moved, kept), jnp.where(even, kept, moved))
             for f in range(2):
                 part = pair[f].astype(jnp.bfloat16)
-                for j, out in enumerate((outs[f], outs[2 + f])):
+                for j, out in enumerate((outs[2 * f], outs[2 * f + 1])):
                     out[spans[i]] = part[j * half_tok : (j + 1) * half_tok]
 
 
-def from_tokens_kernel(h_ref, far_up, near_up, far_lo, near_lo, out_ref, rows, wide, ready, sems):
+def from_tokens_kernel(h_ref, far_up, far_lo, near_up, near_lo, out_ref, rows, wide, ready, sems):
     edge = WIN // 2
 
     def place(h):
@@ -459,12 +459,12 @@
         pieces.append((moved_up, moved_lo, kept_up, kept_lo))
     home = []
     for k in chunks:
-        far_up, near_up, far_lo, near_lo = layer_two(k, h, pieces[k], w_two)
+        far_up, far_lo, near_up, near_lo = layer_two(k, h, pieces[k], w_two)
         far_up = send(far_up, -1, -1, 1)
+        far_lo = send(far_lo, -1, -1, 0)
         near_up = send(near_up, 0, -2, 1)
-        far_lo = send(far_lo, -1, -1, 0)
         near_lo = send(near_lo, 0, -2, 0)
-        home += [far_up, near_up, far_lo, near_lo]
+        home += [far_up, far_lo, near_up, near_lo]
     return from_tokens(h, home)[None]
 
 

time: 54.7 us -> 55.3 us (1.011)
  the two profiles are of different devices: /device:TPU:1 before, /device:TPU:17 now
where the time goes in v12:
time: 55.3 us; the launch traced here: 55.1 us
  waiting for transfers between devices  22.1 us (40%)
  Pallas kernels  19.2 us (35%)
  starting transfers between devices  13.7 us (25%)
    ppermute x8, waiting for transfers between devices, send(): return lax.ppermute(value, ('frame', 'strip'), pairs)  22.1 us
    ppermute x8, starting transfers between devices, send(): return lax.ppermute(value, ('frame', 'strip'), pairs)  13.7 us
    pallas_call x1, Pallas kernels, layer_one(): pl.pallas_call(functools.partial(layer_one_kernel, count, first, last), o...  7.56 us
    pallas_call x1, Pallas kernels, layer_two(): pl.pallas_call(functools.partial(layer_two_kernel, count), out_shape=[tok...  7.18 us
    pallas_call x1, Pallas kernels, prepared(): pl.pallas_call(prepare_kernel, out_shape=[pltpu.VMEM(shape, jnp.bfloat16)...  1.94 us
    pallas_call x1, Pallas kernels, to_tokens(): pl.pallas_call(to_tokens_kernel, out_shape=[tokens_shape((HALF + 1) * TOK...  1.32 us
    pallas_call x1, Pallas kernels, from_tokens(): pl.pallas_call(from_tokens_kernel, out_shape=jax.ShapeDtypeStruct((C, WIN...  1.16 us
  transfers between devices with their start and end apart: 8, of which 4 were waited for; matrix products, arithmetic and copies ran while one was open for 0% of the time, Pallas kernels for 4%

profile of v12, /device:TPU:17, one launch (start us, length us, event | category | flops | bytes accessed | tf_op | source)
XLA Modules:
  0.0 55.1 jit_solution(17829549796279649954)
XLA Ops:
  0.0 1.3 %to_tokens.1 = (bf16[1088,128]{1,0:T(8,128)(2,1)S(1)}, bf16[1088,128]{1,0:T(8,128)(2,1)S(1)}) custom-call(s32[1]{0:T(128)} %bitcast.h_ref, bf16[120,8,256]{2,1,0:T(8,128)(2,1)} %bitcast.3), custom_call_target="tpu_custom_call" | custom-call | tf_op jit(solution)/shard_map/to_tokens/pallas_call | solution.py:321
  1.3 0.1 collective-permute-start
  1.4 1.9 %prepare.1 = (bf16[128,256]{1,0:T(8,128)(2,1)S(1)}, bf16[512,128]{1,0:T(8,128)(2,1)S(1)}, bf16[240,128]{1,0:T(8,128)(2,1)S(1)}, bf16[128,512]{1,0:T(8,128)(2,1)S...) custom-call(bf16[2,120,360]{2,1,0:T(8,128)(2,1)} %w_mut.1, ...), custom_call_target="tpu_custom_call" | custom-call | tf_op jit(solution)/shard_map/prepare/pallas_call | solution.py:423
  3.4 7.1 %collective-permute-done.oth_ref = bf16[1088,128]{1,0:T(8,128)(2,1)S(1)} collective-permute-done((bf16[1088,128]{1,0:T(8,128)(2,1)S(1)}, bf16[1088,128]{1,0:T(8,128)(2,1)S(1)}, u32[]{:S(2)}, u32[]{:S(2)}) %collective-permute-start) | collective-permute-done | bytes 278560 | tf_op jit(solution)/shard_map/ppermute | solution.py:442
  10.4 7.6 %layer_one.1 = (bf16[512,128]{1,0:T(8,128)(2,1)S(1)}, bf16[512,128]{1,0:T(8,128)(2,1)S(1)}, bf16[512,128]{1,0:T(8,128)(2,1)S(1)}, bf16[512,128]{1,0:T(8,128)(2,1)S(1)}) custom-call(s32[1]{0:T(128)} %bitcast.h_ref, bf16[1088,128]{1,0:T(8,128)(2,1)S(1)} %get-tuple-element.25.own_ref, bf16[1088,128]{1,0:T(8,128)(2,1)S(1)} %collective-permute-done.oth_ref, ...), custom_call_target="tpu_custom_call" | custom-call | flops 8000000000 | bytes 1048576 | tf_op jit(solution)/shard_map/layer_one/pallas_call | solution.py:344
  18.0 2.7 %collective-permute-start.1 = (bf16[512,128]{1,0:T(8,128)(2,1)S(1)}, bf16[512,128]{1,0:T(8,128)(2,1)S(1)}, u32[]{:S(2)}, u32[]{:S(2)}) collective-permute-start(bf16[512,128]{1,0:T(8,128)(2,1)S(1)} %get-tuple-element.32), channel_id=1, source_target_pairs={{0,11},{1,8},{2,9},{3,10},{4,15},{5,12},{6,13},{7,14},{8,19},{9,16... | collective-permute-start | bytes 393224 | tf_op jit(solution)/shard_map/ppermute | solution.py:442
  20.7 1.2 %collective-permute-start.2 = (bf16[512,128]{1,0:T(8,128)(2,1)S(1)}, bf16[512,128]{1,0:T(8,128)(2,1)S(1)}, u32[]{:S(2)}, u32[]{:S(2)}) collective-permute-start(bf16[512,128]{1,0:T(8,128)(2,1)S(1)} %get-tuple-element.33), channel_id=1, source_target_pairs={{0,8},{1,9},{2,10},{3,11},{4,12},{5,13},{6,14},{7,15},{8,16},{9,17... | collective-permute-start | bytes 393224 | tf_op jit(solution)/shard_map/ppermute | solution.py:442
  21.9 0.0 collective-permute-start.3
  22.0 9.8 %collective-permute-done.1.rest_0_ = bf16[512,128]{1,0:T(8,128)(2,1)S(1)} collective-permute-done((bf16[512,128]{1,0:T(8,128)(2,1)S(1)}, bf16[512,128]{1,0:T(8,128)(2,1)S(1)}, u32[]{:S(2)}, u32[]{:S(2)}) %collective-permute-start.1) | collective-permute-done | bytes 131104 | tf_op jit(solution)/shard_map/ppermute | solution.py:442
  31.8 0.0 collective-permute-done.2.rest_1_
  31.8 0.0 collective-permute-done.3.rest_2_
  31.8 7.2 %layer_two.1 = (bf16[512,128]{1,0:T(8,128)(2,1)S(1)}, bf16[512,128]{1,0:T(8,128)(2,1)S(1)}, bf16[512,128]{1,0:T(8,128)(2,1)S(1)}, bf16[512,128]{1,0:T(8,128)(2,1)S(1)}) custom-call(s32[1]{0:T(128)} %bitcast.h_ref, bf16[512,128]{1,0:T(8,128)(2,1)S(1)} %collective-permute-done.1.rest_0_, bf16[512,128]{1,0:T(8,128)(2,1)S(1)} %collective-permute-done.2.rest_1_, ...), custom_call_target="tpu_custom_call" | custom-call | flops 8000000000 | bytes 1048576 | tf_op jit(solution)/shard_map/layer_two/pallas_call | solution.py:362
  38.9 1.5 %collective-permute-start.4 = (bf16[512,128]{1,0:T(8,128)(2,1)S(1)}, bf16[512,128]{1,0:T(8,128)(2,1)S(1)}, u32[]{:S(2)}, u32[]{:S(2)}) collective-permute-start(bf16[512,128]{1,0:T(8,128)(2,1)S(1)} %get-tuple-element.41), channel_id=1, source_target_pairs={{0,253},{1,254},{2,255},{3,252},{4,1},{5,2},{6,3},{7,0},{8,5},{9,6... | collective-permute-start | bytes 393224 | tf_op jit(solution)/shard_map/ppermute | solution.py:442
  40.4 4.1 %collective-permute-start.5 = (bf16[512,128]{1,0:T(8,128)(2,1)S(1)}, bf16[512,128]{1,0:T(8,128)(2,1)S(1)}, u32[]{:S(2)}, u32[]{:S(2)}) collective-permute-start(bf16[512,128]{1,0:T(8,128)(2,1)S(1)} %get-tuple-element.42), channel_id=1, source_target_pairs={{0,252},{1,253},{2,254},{3,255},{4,0},{5,1},{6,2},{7,3},{8,4},{9,5... | collective-permute-start | bytes 393224 | tf_op jit(solution)/shard_map/ppermute | solution.py:442
  44.5 1.9 %collective-permute-start.6 = (bf16[512,128]{1,0:T(8,128)(2,1)S(1)}, bf16[512,128]{1,0:T(8,128)(2,1)S(1)}, u32[]{:S(2)}, u32[]{:S(2)}) collective-permute-start(bf16[512,128]{1,0:T(8,128)(2,1)S(1)} %get-tuple-element.43), channel_id=1, source_target_pairs={{0,1},{1,2},{2,3},{3,0},{4,253},{5,254},{6,255},{7,252},{8,9},{9,1... | collective-permute-start | bytes 393224 | tf_op jit(solution)/shard_map/ppermute | solution.py:442
  46.4 2.2 %collective-permute-start.7 = (bf16[512,128]{1,0:T(8,128)(2,1)S(1)}, bf16[512,128]{1,0:T(8,128)(2,1)S(1)}, u32[]{:S(2)}, u32[]{:S(2)}) collective-permute-start(bf16[512,128]{1,0:T(8,128)(2,1)S(1)} %get-tuple-element.44), channel_id=1, source_target_pairs={{0,0},{1,1},{2,2},{3,3},{4,252},{5,253},{6,254},{7,255},{8,8},{9,9... | collective-permute-start | bytes 393224 | tf_op jit(solution)/shard_map/ppermute | solution.py:442
  48.6 0.0 collective-permute-done.4.far_up
  48.6 1.5 %collective-permute-done.5.far_lo = bf16[512,128]{1,0:T(8,128)(2,1)S(1)} collective-permute-done((bf16[512,128]{1,0:T(8,128)(2,1)S(1)}, bf16[512,128]{1,0:T(8,128)(2,1)S(1)}, u32[]{:S(2)}, u32[]{:S(2)}) %collective-permute-start.5) | collective-permute-done | bytes 131104 | tf_op jit(solution)/shard_map/ppermute | solution.py:442
  50.1 0.0 collective-permute-done.6.near_up
  50.1 3.7 %collective-permute-done.7.near_lo = bf16[512,128]{1,0:T(8,128)(2,1)S(1)} collective-permute-done((bf16[512,128]{1,0:T(8,128)(2,1)S(1)}, bf16[512,128]{1,0:T(8,128)(2,1)S(1)}, u32[]{:S(2)}, u32[]{:S(2)}) %collective-permute-start.7) | collective-permute-done | bytes 131104 | tf_op jit(solution)/shard_map/ppermute | solution.py:442
  53.8 1.2 %from_tokens.1 = bf16[120,8,256]{2,1,0:T(8,128)(2,1)} custom-call(s32[1]{0:T(128)} %bitcast.h_ref, bf16[512,128]{1,0:T(8,128)(2,1)S(1)} %collective-permute-done.4.far_up, bf16[512,128]{1,0:T(8,128)(2,1)S(1)} %collective-permute-done.5.far_lo, bf16[512,128]{1,0:T(8,128)(2,1)S(1)} %collective-permute-done.6.near_up, ...), custom_call_target="tpu_custom_call" | custom-call | tf_op jit(solution)/shard_map/from_tokens/pallas_call | solution.py:375
Async XLA Ops:
  1.3 9.1 %collective-permute-start = (bf16[1088,128]{1,0:T(8,128)(2,1)S(1)}, bf16[1088,128]{1,0:T(8,128)(2,1)S(1)}, u32[]{:S(2)}, u32[]{:S(2)}) collective-permute-start(bf16[1088,128]{1,0:T(8,128)(2,1)S(1)} %get-tuple-element.26), channel_id=1, source_target_pairs={{0,4},{1,5},{2,6},{3,7},{4,0},{5,1},{6,2},{7,3},{8,12},{9,13},{10,... | collective-permute-start | bytes 835592 | tf_op jit(solution)/shard_map/ppermute | solution.py:442
  18.0 13.7 %collective-permute-start.1 = (bf16[512,128]{1,0:T(8,128)(2,1)S(1)}, bf16[512,128]{1,0:T(8,128)(2,1)S(1)}, u32[]{:S(2)}, u32[]{:S(2)}) collective-permute-start(bf16[512,128]{1,0:T(8,128)(2,1)S(1)} %get-tuple-element.32), channel_id=1, source_target_pairs={{0,11},{1,8},{2,9},{3,10},{4,15},{5,12},{6,13},{7,14},{8,19},{9,16... | collective-permute-start | bytes 393224 | tf_op jit(solution)/shard_map/ppermute | solution.py:442
  20.7 11.0 %collective-permute-start.2 = (bf16[512,128]{1,0:T(8,128)(2,1)S(1)}, bf16[512,128]{1,0:T(8,128)(2,1)S(1)}, u32[]{:S(2)}, u32[]{:S(2)}) collective-permute-start(bf16[512,128]{1,0:T(8,128)(2,1)S(1)} %get-tuple-element.33), channel_id=1, source_target_pairs={{0,8},{1,9},{2,10},{3,11},{4,12},{5,13},{6,14},{7,15},{8,16},{9,17... | collective-permute-start | bytes 393224 | tf_op jit(solution)/shard_map/ppermute | solution.py:442
  21.9 9.8 %collective-permute-start.3 = (bf16[512,128]{1,0:T(8,128)(2,1)S(1)}, bf16[512,128]{1,0:T(8,128)(2,1)S(1)}, u32[]{:S(2)}, u32[]{:S(2)}) collective-permute-start(bf16[512,128]{1,0:T(8,128)(2,1)S(1)} %get-tuple-element.34), channel_id=1, source_target_pairs={{0,3},{1,0},{2,1},{3,2},{4,7},{5,4},{6,5},{7,6},{8,11},{9,8},{10,9... | collective-permute-start | bytes 393224 | tf_op jit(solution)/shard_map/ppermute | solution.py:442
  38.9 9.7 %collective-permute-start.4 = (bf16[512,128]{1,0:T(8,128)(2,1)S(1)}, bf16[512,128]{1,0:T(8,128)(2,1)S(1)}, u32[]{:S(2)}, u32[]{:S(2)}) collective-permute-start(bf16[512,128]{1,0:T(8,128)(2,1)S(1)} %get-tuple-element.41), channel_id=1, source_target_pairs={{0,253},{1,254},{2,255},{3,252},{4,1},{5,2},{6,3},{7,0},{8,5},{9,6... | collective-permute-start | bytes 393224 | tf_op jit(solution)/shard_map/ppermute | solution.py:442
  40.4 9.7 %collective-permute-start.5 = (bf16[512,128]{1,0:T(8,128)(2,1)S(1)}, bf16[512,128]{1,0:T(8,128)(2,1)S(1)}, u32[]{:S(2)}, u32[]{:S(2)}) collective-permute-start(bf16[512,128]{1,0:T(8,128)(2,1)S(1)} %get-tuple-element.42), channel_id=1, source_target_pairs={{0,252},{1,253},{2,254},{3,255},{4,0},{5,1},{6,2},{7,3},{8,4},{9,5... | collective-permute-start | bytes 393224 | tf_op jit(solution)/shard_map/ppermute | solution.py:442
  44.5 5.6 %collective-permute-start.6 = (bf16[512,128]{1,0:T(8,128)(2,1)S(1)}, bf16[512,128]{1,0:T(8,128)(2,1)S(1)}, u32[]{:S(2)}, u32[]{:S(2)}) collective-permute-start(bf16[512,128]{1,0:T(8,128)(2,1)S(1)} %get-tuple-element.43), channel_id=1, source_target_pairs={{0,1},{1,2},{2,3},{3,0},{4,253},{5,254},{6,255},{7,252},{8,9},{9,1... | collective-permute-start | bytes 393224 | tf_op jit(solution)/shard_map/ppermute | solution.py:442
  46.4 7.4 %collective-permute-start.7 = (bf16[512,128]{1,0:T(8,128)(2,1)S(1)}, bf16[512,128]{1,0:T(8,128)(2,1)S(1)}, u32[]{:S(2)}, u32[]{:S(2)}) collective-permute-start(bf16[512,128]{1,0:T(8,128)(2,1)S(1)} %get-tuple-element.44), channel_id=1, source_target_pairs={{0,0},{1,1},{2,2},{3,3},{4,252},{5,253},{6,254},{7,255},{8,8},{9,9... | collective-permute-start | bytes 393224 | tf_op jit(solution)/shard_map/ppermute | solution.py:442

commit v13 on v11

--- a/solution.py
+++ b/solution.py
@@ -146,10 +146,11 @@
                 span = slice(j * LANES, (j + 1) * LANES)
                 mutual, own = mutual_scores[i % 2, pair, :, span], self_scores[i % 2, pair, :, span]
                 mixed.append(mix_head(2 * pair + j, mutual, own, qv_t, i))
-        for kind in range(2):
-            span = slice(kind * LANES, (kind + 1) * LANES)
-            part = by_channel([block[:, span] for block in mixed])
-            joined[i, kind * C : (kind + 1) * C] = part.astype(jnp.bfloat16)
+        parts = [
+            by_channel([block[:, kind * LANES : (kind + 1) * LANES] for block in mixed])
+            for kind in range(2)
+        ]
+        joined[i] = jnp.concatenate(parts, axis=0).astype(jnp.bfloat16)
 
 
 def finished(x, joined, w_prj, w_gu, w_dwn):
@@ -388,6 +389,11 @@
     )(h, *in_vmem(*pieces))
 
 
+def all_rows(part):
+    pad = jnp.zeros((LANES - C, part.shape[1]), jnp.float32)
+    return jnp.concatenate([part, pad], axis=0).astype(jnp.bfloat16)
+
+
 def prepare_kernel(w_mut, w_slf, w_prj, w_gte, w_upp, w_dwn, *outs):
     row = lax.broadcasted_iota(jnp.int32, (LANES, 3 * C), 0)
     col = lax.broadcasted_iota(jnp.int32, (LANES, 3 * C), 1)
@@ -402,13 +408,13 @@
         for i, w in enumerate((w_mut, w_slf)):
             w = w[layer]
             span = slice(i * LANES, (i + 1) * LANES)
-            w_k[:C, span] = matmul_nt(w, picks[1]).astype(jnp.bfloat16)
+            w_k[:, span] = all_rows(matmul_nt(w, picks[1]))
             w_qv[span, :C] = matmul_nt(picks[0], w).astype(jnp.bfloat16)
             span = slice((2 + i) * LANES, (3 + i) * LANES)
             w_qv[span, :C] = matmul_nt(picks[2], w).astype(jnp.bfloat16)
         w_p[:, :C] = w_prj[layer]
-        w_gu[:C, :FFN] = w_gte[layer]
-        w_gu[:C, 2 * LANES : 2 * LANES + FFN] = w_upp[layer]
+        w_gu[:, :FFN] = all_rows(w_gte[layer].astype(jnp.float32))
+        w_gu[:, 2 * LANES : 2 * LANES + FFN] = all_rows(w_upp[layer].astype(jnp.float32))
         w_d[:FFN, :C] = w_dwn[layer]
 
 

time: 54.7 us -> 54.7 us (level)
  no operation moved by 1% of the time
where the time goes in v13:
time: 54.7 us; the launch traced here: 53.7 us
  Pallas kernels  19.2 us (35%)
  waiting for transfers between devices  17.3 us (32%)
  starting transfers between devices  17.1 us (31%)
    ppermute x8, waiting for transfers between devices, send(): return lax.ppermute(value, ('frame', 'strip'), pairs)  17.3 us
    ppermute x8, starting transfers between devices, send(): return lax.ppermute(value, ('frame', 'strip'), pairs)  17.1 us
    pallas_call x1, Pallas kernels, layer_one(): pl.pallas_call(functools.partial(layer_one_kernel, count, first, last), o...  7.57 us
    pallas_call x1, Pallas kernels, layer_two(): pl.pallas_call(functools.partial(layer_two_kernel, count), out_shape=[tok...  7.19 us
    pallas_call x1, Pallas kernels, prepared(): pl.pallas_call(prepare_kernel, out_shape=[pltpu.VMEM(shape, jnp.bfloat16)...  1.92 us
    pallas_call x1, Pallas kernels, to_tokens(): pl.pallas_call(to_tokens_kernel, out_shape=[tokens_shape((HALF + 1) * TOK...  1.32 us
    pallas_call x1, Pallas kernels, from_tokens(): pl.pallas_call(from_tokens_kernel, out_shape=jax.ShapeDtypeStruct((C, WIN...  1.17 us
  transfers between devices with their start and end apart: 8, of which 3 were waited for; matrix products, arithmetic and copies ran while one was open for 0% of the time, Pallas kernels for 4%

profile of v13, /device:TPU:1, one launch (start us, length us, event | category | flops | bytes accessed | tf_op | source)
XLA Modules:
  0.0 53.7 jit_solution(10071654709998267099)
XLA Ops:
  0.0 1.3 %to_tokens.1 = (bf16[1088,128]{1,0:T(8,128)(2,1)S(1)}, bf16[1088,128]{1,0:T(8,128)(2,1)S(1)}) custom-call(s32[1]{0:T(128)} %bitcast.h_ref, bf16[120,8,256]{2,1,0:T(8,128)(2,1)} %bitcast.3), custom_call_target="tpu_custom_call" | custom-call | tf_op jit(solution)/shard_map/to_tokens/pallas_call | solution.py:322
  1.3 3.8 %collective-permute-start = (bf16[1088,128]{1,0:T(8,128)(2,1)S(1)}, bf16[1088,128]{1,0:T(8,128)(2,1)S(1)}, u32[]{:S(2)}, u32[]{:S(2)}) collective-permute-start(bf16[1088,128]{1,0:T(8,128)(2,1)S(1)} %get-tuple-element.26), channel_id=1, source_target_pairs={{0,4},{1,5},{2,6},{3,7},{4,0},{5,1},{6,2},{7,3},{8,12},{9,13},{10,... | collective-permute-start | bytes 835592 | tf_op jit(solution)/shard_map/ppermute | solution.py:448
  5.2 1.9 %prepare.1 = (bf16[128,256]{1,0:T(8,128)(2,1)S(1)}, bf16[512,128]{1,0:T(8,128)(2,1)S(1)}, bf16[240,128]{1,0:T(8,128)(2,1)S(1)}, bf16[128,512]{1,0:T(8,128)(2,1)S...) custom-call(bf16[2,120,360]{2,1,0:T(8,128)(2,1)} %w_mut.1, ...), custom_call_target="tpu_custom_call" | custom-call | tf_op jit(solution)/shard_map/prepare/pallas_call | solution.py:429
  7.1 3.4 %collective-permute-done.oth_ref = bf16[1088,128]{1,0:T(8,128)(2,1)S(1)} collective-permute-done((bf16[1088,128]{1,0:T(8,128)(2,1)S(1)}, bf16[1088,128]{1,0:T(8,128)(2,1)S(1)}, u32[]{:S(2)}, u32[]{:S(2)}) %collective-permute-start) | collective-permute-done | bytes 278560 | tf_op jit(solution)/shard_map/ppermute | solution.py:448
  10.5 7.6 %layer_one.1 = (bf16[512,128]{1,0:T(8,128)(2,1)S(1)}, bf16[512,128]{1,0:T(8,128)(2,1)S(1)}, bf16[512,128]{1,0:T(8,128)(2,1)S(1)}, bf16[512,128]{1,0:T(8,128)(2,1)S(1)}) custom-call(s32[1]{0:T(128)} %bitcast.h_ref, bf16[1088,128]{1,0:T(8,128)(2,1)S(1)} %get-tuple-element.25.own_ref, bf16[1088,128]{1,0:T(8,128)(2,1)S(1)} %collective-permute-done.oth_ref, ...), custom_call_target="tpu_custom_call" | custom-call | flops 8000000000 | bytes 1048576 | tf_op jit(solution)/shard_map/layer_one/pallas_call | solution.py:345
  18.1 3.5 %collective-permute-start.1 = (bf16[512,128]{1,0:T(8,128)(2,1)S(1)}, bf16[512,128]{1,0:T(8,128)(2,1)S(1)}, u32[]{:S(2)}, u32[]{:S(2)}) collective-permute-start(bf16[512,128]{1,0:T(8,128)(2,1)S(1)} %get-tuple-element.32), channel_id=1, source_target_pairs={{0,11},{1,8},{2,9},{3,10},{4,15},{5,12},{6,13},{7,14},{8,19},{9,16... | collective-permute-start | bytes 393224 | tf_op jit(solution)/shard_map/ppermute | solution.py:448
  21.6 1.2 %collective-permute-start.2 = (bf16[512,128]{1,0:T(8,128)(2,1)S(1)}, bf16[512,128]{1,0:T(8,128)(2,1)S(1)}, u32[]{:S(2)}, u32[]{:S(2)}) collective-permute-start(bf16[512,128]{1,0:T(8,128)(2,1)S(1)} %get-tuple-element.33), channel_id=1, source_target_pairs={{0,8},{1,9},{2,10},{3,11},{4,12},{5,13},{6,14},{7,15},{8,16},{9,17... | collective-permute-start | bytes 393224 | tf_op jit(solution)/shard_map/ppermute | solution.py:448
  22.8 0.3 collective-permute-start.3
  23.1 9.8 %collective-permute-done.1.rest_0_ = bf16[512,128]{1,0:T(8,128)(2,1)S(1)} collective-permute-done((bf16[512,128]{1,0:T(8,128)(2,1)S(1)}, bf16[512,128]{1,0:T(8,128)(2,1)S(1)}, u32[]{:S(2)}, u32[]{:S(2)}) %collective-permute-start.1) | collective-permute-done | bytes 131104 | tf_op jit(solution)/shard_map/ppermute | solution.py:448
  32.9 0.0 collective-permute-done.2.rest_1_
  32.9 0.0 collective-permute-done.3.rest_2_
  32.9 7.2 %layer_two.1 = (bf16[512,128]{1,0:T(8,128)(2,1)S(1)}, bf16[512,128]{1,0:T(8,128)(2,1)S(1)}, bf16[512,128]{1,0:T(8,128)(2,1)S(1)}, bf16[512,128]{1,0:T(8,128)(2,1)S(1)}) custom-call(s32[1]{0:T(128)} %bitcast.h_ref, bf16[512,128]{1,0:T(8,128)(2,1)S(1)} %collective-permute-done.1.rest_0_, bf16[512,128]{1,0:T(8,128)(2,1)S(1)} %collective-permute-done.2.rest_1_, ...), custom_call_target="tpu_custom_call" | custom-call | flops 8000000000 | bytes 1048576 | tf_op jit(solution)/shard_map/layer_two/pallas_call | solution.py:363
  40.1 5.2 %collective-permute-start.4 = (bf16[512,128]{1,0:T(8,128)(2,1)S(1)}, bf16[512,128]{1,0:T(8,128)(2,1)S(1)}, u32[]{:S(2)}, u32[]{:S(2)}) collective-permute-start(bf16[512,128]{1,0:T(8,128)(2,1)S(1)} %get-tuple-element.41), channel_id=1, source_target_pairs={{0,253},{1,254},{2,255},{3,252},{4,1},{5,2},{6,3},{7,0},{8,5},{9,6... | collective-permute-start | bytes 393224 | tf_op jit(solution)/shard_map/ppermute | solution.py:448
  45.3 0.9 %collective-permute-start.5 = (bf16[512,128]{1,0:T(8,128)(2,1)S(1)}, bf16[512,128]{1,0:T(8,128)(2,1)S(1)}, u32[]{:S(2)}, u32[]{:S(2)}) collective-permute-start(bf16[512,128]{1,0:T(8,128)(2,1)S(1)} %get-tuple-element.42), channel_id=1, source_target_pairs={{0,1},{1,2},{2,3},{3,0},{4,253},{5,254},{6,255},{7,252},{8,9},{9,1... | collective-permute-start | bytes 393224 | tf_op jit(solution)/shard_map/ppermute | solution.py:448
  46.1 1.5 %collective-permute-start.6 = (bf16[512,128]{1,0:T(8,128)(2,1)S(1)}, bf16[512,128]{1,0:T(8,128)(2,1)S(1)}, u32[]{:S(2)}, u32[]{:S(2)}) collective-permute-start(bf16[512,128]{1,0:T(8,128)(2,1)S(1)} %get-tuple-element.43), channel_id=1, source_target_pairs={{0,252},{1,253},{2,254},{3,255},{4,0},{5,1},{6,2},{7,3},{8,4},{9,5... | collective-permute-start | bytes 393224 | tf_op jit(solution)/shard_map/ppermute | solution.py:448
  47.7 0.7 %collective-permute-start.7 = (bf16[512,128]{1,0:T(8,128)(2,1)S(1)}, bf16[512,128]{1,0:T(8,128)(2,1)S(1)}, u32[]{:S(2)}, u32[]{:S(2)}) collective-permute-start(bf16[512,128]{1,0:T(8,128)(2,1)S(1)} %get-tuple-element.44), channel_id=1, source_target_pairs={{0,0},{1,1},{2,2},{3,3},{4,252},{5,253},{6,254},{7,255},{8,8},{9,9... | collective-permute-start | bytes 393224 | tf_op jit(solution)/shard_map/ppermute | solution.py:448
  48.3 0.0 collective-permute-done.4.far_up
  48.3 0.0 collective-permute-done.5.near_up
  48.4 4.0 %collective-permute-done.6.far_lo = bf16[512,128]{1,0:T(8,128)(2,1)S(1)} collective-permute-done((bf16[512,128]{1,0:T(8,128)(2,1)S(1)}, bf16[512,128]{1,0:T(8,128)(2,1)S(1)}, u32[]{:S(2)}, u32[]{:S(2)}) %collective-permute-start.6) | collective-permute-done | bytes 131104 | tf_op jit(solution)/shard_map/ppermute | solution.py:448
  52.4 0.0 collective-permute-done.7.near_lo
  52.4 1.2 %from_tokens.1 = bf16[120,8,256]{2,1,0:T(8,128)(2,1)} custom-call(s32[1]{0:T(128)} %bitcast.h_ref, bf16[512,128]{1,0:T(8,128)(2,1)S(1)} %collective-permute-done.4.far_up, bf16[512,128]{1,0:T(8,128)(2,1)S(1)} %collective-permute-done.5.near_up, bf16[512,128]{1,0:T(8,128)(2,1)S(1)} %collective-permute-done.6.far_lo, ...), custom_call_target="tpu_custom_call" | custom-call | tf_op jit(solution)/shard_map/from_tokens/pallas_call | solution.py:376
Async XLA Ops:
  1.3 9.2 %collective-permute-start = (bf16[1088,128]{1,0:T(8,128)(2,1)S(1)}, bf16[1088,128]{1,0:T(8,128)(2,1)S(1)}, u32[]{:S(2)}, u32[]{:S(2)}) collective-permute-start(bf16[1088,128]{1,0:T(8,128)(2,1)S(1)} %get-tuple-element.26), channel_id=1, source_target_pairs={{0,4},{1,5},{2,6},{3,7},{4,0},{5,1},{6,2},{7,3},{8,12},{9,13},{10,... | collective-permute-start | bytes 835592 | tf_op jit(solution)/shard_map/ppermute | solution.py:448
  18.1 14.8 %collective-permute-start.1 = (bf16[512,128]{1,0:T(8,128)(2,1)S(1)}, bf16[512,128]{1,0:T(8,128)(2,1)S(1)}, u32[]{:S(2)}, u32[]{:S(2)}) collective-permute-start(bf16[512,128]{1,0:T(8,128)(2,1)S(1)} %get-tuple-element.32), channel_id=1, source_target_pairs={{0,11},{1,8},{2,9},{3,10},{4,15},{5,12},{6,13},{7,14},{8,19},{9,16... | collective-permute-start | bytes 393224 | tf_op jit(solution)/shard_map/ppermute | solution.py:448
  21.6 11.3 %collective-permute-start.2 = (bf16[512,128]{1,0:T(8,128)(2,1)S(1)}, bf16[512,128]{1,0:T(8,128)(2,1)S(1)}, u32[]{:S(2)}, u32[]{:S(2)}) collective-permute-start(bf16[512,128]{1,0:T(8,128)(2,1)S(1)} %get-tuple-element.33), channel_id=1, source_target_pairs={{0,8},{1,9},{2,10},{3,11},{4,12},{5,13},{6,14},{7,15},{8,16},{9,17... | collective-permute-start | bytes 393224 | tf_op jit(solution)/shard_map/ppermute | solution.py:448
  22.8 10.1 %collective-permute-start.3 = (bf16[512,128]{1,0:T(8,128)(2,1)S(1)}, bf16[512,128]{1,0:T(8,128)(2,1)S(1)}, u32[]{:S(2)}, u32[]{:S(2)}) collective-permute-start(bf16[512,128]{1,0:T(8,128)(2,1)S(1)} %get-tuple-element.34), channel_id=1, source_target_pairs={{0,3},{1,0},{2,1},{3,2},{4,7},{5,4},{6,5},{7,6},{8,11},{9,8},{10,9... | collective-permute-start | bytes 393224 | tf_op jit(solution)/shard_map/ppermute | solution.py:448
  40.1 8.3 %collective-permute-start.4 = (bf16[512,128]{1,0:T(8,128)(2,1)S(1)}, bf16[512,128]{1,0:T(8,128)(2,1)S(1)}, u32[]{:S(2)}, u32[]{:S(2)}) collective-permute-start(bf16[512,128]{1,0:T(8,128)(2,1)S(1)} %get-tuple-element.41), channel_id=1, source_target_pairs={{0,253},{1,254},{2,255},{3,252},{4,1},{5,2},{6,3},{7,0},{8,5},{9,6... | collective-permute-start | bytes 393224 | tf_op jit(solution)/shard_map/ppermute | solution.py:448
  45.3 3.1 %collective-permute-start.5 = (bf16[512,128]{1,0:T(8,128)(2,1)S(1)}, bf16[512,128]{1,0:T(8,128)(2,1)S(1)}, u32[]{:S(2)}, u32[]{:S(2)}) collective-permute-start(bf16[512,128]{1,0:T(8,128)(2,1)S(1)} %get-tuple-element.42), channel_id=1, source_target_pairs={{0,1},{1,2},{2,3},{3,0},{4,253},{5,254},{6,255},{7,252},{8,9},{9,1... | collective-permute-start | bytes 393224 | tf_op jit(solution)/shard_map/ppermute | solution.py:448
  46.1 6.3 %collective-permute-start.6 = (bf16[512,128]{1,0:T(8,128)(2,1)S(1)}, bf16[512,128]{1,0:T(8,128)(2,1)S(1)}, u32[]{:S(2)}, u32[]{:S(2)}) collective-permute-start(bf16[512,128]{1,0:T(8,128)(2,1)S(1)} %get-tuple-element.43), channel_id=1, source_target_pairs={{0,252},{1,253},{2,254},{3,255},{4,0},{5,1},{6,2},{7,3},{8,4},{9,5... | collective-permute-start | bytes 393224 | tf_op jit(solution)/shard_map/ppermute | solution.py:448
  47.7 4.7 %collective-permute-start.7 = (bf16[512,128]{1,0:T(8,128)(2,1)S(1)}, bf16[512,128]{1,0:T(8,128)(2,1)S(1)}, u32[]{:S(2)}, u32[]{:S(2)}) collective-permute-start(bf16[512,128]{1,0:T(8,128)(2,1)S(1)} %get-tuple-element.44), channel_id=1, source_target_pairs={{0,0},{1,1},{2,2},{3,3},{4,252},{5,253},{6,254},{7,255},{8,8},{9,9... | collective-permute-start | bytes 393224 | tf_op jit(solution)/shard_map/ppermute | solution.py:448

commit v14 on v13

--- a/solution.py
+++ b/solution.py
@@ -256,11 +256,11 @@
             pair = (jnp.where(even, moved, kept), jnp.where(even, kept, moved))
             for f in range(2):
                 part = pair[f].astype(jnp.bfloat16)
-                for j, out in enumerate((outs[f], outs[2 + f])):
+                for j, out in enumerate((outs[f], outs[3 - f])):
                     out[spans[i]] = part[j * half_tok : (j + 1) * half_tok]
 
 
-def from_tokens_kernel(h_ref, far_up, near_up, far_lo, near_lo, out_ref, rows, wide, ready, sems):
+def from_tokens_kernel(h_ref, far_up, near_up, near_lo, far_lo, out_ref, rows, wide, ready, sems):
     edge = WIN // 2
 
     def place(h):
@@ -465,12 +465,12 @@
         pieces.append((moved_up, moved_lo, kept_up, kept_lo))
     home = []
     for k in chunks:
-        far_up, near_up, far_lo, near_lo = layer_two(k, h, pieces[k], w_two)
+        far_up, near_up, near_lo, far_lo = layer_two(k, h, pieces[k], w_two)
         far_up = send(far_up, -1, -1, 1)
         near_up = send(near_up, 0, -2, 1)
+        near_lo = send(near_lo, 0, -2, 0)
         far_lo = send(far_lo, -1, -1, 0)
-        near_lo = send(near_lo, 0, -2, 0)
-        home += [far_up, near_up, far_lo, near_lo]
+        home += [far_up, near_up, near_lo, far_lo]
     return from_tokens(h, home)[None]
 
 

time: 54.7 us -> 55.4 us (1.013)
  starting transfers between devices: 17.1 us -> 18.6 us
  waiting for transfers between devices: 17.3 us -> 16.6 us
    ppermute x8, starting transfers between devices: 17.1 us -> 18.6 us  [send(): return lax.ppermute(value, ('frame', 'strip'), pairs)]
    ppermute x8, waiting for transfers between devices: 17.3 us -> 16.6 us  [send(): return lax.ppermute(value, ('frame', 'strip'), pairs)]
where the time goes in v14:
time: 55.4 us; the launch traced here: 54.7 us
  Pallas kernels  19.2 us (35%)
  starting transfers between devices  18.6 us (34%)
  waiting for transfers between devices  16.6 us (30%)
    ppermute x8, starting transfers between devices, send(): return lax.ppermute(value, ('frame', 'strip'), pairs)  18.6 us
    ppermute x8, waiting for transfers between devices, send(): return lax.ppermute(value, ('frame', 'strip'), pairs)  16.6 us
    pallas_call x1, Pallas kernels, layer_one(): pl.pallas_call(functools.partial(layer_one_kernel, count, first, last), o...  7.57 us
    pallas_call x1, Pallas kernels, layer_two(): pl.pallas_call(functools.partial(layer_two_kernel, count), out_shape=[tok...  7.19 us
    pallas_call x1, Pallas kernels, prepared(): pl.pallas_call(prepare_kernel, out_shape=[pltpu.VMEM(shape, jnp.bfloat16)...  1.92 us
    pallas_call x1, Pallas kernels, to_tokens(): pl.pallas_call(to_tokens_kernel, out_shape=[tokens_shape((HALF + 1) * TOK...  1.32 us
    pallas_call x1, Pallas kernels, from_tokens(): pl.pallas_call(from_tokens_kernel, out_shape=jax.ShapeDtypeStruct((C, WIN...  1.17 us
  transfers between devices with their start and end apart: 8, of which 3 were waited for; matrix products, arithmetic and copies ran while one was open for 0% of the time, Pallas kernels for 4%

profile of v14, /device:TPU:1, one launch (start us, length us, event | category | flops | bytes accessed | tf_op | source)
XLA Modules:
  0.0 54.7 jit_solution(16446568619810234796)
XLA Ops:
  0.0 1.3 %to_tokens.1 = (bf16[1088,128]{1,0:T(8,128)(2,1)S(1)}, bf16[1088,128]{1,0:T(8,128)(2,1)S(1)}) custom-call(s32[1]{0:T(128)} %bitcast.h_ref, bf16[120,8,256]{2,1,0:T(8,128)(2,1)} %bitcast.3), custom_call_target="tpu_custom_call" | custom-call | tf_op jit(solution)/shard_map/to_tokens/pallas_call | solution.py:322
  1.3 3.8 %collective-permute-start = (bf16[1088,128]{1,0:T(8,128)(2,1)S(1)}, bf16[1088,128]{1,0:T(8,128)(2,1)S(1)}, u32[]{:S(2)}, u32[]{:S(2)}) collective-permute-start(bf16[1088,128]{1,0:T(8,128)(2,1)S(1)} %get-tuple-element.26), channel_id=1, source_target_pairs={{0,4},{1,5},{2,6},{3,7},{4,0},{5,1},{6,2},{7,3},{8,12},{9,13},{10,... | collective-permute-start | bytes 835592 | tf_op jit(solution)/shard_map/ppermute | solution.py:448
  5.2 1.9 %prepare.1 = (bf16[128,256]{1,0:T(8,128)(2,1)S(1)}, bf16[512,128]{1,0:T(8,128)(2,1)S(1)}, bf16[240,128]{1,0:T(8,128)(2,1)S(1)}, bf16[128,512]{1,0:T(8,128)(2,1)S...) custom-call(bf16[2,120,360]{2,1,0:T(8,128)(2,1)} %w_mut.1, ...), custom_call_target="tpu_custom_call" | custom-call | tf_op jit(solution)/shard_map/prepare/pallas_call | solution.py:429
  7.1 3.4 %collective-permute-done.oth_ref = bf16[1088,128]{1,0:T(8,128)(2,1)S(1)} collective-permute-done((bf16[1088,128]{1,0:T(8,128)(2,1)S(1)}, bf16[1088,128]{1,0:T(8,128)(2,1)S(1)}, u32[]{:S(2)}, u32[]{:S(2)}) %collective-permute-start) | collective-permute-done | bytes 278560 | tf_op jit(solution)/shard_map/ppermute | solution.py:448
  10.5 7.6 %layer_one.1 = (bf16[512,128]{1,0:T(8,128)(2,1)S(1)}, bf16[512,128]{1,0:T(8,128)(2,1)S(1)}, bf16[512,128]{1,0:T(8,128)(2,1)S(1)}, bf16[512,128]{1,0:T(8,128)(2,1)S(1)}) custom-call(s32[1]{0:T(128)} %bitcast.h_ref, bf16[1088,128]{1,0:T(8,128)(2,1)S(1)} %get-tuple-element.25.own_ref, bf16[1088,128]{1,0:T(8,128)(2,1)S(1)} %collective-permute-done.oth_ref, ...), custom_call_target="tpu_custom_call" | custom-call | flops 8000000000 | bytes 1048576 | tf_op jit(solution)/shard_map/layer_one/pallas_call | solution.py:345
  18.1 3.5 %collective-permute-start.1 = (bf16[512,128]{1,0:T(8,128)(2,1)S(1)}, bf16[512,128]{1,0:T(8,128)(2,1)S(1)}, u32[]{:S(2)}, u32[]{:S(2)}) collective-permute-start(bf16[512,128]{1,0:T(8,128)(2,1)S(1)} %get-tuple-element.32), channel_id=1, source_target_pairs={{0,11},{1,8},{2,9},{3,10},{4,15},{5,12},{6,13},{7,14},{8,19},{9,16... | collective-permute-start | bytes 393224 | tf_op jit(solution)/shard_map/ppermute | solution.py:448
  21.6 1.2 %collective-permute-start.2 = (bf16[512,128]{1,0:T(8,128)(2,1)S(1)}, bf16[512,128]{1,0:T(8,128)(2,1)S(1)}, u32[]{:S(2)}, u32[]{:S(2)}) collective-permute-start(bf16[512,128]{1,0:T(8,128)(2,1)S(1)} %get-tuple-element.33), channel_id=1, source_target_pairs={{0,8},{1,9},{2,10},{3,11},{4,12},{5,13},{6,14},{7,15},{8,16},{9,17... | collective-permute-start | bytes 393224 | tf_op jit(solution)/shard_map/ppermute | solution.py:448
  22.8 0.3 collective-permute-start.3
  23.1 9.8 %collective-permute-done.1.rest_0_ = bf16[512,128]{1,0:T(8,128)(2,1)S(1)} collective-permute-done((bf16[512,128]{1,0:T(8,128)(2,1)S(1)}, bf16[512,128]{1,0:T(8,128)(2,1)S(1)}, u32[]{:S(2)}, u32[]{:S(2)}) %collective-permute-start.1) | collective-permute-done | bytes 131104 | tf_op jit(solution)/shard_map/ppermute | solution.py:448
  32.9 0.0 collective-permute-done.2.rest_1_
  32.9 0.0 collective-permute-done.3.rest_2_
  32.9 7.2 %layer_two.1 = (bf16[512,128]{1,0:T(8,128)(2,1)S(1)}, bf16[512,128]{1,0:T(8,128)(2,1)S(1)}, bf16[512,128]{1,0:T(8,128)(2,1)S(1)}, bf16[512,128]{1,0:T(8,128)(2,1)S(1)}) custom-call(s32[1]{0:T(128)} %bitcast.h_ref, bf16[512,128]{1,0:T(8,128)(2,1)S(1)} %collective-permute-done.1.rest_0_, bf16[512,128]{1,0:T(8,128)(2,1)S(1)} %collective-permute-done.2.rest_1_, ...), custom_call_target="tpu_custom_call" | custom-call | flops 8000000000 | bytes 1048576 | tf_op jit(solution)/shard_map/layer_two/pallas_call | solution.py:363
  40.1 5.2 %collective-permute-start.4 = (bf16[512,128]{1,0:T(8,128)(2,1)S(1)}, bf16[512,128]{1,0:T(8,128)(2,1)S(1)}, u32[]{:S(2)}, u32[]{:S(2)}) collective-permute-start(bf16[512,128]{1,0:T(8,128)(2,1)S(1)} %get-tuple-element.41), channel_id=1, source_target_pairs={{0,253},{1,254},{2,255},{3,252},{4,1},{5,2},{6,3},{7,0},{8,5},{9,6... | collective-permute-start | bytes 393224 | tf_op jit(solution)/shard_map/ppermute | solution.py:448
  45.3 0.9 %collective-permute-start.5 = (bf16[512,128]{1,0:T(8,128)(2,1)S(1)}, bf16[512,128]{1,0:T(8,128)(2,1)S(1)}, u32[]{:S(2)}, u32[]{:S(2)}) collective-permute-start(bf16[512,128]{1,0:T(8,128)(2,1)S(1)} %get-tuple-element.42), channel_id=1, source_target_pairs={{0,1},{1,2},{2,3},{3,0},{4,253},{5,254},{6,255},{7,252},{8,9},{9,1... | collective-permute-start | bytes 393224 | tf_op jit(solution)/shard_map/ppermute | solution.py:448
  46.1 0.7 %collective-permute-start.6 = (bf16[512,128]{1,0:T(8,128)(2,1)S(1)}, bf16[512,128]{1,0:T(8,128)(2,1)S(1)}, u32[]{:S(2)}, u32[]{:S(2)}) collective-permute-start(bf16[512,128]{1,0:T(8,128)(2,1)S(1)} %get-tuple-element.43), channel_id=1, source_target_pairs={{0,0},{1,1},{2,2},{3,3},{4,252},{5,253},{6,254},{7,255},{8,8},{9,9... | collective-permute-start | bytes 393224 | tf_op jit(solution)/shard_map/ppermute | solution.py:448
  46.8 3.1 %collective-permute-start.7 = (bf16[512,128]{1,0:T(8,128)(2,1)S(1)}, bf16[512,128]{1,0:T(8,128)(2,1)S(1)}, u32[]{:S(2)}, u32[]{:S(2)}) collective-permute-start(bf16[512,128]{1,0:T(8,128)(2,1)S(1)} %get-tuple-element.44), channel_id=1, source_target_pairs={{0,252},{1,253},{2,254},{3,255},{4,0},{5,1},{6,2},{7,3},{8,4},{9,5... | collective-permute-start | bytes 393224 | tf_op jit(solution)/shard_map/ppermute | solution.py:448
  49.9 0.0 collective-permute-done.4.far_up
  49.9 0.0 collective-permute-done.5.near_up
  49.9 0.0 collective-permute-done.6.near_lo
  49.9 3.4 %collective-permute-done.7.far_lo = bf16[512,128]{1,0:T(8,128)(2,1)S(1)} collective-permute-done((bf16[512,128]{1,0:T(8,128)(2,1)S(1)}, bf16[512,128]{1,0:T(8,128)(2,1)S(1)}, u32[]{:S(2)}, u32[]{:S(2)}) %collective-permute-start.7) | collective-permute-done | bytes 131104 | tf_op jit(solution)/shard_map/ppermute | solution.py:448
  53.3 1.2 %from_tokens.1 = bf16[120,8,256]{2,1,0:T(8,128)(2,1)} custom-call(s32[1]{0:T(128)} %bitcast.h_ref, bf16[512,128]{1,0:T(8,128)(2,1)S(1)} %collective-permute-done.4.far_up, bf16[512,128]{1,0:T(8,128)(2,1)S(1)} %collective-permute-done.5.near_up, bf16[512,128]{1,0:T(8,128)(2,1)S(1)} %collective-permute-done.6.near_lo, ...), custom_call_target="tpu_custom_call" | custom-call | tf_op jit(solution)/shard_map/from_tokens/pallas_call | solution.py:376
Async XLA Ops:
  1.3 9.2 %collective-permute-start = (bf16[1088,128]{1,0:T(8,128)(2,1)S(1)}, bf16[1088,128]{1,0:T(8,128)(2,1)S(1)}, u32[]{:S(2)}, u32[]{:S(2)}) collective-permute-start(bf16[1088,128]{1,0:T(8,128)(2,1)S(1)} %get-tuple-element.26), channel_id=1, source_target_pairs={{0,4},{1,5},{2,6},{3,7},{4,0},{5,1},{6,2},{7,3},{8,12},{9,13},{10,... | collective-permute-start | bytes 835592 | tf_op jit(solution)/shard_map/ppermute | solution.py:448
  18.1 14.8 %collective-permute-start.1 = (bf16[512,128]{1,0:T(8,128)(2,1)S(1)}, bf16[512,128]{1,0:T(8,128)(2,1)S(1)}, u32[]{:S(2)}, u32[]{:S(2)}) collective-permute-start(bf16[512,128]{1,0:T(8,128)(2,1)S(1)} %get-tuple-element.32), channel_id=1, source_target_pairs={{0,11},{1,8},{2,9},{3,10},{4,15},{5,12},{6,13},{7,14},{8,19},{9,16... | collective-permute-start | bytes 393224 | tf_op jit(solution)/shard_map/ppermute | solution.py:448
  21.6 11.3 %collective-permute-start.2 = (bf16[512,128]{1,0:T(8,128)(2,1)S(1)}, bf16[512,128]{1,0:T(8,128)(2,1)S(1)}, u32[]{:S(2)}, u32[]{:S(2)}) collective-permute-start(bf16[512,128]{1,0:T(8,128)(2,1)S(1)} %get-tuple-element.33), channel_id=1, source_target_pairs={{0,8},{1,9},{2,10},{3,11},{4,12},{5,13},{6,14},{7,15},{8,16},{9,17... | collective-permute-start | bytes 393224 | tf_op jit(solution)/shard_map/ppermute | solution.py:448
  22.8 10.1 %collective-permute-start.3 = (bf16[512,128]{1,0:T(8,128)(2,1)S(1)}, bf16[512,128]{1,0:T(8,128)(2,1)S(1)}, u32[]{:S(2)}, u32[]{:S(2)}) collective-permute-start(bf16[512,128]{1,0:T(8,128)(2,1)S(1)} %get-tuple-element.34), channel_id=1, source_target_pairs={{0,3},{1,0},{2,1},{3,2},{4,7},{5,4},{6,5},{7,6},{8,11},{9,8},{10,9... | collective-permute-start | bytes 393224 | tf_op jit(solution)/shard_map/ppermute | solution.py:448
  40.1 9.8 %collective-permute-start.4 = (bf16[512,128]{1,0:T(8,128)(2,1)S(1)}, bf16[512,128]{1,0:T(8,128)(2,1)S(1)}, u32[]{:S(2)}, u32[]{:S(2)}) collective-permute-start(bf16[512,128]{1,0:T(8,128)(2,1)S(1)} %get-tuple-element.41), channel_id=1, source_target_pairs={{0,253},{1,254},{2,255},{3,252},{4,1},{5,2},{6,3},{7,0},{8,5},{9,6... | collective-permute-start | bytes 393224 | tf_op jit(solution)/shard_map/ppermute | solution.py:448
  45.3 4.6 %collective-permute-start.5 = (bf16[512,128]{1,0:T(8,128)(2,1)S(1)}, bf16[512,128]{1,0:T(8,128)(2,1)S(1)}, u32[]{:S(2)}, u32[]{:S(2)}) collective-permute-start(bf16[512,128]{1,0:T(8,128)(2,1)S(1)} %get-tuple-element.42), channel_id=1, source_target_pairs={{0,1},{1,2},{2,3},{3,0},{4,253},{5,254},{6,255},{7,252},{8,9},{9,1... | collective-permute-start | bytes 393224 | tf_op jit(solution)/shard_map/ppermute | solution.py:448
  46.1 3.8 %collective-permute-start.6 = (bf16[512,128]{1,0:T(8,128)(2,1)S(1)}, bf16[512,128]{1,0:T(8,128)(2,1)S(1)}, u32[]{:S(2)}, u32[]{:S(2)}) collective-permute-start(bf16[512,128]{1,0:T(8,128)(2,1)S(1)} %get-tuple-element.43), channel_id=1, source_target_pairs={{0,0},{1,1},{2,2},{3,3},{4,252},{5,253},{6,254},{7,255},{8,8},{9,9... | collective-permute-start | bytes 393224 | tf_op jit(solution)/shard_map/ppermute | solution.py:448
  46.8 6.5 %collective-permute-start.7 = (bf16[512,128]{1,0:T(8,128)(2,1)S(1)}, bf16[512,128]{1,0:T(8,128)(2,1)S(1)}, u32[]{:S(2)}, u32[]{:S(2)}) collective-permute-start(bf16[512,128]{1,0:T(8,128)(2,1)S(1)} %get-tuple-element.44), channel_id=1, source_target_pairs={{0,252},{1,253},{2,254},{3,255},{4,0},{5,1},{6,2},{7,3},{8,4},{9,5... | collective-permute-start | bytes 393224 | tf_op jit(solution)/shard_map/ppermute | solution.py:448
